TPU v7x, 128 devices: a whole 4x4x4 slice. The times are simulated.
128 devices in a mesh: dp: 16 (over x_lo, z, core), seq: 8 (over x_hi, y).
Axes of the slice: x: 4 (x_hi: 2, x_lo: 2; x = x_hi * 2 + x_lo), y: 4, z: 4, core: 2. Of those that a mesh axis runs over, the one named last changes fastest.
Arguments:
- hidden_acts: bfloat16 [65536, 14336], P(('dp', 'seq')), may hold values from -8 to 8
- out_grads: bfloat16 [65536, 8192], P(('dp', 'seq')), may hold values from -8 to 8
- val_acts: bfloat16 [512, 14336], P(('dp', 'seq')), may hold values from -6 to 6
- val_grads: bfloat16 [512, 8192], P(('dp', 'seq')), may hold values from -6 to 6
- val_ids: int32 [512], P(('dp', 'seq')), may hold values from 0 to 3, never falling along the last dimension, each value on 1 to 256 neighbouring positions
Outputs:
- token_scores: float32 [4, 65536], P(None, ('dp', 'seq'))
- block_gram: float32 [512, 4], P(('dp', 'seq'))
Inputs may be any that keep to these rules, and one draw needn't show every extreme that they name: val_ids never fall along the array; each of the 4 validation sequences has 1 to 256 tokens, and one has exactly 256.
All inputs are finite; a program needn't handle non-finite values.
Results may differ from a plain program's by a relative error of at most 0.0003.
Values may be sent and summed in bfloat16 or wider, within the bound.
No kernel may reach another device: no remote copies, remote signals or barrier semaphores. Data moves between devices by JAX's collectives and lax.ppermute only.
A program may use at most 128 MiB of HBM per device.

v0:
```python
import math

import jax
import jax.numpy as jnp
from jax import lax
from jax.sharding import PartitionSpec as P

D = 8192
FF = 14336
BLK = 128
NVAL = 4


def shards(hidden_acts, out_grads, val_acts, val_grads, val_ids):
    tok_count = hidden_acts.shape[0]
    labels = jnp.arange(NVAL, dtype=jnp.int32)
    own_onehot = (val_ids[:, None] == labels[None, :]).astype(jnp.float32)
    piece_acts = lax.all_gather(val_acts, ("dp", "seq"), axis=0, tiled=True)
    piece_grads = lax.all_gather(val_grads, ("dp", "seq"), axis=0, tiled=True)
    piece_ids = lax.all_gather(val_ids, ("dp", "seq"), axis=0, tiled=True)
    piece_onehot = (piece_ids[:, None] == labels[None, :]).astype(jnp.float32)
    cross = jnp.dot(hidden_acts, piece_acts.T, preferred_element_type=jnp.float32) * jnp.dot(
        out_grads, piece_grads.T, preferred_element_type=jnp.float32
    )
    scores_raw = jnp.einsum("tp,pv->vt", cross, piece_onehot, precision=lax.Precision.HIGHEST)
    val_kernel = jnp.dot(val_acts, piece_acts.T, preferred_element_type=jnp.float32) * jnp.dot(
        val_grads, piece_grads.T, preferred_element_type=jnp.float32
    )
    partial_value = jnp.einsum(
        "sv,sp,pv->v", own_onehot, val_kernel, piece_onehot, precision=lax.Precision.HIGHEST
    )
    scores_raw, partial_value = (scores_raw, partial_value)
    val_norm = lax.psum(partial_value, ("dp", "seq"))
    token_scores = scores_raw * lax.rsqrt(val_norm + 1e-06)[:, None]
    self_kernel = jnp.dot(hidden_acts, hidden_acts.T, preferred_element_type=jnp.float32) * jnp.dot(
        out_grads, out_grads.T, preferred_element_type=jnp.float32
    )
    block_count = tok_count // BLK
    divisor = float(BLK) * math.sqrt(float(FF) * float(D))
    blocks = self_kernel.reshape(block_count, BLK, block_count, BLK).sum(axis=(1, 3)) / divisor
    block_gram = jnp.tril(blocks, -1)
    return (token_scores, block_gram)


def solution(mesh):
    return jax.shard_map(
        shards,
        mesh=mesh,
        in_specs=(
            P(("dp", "seq"), None),
            P(("dp", "seq"), None),
            P(("dp", "seq"), None),
            P(("dp", "seq"), None),
            P(("dp", "seq")),
        ),
        out_specs=(P(None, ("dp", "seq")), P(("dp", "seq"), None)),
        check_vma=False,
    )
```

profile of v0, /device:TPU:1, one launch (start us, length us, event | category | flops | bytes accessed | tf_op | source)
XLA Modules:
  0.0 779.7 jit_solution(11515166079979061487)
XLA Ops:
  7.2 0.0 all-gather.7.cloned.1.call-start
  7.2 0.7 all-gather.7.cloned.1.call-update
  7.9 0.0 all-gather.5.cloned.1.call-start
  7.9 0.7 all-gather.5.cloned.1.call-update
  8.7 0.7 fusion.7
  9.4 0.1 copy.11
  9.5 10.4 %fusion.10 = f32[512,512]{1,0:T(8,128)S(1)} fusion(bf16[512,8192]{1,0:T(8,128)(2,1)} %param.6), kind=kOutput, calls=%fused_computation.19 | convolution fusion | flops 4294967296 | bytes 9437184 | tf_op jit(solution)/shard_map/dot_general | solution.py:35
  19.9 0.0 copy-start.3
  19.9 17.5 %convolution_multiply_fusion = f32[512,512]{1,0:T(8,128)S(1)} fusion(f32[512,512]{1,0:T(8,128)S(1)} %fusion.10, bf16[512,14336]{1,0:T(8,128)(2,1)} %param.5), kind=kOutput, calls=%fused_computation | convolution fusion | flops 7516454912 | bytes 16777216 | tf_op jit(solution)/shard_map/dot_general | solution.py:35
  37.4 0.0 copy-start.2
  37.4 0.4 reshape.10
  37.8 0.0 copy-done.3
  37.8 0.2 dynamic-update-slice
  38.0 0.3 reduce_sum.9
  38.3 68.8 %all-reduce = s32[512]{0:T(512)S(1)} all-reduce(s32[512]{0:T(512)S(1)} %dynamic-update-slice), channel_id=1, replica_groups=mesh['dp'=16,'seq'=8] {'dp','seq'}, use_global_device_ids=true, to_apply=%add | all-reduce | flops 512 | bytes 4096
  107.1 0.7 multiply_select_fusion
  107.8 217.8 %all-gather.7.cloned.1.call-done = bf16[128,4,8192]{2,1,0:T(4,128)(2,1)} async-done(((bf16[1,4,8192]{2,1,0:T(4,128)(2,1)}), bf16[128,4,8192]{2,1,0:T(4,128)(2,1)}) %all-gather.7.cloned.1.call-update) | async-done | bytes 8388624 | tf_op jit(solution)/shard_map/all_gather | solution.py:19
  325.6 12.5 %reshape.16 = bf16[512,8192]{1,0:T(8,128)(2,1)} reshape(bf16[128,4,8192]{2,1,0:T(4,128)(2,1)} %all-gather.7.cloned.1.call-done) | data formatting | bytes 16777216
  338.1 0.0 copy-done.2
  338.1 5.7 fusion.9
  343.8 0.0 copy-start.1
  343.8 308.1 %all-gather.5.cloned.1.call-done = bf16[128,4,14336]{2,1,0:T(4,128)(2,1)} async-done(((bf16[1,4,14336]{2,1,0:T(4,128)(2,1)}), bf16[128,4,14336]{2,1,0:T(4,128)(2,1)}) %all-gather.5.cloned.1.call-update) | async-done | bytes 14680080 | tf_op jit(solution)/shard_map/all_gather | solution.py:18
  651.9 20.7 %reshape.14 = bf16[512,14336]{1,0:T(8,128)(2,1)} reshape(bf16[128,4,14336]{2,1,0:T(4,128)(2,1)} %all-gather.5.cloned.1.call-done) | data formatting | bytes 29360128
  672.6 0.0 copy-done.1
  672.6 0.0 copy-start
  672.6 9.2 %convolution_multiply_fusion.2 = f32[4,512]{1,0:T(4,128)S(1)} fusion(f32[4,512]{1,0:T(4,128)S(1)} %fusion.9, bf16[4,14336]{1,0:T(4,128)(2,1)S(1)} %copy-done.1, bf16[512,14336]{1,0:T(8,128)(2,1)} %reshape.14), kind=kOutput, calls=%fused_computation.2 | convolution fusion | flops 58722304 | bytes 14811136 | tf_op jit(solution)/shard_map/dot_general | solution.py:26
  681.8 0.5 fusion
  682.3 0.0 copy-done
  682.3 8.4 %fusion.8 = f32[512,512]{1,0:T(8,128)S(1)} fusion(bf16[512,8192]{1,0:T(8,128)(2,1)} %param.6, bf16[512,8192]{1,0:T(8,128)(2,1)S(1)} %copy-done), kind=kOutput, calls=%fused_computation.17 | convolution fusion | flops 4294967296 | bytes 17825792 | tf_op jit(solution)/shard_map/dot_general | solution.py:22
  690.7 65.5 %psum.7 = f32[4]{0:T(128)S(1)} all-reduce(f32[4]{0:T(128)S(1)} %fusion), channel_id=1, replica_groups=mesh['dp'=16,'seq'=8] {'dp','seq'}, use_global_device_ids=true, to_apply=%region_0.0 | all-reduce | flops 4 | bytes 32 | tf_op jit(solution)/shard_map/psum | solution.py:33
  756.1 15.4 %convolution_multiply_fusion.1 = f32[512,512]{1,0:T(8,128)S(1)} fusion(f32[512,512]{1,0:T(8,128)S(1)} %fusion.8, bf16[512,14336]{1,0:T(8,128)(2,1)} %param.5, bf16[512,14336]{1,0:T(8,128)(2,1)} %reshape.14), kind=kOutput, calls=%fused_computation.1 | convolution fusion | flops 7516454912 | bytes 31457280 | tf_op jit(solution)/shard_map/dot_general | solution.py:22
  771.5 1.3 convolution_multiply_fusion.3
  (3 shorter events, 0.0 us)
Async XLA Ops:
  7.2 318.4 %all-gather.7.cloned.1.call-start = ((), (), s32[]{:S(2)}) async-start(), calls=%async_computation.1 | async-start | bytes 8454144 | tf_op jit(solution)/shard_map/all_gather | solution.py:19
  7.9 644.0 %all-gather.5.cloned.1.call-start = ((), (), s32[]{:S(2)}) async-start(), calls=%async_computation | async-start | bytes 14794752 | tf_op jit(solution)/shard_map/all_gather | solution.py:18
  19.9 17.9 %copy-start.3 = (s32[4]{0:T(128)S(1)}, s32[4]{0:T(128)}, u32[]{:S(2)}) copy-start(s32[4]{0:T(128)} %param.9) | copy-start | bytes 52
  37.4 300.7 %copy-start.2 = (bf16[4,8192]{1,0:T(4,128)(2,1)S(1)}, bf16[4,8192]{1,0:T(4,128)(2,1)}, u32[]{:S(2)}) copy-start(bf16[4,8192]{1,0:T(4,128)(2,1)} %param.8) | copy-start | bytes 196612
  343.8 328.8 %copy-start.1 = (bf16[4,14336]{1,0:T(4,128)(2,1)S(1)}, bf16[4,14336]{1,0:T(4,128)(2,1)}, u32[]{:S(2)}) copy-start(bf16[4,14336]{1,0:T(4,128)(2,1)} %param.7) | copy-start | bytes 344068
  672.6 9.7 %copy-start = (bf16[512,8192]{1,0:T(8,128)(2,1)S(1)}, bf16[512,8192]{1,0:T(8,128)(2,1)}, u32[]{:S(2)}) copy-start(bf16[512,8192]{1,0:T(8,128)(2,1)} %reshape.16) | copy-start | bytes 25165828
Sparse Core Ops, SparseCore 0:
  9.7 315.8 all-gather.6
  327.3 324.5 all-gather.4
where the time goes:
time: 781 us; the launch traced here: 780 us
  waiting for transfers between devices  527 us (67%)
  blocking collectives  134 us (17%)
  matrix products  68.3 us (9%)
  local copies, waits for them, and re-layouts  33.9 us (4%)
  between operations  14.1 us (2%)
    all_gather x1, waiting for transfers between devices, shards(): piece_acts = lax.all_gather(val_acts, ('dp', 'seq'), axis=0, tiled=True)  308 us
    all_gather x1, waiting for transfers between devices, shards(): piece_grads = lax.all_gather(val_grads, ('dp', 'seq'), axis=0, tiled=True)  218 us
    unnamed x1, blocking collectives  68.8 us
    psum x1, blocking collectives, shards(): val_norm = lax.psum(partial_value, ('dp', 'seq'))  65.5 us
    unnamed x13, local copies, waits for them, and re-layouts  33.6 us
    dot_general x1, matrix products, shards(): jnp.dot(hidden_acts, hidden_acts.T, preferred_element_type=jnp.float32)  17.5 us
  transfers between devices with their start and end apart: 2, of which 2 were waited for; matrix products, arithmetic and copies ran while one was open for 6% of the time, Pallas kernels for 0%

commit v1 on v0

v1 whole, which is shorter than its diff:
```python
import functools
import math

import jax
import jax.numpy as jnp
from jax import lax
from jax.experimental import pallas as pl
from jax.experimental.pallas import tpu as pltpu
from jax.sharding import PartitionSpec as P

D = 8192
FF = 14336
BLK = 128
NVAL = 4
TOK = 512
VAL = 512
AXES = ("dp", "seq")
HA = FF // 2
HG = D // 2
C1 = 3840
C2A = HA - C1
C2G = 512
C2 = C2A + C2G
C3G = HG - C2G
IDW = 128
C3 = C3G + IDW
MASKS = ((1, 3), (3, 1))


def coords(i):
    dp, seq = divmod(i, 8)
    c = dp % 2
    z = (dp // 2) % 4
    x = (seq // 4) * 2 + dp // 8
    return {"x": x, "y": seq % 4, "z": z, "c": c}


def index(p):
    dp = ((p["x"] % 2) * 4 + p["z"]) * 2 + p["c"]
    return dp * 8 + (p["x"] // 2) * 4 + p["y"]


def ring_pairs(axis, step):
    pairs = []
    for i in range(128):
        p = coords(i)
        p[axis] ^= MASKS[p["c"]][step]
        pairs.append((i, index(p)))
    return pairs


def core_pairs():
    pairs = []
    for i in range(128):
        p = coords(i)
        p["c"] ^= 1
        pairs.append((i, index(p)))
    return pairs


def swap(x):
    return lax.ppermute(x, AXES, core_pairs())


def hop(x, axis, step):
    return lax.ppermute(x, AXES, ring_pairs(axis, step))


def grow(x, axis, dim, first):
    a1 = hop(x, axis, 0)
    b = hop(jnp.stack([x, a1]), axis, 1)
    return jnp.stack(
        [x, jnp.where(first, a1, b[0]), jnp.where(first, b[0], a1), b[1]], axis=dim
    )


def nt(a, b):
    return lax.dot_general(a, b, (((1,), (1,)), ((), ())), preferred_element_type=jnp.float32)


def self_body(acts_ref, grads_ref, out_ref, sa, sg, *, na, ng):
    i = pl.program_id(0)

    @pl.when(i == 0)
    def _():
        sa[...] = jnp.zeros_like(sa)
        sg[...] = jnp.zeros_like(sg)

    def add(acc, ref):
        acc[0:256, :] += nt(ref[256:512, :], ref[0:256, :])
        acc[256:384, 0:128] += nt(ref[128:256, :], ref[0:128, :])
        acc[384:512, 0:128] += nt(ref[384:512, :], ref[256:384, :])

    @pl.when(i < na)
    def _():
        add(sa, acts_ref)

    @pl.when(i >= na)
    def _():
        add(sg, grads_ref)

    @pl.when(i == na + ng - 1)
    def _():
        k = sa[...] * sg[...]
        rows = lax.broadcasted_iota(jnp.int32, (4, 4), 0)
        cols = lax.broadcasted_iota(jnp.int32, (4, 4), 1)
        out = jnp.zeros((4, 4), jnp.float32)
        spots = (
            (2, 0, 0, 0), (2, 1, 0, 128), (3, 0, 128, 0), (3, 1, 128, 128),
            (1, 0, 256, 0), (3, 2, 384, 0),
        )
        for b, c, r0, c0 in spots:
            s = jnp.sum(k[r0:r0 + 128, c0:c0 + 128])
            out = jnp.where((rows == b) & (cols == c), s, out)
        out_ref[...] = out / (float(BLK) * math.sqrt(float(FF) * float(D)))


def self_gram(acts, grads):
    kc = 2048
    na, ng = FF // kc, D // kc
    return pl.pallas_call(
        functools.partial(self_body, na=na, ng=ng),
        grid=(na + ng,),
        in_specs=[
            pl.BlockSpec((TOK, kc), lambda i: (0, jnp.minimum(i, na - 1))),
            pl.BlockSpec((TOK, kc), lambda i: (0, jnp.maximum(i - na, 0))),
        ],
        out_specs=pl.BlockSpec((4, 4), lambda i: (0, 0)),
        out_shape=jax.ShapeDtypeStruct((4, 4), jnp.float32),
        scratch_shapes=[pltpu.VMEM((512, 256), jnp.float32)] * 2,
        compiler_params=pltpu.CompilerParams(vmem_limit_bytes=24 << 20),
        cost_estimate=pl.CostEstimate(
            flops=2 * 512 * 256 * (FF + D), bytes_accessed=2 * TOK * (FF + D), transcendentals=0
        ),
    )(acts, grads)


def cross_body(core_ref, acts, grads, *refs):
    pieces = refs[:24]
    raw_ref, norm_ref = refs[24:26]
    v1, v2, v3, h1, h2, h3, ca, cg, ka, kg, ids, sems = refs[26:]
    c = core_ref[0]
    vbufs = (v1, v2, v3)
    hbufs = (h1, h2, h3)

    def slots(half):
        o = c if half == 0 else 1 - c
        return (0, 1 + o, 2 - o, 3)

    def copies(half, part):
        out = []
        ss = slots(half)
        for k in range(4):
            src = pieces[half * 12 + part * 4 + k]
            if part == 0:
                dst = vbufs[0].at[half, ss[k]]
            elif part == 1:
                dst = vbufs[1].at[half, :, ss[k]]
            else:
                dst = vbufs[2].at[half, :, :, ss[k]]
            out.append((src, dst))
        o = c if half == 0 else 1 - c
        a0 = pl.multiple_of(o * HA, 128)
        g0 = pl.multiple_of(o * HG, 128)
        if part == 0:
            out.append((acts.at[:, pl.ds(a0, C1)], hbufs[0].at[half]))
        elif part == 1:
            out.append((acts.at[:, pl.ds(a0 + C1, C2A)], hbufs[1].at[half, :, pl.ds(0, C2A)]))
            out.append((grads.at[:, pl.ds(g0, C2G)], hbufs[1].at[half, :, pl.ds(C2A, C2G)]))
        else:
            out.append((grads.at[:, pl.ds(g0 + C2G, C3G)], hbufs[2].at[half]))
        return [
            pltpu.make_async_copy(s, d, sems.at[half, part, n]) for n, (s, d) in enumerate(out)
        ]

    order = [(half, part) for half in range(2) for part in range(3)]
    for half, part in order:
        for cp in copies(half, part):
            cp.start()
    seen = set()
    for half, part in order:
        for cp in copies(half, part):
            cp.wait()
        v = vbufs[part]
        width = (C1, C2, C3)[part]
        rows = v[half].reshape(VAL, width)
        mine = v[half, pl.ds(2 * c, 2)].reshape(VAL // 2, width)
        if part == 0:
            segments = ((ca, ka, 0, C1),)
        elif part == 1:
            segments = ((ca, ka, 0, C2A), (cg, kg, C2A, C2G))
        else:
            segments = ((cg, kg, 0, C3G),)
        for cross, kern, at, n in segments:
            r = rows[:, at:at + n]
            x = nt(r, hbufs[part][half, :, at:at + n])
            y = nt(mine[:, at:at + n], r)
            name = "a" if cross is ca else "g"
            if name in seen:
                cross[...] += x
                kern[...] += y
            else:
                cross[...] = x
                kern[...] = y
                seen.add(name)
        if half == 0 and part == 2:
            ids[...] = rows[:, C3G:].astype(jnp.float32)

    cross = ca[...] * cg[...]
    kern = ka[...] * kg[...]
    row_ids = jnp.transpose(ids[...])[0:1, :]
    half_ids = ids[pl.ds(pl.multiple_of(c * 256, 256), 256), :]
    for v in range(NVAL):
        keep = jnp.where(ids[...] == float(v), 1.0, 0.0)
        keep = jnp.concatenate([keep] * 4, axis=1)
        raw_ref[v:v + 1, :] = jnp.sum(cross * keep, axis=0, keepdims=True)
        keep = jnp.where(half_ids == float(v), 1.0, 0.0)
        keep = jnp.concatenate([keep] * 4, axis=1)
        part = jnp.sum(kern * keep, axis=0, keepdims=True)
        part = jnp.sum(jnp.where(row_ids == float(v), part, 0.0))
        norm_ref[v:v + 1, :] = jnp.full((1, 128), part, jnp.float32)


def cross_scores(core, acts, grads, pieces):
    anyspec = pl.BlockSpec(memory_space=pl.ANY)
    return pl.pallas_call(
        cross_body,
        in_specs=[pl.BlockSpec(memory_space=pltpu.SMEM)] + [anyspec] * (2 + len(pieces)),
        out_specs=[pl.BlockSpec(memory_space=pltpu.VMEM)] * 2,
        out_shape=[
            jax.ShapeDtypeStruct((NVAL, TOK), jnp.float32),
            jax.ShapeDtypeStruct((NVAL, 128), jnp.float32),
        ],
        scratch_shapes=[
            pltpu.VMEM((2, 4, 4, 4, 8, C1), jnp.bfloat16),
            pltpu.VMEM((2, 4, 4, 4, 8, C2), jnp.bfloat16),
            pltpu.VMEM((2, 4, 4, 4, 8, C3), jnp.bfloat16),
            pltpu.VMEM((2, TOK, C1), jnp.bfloat16),
            pltpu.VMEM((2, TOK, C2), jnp.bfloat16),
            pltpu.VMEM((2, TOK, C3G), jnp.bfloat16),
            pltpu.VMEM((VAL, TOK), jnp.float32),
            pltpu.VMEM((VAL, TOK), jnp.float32),
            pltpu.VMEM((VAL // 2, VAL), jnp.float32),
            pltpu.VMEM((VAL // 2, VAL), jnp.float32),
            pltpu.VMEM((VAL, IDW), jnp.float32),
            pltpu.SemaphoreType.DMA((2, 3, 6)),
        ],
        compiler_params=pltpu.CompilerParams(vmem_limit_bytes=58 << 20),
        cost_estimate=pl.CostEstimate(
            flops=2 * 512 * 768 * (FF + D), bytes_accessed=4 * TOK * (FF + D), transcendentals=0
        ),
    )(core, acts, grads, *pieces)


def shards(hidden_acts, out_grads, val_acts, val_grads, val_ids):
    core = lax.axis_index("dp") % 2
    first = core == 0
    idcol = jnp.broadcast_to(val_ids[:, None].astype(jnp.bfloat16), (4, IDW))
    halves = [
        jnp.concatenate(
            [val_acts[:, h * HA:(h + 1) * HA], val_grads[:, h * HG:(h + 1) * HG], idcol], axis=1
        )
        for h in range(2)
    ]
    keep = jnp.where(first, halves[0], halves[1])
    got = swap(jnp.where(first, halves[1], halves[0]))
    rows = jnp.concatenate([jnp.where(first, keep, got), jnp.where(first, got, keep)], axis=0)
    parts = (rows[:, :C1], rows[:, C1:C1 + C2], rows[:, C1 + C2:])

    plans = (
        (("z", 0), ("y", 0), "x"),
        (("x", 0), ("z", 1), "y"),
        (("y", 0), ("x", 0), "z"),
    )
    grown = list(parts)
    for stage in range(2):
        for j, plan in enumerate(plans):
            axis, dim = plan[stage]
            grown[j] = grow(grown[j], axis, dim, first)
    own, other = [], []
    for j, plan in enumerate(plans):
        x = grown[j]
        a1 = hop(x, plan[2], 0)
        b0 = hop(x, plan[2], 1)
        b1 = hop(a1, plan[2], 1)
        own += [x, a1, b0, b1]
        other += [swap(x), swap(a1), swap(b0), swap(b1)]

    block_gram = self_gram(hidden_acts, out_grads)
    raw, norm = cross_scores(core.reshape(1).astype(jnp.int32), hidden_acts, out_grads, own + other)
    norm = norm + swap(norm)
    token_scores = raw * lax.rsqrt(norm[:, :1] + 1e-06)
    return (token_scores, block_gram)


def solution(mesh):
    return jax.shard_map(
        shards,
        mesh=mesh,
        in_specs=(
            P(AXES, None),
            P(AXES, None),
            P(AXES, None),
            P(AXES, None),
            P(AXES),
        ),
        out_specs=(P(None, AXES), P(AXES, None)),
        check_vma=False,
    )
```

time: 781 us -> 158 us (0.20)
  waiting for transfers between devices: 527 us -> 46.2 us
  blocking collectives: 134 us -> 0 us
  matrix products: 68.3 us -> 0 us
  starting transfers between devices: 0.08 us -> 51 us
  Pallas kernels: 0 us -> 34.2 us
  between operations: 14.1 us -> 1.1 us
  local copies, waits for them, and re-layouts: 33.9 us -> 22.3 us
    all_gather x2 -> x0, waiting for transfers between devices: 526 us -> none  [the longest x1 308 us: shards(): piece_acts = lax.all_gather(val_acts, ('dp', 'seq'), axis=0, tiled=True)]
    unnamed x1 -> x0, blocking collectives: 68.8 us -> none
    dot_general x8 -> x0, matrix products: 68.3 us -> none  [the longest x1 17.5 us: shards(): jnp.dot(hidden_acts, hidden_acts.T, preferred_element_type=jnp.float32)]
    psum x1 -> x0, blocking collectives: 65.5 us -> none  [shards(): val_norm = lax.psum(partial_value, ('dp', 'seq'))]
    ppermute x0 -> x35, starting transfers between devices: none -> 51 us  [the longest x14 31.8 us: swap(): return lax.ppermute(x, AXES, core_pairs())]
    ppermute x0 -> x35, waiting for transfers between devices: none -> 46.2 us  [the longest x21 42.2 us: hop(): return lax.ppermute(x, AXES, ring_pairs(axis, step))]
    pallas_call x0 -> x2, Pallas kernels: none -> 34.2 us  [the longest x1 23.4 us: cross_scores(): pl.pallas_call(cross_body, in_specs=[pl.BlockSpec(memory_space=pltpu.SMEM...]
    unnamed x13 -> x40, local copies, waits for them, and re-layouts: 33.6 us -> 12 us
  transfers between devices with their start and end apart: 2 -> 35, of which waited for: 2 -> 12; matrix products, arithmetic and copies ran while one was open for 6% -> 6% of each run, Pallas kernels for 0% -> 7%
where the time goes in v1:
time: 158 us; the launch traced here: 157 us
  starting transfers between devices  51 us (32%)
  waiting for transfers between devices  46.2 us (29%)
  Pallas kernels  34.2 us (22%)
  local copies, waits for them, and re-layouts  22.3 us (14%)
  other arithmetic  2.65 us (2%)
    ppermute x21, waiting for transfers between devices, hop(): return lax.ppermute(x, AXES, ring_pairs(axis, step))  42.2 us
    ppermute x14, starting transfers between devices, swap(): return lax.ppermute(x, AXES, core_pairs())  31.8 us
    pallas_call x1, Pallas kernels, cross_scores(): pl.pallas_call(cross_body, in_specs=[pl.BlockSpec(memory_space=pltpu.SMEM...  23.4 us
    ppermute x21, starting transfers between devices, hop(): return lax.ppermute(x, AXES, ring_pairs(axis, step))  19.2 us
    unnamed x40, local copies, waits for them, and re-layouts  12 us
    pallas_call x1, Pallas kernels, self_gram(): pl.pallas_call(functools.partial(self_body, na=na, ng=ng), grid=(na + ng,...  10.8 us
    ppermute x4, local copies, waits for them, and re-layouts, swap(): return lax.ppermute(x, AXES, core_pairs())  4.21 us
    ppermute x14, waiting for transfers between devices, swap(): return lax.ppermute(x, AXES, core_pairs())  3.99 us
  transfers between devices with their start and end apart: 35, of which 12 were waited for; matrix products, arithmetic and copies ran while one was open for 6% of the time, Pallas kernels for 7%

profile of v1, /device:TPU:1, one launch (start us, length us, event | category | flops | bytes accessed | tf_op | source)
XLA Modules:
  0.0 157.5 jit_solution(8045619167665728328)
XLA Ops:
  0.6 0.9 fusion.6
  1.5 0.8 fusion.7
  2.3 0.7 convert_element_type.4
  3.2 1.5 collective-permute-start
  4.7 0.9 collective-permute-done
  5.8 2.9 %collective-permute-start.15 = (bf16[8,3712]{1,0:T(8,128)(2,1)S(1)}, bf16[8,3712]{1,0:T(8,128)(2,1)S(1)}, u32[]{:S(2)}, u32[]{:S(2)}) collective-permute-start(bf16[8,3712]{1,0:T(8,128)(2,1)S(1)} %pad_maximum_fusion.14), channel_id=1, source_target_pairs={{0,1},{1,0},{2,3},{3,2},{4,5},{5,4},{6,7},{7,6},{8,11},{9,10},{10,... | collective-permute-start | bytes 178184 | tf_op jit(solution)/shard_map/ppermute | solution.py:66
  8.7 2.6 %collective-permute-start.8 = (bf16[8,3840]{1,0:T(8,128)(2,1)S(1)}, bf16[8,3840]{1,0:T(8,128)(2,1)S(1)}, u32[]{:S(2)}, u32[]{:S(2)}) collective-permute-start(bf16[8,3840]{1,0:T(8,128)(2,1)S(1)} %get-tuple-element.25), channel_id=1, source_target_pairs={{0,64},{1,65},{2,66},{3,67},{4,68},{5,69},{6,70},{7,71},{8,76},{9,... | collective-permute-start | bytes 184328 | tf_op jit(solution)/shard_map/ppermute | solution.py:66
  11.3 3.8 %collective-permute-start.1 = (bf16[8,3840]{1,0:T(8,128)(2,1)S(1)}, bf16[8,3840]{1,0:T(8,128)(2,1)S(1)}, u32[]{:S(2)}, u32[]{:S(2)}) collective-permute-start(bf16[8,3840]{1,0:T(8,128)(2,1)S(1)} %get-tuple-element.26), channel_id=1, source_target_pairs={{0,16},{1,17},{2,18},{3,19},{4,20},{5,21},{6,22},{7,23},{8,56},{9,... | collective-permute-start | bytes 184328 | tf_op jit(solution)/shard_map/ppermute | solution.py:66
  15.3 1.7 %collective-permute-done.1 = bf16[8,3840]{1,0:T(8,128)(2,1)S(1)} collective-permute-done((bf16[8,3840]{1,0:T(8,128)(2,1)S(1)}, bf16[8,3840]{1,0:T(8,128)(2,1)S(1)}, u32[]{:S(2)}, u32[]{:S(2)}) %collective-permute-start.1) | collective-permute-done | bytes 61472 | tf_op jit(solution)/shard_map/ppermute | solution.py:66
  17.1 2.1 %collective-permute-done.16 = bf16[2,8,3712]{2,1,0:T(8,128)(2,1)S(1)} collective-permute-done((bf16[2,8,3712]{2,1,0:T(8,128)(2,1)S(1)}, bf16[2,8,3712]{2,1,0:T(8,128)(2,1)S(1)}, u32[]{:S(2)}, u32[]{:S(2)}) %collective-permute-start.16) | collective-permute-done | bytes 118816 | tf_op jit(solution)/shard_map/ppermute | solution.py:66
  19.4 1.4 collective-permute-start.10
  20.9 2.5 %collective-permute-start.3 = (bf16[4,8,3840]{2,1,0:T(8,128)(2,1)S(1)}, bf16[4,8,3840]{2,1,0:T(8,128)(2,1)S(1)}, u32[]{:S(2)}, u32[]{:S(2)}) collective-permute-start(bf16[4,8,3840]{2,1,0:T(8,128)(2,1)S(1)} %get-tuple-element.18), channel_id=1, source_target_pairs={{0,1},{1,0},{2,3},{3,2},{4,5},{5,4},{6,7},{7,6},{8,11},{9,10},{10,... | collective-permute-start | bytes 737288 | tf_op jit(solution)/shard_map/ppermute | solution.py:66
  23.5 2.0 %collective-permute-done.17 = bf16[4,8,3712]{2,1,0:T(8,128)(2,1)S(1)} collective-permute-done((bf16[4,8,3712]{2,1,0:T(8,128)(2,1)S(1)}, bf16[4,8,3712]{2,1,0:T(8,128)(2,1)S(1)}, u32[]{:S(2)}, u32[]{:S(2)}) %collective-permute-start.17) | collective-permute-done | bytes 237600 | tf_op jit(solution)/shard_map/ppermute | solution.py:66
  25.9 1.4 collective-permute-done.3
  27.4 6.0 %collective-permute-done.18 = bf16[2,4,8,3712]{3,2,1,0:T(8,128)(2,1)S(1)} collective-permute-done((bf16[2,4,8,3712]{3,2,1,0:T(8,128)(2,1)S(1)}, bf16[2,4,8,3712]{3,2,1,0:T(8,128)(2,1)S(1)}, u32[]{:S(2)}, u32[]{:S(2)}) %collective-permute-start.18) | collective-permute-done | bytes 475168 | tf_op jit(solution)/shard_map/ppermute | solution.py:66
  33.6 1.0 collective-permute-start.19
  34.6 0.8 collective-permute-done.4
  35.7 2.4 %collective-permute-start.12 = (bf16[4,4,8,3840]{3,2,0,1:T(8,128)(2,1)S(1)}, bf16[4,4,8,3840]{3,2,0,1:T(8,128)(2,1)S(1)}, u32[]{:S(2)}, u32[]{:S(2)}) collective-permute-start(bf16[4,4,8,3840]{3,2,0,1:T(8,128)(2,1)S(1)} %pad_maximum_fusion.1), channel_id=1, source_target_pairs={{0,1},{1,0},{2,3},{3,2},{4,5},{5,4},{6,7},{7,6},{8,11},{9,10},{10,... | collective-permute-start | bytes 2949128 | tf_op jit(solution)/shard_map/ppermute | solution.py:66
  38.1 8.4 %collective-permute-start.30 = (bf16[4,4,8,3712]{3,2,1,0:T(8,128)(2,1)S(1)}, bf16[4,4,8,3712]{3,2,1,0:T(8,128)(2,1)S(1)}, u32[]{:S(2)}, u32[]{:S(2)}) collective-permute-start(bf16[4,4,8,3712]{3,2,1,0:T(8,128)(2,1)S(1)} %pad_maximum_fusion.2.refs_8_), channel_id=1, source_target_pairs={{0,8},{1,9},{2,10},{3,11},{4,12},{5,13},{6,14},{7,15},{8,0},{9,1},... | collective-permute-start | bytes 2850824 | tf_op jit(solution)/shard_map/ppermute | solution.py:62
  46.5 1.4 collective-permute-done.19.refs_9_
  47.9 12.8 %collective-permute-start.26 = (bf16[4,4,8,3840]{3,2,0,1:T(8,128)(2,1)S(1)}, bf16[4,4,8,3840]{3,2,0,1:T(8,128)(2,1)S(1)}, u32[]{:S(2)}, u32[]{:S(2)}) collective-permute-start(bf16[4,4,8,3840]{3,2,0,1:T(8,128)(2,1)S(1)} %pad_maximum_fusion.1), channel_id=1, source_target_pairs={{0,8},{1,9},{2,10},{3,11},{4,12},{5,13},{6,14},{7,15},{8,0},{9,1},... | collective-permute-start | bytes 2949128 | tf_op jit(solution)/shard_map/ppermute | solution.py:62
  61.2 2.0 %collective-permute-start.22 = (bf16[4,4,8,3840]{3,2,1,0:T(8,128)(2,1)S(1)}, bf16[4,4,8,3840]{3,2,1,0:T(8,128)(2,1)S(1)}, u32[]{:S(2)}, u32[]{:S(2)}) collective-permute-start(bf16[4,4,8,3840]{3,2,1,0:T(8,128)(2,1)S(1)} %pad_maximum_fusion.refs_0_), channel_id=1, source_target_pairs={{0,8},{1,9},{2,10},{3,11},{4,12},{5,13},{6,14},{7,15},{8,0},{9,1},... | collective-permute-start | bytes 2949128 | tf_op jit(solution)/shard_map/ppermute | solution.py:62
  63.2 1.7 %collective-permute-start.14 = (bf16[4,4,8,3840]{3,2,0,1:T(8,128)(2,1)S(1)}, bf16[4,4,8,3840]{3,2,0,1:T(8,128)(2,1)S(1)}, u32[]{:S(2)}, u32[]{:S(2)}) collective-permute-start(bf16[4,4,8,3840]{3,2,0,1:T(8,128)(2,1)S(1)} %collective-permute-done.12), channel_id=1, source_target_pairs={{0,3},{1,2},{2,1},{3,0},{4,7},{5,6},{6,5},{7,4},{8,9},{9,8},{10,11... | collective-permute-start | bytes 2949128 | tf_op jit(solution)/shard_map/ppermute | solution.py:66
  64.9 20.5 %collective-permute-done.5.refs_1_ = bf16[4,4,8,3840]{3,2,1,0:T(8,128)(2,1)S(1)} collective-permute-done((bf16[4,4,8,3840]{3,2,1,0:T(8,128)(2,1)S(1)}, bf16[4,4,8,3840]{3,2,1,0:T(8,128)(2,1)S(1)}, u32[]{:S(2)}, u32[]{:S(2)}) %collective-permute-start.5) | collective-permute-done | bytes 983072 | tf_op jit(solution)/shard_map/ppermute | solution.py:66
  85.5 2.1 %collective-permute-start.28 = (bf16[4,4,8,3840]{3,2,0,1:T(8,128)(2,1)S(1)}, bf16[4,4,8,3840]{3,2,0,1:T(8,128)(2,1)S(1)}, u32[]{:S(2)}, u32[]{:S(2)}) collective-permute-start(bf16[4,4,8,3840]{3,2,0,1:T(8,128)(2,1)S(1)} %collective-permute-done.13), channel_id=1, source_target_pairs={{0,8},{1,9},{2,10},{3,11},{4,12},{5,13},{6,14},{7,15},{8,0},{9,1},... | collective-permute-start | bytes 2949128 | tf_op jit(solution)/shard_map/ppermute | solution.py:62
  87.7 0.4 collective-permute-start.29
  88.1 3.0 %collective-permute-done.31.refs_21_ = bf16[4,4,8,3712]{3,2,1,0:T(8,128)(2,1)S(1)} collective-permute-done((bf16[4,4,8,3712]{3,2,1,0:T(8,128)(2,1)S(1)}, bf16[4,4,8,3712]{3,2,1,0:T(8,128)(2,1)S(1)}, u32[]{:S(2)}, u32[]{:S(2)}) %collective-permute-start.31) | collective-permute-done | bytes 950304 | tf_op jit(solution)/shard_map/ppermute | solution.py:62
  91.5 0.6 copy-done.17
  92.2 0.4 collective-permute-start.24
  92.5 6.2 %collective-permute-done.7.refs_3_ = bf16[4,4,8,3840]{3,2,1,0:T(8,128)(2,1)S(1)} collective-permute-done((bf16[4,4,8,3840]{3,2,1,0:T(8,128)(2,1)S(1)}, bf16[4,4,8,3840]{3,2,1,0:T(8,128)(2,1)S(1)}, u32[]{:S(2)}, u32[]{:S(2)}) %collective-permute-start.7) | collective-permute-done | bytes 983072 | tf_op jit(solution)/shard_map/ppermute | solution.py:66
  98.8 2.9 %collective-permute-start.25 = (bf16[4,4,8,3840]{3,2,1,0:T(8,128)(2,1)S(1)}, bf16[4,4,8,3840]{3,2,1,0:T(8,128)(2,1)S(1)}, u32[]{:S(2)}, u32[]{:S(2)}) collective-permute-start(bf16[4,4,8,3840]{3,2,1,0:T(8,128)(2,1)S(1)} %collective-permute-done.7.refs_3_), channel_id=1, source_target_pairs={{0,8},{1,9},{2,10},{3,11},{4,12},{5,13},{6,14},{7,15},{8,0},{9,1},... | collective-permute-start | bytes 2949128 | tf_op jit(solution)/shard_map/ppermute | solution.py:62
  101.8 0.4 collective-permute-start.33
  102.2 1.0 copy.15.refs_4_
  103.2 1.0 copy.16.refs_5_
  104.3 1.0 copy.17.refs_6_
  105.3 1.1 copy.19.refs_16_
  106.4 1.1 copy.18.refs_7_
  107.5 1.0 copy.20.refs_17_
  108.5 1.0 copy.21.refs_18_
  109.6 1.0 copy.22.refs_19_
  110.7 0.9 copy-done.18
  111.6 0.4 copy-done.10
  112.5 1.0 copy-done.12
  113.5 23.4 %shard_map.68 = (f32[4,512]{1,0:T(4,128)}, f32[4,128]{1,0:T(4,128)}) custom-call(s32[1]{0:T(128)} %bitcast.core_ref, bf16[512,14336]{1,0:T(8,128)(2,1)} %acts_ref.1, bf16[512,8192]{1,0:T(8,128)(2,1)} %grads_ref.1, bf16[4,4,8,3840]{3,2,1,0:T(8,128)(2,1)} %copy-done.2, bf16[4,4,8,3840]{3,2,1,0:T(8,128)(2,1)} %copy-done.6, bf16[4,4,8,3840]{3,2,1,0:T(8,128)(2,1)} %copy-done.7, ...), custom_call_target="tpu_custom_call" | custom-call | flops 17716740096 | bytes 46137344 | tf_op jit(solution)/shard_map/pallas_call | solution.py:226
  137.3 5.2 %copy-done = bf16[512,14336]{1,0:T(8,128)(2,1)S(1)} copy-done((bf16[512,14336]{1,0:T(8,128)(2,1)S(1)}, bf16[512,14336]{1,0:T(8,128)(2,1)}, u32[]{:S(2)}) %copy-start) | copy-done | bytes 14680088
  142.5 3.4 %copy-done.1 = bf16[512,8192]{1,0:T(8,128)(2,1)S(1)} copy-done((bf16[512,8192]{1,0:T(8,128)(2,1)S(1)}, bf16[512,8192]{1,0:T(8,128)(2,1)}, u32[]{:S(2)}) %copy-start.1) | copy-done | bytes 8388632
  145.9 10.8 %shard_map.69 = f32[4,4]{1,0:T(4,128)} custom-call(bf16[512,14336]{1,0:T(8,128)(2,1)S(1)} %copy-done, bf16[512,8192]{1,0:T(8,128)(2,1)S(1)} %copy-done.1), custom_call_target="tpu_custom_call" | custom-call | flops 5905580032 | bytes 23068672 | tf_op jit(solution)/shard_map/pallas_call | solution.py:121
  156.8 0.7 broadcast_multiply_fusion
  (106 shorter events, 4.2 us)
Async XLA Ops:
  3.2 2.4 %collective-permute-start = (bf16[4,11392]{1,0:T(4,128)(2,1)S(1)}, bf16[4,11392]{1,0:T(4,128)(2,1)S(1)}, u32[]{:S(2)}, u32[]{:S(2)}) collective-permute-start(bf16[4,11392]{1,0:T(4,128)(2,1)S(1)} %broadcast_select_fusion.2), channel_id=1, source_target_pairs={{0,8},{1,9},{2,10},{3,11},{4,12},{5,13},{6,14},{7,15},{8,0},{9,1},... | collective-permute-start | bytes 273416 | tf_op jit(solution)/shard_map/ppermute | solution.py:62
  5.8 9.3 %collective-permute-start.15 = (bf16[8,3712]{1,0:T(8,128)(2,1)S(1)}, bf16[8,3712]{1,0:T(8,128)(2,1)S(1)}, u32[]{:S(2)}, u32[]{:S(2)}) collective-permute-start(bf16[8,3712]{1,0:T(8,128)(2,1)S(1)} %pad_maximum_fusion.14), channel_id=1, source_target_pairs={{0,1},{1,0},{2,3},{3,2},{4,5},{5,4},{6,7},{7,6},{8,11},{9,10},{10,... | collective-permute-start | bytes 178184 | tf_op jit(solution)/shard_map/ppermute | solution.py:66
  8.7 6.4 %collective-permute-start.8 = (bf16[8,3840]{1,0:T(8,128)(2,1)S(1)}, bf16[8,3840]{1,0:T(8,128)(2,1)S(1)}, u32[]{:S(2)}, u32[]{:S(2)}) collective-permute-start(bf16[8,3840]{1,0:T(8,128)(2,1)S(1)} %get-tuple-element.25), channel_id=1, source_target_pairs={{0,64},{1,65},{2,66},{3,67},{4,68},{5,69},{6,70},{7,71},{8,76},{9,... | collective-permute-start | bytes 184328 | tf_op jit(solution)/shard_map/ppermute | solution.py:66
  11.3 5.7 %collective-permute-start.1 = (bf16[8,3840]{1,0:T(8,128)(2,1)S(1)}, bf16[8,3840]{1,0:T(8,128)(2,1)S(1)}, u32[]{:S(2)}, u32[]{:S(2)}) collective-permute-start(bf16[8,3840]{1,0:T(8,128)(2,1)S(1)} %get-tuple-element.26), channel_id=1, source_target_pairs={{0,16},{1,17},{2,18},{3,19},{4,20},{5,21},{6,22},{7,23},{8,56},{9,... | collective-permute-start | bytes 184328 | tf_op jit(solution)/shard_map/ppermute | solution.py:66
  15.1 4.1 %collective-permute-start.16 = (bf16[2,8,3712]{2,1,0:T(8,128)(2,1)S(1)}, bf16[2,8,3712]{2,1,0:T(8,128)(2,1)S(1)}, u32[]{:S(2)}, u32[]{:S(2)}) collective-permute-start(bf16[2,8,3712]{2,1,0:T(8,128)(2,1)S(1)} %pad_maximum_fusion.11), channel_id=1, source_target_pairs={{0,3},{1,2},{2,1},{3,0},{4,7},{5,6},{6,5},{7,4},{8,9},{9,8},{10,11... | collective-permute-start | bytes 356360 | tf_op jit(solution)/shard_map/ppermute | solution.py:66
  15.2 4.1 %collective-permute-start.9 = (bf16[2,8,3840]{2,1,0:T(8,128)(2,1)S(1)}, bf16[2,8,3840]{2,1,0:T(8,128)(2,1)S(1)}, u32[]{:S(2)}, u32[]{:S(2)}) collective-permute-start(bf16[2,8,3840]{2,1,0:T(8,128)(2,1)S(1)} %pad_maximum_fusion.10), channel_id=1, source_target_pairs={{0,68},{1,69},{2,70},{3,71},{4,64},{5,65},{6,66},{7,67},{8,72},{9,... | collective-permute-start | bytes 368648 | tf_op jit(solution)/shard_map/ppermute | solution.py:66
  17.0 3.9 %collective-permute-start.2 = (bf16[2,8,3840]{2,1,0:T(8,128)(2,1)S(1)}, bf16[2,8,3840]{2,1,0:T(8,128)(2,1)S(1)}, u32[]{:S(2)}, u32[]{:S(2)}) collective-permute-start(bf16[2,8,3840]{2,1,0:T(8,128)(2,1)S(1)} %pad_maximum_fusion.9), channel_id=1, source_target_pairs={{0,48},{1,49},{2,50},{3,51},{4,52},{5,53},{6,54},{7,55},{8,24},{9,... | collective-permute-start | bytes 368648 | tf_op jit(solution)/shard_map/ppermute | solution.py:66
  19.2 6.2 %collective-permute-start.17 = (bf16[4,8,3712]{2,1,0:T(8,128)(2,1)S(1)}, bf16[4,8,3712]{2,1,0:T(8,128)(2,1)S(1)}, u32[]{:S(2)}, u32[]{:S(2)}) collective-permute-start(bf16[4,8,3712]{2,1,0:T(8,128)(2,1)S(1)} %get-tuple-element.20), channel_id=1, source_target_pairs={{0,64},{1,65},{2,66},{3,67},{4,68},{5,69},{6,70},{7,71},{8,76},{9,... | collective-permute-start | bytes 712712 | tf_op jit(solution)/shard_map/ppermute | solution.py:66
  19.4 6.3 %collective-permute-start.10 = (bf16[4,8,3840]{2,1,0:T(8,128)(2,1)S(1)}, bf16[4,8,3840]{2,1,0:T(8,128)(2,1)S(1)}, u32[]{:S(2)}, u32[]{:S(2)}) collective-permute-start(bf16[4,8,3840]{2,1,0:T(8,128)(2,1)S(1)} %get-tuple-element.16), channel_id=1, source_target_pairs={{0,16},{1,17},{2,18},{3,19},{4,20},{5,21},{6,22},{7,23},{8,56},{9,... | collective-permute-start | bytes 737288 | tf_op jit(solution)/shard_map/ppermute | solution.py:66
  20.9 6.3 %collective-permute-start.3 = (bf16[4,8,3840]{2,1,0:T(8,128)(2,1)S(1)}, bf16[4,8,3840]{2,1,0:T(8,128)(2,1)S(1)}, u32[]{:S(2)}, u32[]{:S(2)}) collective-permute-start(bf16[4,8,3840]{2,1,0:T(8,128)(2,1)S(1)} %get-tuple-element.18), channel_id=1, source_target_pairs={{0,1},{1,0},{2,3},{3,2},{4,5},{5,4},{6,7},{7,6},{8,11},{9,10},{10,... | collective-permute-start | bytes 737288 | tf_op jit(solution)/shard_map/ppermute | solution.py:66
  25.5 7.9 %collective-permute-start.18 = (bf16[2,4,8,3712]{3,2,1,0:T(8,128)(2,1)S(1)}, bf16[2,4,8,3712]{3,2,1,0:T(8,128)(2,1)S(1)}, u32[]{:S(2)}, u32[]{:S(2)}) collective-permute-start(bf16[2,4,8,3712]{3,2,1,0:T(8,128)(2,1)S(1)} %pad_maximum_fusion.5), channel_id=1, source_target_pairs={{0,68},{1,69},{2,70},{3,71},{4,64},{5,65},{6,66},{7,67},{8,72},{9,... | collective-permute-start | bytes 1425416 | tf_op jit(solution)/shard_map/ppermute | solution.py:66
  25.8 8.8 %collective-permute-start.11 = (bf16[2,4,8,3840]{3,2,1,0:T(8,128)(2,1)S(1)}, bf16[2,4,8,3840]{3,2,1,0:T(8,128)(2,1)S(1)}, u32[]{:S(2)}, u32[]{:S(2)}) collective-permute-start(bf16[2,4,8,3840]{3,2,1,0:T(8,128)(2,1)S(1)} %pad_maximum_fusion.4), channel_id=1, source_target_pairs={{0,48},{1,49},{2,50},{3,51},{4,52},{5,53},{6,54},{7,55},{8,24},{9,... | collective-permute-start | bytes 1474568 | tf_op jit(solution)/shard_map/ppermute | solution.py:66
  27.3 8.1 %collective-permute-start.4 = (bf16[2,4,8,3840]{3,2,1,0:T(8,128)(2,1)S(1)}, bf16[2,4,8,3840]{3,2,1,0:T(8,128)(2,1)S(1)}, u32[]{:S(2)}, u32[]{:S(2)}) collective-permute-start(bf16[2,4,8,3840]{3,2,1,0:T(8,128)(2,1)S(1)} %pad_maximum_fusion.3), channel_id=1, source_target_pairs={{0,3},{1,2},{2,1},{3,0},{4,7},{5,6},{6,5},{7,4},{8,9},{9,8},{10,11... | collective-permute-start | bytes 1474568 | tf_op jit(solution)/shard_map/ppermute | solution.py:66
  33.6 79.9 %copy-start.3 = (bf16[4,4,8,3712]{3,2,1,0:T(8,128)(2,1)}, bf16[4,4,8,3712]{3,2,1,0:T(8,128)(2,1)S(1)}, u32[]{:S(2)}) copy-start(bf16[4,4,8,3712]{3,2,1,0:T(8,128)(2,1)S(1)} %pad_maximum_fusion.2.refs_8_) | copy-start | bytes 2850820
  33.6 14.3 %collective-permute-start.19 = (bf16[4,4,8,3712]{3,2,1,0:T(8,128)(2,1)S(1)}, bf16[4,4,8,3712]{3,2,1,0:T(8,128)(2,1)S(1)}, u32[]{:S(2)}, u32[]{:S(2)}) collective-permute-start(bf16[4,4,8,3712]{3,2,1,0:T(8,128)(2,1)S(1)} %pad_maximum_fusion.2.refs_8_), channel_id=1, source_target_pairs={{0,16},{1,17},{2,18},{3,19},{4,20},{5,21},{6,22},{7,23},{8,56},{9,... | collective-permute-start | bytes 2850824 | tf_op jit(solution)/shard_map/ppermute | solution.py:66
  35.7 25.5 %collective-permute-start.12 = (bf16[4,4,8,3840]{3,2,0,1:T(8,128)(2,1)S(1)}, bf16[4,4,8,3840]{3,2,0,1:T(8,128)(2,1)S(1)}, u32[]{:S(2)}, u32[]{:S(2)}) collective-permute-start(bf16[4,4,8,3840]{3,2,0,1:T(8,128)(2,1)S(1)} %pad_maximum_fusion.1), channel_id=1, source_target_pairs={{0,1},{1,0},{2,3},{3,2},{4,5},{5,4},{6,7},{7,6},{8,11},{9,10},{10,... | collective-permute-start | bytes 2949128 | tf_op jit(solution)/shard_map/ppermute | solution.py:66
  38.1 22.7 %collective-permute-start.20 = (bf16[4,4,8,3712]{3,2,1,0:T(8,128)(2,1)S(1)}, bf16[4,4,8,3712]{3,2,1,0:T(8,128)(2,1)S(1)}, u32[]{:S(2)}, u32[]{:S(2)}) collective-permute-start(bf16[4,4,8,3712]{3,2,1,0:T(8,128)(2,1)S(1)} %pad_maximum_fusion.2.refs_8_), channel_id=1, source_target_pairs={{0,48},{1,49},{2,50},{3,51},{4,52},{5,53},{6,54},{7,55},{8,24},{9,... | collective-permute-start | bytes 2850824 | tf_op jit(solution)/shard_map/ppermute | solution.py:66
  38.1 25.1 %collective-permute-start.13 = (bf16[4,4,8,3840]{3,2,0,1:T(8,128)(2,1)S(1)}, bf16[4,4,8,3840]{3,2,0,1:T(8,128)(2,1)S(1)}, u32[]{:S(2)}, u32[]{:S(2)}) collective-permute-start(bf16[4,4,8,3840]{3,2,0,1:T(8,128)(2,1)S(1)} %pad_maximum_fusion.1), channel_id=1, source_target_pairs={{0,3},{1,2},{2,1},{3,0},{4,7},{5,6},{6,5},{7,4},{8,9},{9,8},{10,11... | collective-permute-start | bytes 2949128 | tf_op jit(solution)/shard_map/ppermute | solution.py:66
  38.1 23.0 %collective-permute-start.30 = (bf16[4,4,8,3712]{3,2,1,0:T(8,128)(2,1)S(1)}, bf16[4,4,8,3712]{3,2,1,0:T(8,128)(2,1)S(1)}, u32[]{:S(2)}, u32[]{:S(2)}) collective-permute-start(bf16[4,4,8,3712]{3,2,1,0:T(8,128)(2,1)S(1)} %pad_maximum_fusion.2.refs_8_), channel_id=1, source_target_pairs={{0,8},{1,9},{2,10},{3,11},{4,12},{5,13},{6,14},{7,15},{8,0},{9,1},... | collective-permute-start | bytes 2850824 | tf_op jit(solution)/shard_map/ppermute | solution.py:62
  47.9 40.2 %copy-start.13 = (bf16[4,4,8,3712]{3,2,1,0:T(8,128)(2,1)}, bf16[4,4,8,3712]{3,2,1,0:T(8,128)(2,1)S(1)}, u32[]{:S(2)}) copy-start(bf16[4,4,8,3712]{3,2,1,0:T(8,128)(2,1)S(1)} %collective-permute-done.19.refs_9_) | copy-start | bytes 2850820
  47.9 17.0 %collective-permute-start.26 = (bf16[4,4,8,3840]{3,2,0,1:T(8,128)(2,1)S(1)}, bf16[4,4,8,3840]{3,2,0,1:T(8,128)(2,1)S(1)}, u32[]{:S(2)}, u32[]{:S(2)}) collective-permute-start(bf16[4,4,8,3840]{3,2,0,1:T(8,128)(2,1)S(1)} %pad_maximum_fusion.1), channel_id=1, source_target_pairs={{0,8},{1,9},{2,10},{3,11},{4,12},{5,13},{6,14},{7,15},{8,0},{9,1},... | collective-permute-start | bytes 2949128 | tf_op jit(solution)/shard_map/ppermute | solution.py:62
  60.9 52.6 %copy-start.2 = (bf16[4,4,8,3840]{3,2,1,0:T(8,128)(2,1)}, bf16[4,4,8,3840]{3,2,1,0:T(8,128)(2,1)S(1)}, u32[]{:S(2)}) copy-start(bf16[4,4,8,3840]{3,2,1,0:T(8,128)(2,1)S(1)} %pad_maximum_fusion.refs_0_) | copy-start | bytes 2949124
  60.9 49.8 %copy-start.14 = (bf16[4,4,8,3712]{3,2,1,0:T(8,128)(2,1)}, bf16[4,4,8,3712]{3,2,1,0:T(8,128)(2,1)S(1)}, u32[]{:S(2)}) copy-start(bf16[4,4,8,3712]{3,2,1,0:T(8,128)(2,1)S(1)} %collective-permute-done.20.refs_10_) | copy-start | bytes 2850820
  60.9 24.5 %collective-permute-start.5 = (bf16[4,4,8,3840]{3,2,1,0:T(8,128)(2,1)S(1)}, bf16[4,4,8,3840]{3,2,1,0:T(8,128)(2,1)S(1)}, u32[]{:S(2)}, u32[]{:S(2)}) collective-permute-start(bf16[4,4,8,3840]{3,2,1,0:T(8,128)(2,1)S(1)} %pad_maximum_fusion.refs_0_), channel_id=1, source_target_pairs={{0,64},{1,65},{2,66},{3,67},{4,68},{5,69},{6,70},{7,71},{8,76},{9,... | collective-permute-start | bytes 2949128 | tf_op jit(solution)/shard_map/ppermute | solution.py:66
  61.2 27.0 %copy-start.15 = (bf16[4,4,8,3712]{3,2,1,0:T(8,128)(2,1)}, bf16[4,4,8,3712]{3,2,1,0:T(8,128)(2,1)S(1)}, u32[]{:S(2)}) copy-start(bf16[4,4,8,3712]{3,2,1,0:T(8,128)(2,1)S(1)} %collective-permute-done.30.refs_20_) | copy-start | bytes 2850820
  61.2 24.2 %collective-permute-start.6 = (bf16[4,4,8,3840]{3,2,1,0:T(8,128)(2,1)S(1)}, bf16[4,4,8,3840]{3,2,1,0:T(8,128)(2,1)S(1)}, u32[]{:S(2)}, u32[]{:S(2)}) collective-permute-start(bf16[4,4,8,3840]{3,2,1,0:T(8,128)(2,1)S(1)} %pad_maximum_fusion.refs_0_), channel_id=1, source_target_pairs={{0,68},{1,69},{2,70},{3,71},{4,64},{5,65},{6,66},{7,67},{8,72},{9,... | collective-permute-start | bytes 2949128 | tf_op jit(solution)/shard_map/ppermute | solution.py:66
  61.2 24.3 %collective-permute-start.22 = (bf16[4,4,8,3840]{3,2,1,0:T(8,128)(2,1)S(1)}, bf16[4,4,8,3840]{3,2,1,0:T(8,128)(2,1)S(1)}, u32[]{:S(2)}, u32[]{:S(2)}) collective-permute-start(bf16[4,4,8,3840]{3,2,1,0:T(8,128)(2,1)S(1)} %pad_maximum_fusion.refs_0_), channel_id=1, source_target_pairs={{0,8},{1,9},{2,10},{3,11},{4,12},{5,13},{6,14},{7,15},{8,0},{9,1},... | collective-permute-start | bytes 2949128 | tf_op jit(solution)/shard_map/ppermute | solution.py:62
  63.2 24.5 %collective-permute-start.14 = (bf16[4,4,8,3840]{3,2,0,1:T(8,128)(2,1)S(1)}, bf16[4,4,8,3840]{3,2,0,1:T(8,128)(2,1)S(1)}, u32[]{:S(2)}, u32[]{:S(2)}) collective-permute-start(bf16[4,4,8,3840]{3,2,0,1:T(8,128)(2,1)S(1)} %collective-permute-done.12), channel_id=1, source_target_pairs={{0,3},{1,2},{2,1},{3,0},{4,7},{5,6},{6,5},{7,4},{8,9},{9,8},{10,11... | collective-permute-start | bytes 2949128 | tf_op jit(solution)/shard_map/ppermute | solution.py:66
  64.9 22.7 %collective-permute-start.21 = (bf16[4,4,8,3712]{3,2,1,0:T(8,128)(2,1)S(1)}, bf16[4,4,8,3712]{3,2,1,0:T(8,128)(2,1)S(1)}, u32[]{:S(2)}, u32[]{:S(2)}) collective-permute-start(bf16[4,4,8,3712]{3,2,1,0:T(8,128)(2,1)S(1)} %collective-permute-done.19.refs_9_), channel_id=1, source_target_pairs={{0,48},{1,49},{2,50},{3,51},{4,52},{5,53},{6,54},{7,55},{8,24},{9,... | collective-permute-start | bytes 2850824 | tf_op jit(solution)/shard_map/ppermute | solution.py:66
  85.4 28.1 %copy-start.6 = (bf16[4,4,8,3840]{3,2,1,0:T(8,128)(2,1)}, bf16[4,4,8,3840]{3,2,1,0:T(8,128)(2,1)S(1)}, u32[]{:S(2)}) copy-start(bf16[4,4,8,3840]{3,2,1,0:T(8,128)(2,1)S(1)} %collective-permute-done.5.refs_1_) | copy-start | bytes 2949124
  85.4 6.7 %collective-permute-start.27 = (bf16[4,4,8,3840]{3,2,0,1:T(8,128)(2,1)S(1)}, bf16[4,4,8,3840]{3,2,0,1:T(8,128)(2,1)S(1)}, u32[]{:S(2)}, u32[]{:S(2)}) collective-permute-start(bf16[4,4,8,3840]{3,2,0,1:T(8,128)(2,1)S(1)} %collective-permute-done.12), channel_id=1, source_target_pairs={{0,8},{1,9},{2,10},{3,11},{4,12},{5,13},{6,14},{7,15},{8,0},{9,1},... | collective-permute-start | bytes 2949128 | tf_op jit(solution)/shard_map/ppermute | solution.py:62
  85.4 28.1 %copy-start.7 = (bf16[4,4,8,3840]{3,2,1,0:T(8,128)(2,1)}, bf16[4,4,8,3840]{3,2,1,0:T(8,128)(2,1)S(1)}, u32[]{:S(2)}) copy-start(bf16[4,4,8,3840]{3,2,1,0:T(8,128)(2,1)S(1)} %collective-permute-done.6.refs_2_) | copy-start | bytes 2949124
  85.4 13.3 %collective-permute-start.7 = (bf16[4,4,8,3840]{3,2,1,0:T(8,128)(2,1)S(1)}, bf16[4,4,8,3840]{3,2,1,0:T(8,128)(2,1)S(1)}, u32[]{:S(2)}, u32[]{:S(2)}) collective-permute-start(bf16[4,4,8,3840]{3,2,1,0:T(8,128)(2,1)S(1)} %collective-permute-done.5.refs_1_), channel_id=1, source_target_pairs={{0,68},{1,69},{2,70},{3,71},{4,64},{5,65},{6,66},{7,67},{8,72},{9,... | collective-permute-start | bytes 2949128 | tf_op jit(solution)/shard_map/ppermute | solution.py:66
  85.5 28.0 %copy-start.8 = (bf16[4,4,8,3840]{3,2,1,0:T(8,128)(2,1)}, bf16[4,4,8,3840]{3,2,1,0:T(8,128)(2,1)S(1)}, u32[]{:S(2)}) copy-start(bf16[4,4,8,3840]{3,2,1,0:T(8,128)(2,1)S(1)} %collective-permute-done.22.refs_12_) | copy-start | bytes 2949124
  85.5 16.1 %collective-permute-start.28 = (bf16[4,4,8,3840]{3,2,0,1:T(8,128)(2,1)S(1)}, bf16[4,4,8,3840]{3,2,0,1:T(8,128)(2,1)S(1)}, u32[]{:S(2)}, u32[]{:S(2)}) collective-permute-start(bf16[4,4,8,3840]{3,2,0,1:T(8,128)(2,1)S(1)} %collective-permute-done.13), channel_id=1, source_target_pairs={{0,8},{1,9},{2,10},{3,11},{4,12},{5,13},{6,14},{7,15},{8,0},{9,1},... | collective-permute-start | bytes 2949128 | tf_op jit(solution)/shard_map/ppermute | solution.py:62
  87.6 23.1 %copy-start.16 = (bf16[4,4,8,3712]{3,2,1,0:T(8,128)(2,1)}, bf16[4,4,8,3712]{3,2,1,0:T(8,128)(2,1)S(1)}, u32[]{:S(2)}) copy-start(bf16[4,4,8,3712]{3,2,1,0:T(8,128)(2,1)S(1)} %collective-permute-done.21.refs_11_) | copy-start | bytes 2850820
  87.6 3.5 %collective-permute-start.31 = (bf16[4,4,8,3712]{3,2,1,0:T(8,128)(2,1)S(1)}, bf16[4,4,8,3712]{3,2,1,0:T(8,128)(2,1)S(1)}, u32[]{:S(2)}, u32[]{:S(2)}) collective-permute-start(bf16[4,4,8,3712]{3,2,1,0:T(8,128)(2,1)S(1)} %collective-permute-done.19.refs_9_), channel_id=1, source_target_pairs={{0,8},{1,9},{2,10},{3,11},{4,12},{5,13},{6,14},{7,15},{8,0},{9,1},... | collective-permute-start | bytes 2850824 | tf_op jit(solution)/shard_map/ppermute | solution.py:62
  87.7 14.0 %collective-permute-start.29 = (bf16[4,4,8,3840]{3,2,0,1:T(8,128)(2,1)S(1)}, bf16[4,4,8,3840]{3,2,0,1:T(8,128)(2,1)S(1)}, u32[]{:S(2)}, u32[]{:S(2)}) collective-permute-start(bf16[4,4,8,3840]{3,2,0,1:T(8,128)(2,1)S(1)} %collective-permute-done.14), channel_id=1, source_target_pairs={{0,8},{1,9},{2,10},{3,11},{4,12},{5,13},{6,14},{7,15},{8,0},{9,1},... | collective-permute-start | bytes 2949128 | tf_op jit(solution)/shard_map/ppermute | solution.py:62
  91.2 19.4 %collective-permute-start.23 = (bf16[4,4,8,3840]{3,2,1,0:T(8,128)(2,1)S(1)}, bf16[4,4,8,3840]{3,2,1,0:T(8,128)(2,1)S(1)}, u32[]{:S(2)}, u32[]{:S(2)}) collective-permute-start(bf16[4,4,8,3840]{3,2,1,0:T(8,128)(2,1)S(1)} %collective-permute-done.5.refs_1_), channel_id=1, source_target_pairs={{0,8},{1,9},{2,10},{3,11},{4,12},{5,13},{6,14},{7,15},{8,0},{9,1},... | collective-permute-start | bytes 2949128 | tf_op jit(solution)/shard_map/ppermute | solution.py:62
  92.2 18.5 %collective-permute-start.24 = (bf16[4,4,8,3840]{3,2,1,0:T(8,128)(2,1)S(1)}, bf16[4,4,8,3840]{3,2,1,0:T(8,128)(2,1)S(1)}, u32[]{:S(2)}, u32[]{:S(2)}) collective-permute-start(bf16[4,4,8,3840]{3,2,1,0:T(8,128)(2,1)S(1)} %collective-permute-done.6.refs_2_), channel_id=1, source_target_pairs={{0,8},{1,9},{2,10},{3,11},{4,12},{5,13},{6,14},{7,15},{8,0},{9,1},... | collective-permute-start | bytes 2949128 | tf_op jit(solution)/shard_map/ppermute | solution.py:62
  98.8 14.8 %copy-start.9 = (bf16[4,4,8,3840]{3,2,1,0:T(8,128)(2,1)}, bf16[4,4,8,3840]{3,2,1,0:T(8,128)(2,1)S(1)}, u32[]{:S(2)}) copy-start(bf16[4,4,8,3840]{3,2,1,0:T(8,128)(2,1)S(1)} %collective-permute-done.7.refs_3_) | copy-start | bytes 2949124
  98.8 11.9 %collective-permute-start.25 = (bf16[4,4,8,3840]{3,2,1,0:T(8,128)(2,1)S(1)}, bf16[4,4,8,3840]{3,2,1,0:T(8,128)(2,1)S(1)}, u32[]{:S(2)}, u32[]{:S(2)}) collective-permute-start(bf16[4,4,8,3840]{3,2,1,0:T(8,128)(2,1)S(1)} %collective-permute-done.7.refs_3_), channel_id=1, source_target_pairs={{0,8},{1,9},{2,10},{3,11},{4,12},{5,13},{6,14},{7,15},{8,0},{9,1},... | collective-permute-start | bytes 2949128 | tf_op jit(solution)/shard_map/ppermute | solution.py:62
  101.7 8.9 %collective-permute-start.32 = (bf16[4,4,8,3712]{3,2,1,0:T(8,128)(2,1)S(1)}, bf16[4,4,8,3712]{3,2,1,0:T(8,128)(2,1)S(1)}, u32[]{:S(2)}, u32[]{:S(2)}) collective-permute-start(bf16[4,4,8,3712]{3,2,1,0:T(8,128)(2,1)S(1)} %collective-permute-done.20.refs_10_), channel_id=1, source_target_pairs={{0,8},{1,9},{2,10},{3,11},{4,12},{5,13},{6,14},{7,15},{8,0},{9,1},... | collective-permute-start | bytes 2850824 | tf_op jit(solution)/shard_map/ppermute | solution.py:62
  101.8 8.9 %collective-permute-start.33 = (bf16[4,4,8,3712]{3,2,1,0:T(8,128)(2,1)S(1)}, bf16[4,4,8,3712]{3,2,1,0:T(8,128)(2,1)S(1)}, u32[]{:S(2)}, u32[]{:S(2)}) collective-permute-start(bf16[4,4,8,3712]{3,2,1,0:T(8,128)(2,1)S(1)} %collective-permute-done.21.refs_11_), channel_id=1, source_target_pairs={{0,8},{1,9},{2,10},{3,11},{4,12},{5,13},{6,14},{7,15},{8,0},{9,1},... | collective-permute-start | bytes 2850824 | tf_op jit(solution)/shard_map/ppermute | solution.py:62
  137.0 19.7 %collective-permute-start.34 = (f32[4,128]{1,0:T(4,128)}, f32[4,128]{1,0:T(4,128)S(1)}, u32[]{:S(2)}, u32[]{:S(2)}) collective-permute-start(f32[4,128]{1,0:T(4,128)} %get-tuple-element.5), channel_id=1, source_target_pairs={{0,8},{1,9},{2,10},{3,11},{4,12},{5,13},{6,14},{7,15},{8,0},{9,1},... | collective-permute-start | bytes 6152 | tf_op jit(solution)/shard_map/ppermute | solution.py:62
  137.3 5.2 %copy-start = (bf16[512,14336]{1,0:T(8,128)(2,1)S(1)}, bf16[512,14336]{1,0:T(8,128)(2,1)}, u32[]{:S(2)}) copy-start(bf16[512,14336]{1,0:T(8,128)(2,1)} %acts_ref.1) | copy-start | bytes 44040196
  145.9 10.8 %copy-start.5 = (f32[4,128]{1,0:T(4,128)S(1)}, f32[4,128]{1,0:T(4,128)}, u32[]{:S(2)}) copy-start(f32[4,128]{1,0:T(4,128)} %get-tuple-element.5) | copy-start | bytes 6148
  145.9 10.9 %copy-start.4 = (f32[4,512]{1,0:T(4,128)S(1)}, f32[4,512]{1,0:T(4,128)}, u32[]{:S(2)}) copy-start(f32[4,512]{1,0:T(4,128)} %get-tuple-element.4) | copy-start | bytes 24580
  (7 other events, 11.1 us)

commit v2 on v1

v2 whole, which is shorter than its diff:
```python
import functools
import math

import jax
import jax.numpy as jnp
from jax import lax
from jax.experimental import pallas as pl
from jax.experimental.pallas import tpu as pltpu
from jax.sharding import PartitionSpec as P

D = 8192
FF = 14336
BLK = 128
NVAL = 4
TOK = 512
VAL = 512
AXES = ("dp", "seq")
HA = FF // 2
HG = D // 2
C1 = 3840
C2A = HA - C1
C2G = 512
C2 = C2A + C2G
C3G = HG - C2G
IDW = 128
C3 = C3G + IDW
MASKS = ((1, 3), (3, 1))


def coords(i):
    dp, seq = divmod(i, 8)
    c = dp % 2
    z = (dp // 2) % 4
    x = (seq // 4) * 2 + dp // 8
    return {"x": x, "y": seq % 4, "z": z, "c": c}


def index(p):
    dp = ((p["x"] % 2) * 4 + p["z"]) * 2 + p["c"]
    return dp * 8 + (p["x"] // 2) * 4 + p["y"]


def ring_pairs(axis, step):
    pairs = []
    for i in range(128):
        p = coords(i)
        p[axis] ^= MASKS[p["c"]][step]
        pairs.append((i, index(p)))
    return pairs


def core_pairs():
    pairs = []
    for i in range(128):
        p = coords(i)
        p["c"] ^= 1
        pairs.append((i, index(p)))
    return pairs


def swap(x):
    return lax.ppermute(x, AXES, core_pairs())


def hop(x, axis, step):
    return lax.ppermute(x, AXES, ring_pairs(axis, step))


def double(x, axis, step):
    return jnp.stack([x, hop(x, axis, step)])


def gate(xs, dep):
    n = len(xs)
    anyspec = pl.BlockSpec(memory_space=pl.ANY)
    return pl.pallas_call(
        lambda *refs: None,
        in_specs=[anyspec] * (n + 1),
        out_specs=[anyspec] * n,
        out_shape=[jax.ShapeDtypeStruct(x.shape, x.dtype) for x in xs],
        input_output_aliases={i: i for i in range(n)},
        cost_estimate=pl.CostEstimate(flops=0, bytes_accessed=0, transcendentals=0),
    )(*xs, dep)


def nt(a, b):
    return lax.dot_general(a, b, (((1,), (1,)), ((), ())), preferred_element_type=jnp.float32)


def self_add(acc, ref):
    acc[0:256, :] += nt(ref[256:512, :], ref[0:256, :])
    acc[256:384, 0:128] += nt(ref[128:256, :], ref[0:128, :])
    acc[384:512, 0:128] += nt(ref[384:512, :], ref[256:384, :])


def self_acts_body(acts_ref, dep_ref, out_ref):
    @pl.when(pl.program_id(0) == 0)
    def _():
        out_ref[...] = jnp.zeros_like(out_ref)

    self_add(out_ref, acts_ref)


def self_grads_body(grads_ref, sa_ref, dep_ref, out_ref, sg, *, steps):
    i = pl.program_id(0)

    @pl.when(i == 0)
    def _():
        sg[...] = jnp.zeros_like(sg)

    self_add(sg, grads_ref)

    @pl.when(i == steps - 1)
    def _():
        k = sa_ref[...] * sg[...]
        rows = lax.broadcasted_iota(jnp.int32, (4, 4), 0)
        cols = lax.broadcasted_iota(jnp.int32, (4, 4), 1)
        out = jnp.zeros((4, 4), jnp.float32)
        spots = (
            (2, 0, 0, 0), (2, 1, 0, 128), (3, 0, 128, 0), (3, 1, 128, 128),
            (1, 0, 256, 0), (3, 2, 384, 0),
        )
        for b, c, r0, c0 in spots:
            s = jnp.sum(k[r0:r0 + 128, c0:c0 + 128])
            out = jnp.where((rows == b) & (cols == c), s, out)
        out_ref[...] = out / (float(BLK) * math.sqrt(float(FF) * float(D)))


KC = 2048


def self_acts(acts, dep):
    return pl.pallas_call(
        self_acts_body,
        grid=(FF // KC,),
        in_specs=[
            pl.BlockSpec((TOK, KC), lambda i: (0, i)),
            pl.BlockSpec(memory_space=pl.ANY),
        ],
        out_specs=pl.BlockSpec((512, 256), lambda i: (0, 0)),
        out_shape=jax.ShapeDtypeStruct((512, 256), jnp.float32),
        compiler_params=pltpu.CompilerParams(vmem_limit_bytes=16 << 20),
        cost_estimate=pl.CostEstimate(
            flops=2 * 512 * 256 * FF, bytes_accessed=2 * TOK * FF, transcendentals=0
        ),
    )(acts, dep)


def self_grads(grads, sa, dep):
    return pl.pallas_call(
        functools.partial(self_grads_body, steps=D // KC),
        grid=(D // KC,),
        in_specs=[
            pl.BlockSpec((TOK, KC), lambda i: (0, i)),
            pl.BlockSpec((512, 256), lambda i: (0, 0)),
            pl.BlockSpec(memory_space=pl.ANY),
        ],
        out_specs=pl.BlockSpec((4, 4), lambda i: (0, 0)),
        out_shape=jax.ShapeDtypeStruct((4, 4), jnp.float32),
        scratch_shapes=[pltpu.VMEM((512, 256), jnp.float32)],
        compiler_params=pltpu.CompilerParams(vmem_limit_bytes=16 << 20),
        cost_estimate=pl.CostEstimate(
            flops=2 * 512 * 256 * D, bytes_accessed=2 * TOK * D, transcendentals=0
        ),
    )(grads, sa, dep)


RUNS = ("y", "z", "x")
STEP5 = ("z", "x", "y")
STEP6 = ("x", "y", "z")
WEIGHT = {"x": 4, "y": 2, "z": 1}


def place(part, k, s4):
    n = s4 * WEIGHT[RUNS[part]]
    if k in (1, 3):
        n += WEIGHT[STEP5[part]]
    if k in (2, 3):
        n += WEIGHT[STEP6[part]]
    return n


WIDTHS = (C1, C2, C3)
STARTS = (0, C1, C1 + C2)
ALLW = C1 + C2 + C3
ORDER = tuple((half, part) for half in range(2) for part in range(3))
SEGMENTS = ((("a", 0, C1),), (("a", 0, C2A), ("g", C2A, C2G)), (("g", 0, C3G),))


def train_copies(acts, grads, o, part, dst):
    a0 = pl.multiple_of(o * HA, 128)
    g0 = pl.multiple_of(o * HG, 128)
    if part == 0:
        return [(acts.at[:, pl.ds(a0, C1)], dst.at[:, pl.ds(0, C1)])]
    if part == 1:
        return [
            (acts.at[:, pl.ds(a0 + C1, C2A)], dst.at[:, pl.ds(0, C2A)]),
            (grads.at[:, pl.ds(g0, C2G)], dst.at[:, pl.ds(C2A, C2G)]),
        ]
    return [(grads.at[:, pl.ds(g0 + C2G, C3G)], dst.at[:, pl.ds(0, C3G)])]


def add_rows(acc, half, at, x):
    if half == 0:
        acc[at] += x.reshape(8, 8, TOK)
    else:
        acc[:, at] += x.reshape(8, 8, TOK)


def early_body(core_ref, acts, grads, *refs, half):
    if half == 0:
        pieces = refs[:9]
        ca, cg, pbuf, hbuf, sems = refs[9:]
        ca[...] = jnp.zeros_like(ca)
        cg[...] = jnp.zeros_like(cg)
    else:
        pieces = refs[:3]
        ain, gin, ca, cg, pbuf, hbuf, sems = refs[3:]
    c = core_ref[0]
    o = c if half == 0 else 1 - c
    todo = []
    for part in range(3):
        w, s = WIDTHS[part], STARTS[part]
        out = []
        for k in range(3):
            if half == 0:
                out.append((pieces[part * 3 + k], pbuf.at[k, :, :, :, pl.ds(s, w)]))
            else:
                out.append(
                    (pieces[k].at[:, :, :, pl.ds(s, w)], pbuf.at[k, :, :, :, pl.ds(s, w)])
                )
        out += train_copies(acts, grads, o, part, hbuf.at[part])
        cps = [pltpu.make_async_copy(a, b, sems.at[part, i]) for i, (a, b) in enumerate(out)]
        for cp in cps:
            cp.start()
        todo.append(cps)
    if half == 1:
        moves = [
            pltpu.make_async_copy(ain, ca, sems.at[3, 0]),
            pltpu.make_async_copy(gin, cg, sems.at[3, 1]),
        ]
        for cp in moves:
            cp.start()
        for cp in moves:
            cp.wait()
    for part in range(3):
        for cp in todo[part]:
            cp.wait()
        for name, at, w in SEGMENTS[part]:
            acc = ca if name == "a" else cg
            p0 = STARTS[part] + at
            rows = pbuf[:, :, :, :, p0:p0 + w].reshape(384, w)
            x = nt(rows, hbuf[part, :, at:at + w])
            for k in range(3):
                for s4 in range(2):
                    r = k * 128 + s4 * 64
                    add_rows(acc, half, place(part, k, s4), x[r:r + 64])


def early_cross(core, acts, grads, pieces, accs, half):
    anyspec = pl.BlockSpec(memory_space=pl.ANY)
    vmem = pl.BlockSpec(memory_space=pltpu.VMEM)
    args = list(pieces) + list(accs)
    return pl.pallas_call(
        functools.partial(early_body, half=half),
        in_specs=[pl.BlockSpec(memory_space=pltpu.SMEM)] + [anyspec] * (2 + len(args)),
        out_specs=[vmem] * 2,
        out_shape=[jax.ShapeDtypeStruct((8, 8, 8, TOK), jnp.float32)] * 2,
        scratch_shapes=[
            pltpu.VMEM((3, 2, 8, 8, ALLW), jnp.bfloat16),
            pltpu.VMEM((3, TOK, C1), jnp.bfloat16),
            pltpu.SemaphoreType.DMA((4, 6)),
        ],
        compiler_params=pltpu.CompilerParams(vmem_limit_bytes=28 << 20),
        cost_estimate=pl.CostEstimate(
            flops=2 * 512 * 384 * (HA + HG), bytes_accessed=2 * TOK * (FF + D), transcendentals=0
        ),
    )(core, acts, grads, *args)


def late_body(core_ref, acts, grads, gram_ref, ain, gin, *refs):
    own, other = refs[:12], refs[12:16]
    raw_ref, norm_ref, vbuf, hbuf, ca, cg, ka, kg, ids, sems, asem = refs[16:]
    c = core_ref[0]

    def copies(n):
        half, part = ORDER[n]
        b = n % 2
        w, s = WIDTHS[part], STARTS[part]
        out = []
        for k in range(4):
            for s4 in range(2):
                at = place(part, k, s4)
                if half == 0:
                    out.append((own[part * 4 + k].at[s4], vbuf.at[b, at, :, :, pl.ds(0, w)]))
                else:
                    out.append(
                        (other[k].at[s4, :, :, pl.ds(s, w)], vbuf.at[b, :, at, :, pl.ds(0, w)])
                    )
        o = c if half == 0 else 1 - c
        out += train_copies(acts, grads, o, part, hbuf.at[b])
        return [pltpu.make_async_copy(x, y, sems.at[b, i]) for i, (x, y) in enumerate(out)]

    for cp in copies(0):
        cp.start()
    moves = [
        pltpu.make_async_copy(ain, ca, asem.at[0]),
        pltpu.make_async_copy(gin, cg, asem.at[1]),
    ]
    for cp in moves:
        cp.start()
    for cp in moves:
        cp.wait()
    seen = set()
    for n, (half, part) in enumerate(ORDER):
        b = n % 2
        if n + 1 < len(ORDER):
            for cp in copies(n + 1):
                cp.start()
        for cp in copies(n):
            cp.wait()
        for name, at, w in SEGMENTS[part]:
            cross, kern = (ca, ka) if name == "a" else (cg, kg)
            cols = slice(at, at + w)
            rows = vbuf[b, :, :, :, cols].reshape(VAL, w)
            even = vbuf[b, :, 0:4, :, cols].reshape(VAL // 2, w)
            late = vbuf[b, 4:8, :, :, cols].reshape(VAL // 2, w)
            mine = jnp.where(c == 0, even, late)
            y = nt(mine, rows)
            if name in seen:
                kern[...] += y
            else:
                kern[...] = y
                seen.add(name)
            spots = [place(part, 3, s4) for s4 in range(2)]
            if half == 0:
                last = [vbuf[b, at4, :, :, cols].reshape(64, w) for at4 in spots]
            else:
                last = [vbuf[b, :, at4, :, cols].reshape(64, w) for at4 in spots]
            x = nt(jnp.concatenate(last, axis=0), hbuf[b, :, cols])
            for s4 in range(2):
                add_rows(cross, half, spots[s4], x[s4 * 64:s4 * 64 + 64])
        if n == 2:
            ids[...] = vbuf[b, :, :, :, C3G:C3].astype(jnp.float32)

    cross = ca[...].reshape(VAL, TOK) * cg[...].reshape(VAL, TOK)
    kern = ka[...] * kg[...]
    all_ids = ids[...].reshape(VAL, IDW)
    row_ids = jnp.transpose(all_ids)[0:1, :]
    half_ids = jnp.where(
        c == 0,
        ids[:, 0:4].reshape(VAL // 2, IDW),
        ids[4:8].reshape(VAL // 2, IDW),
    )
    for v in range(NVAL):
        keep = jnp.where(all_ids == float(v), 1.0, 0.0)
        keep = jnp.concatenate([keep] * 4, axis=1)
        raw_ref[v:v + 1, :] = jnp.sum(cross * keep, axis=0, keepdims=True)
        keep = jnp.where(half_ids == float(v), 1.0, 0.0)
        keep = jnp.concatenate([keep] * 4, axis=1)
        part = jnp.sum(kern * keep, axis=0, keepdims=True)
        part = jnp.sum(jnp.where(row_ids == float(v), part, 0.0))
        norm_ref[v:v + 1, :] = jnp.full((1, 128), part, jnp.float32)


def late_cross(core, acts, grads, gram, accs, own, other):
    anyspec = pl.BlockSpec(memory_space=pl.ANY)
    args = list(accs) + list(own) + list(other)
    return pl.pallas_call(
        late_body,
        in_specs=[pl.BlockSpec(memory_space=pltpu.SMEM)] + [anyspec] * (3 + len(args)),
        out_specs=[pl.BlockSpec(memory_space=pltpu.VMEM)] * 2,
        out_shape=[
            jax.ShapeDtypeStruct((NVAL, TOK), jnp.float32),
            jax.ShapeDtypeStruct((NVAL, 128), jnp.float32),
        ],
        scratch_shapes=[
            pltpu.VMEM((2, 8, 8, 8, C1), jnp.bfloat16),
            pltpu.VMEM((2, TOK, C1), jnp.bfloat16),
            pltpu.VMEM((8, 8, 8, TOK), jnp.float32),
            pltpu.VMEM((8, 8, 8, TOK), jnp.float32),
            pltpu.VMEM((VAL // 2, VAL), jnp.float32),
            pltpu.VMEM((VAL // 2, VAL), jnp.float32),
            pltpu.VMEM((8, 8, 8, IDW), jnp.float32),
            pltpu.SemaphoreType.DMA((2, 10)),
            pltpu.SemaphoreType.DMA((2,)),
        ],
        compiler_params=pltpu.CompilerParams(vmem_limit_bytes=28 << 20),
        cost_estimate=pl.CostEstimate(
            flops=2 * 512 * 384 * (FF + D), bytes_accessed=4 * TOK * (FF + D), transcendentals=0
        ),
    )(core, acts, grads, gram, *args)


def shards(hidden_acts, out_grads, val_acts, val_grads, val_ids):
    hidden_acts = pltpu.with_memory_space_constraint(hidden_acts, pltpu.HBM)
    out_grads = pltpu.with_memory_space_constraint(out_grads, pltpu.HBM)
    core = lax.axis_index("dp") % 2
    first = core == 0
    idcol = jnp.broadcast_to(val_ids[:, None].astype(jnp.bfloat16), (4, IDW))
    halves = [
        jnp.concatenate(
            [val_acts[:, h * HA:(h + 1) * HA], val_grads[:, h * HG:(h + 1) * HG], idcol], axis=1
        )
        for h in range(2)
    ]
    keep = jnp.where(first, halves[0], halves[1])
    got = swap(jnp.where(first, halves[1], halves[0]))
    rows = jnp.concatenate([jnp.where(first, keep, got), jnp.where(first, got, keep)], axis=0)

    rows = double(rows, "z", 0)
    rows = double(rows, "y", 0)
    sa = self_acts(hidden_acts, rows)
    (rows,) = gate([double(rows, "x", 0)], sa)
    rows = rows.reshape(8, 8, ALLW)
    block_gram = self_grads(out_grads, sa, rows)
    piece = [[rows[..., s:s + w]] for s, w in zip(STARTS, WIDTHS)]
    grown = [double(piece[j][0], RUNS[j], 1) for j in range(3)]
    piece = [[x] for x in gate(grown, block_gram)]
    for j in range(3):
        piece[j].append(hop(piece[j][0], STEP5[j], 1))
    for j in range(3):
        piece[j].append(hop(piece[j][0], STEP6[j], 1))
    for j in range(3):
        piece[j].append(hop(piece[j][1], STEP6[j], 1))
    joined = [jnp.concatenate([piece[j][k] for j in range(3)], axis=-1) for k in range(4)]
    other = [swap(x) for x in joined[:3]]
    core = core.reshape(1).astype(jnp.int32)
    accs = early_cross(
        core, hidden_acts, out_grads, [piece[j][k] for j in range(3) for k in range(3)], [], 0
    )
    other += [swap(x) for x in gate(joined[3:], accs[0])]
    accs = early_cross(core, hidden_acts, out_grads, other[:3], accs, 1)
    raw, norm = late_cross(
        core, hidden_acts, out_grads, block_gram, accs,
        [piece[j][k] for j in range(3) for k in range(4)], other,
    )
    norm = norm + swap(norm)
    token_scores = raw * lax.rsqrt(norm[:, :1] + 1e-06)
    return (token_scores, block_gram)


def solution(mesh):
    return jax.shard_map(
        shards,
        mesh=mesh,
        in_specs=(
            P(AXES, None),
            P(AXES, None),
            P(AXES, None),
            P(AXES, None),
            P(AXES),
        ),
        out_specs=(P(None, AXES), P(AXES, None)),
        check_vma=False,
    )
```

time: 158 us -> 144 us (0.911)
  waiting for transfers between devices: 46.2 us -> 22.7 us
  Pallas kernels: 34.2 us -> 53.9 us
  local copies, waits for them, and re-layouts: 22.3 us -> 8.95 us
  other arithmetic: 2.65 us -> 15.6 us
  starting transfers between devices: 51 us -> 41.1 us
    ppermute x21 -> x15, waiting for transfers between devices: 42.2 us -> 20.8 us  [hop(): return lax.ppermute(x, AXES, ring_pairs(axis, step))]
    pallas_call x2 -> x8, Pallas kernels: 34.2 us -> 53.9 us  [the longest x1 21.6 us: late_cross(): pl.pallas_call(late_body, in_specs=[pl.BlockSpec(memory_space=pltpu.SMEM)...]
    concatenate x2 -> x4, other arithmetic: 0.1 us -> 9.25 us  [shards(): jnp.concatenate([piece[j][k] for j in range(3)], axis=-1)]
    unnamed x40 -> x58, local copies, waits for them, and re-layouts: 12 us -> 4.65 us
    ppermute x7 -> x0, local copies, waits for them, and re-layouts: 7.36 us -> none  [the longest x4 4.21 us: swap(): return lax.ppermute(x, AXES, core_pairs())]
    ppermute x14 -> x6, starting transfers between devices: 31.8 us -> 25.1 us  [swap(): return lax.ppermute(x, AXES, core_pairs())]
    another operation x17 -> x7, other arithmetic: 0.9 us -> 4.68 us  [double(): return jnp.stack([x, hop(x, axis, step)])]
    ppermute x21 -> x15, starting transfers between devices: 19.2 us -> 16 us  [hop(): return lax.ppermute(x, AXES, ring_pairs(axis, step))]
  transfers between devices with their start and end apart: 35 -> 21, of which waited for: 12 -> 8; matrix products, arithmetic and copies ran while one was open for 6% -> 9% of each run, Pallas kernels for 7% -> 23%
where the time goes in v2:
time: 144 us; the launch traced here: 143 us
  Pallas kernels  53.9 us (37%)
  starting transfers between devices  41.1 us (29%)
  waiting for transfers between devices  22.7 us (16%)
  other arithmetic  15.6 us (11%)
  local copies, waits for them, and re-layouts  8.95 us (6%)
    ppermute x6, starting transfers between devices, swap(): return lax.ppermute(x, AXES, core_pairs())  25.1 us
    pallas_call x1, Pallas kernels, late_cross(): pl.pallas_call(late_body, in_specs=[pl.BlockSpec(memory_space=pltpu.SMEM)...  21.6 us
    ppermute x15, waiting for transfers between devices, hop(): return lax.ppermute(x, AXES, ring_pairs(axis, step))  20.8 us
    pallas_call x2, Pallas kernels, early_cross(): pl.pallas_call(functools.partial(early_body, half=half), in_specs=[pl.Blo...  16.5 us
    ppermute x15, starting transfers between devices, hop(): return lax.ppermute(x, AXES, ring_pairs(axis, step))  16 us
    pallas_call x1, Pallas kernels, self_acts(): pl.pallas_call(self_acts_body, grid=(FF // KC,), in_specs=[pl.BlockSpec((...  9.48 us
    concatenate x4, other arithmetic, shards(): jnp.concatenate([piece[j][k] for j in range(3)], axis=-1)  9.25 us
    pallas_call x1, Pallas kernels, self_grads(): pl.pallas_call(functools.partial(self_grads_body, steps=D // KC), grid=(D...  6.35 us
  transfers between devices with their start and end apart: 21, of which 8 were waited for; matrix products, arithmetic and copies ran while one was open for 9% of the time, Pallas kernels for 23%

profile of v2, /device:TPU:1, one launch (start us, length us, event | category | flops | bytes accessed | tf_op | source)
XLA Modules:
  0.0 143.3 jit_solution(2977690708984094999)
XLA Ops:
  0.6 0.7 convert_element_type.4
  1.3 0.8 fusion.4
  2.1 0.9 fusion.3
  3.2 1.5 %collective-permute-start = (bf16[4,11392]{1,0:T(4,128)(2,1)S(1)}, bf16[4,11392]{1,0:T(4,128)(2,1)S(1)}, u32[]{:S(2)}, u32[]{:S(2)}) collective-permute-start(bf16[4,11392]{1,0:T(4,128)(2,1)S(1)} %broadcast_select_fusion.2), channel_id=1, source_target_pairs={{0,8},{1,9},{2,10},{3,11},{4,12},{5,13},{6,14},{7,15},{8,0},{9,1},... | collective-permute-start | bytes 273416 | tf_op jit(solution)/shard_map/ppermute | solution.py:62
  4.7 0.9 collective-permute-done
  5.6 0.1 broadcast_select_fusion.1
  5.8 3.9 %collective-permute-start.1 = (bf16[8,11392]{1,0:T(8,128)(2,1)S(1)}, bf16[8,11392]{1,0:T(8,128)(2,1)S(1)}, u32[]{:S(2)}, u32[]{:S(2)}) collective-permute-start(bf16[8,11392]{1,0:T(8,128)(2,1)S(1)} %get-tuple-element.33), channel_id=1, source_target_pairs={{0,16},{1,17},{2,18},{3,19},{4,20},{5,21},{6,22},{7,23},{8,56},{9,... | collective-permute-start | bytes 546824 | tf_op jit(solution)/shard_map/ppermute | solution.py:66
  9.7 2.9 %collective-permute-done.1 = bf16[8,11392]{1,0:T(8,128)(2,1)S(1)} collective-permute-done((bf16[8,11392]{1,0:T(8,128)(2,1)S(1)}, bf16[8,11392]{1,0:T(8,128)(2,1)S(1)}, u32[]{:S(2)}, u32[]{:S(2)}) %collective-permute-start.1) | collective-permute-done | bytes 182304 | tf_op jit(solution)/shard_map/ppermute | solution.py:66
  12.7 2.8 %collective-permute-start.2 = (bf16[2,8,11392]{2,1,0:T(8,128)(2,1)S(1)}, bf16[2,8,11392]{2,1,0:T(8,128)(2,1)S(1)}, u32[]{:S(2)}, u32[]{:S(2)}) collective-permute-start(bf16[2,8,11392]{2,1,0:T(8,128)(2,1)S(1)} %get-tuple-element.29), channel_id=1, source_target_pairs={{0,1},{1,0},{2,3},{3,2},{4,5},{5,4},{6,7},{7,6},{8,11},{9,10},{10,... | collective-permute-start | bytes 1093640 | tf_op jit(solution)/shard_map/ppermute | solution.py:66
  15.5 4.9 %collective-permute-done.2 = bf16[2,8,11392]{2,1,0:T(8,128)(2,1)S(1)} collective-permute-done((bf16[2,8,11392]{2,1,0:T(8,128)(2,1)S(1)}, bf16[2,8,11392]{2,1,0:T(8,128)(2,1)S(1)}, u32[]{:S(2)}, u32[]{:S(2)}) %collective-permute-start.2) | collective-permute-done | bytes 364576 | tf_op jit(solution)/shard_map/ppermute | solution.py:66
  20.5 2.6 %collective-permute-start.3 = (bf16[2,2,8,11392]{3,2,1,0:T(8,128)(2,1)S(1)}, bf16[2,2,8,11392]{3,2,1,0:T(8,128)(2,1)S(1)}, u32[]{:S(2)}, u32[]{:S(2)}) collective-permute-start(bf16[2,2,8,11392]{3,2,1,0:T(8,128)(2,1)S(1)} %get-tuple-element.27.dep_ref), channel_id=1, source_target_pairs={{0,64},{1,65},{2,66},{3,67},{4,68},{5,69},{6,70},{7,71},{8,76},{9,... | collective-permute-start | bytes 2187272 | tf_op jit(solution)/shard_map/ppermute | solution.py:66
  23.0 9.5 %shard_map.68.refs_1_.sa_ref = f32[512,256]{1,0:T(8,128)S(1)} custom-call(bf16[512,14336]{1,0:T(8,128)(2,1)} %acts.5, bf16[2,2,8,11392]{3,2,1,0:T(8,128)(2,1)S(1)} %get-tuple-element.27.dep_ref), custom_call_target="tpu_custom_call" | custom-call | flops 3758096384 | bytes 14680064 | tf_op jit(solution)/shard_map/pallas_call | solution.py:133
  32.5 0.8 copy-done.16
  33.3 1.3 pad_maximum_fusion.4.refs_0_
  34.6 1.2 slice_bitcast_fusion
  35.9 1.3 slice_bitcast_fusion.1
  37.4 6.4 %shard_map.70.refs_3_.gram_ref = f32[4,4]{1,0:T(4,128)} custom-call(bf16[512,8192]{1,0:T(8,128)(2,1)} %grads.5, f32[512,256]{1,0:T(8,128)S(1)} %copy-done.17, bf16[8,8,11392]{2,1,0:T(8,128)(2,1)S(1)} %bitcast.22), custom_call_target="tpu_custom_call" | custom-call | flops 2147483648 | bytes 8388608 | tf_op jit(solution)/shard_map/pallas_call | solution.py:150
  43.8 1.1 pad_maximum_fusion.7.refs_2_
  44.9 0.4 collective-permute-done.5
  45.3 1.1 pad_maximum_fusion.6.refs_1_
  46.4 5.0 %collective-permute-done.4 = bf16[8,8,3840]{2,1,0:T(8,128)(2,1)S(1)} collective-permute-done((bf16[8,8,3840]{2,1,0:T(8,128)(2,1)S(1)}, bf16[8,8,3840]{2,1,0:T(8,128)(2,1)S(1)}, u32[]{:S(2)}, u32[]{:S(2)}) %collective-permute-start.4) | collective-permute-done | bytes 491552 | tf_op jit(solution)/shard_map/ppermute | solution.py:66
  51.4 1.0 pad_maximum_fusion.5.refs_0_
  52.4 1.7 %collective-permute-start.14 = (bf16[2,8,8,3712]{3,2,1,0:T(8,128)(2,1)}, bf16[2,8,8,3712]{3,2,1,0:T(8,128)(2,1)S(1)}, u32[]{:S(2)}, u32[]{:S(2)}) collective-permute-start(bf16[2,8,8,3712]{3,2,1,0:T(8,128)(2,1)} %get-tuple-element.13.refs_6_.refs_8_), channel_id=1, source_target_pairs={{0,48},{1,49},{2,50},{3,51},{4,52},{5,53},{6,54},{7,55},{8,24},{9,... | collective-permute-start | bytes 2850824 | tf_op jit(solution)/shard_map/ppermute | solution.py:66
  54.2 1.4 %collective-permute-start.12 = (bf16[2,8,8,3840]{3,2,1,0:T(8,128)(2,1)}, bf16[2,8,8,3840]{3,2,1,0:T(8,128)(2,1)S(1)}, u32[]{:S(2)}, u32[]{:S(2)}) collective-permute-start(bf16[2,8,8,3840]{3,2,1,0:T(8,128)(2,1)} %get-tuple-element.11.refs_0_), channel_id=1, source_target_pairs={{0,68},{1,69},{2,70},{3,71},{4,64},{5,65},{6,66},{7,67},{8,72},{9,... | collective-permute-start | bytes 2949128 | tf_op jit(solution)/shard_map/ppermute | solution.py:66
  55.7 1.4 collective-permute-start.13
  57.1 3.6 %pad_maximum_fusion = bf16[2,8,8,11392]{3,2,1,0:T(8,128)(2,1)} fusion(bf16[2,8,8,3712]{3,2,1,0:T(8,128)(2,1)} %get-tuple-element.13.refs_6_.refs_8_, bf16[2,8,8,3840]{3,2,1,0:T(8,128)(2,1)} %get-tuple-element.12.refs_3_.refs_4_, bf16[2,8,8,3840]{3,2,1,0:T(8,128)(2,1)} %get-tuple-element.11.refs_0_), kind=kLoop, calls=%fused_computation | loop fusion | flops 8749056 | bytes 5832704 | tf_op jit(solution)/shard_map/concatenate | solution.py:426
  60.7 5.1 %collective-permute-done.14.refs_8_.refs_10_ = bf16[2,8,8,3712]{3,2,1,0:T(8,128)(2,1)S(1)} collective-permute-done((bf16[2,8,8,3712]{3,2,1,0:T(8,128)(2,1)}, bf16[2,8,8,3712]{3,2,1,0:T(8,128)(2,1)S(1)}, u32[]{:S(2)}, u32[]{:S(2)}) %collective-permute-start.14) | collective-permute-done | bytes 950304 | tf_op jit(solution)/shard_map/ppermute | solution.py:66
  65.8 1.5 %collective-permute-start.9 = (bf16[2,8,8,3840]{3,2,1,0:T(8,128)(2,1)S(1)}, bf16[2,8,8,3840]{3,2,1,0:T(8,128)(2,1)S(1)}, u32[]{:S(2)}, u32[]{:S(2)}) collective-permute-start(bf16[2,8,8,3840]{3,2,1,0:T(8,128)(2,1)S(1)} %copy-done), channel_id=1, source_target_pairs={{0,68},{1,69},{2,70},{3,71},{4,64},{5,65},{6,66},{7,67},{8,72},{9,... | collective-permute-start | bytes 2949128 | tf_op jit(solution)/shard_map/ppermute | solution.py:66
  67.3 8.0 %collective-permute-start.7 = (bf16[2,8,8,11392]{3,2,1,0:T(8,128)(2,1)}, bf16[2,8,8,11392]{3,2,1,0:T(8,128)(2,1)}, u32[]{:S(2)}, u32[]{:S(2)}) collective-permute-start(bf16[2,8,8,11392]{3,2,1,0:T(8,128)(2,1)} %pad_maximum_fusion), channel_id=1, source_target_pairs={{0,8},{1,9},{2,10},{3,11},{4,12},{5,13},{6,14},{7,15},{8,0},{9,1},... | collective-permute-start | bytes 8749064 | tf_op jit(solution)/shard_map/ppermute | solution.py:62
  75.3 2.5 %collective-permute-done.13.refs_5_.refs_6_ = bf16[2,8,8,3840]{3,2,1,0:T(8,128)(2,1)S(1)} collective-permute-done((bf16[2,8,8,3840]{3,2,1,0:T(8,128)(2,1)}, bf16[2,8,8,3840]{3,2,1,0:T(8,128)(2,1)S(1)}, u32[]{:S(2)}, u32[]{:S(2)}) %collective-permute-start.13) | collective-permute-done | bytes 983072 | tf_op jit(solution)/shard_map/ppermute | solution.py:66
  77.8 1.9 %pad_maximum_fusion.2 = bf16[2,8,8,11392]{3,2,1,0:T(8,128)(2,1)} fusion(bf16[2,8,8,3712]{3,2,1,0:T(8,128)(2,1)S(1)} %collective-permute-done.14.refs_8_.refs_10_, bf16[2,8,8,3840]{3,2,1,0:T(8,128)(2,1)S(1)} %collective-permute-done.13.refs_5_.refs_6_, bf16[2,8,8,3840]{3,2,1,0:T(8,128)(2,1)S(1)} %collective-permute-done.12.refs_2_), kind=kLoop, calls=%fused_computation.2 | loop fusion | flops 8749056 | bytes 5832704 | tf_op jit(solution)/shard_map/concatenate | solution.py:426
  79.7 7.2 %collective-permute-start.15 = (bf16[2,8,8,11392]{3,2,1,0:T(8,128)(2,1)}, bf16[2,8,8,11392]{3,2,1,0:T(8,128)(2,1)}, u32[]{:S(2)}, u32[]{:S(2)}) collective-permute-start(bf16[2,8,8,11392]{3,2,1,0:T(8,128)(2,1)} %pad_maximum_fusion.2), channel_id=1, source_target_pairs={{0,8},{1,9},{2,10},{3,11},{4,12},{5,13},{6,14},{7,15},{8,0},{9,1},... | collective-permute-start | bytes 8749064 | tf_op jit(solution)/shard_map/ppermute | solution.py:62
  86.9 0.2 collective-permute-start.17
  87.2 7.7 %shard_map.72 = (f32[8,8,8,512]{3,2,1,0:T(8,128)S(1)}, f32[8,8,8,512]{3,2,1,0:T(8,128)S(1)}) custom-call(s32[1]{0:T(128)} %bitcast.core_ref, bf16[512,14336]{1,0:T(8,128)(2,1)} %acts.5, bf16[512,8192]{1,0:T(8,128)(2,1)} %grads.5, bf16[2,8,8,3840]{3,2,1,0:T(8,128)(2,1)S(1)} %copy-done.1, bf16[2,8,8,3840]{3,2,1,0:T(8,128)(2,1)S(1)} %collective-permute-done.8.refs_1_, ...), custom_call_target="tpu_custom_call" | custom-call | flops 4429185024 | bytes 23068672 | tf_op jit(solution)/shard_map/pallas_call | solution.py:264
  95.0 1.9 %pad_maximum_fusion.1 = bf16[2,8,8,11392]{3,2,1,0:T(8,128)(2,1)} fusion(bf16[2,8,8,3712]{3,2,1,0:T(8,128)(2,1)S(1)} %collective-permute-done.10.refs_7_.refs_9_, bf16[2,8,8,3840]{3,2,1,0:T(8,128)(2,1)S(1)} %collective-permute-done.9.refs_4_.refs_5_, bf16[2,8,8,3840]{3,2,1,0:T(8,128)(2,1)S(1)} %collective-permute-done.8.refs_1_), kind=kLoop, calls=%fused_computation.1 | loop fusion | flops 8749056 | bytes 5832704 | tf_op jit(solution)/shard_map/concatenate | solution.py:426
  96.9 5.5 %collective-permute-start.11 = (bf16[2,8,8,11392]{3,2,1,0:T(8,128)(2,1)}, bf16[2,8,8,11392]{3,2,1,0:T(8,128)(2,1)}, u32[]{:S(2)}, u32[]{:S(2)}) collective-permute-start(bf16[2,8,8,11392]{3,2,1,0:T(8,128)(2,1)} %pad_maximum_fusion.1), channel_id=1, source_target_pairs={{0,8},{1,9},{2,10},{3,11},{4,12},{5,13},{6,14},{7,15},{8,0},{9,1},... | collective-permute-start | bytes 8749064 | tf_op jit(solution)/shard_map/ppermute | solution.py:62
  102.4 1.9 %pad_maximum_fusion.3.refs_0_ = bf16[2,8,8,11392]{3,2,1,0:T(8,128)(2,1)} fusion(bf16[2,8,8,3712]{3,2,1,0:T(8,128)(2,1)S(1)} %collective-permute-done.18.refs_11_, bf16[2,8,8,3840]{3,2,1,0:T(8,128)(2,1)S(1)} %collective-permute-done.17.refs_7_, bf16[2,8,8,3840]{3,2,1,0:T(8,128)(2,1)S(1)} %collective-permute-done.16.refs_3_), kind=kLoop, calls=%fused_computation.3 | loop fusion | flops 8749056 | bytes 5832704 | tf_op jit(solution)/shard_map/concatenate | solution.py:426
  104.3 0.9 copy-done.20
  105.3 2.6 %collective-permute-start.19 = (bf16[2,8,8,11392]{3,2,1,0:T(8,128)(2,1)}, bf16[2,8,8,11392]{3,2,1,0:T(8,128)(2,1)S(1)}, u32[]{:S(2)}, u32[]{:S(2)}) collective-permute-start(bf16[2,8,8,11392]{3,2,1,0:T(8,128)(2,1)} %shard_map.74), channel_id=1, source_target_pairs={{0,8},{1,9},{2,10},{3,11},{4,12},{5,13},{6,14},{7,15},{8,0},{9,1},... | collective-permute-start | bytes 8749064 | tf_op jit(solution)/shard_map/ppermute | solution.py:62
  107.9 1.2 copy-done.19
  109.1 1.2 copy-done.27
  110.4 8.8 %shard_map.73 = (f32[8,8,8,512]{3,2,1,0:T(8,128)S(1)}, f32[8,8,8,512]{3,2,1,0:T(8,128)S(1)}) custom-call(s32[1]{0:T(128)} %bitcast.core_ref, bf16[512,14336]{1,0:T(8,128)(2,1)} %acts.5, bf16[512,8192]{1,0:T(8,128)(2,1)} %grads.5, bf16[2,8,8,11392]{3,2,1,0:T(8,128)(2,1)} %collective-permute-done.7.refs_0_.refs_12_, ...), custom_call_target="tpu_custom_call" | custom-call | flops 4429185024 | bytes 23068672 | tf_op jit(solution)/shard_map/pallas_call | solution.py:264
  119.4 0.3 copy-done.25
  119.7 21.6 %shard_map.75 = (f32[4,512]{1,0:T(4,128)S(1)}, f32[4,128]{1,0:T(4,128)S(1)}) custom-call(s32[1]{0:T(128)} %bitcast.core_ref, bf16[512,14336]{1,0:T(8,128)(2,1)} %acts.5, bf16[512,8192]{1,0:T(8,128)(2,1)} %grads.5, f32[4,4]{1,0:T(4,128)S(1)} %copy-done.28, f32[8,8,8,512]{3,2,1,0:T(8,128)S(1)} %get-tuple-element.16.ain, ...), custom_call_target="tpu_custom_call" | custom-call | flops 8858370048 | bytes 46137344 | tf_op jit(solution)/shard_map/pallas_call | solution.py:369
  141.2 0.3 collective-permute-start.20
  141.5 0.9 collective-permute-done.20
  142.5 0.1 rsqrt_reduce_fusion
  142.6 0.7 broadcast_multiply_fusion
  (82 shorter events, 1.1 us)
Async XLA Ops:
  3.2 2.4 %collective-permute-start = (bf16[4,11392]{1,0:T(4,128)(2,1)S(1)}, bf16[4,11392]{1,0:T(4,128)(2,1)S(1)}, u32[]{:S(2)}, u32[]{:S(2)}) collective-permute-start(bf16[4,11392]{1,0:T(4,128)(2,1)S(1)} %broadcast_select_fusion.2), channel_id=1, source_target_pairs={{0,8},{1,9},{2,10},{3,11},{4,12},{5,13},{6,14},{7,15},{8,0},{9,1},... | collective-permute-start | bytes 273416 | tf_op jit(solution)/shard_map/ppermute | solution.py:62
  5.8 6.8 %collective-permute-start.1 = (bf16[8,11392]{1,0:T(8,128)(2,1)S(1)}, bf16[8,11392]{1,0:T(8,128)(2,1)S(1)}, u32[]{:S(2)}, u32[]{:S(2)}) collective-permute-start(bf16[8,11392]{1,0:T(8,128)(2,1)S(1)} %get-tuple-element.33), channel_id=1, source_target_pairs={{0,16},{1,17},{2,18},{3,19},{4,20},{5,21},{6,22},{7,23},{8,56},{9,... | collective-permute-start | bytes 546824 | tf_op jit(solution)/shard_map/ppermute | solution.py:66
  12.7 7.7 %collective-permute-start.2 = (bf16[2,8,11392]{2,1,0:T(8,128)(2,1)S(1)}, bf16[2,8,11392]{2,1,0:T(8,128)(2,1)S(1)}, u32[]{:S(2)}, u32[]{:S(2)}) collective-permute-start(bf16[2,8,11392]{2,1,0:T(8,128)(2,1)S(1)} %get-tuple-element.29), channel_id=1, source_target_pairs={{0,1},{1,0},{2,3},{3,2},{4,5},{5,4},{6,7},{7,6},{8,11},{9,10},{10,... | collective-permute-start | bytes 1093640 | tf_op jit(solution)/shard_map/ppermute | solution.py:66
  20.5 12.8 %collective-permute-start.3 = (bf16[2,2,8,11392]{3,2,1,0:T(8,128)(2,1)S(1)}, bf16[2,2,8,11392]{3,2,1,0:T(8,128)(2,1)S(1)}, u32[]{:S(2)}, u32[]{:S(2)}) collective-permute-start(bf16[2,2,8,11392]{3,2,1,0:T(8,128)(2,1)S(1)} %get-tuple-element.27.dep_ref), channel_id=1, source_target_pairs={{0,64},{1,65},{2,66},{3,67},{4,68},{5,69},{6,70},{7,71},{8,76},{9,... | collective-permute-start | bytes 2187272 | tf_op jit(solution)/shard_map/ppermute | solution.py:66
  34.6 2.7 %copy-start.3 = (bf16[2,2,2,8,11392]{4,3,2,1,0:T(8,128)(2,1)S(1)}, bf16[2,2,2,8,11392]{4,3,2,1,0:T(8,128)(2,1)}, u32[]{:S(2)}) copy-start(bf16[2,2,2,8,11392]{4,3,2,1,0:T(8,128)(2,1)} %shard_map.69) | copy-start | bytes 4374532
  34.6 2.7 %copy-start.17 = (f32[512,256]{1,0:T(8,128)S(1)}, f32[512,256]{1,0:T(8,128)}, u32[]{:S(2)}) copy-start(f32[512,256]{1,0:T(8,128)} %copy-done.16) | copy-start | bytes 1572868
  35.9 8.0 %collective-permute-start.6 = (bf16[8,8,3712]{2,1,0:T(8,128)(2,1)S(1)}, bf16[8,8,3712]{2,1,0:T(8,128)(2,1)S(1)}, u32[]{:S(2)}, u32[]{:S(2)}) collective-permute-start(bf16[8,8,3712]{2,1,0:T(8,128)(2,1)S(1)} %get-tuple-element.21), channel_id=1, source_target_pairs={{0,68},{1,69},{2,70},{3,71},{4,64},{5,65},{6,66},{7,67},{8,72},{9,... | collective-permute-start | bytes 1425416 | tf_op jit(solution)/shard_map/ppermute | solution.py:66
  37.3 8.1 %collective-permute-start.5 = (bf16[8,8,3840]{2,1,0:T(8,128)(2,1)S(1)}, bf16[8,8,3840]{2,1,0:T(8,128)(2,1)S(1)}, u32[]{:S(2)}, u32[]{:S(2)}) collective-permute-start(bf16[8,8,3840]{2,1,0:T(8,128)(2,1)S(1)} %get-tuple-element.24), channel_id=1, source_target_pairs={{0,48},{1,49},{2,50},{3,51},{4,52},{5,53},{6,54},{7,55},{8,24},{9,... | collective-permute-start | bytes 1474568 | tf_op jit(solution)/shard_map/ppermute | solution.py:66
  43.7 7.7 %collective-permute-start.4 = (bf16[8,8,3840]{2,1,0:T(8,128)(2,1)S(1)}, bf16[8,8,3840]{2,1,0:T(8,128)(2,1)S(1)}, u32[]{:S(2)}, u32[]{:S(2)}) collective-permute-start(bf16[8,8,3840]{2,1,0:T(8,128)(2,1)S(1)} %get-tuple-element.25), channel_id=1, source_target_pairs={{0,3},{1,2},{2,1},{3,0},{4,7},{5,6},{6,5},{7,4},{8,9},{9,8},{10,11... | collective-permute-start | bytes 1474568 | tf_op jit(solution)/shard_map/ppermute | solution.py:66
  52.4 13.4 %collective-permute-start.14 = (bf16[2,8,8,3712]{3,2,1,0:T(8,128)(2,1)}, bf16[2,8,8,3712]{3,2,1,0:T(8,128)(2,1)S(1)}, u32[]{:S(2)}, u32[]{:S(2)}) collective-permute-start(bf16[2,8,8,3712]{3,2,1,0:T(8,128)(2,1)} %get-tuple-element.13.refs_6_.refs_8_), channel_id=1, source_target_pairs={{0,48},{1,49},{2,50},{3,51},{4,52},{5,53},{6,54},{7,55},{8,24},{9,... | collective-permute-start | bytes 2850824 | tf_op jit(solution)/shard_map/ppermute | solution.py:66
  54.2 13.1 %collective-permute-start.10 = (bf16[2,8,8,3712]{3,2,1,0:T(8,128)(2,1)}, bf16[2,8,8,3712]{3,2,1,0:T(8,128)(2,1)S(1)}, u32[]{:S(2)}, u32[]{:S(2)}) collective-permute-start(bf16[2,8,8,3712]{3,2,1,0:T(8,128)(2,1)} %get-tuple-element.13.refs_6_.refs_8_), channel_id=1, source_target_pairs={{0,3},{1,2},{2,1},{3,0},{4,7},{5,6},{6,5},{7,4},{8,9},{9,8},{10,11... | collective-permute-start | bytes 2850824 | tf_op jit(solution)/shard_map/ppermute | solution.py:66
  54.2 21.1 %collective-permute-start.12 = (bf16[2,8,8,3840]{3,2,1,0:T(8,128)(2,1)}, bf16[2,8,8,3840]{3,2,1,0:T(8,128)(2,1)S(1)}, u32[]{:S(2)}, u32[]{:S(2)}) collective-permute-start(bf16[2,8,8,3840]{3,2,1,0:T(8,128)(2,1)} %get-tuple-element.11.refs_0_), channel_id=1, source_target_pairs={{0,68},{1,69},{2,70},{3,71},{4,64},{5,65},{6,66},{7,67},{8,72},{9,... | collective-permute-start | bytes 2949128 | tf_op jit(solution)/shard_map/ppermute | solution.py:66
  55.6 31.2 %collective-permute-start.8 = (bf16[2,8,8,3840]{3,2,1,0:T(8,128)(2,1)}, bf16[2,8,8,3840]{3,2,1,0:T(8,128)(2,1)S(1)}, u32[]{:S(2)}, u32[]{:S(2)}) collective-permute-start(bf16[2,8,8,3840]{3,2,1,0:T(8,128)(2,1)} %get-tuple-element.11.refs_0_), channel_id=1, source_target_pairs={{0,48},{1,49},{2,50},{3,51},{4,52},{5,53},{6,54},{7,55},{8,24},{9,... | collective-permute-start | bytes 2949128 | tf_op jit(solution)/shard_map/ppermute | solution.py:66
  55.7 10.1 %copy-start = (bf16[2,8,8,3840]{3,2,1,0:T(8,128)(2,1)S(1)}, bf16[2,8,8,3840]{3,2,1,0:T(8,128)(2,1)}, u32[]{:S(2)}) copy-start(bf16[2,8,8,3840]{3,2,1,0:T(8,128)(2,1)} %get-tuple-element.12.refs_3_.refs_4_) | copy-start | bytes 2949124
  55.7 22.0 %collective-permute-start.13 = (bf16[2,8,8,3840]{3,2,1,0:T(8,128)(2,1)}, bf16[2,8,8,3840]{3,2,1,0:T(8,128)(2,1)S(1)}, u32[]{:S(2)}, u32[]{:S(2)}) collective-permute-start(bf16[2,8,8,3840]{3,2,1,0:T(8,128)(2,1)} %get-tuple-element.12.refs_3_.refs_4_), channel_id=1, source_target_pairs={{0,3},{1,2},{2,1},{3,0},{4,7},{5,6},{6,5},{7,4},{8,9},{9,8},{10,11... | collective-permute-start | bytes 2949128 | tf_op jit(solution)/shard_map/ppermute | solution.py:66
  60.7 26.5 %copy-start.1 = (bf16[2,8,8,3840]{3,2,1,0:T(8,128)(2,1)S(1)}, bf16[2,8,8,3840]{3,2,1,0:T(8,128)(2,1)}, u32[]{:S(2)}) copy-start(bf16[2,8,8,3840]{3,2,1,0:T(8,128)(2,1)} %get-tuple-element.11.refs_0_) | copy-start | bytes 2949124
  60.7 26.5 %copy-start.2 = (bf16[2,8,8,3712]{3,2,1,0:T(8,128)(2,1)S(1)}, bf16[2,8,8,3712]{3,2,1,0:T(8,128)(2,1)}, u32[]{:S(2)}) copy-start(bf16[2,8,8,3712]{3,2,1,0:T(8,128)(2,1)} %get-tuple-element.13.refs_6_.refs_8_) | copy-start | bytes 2850820
  65.8 21.4 %copy-start.12 = (bf16[2,8,8,3712]{3,2,1,0:T(8,128)(2,1)}, bf16[2,8,8,3712]{3,2,1,0:T(8,128)(2,1)S(1)}, u32[]{:S(2)}) copy-start(bf16[2,8,8,3712]{3,2,1,0:T(8,128)(2,1)S(1)} %collective-permute-done.14.refs_8_.refs_10_) | copy-start | bytes 2850820
  65.8 21.1 %collective-permute-start.9 = (bf16[2,8,8,3840]{3,2,1,0:T(8,128)(2,1)S(1)}, bf16[2,8,8,3840]{3,2,1,0:T(8,128)(2,1)S(1)}, u32[]{:S(2)}, u32[]{:S(2)}) collective-permute-start(bf16[2,8,8,3840]{3,2,1,0:T(8,128)(2,1)S(1)} %copy-done), channel_id=1, source_target_pairs={{0,68},{1,69},{2,70},{3,71},{4,64},{5,65},{6,66},{7,67},{8,72},{9,... | collective-permute-start | bytes 2949128 | tf_op jit(solution)/shard_map/ppermute | solution.py:66
  67.3 27.7 %copy-start.14 = (bf16[2,8,8,3712]{3,2,1,0:T(8,128)(2,1)}, bf16[2,8,8,3712]{3,2,1,0:T(8,128)(2,1)S(1)}, u32[]{:S(2)}) copy-start(bf16[2,8,8,3712]{3,2,1,0:T(8,128)(2,1)S(1)} %collective-permute-done.10.refs_7_.refs_9_) | copy-start | bytes 2850820
  67.3 40.6 %collective-permute-start.7 = (bf16[2,8,8,11392]{3,2,1,0:T(8,128)(2,1)}, bf16[2,8,8,11392]{3,2,1,0:T(8,128)(2,1)}, u32[]{:S(2)}, u32[]{:S(2)}) collective-permute-start(bf16[2,8,8,11392]{3,2,1,0:T(8,128)(2,1)} %pad_maximum_fusion), channel_id=1, source_target_pairs={{0,8},{1,9},{2,10},{3,11},{4,12},{5,13},{6,14},{7,15},{8,0},{9,1},... | collective-permute-start | bytes 8749064 | tf_op jit(solution)/shard_map/ppermute | solution.py:62
  75.3 11.9 %copy-start.4 = (bf16[2,8,8,3840]{3,2,1,0:T(8,128)(2,1)}, bf16[2,8,8,3840]{3,2,1,0:T(8,128)(2,1)S(1)}, u32[]{:S(2)}) copy-start(bf16[2,8,8,3840]{3,2,1,0:T(8,128)(2,1)S(1)} %collective-permute-done.12.refs_2_) | copy-start | bytes 2949124
  75.3 21.6 %collective-permute-start.18 = (bf16[2,8,8,3712]{3,2,1,0:T(8,128)(2,1)S(1)}, bf16[2,8,8,3712]{3,2,1,0:T(8,128)(2,1)S(1)}, u32[]{:S(2)}, u32[]{:S(2)}) collective-permute-start(bf16[2,8,8,3712]{3,2,1,0:T(8,128)(2,1)S(1)} %collective-permute-done.10.refs_7_.refs_9_), channel_id=1, source_target_pairs={{0,48},{1,49},{2,50},{3,51},{4,52},{5,53},{6,54},{7,55},{8,24},{9,... | collective-permute-start | bytes 2850824 | tf_op jit(solution)/shard_map/ppermute | solution.py:66
  77.8 9.4 %copy-start.8 = (bf16[2,8,8,3840]{3,2,1,0:T(8,128)(2,1)}, bf16[2,8,8,3840]{3,2,1,0:T(8,128)(2,1)S(1)}, u32[]{:S(2)}) copy-start(bf16[2,8,8,3840]{3,2,1,0:T(8,128)(2,1)S(1)} %collective-permute-done.13.refs_5_.refs_6_) | copy-start | bytes 2949124
  79.7 28.2 %collective-permute-start.15 = (bf16[2,8,8,11392]{3,2,1,0:T(8,128)(2,1)}, bf16[2,8,8,11392]{3,2,1,0:T(8,128)(2,1)}, u32[]{:S(2)}, u32[]{:S(2)}) collective-permute-start(bf16[2,8,8,11392]{3,2,1,0:T(8,128)(2,1)} %pad_maximum_fusion.2), channel_id=1, source_target_pairs={{0,8},{1,9},{2,10},{3,11},{4,12},{5,13},{6,14},{7,15},{8,0},{9,1},... | collective-permute-start | bytes 8749064 | tf_op jit(solution)/shard_map/ppermute | solution.py:62
  86.8 8.1 %copy-start.6 = (bf16[2,8,8,3840]{3,2,1,0:T(8,128)(2,1)}, bf16[2,8,8,3840]{3,2,1,0:T(8,128)(2,1)S(1)}, u32[]{:S(2)}) copy-start(bf16[2,8,8,3840]{3,2,1,0:T(8,128)(2,1)S(1)} %collective-permute-done.8.refs_1_) | copy-start | bytes 2949124
  86.9 15.6 %collective-permute-start.16 = (bf16[2,8,8,3840]{3,2,1,0:T(8,128)(2,1)S(1)}, bf16[2,8,8,3840]{3,2,1,0:T(8,128)(2,1)S(1)}, u32[]{:S(2)}, u32[]{:S(2)}) collective-permute-start(bf16[2,8,8,3840]{3,2,1,0:T(8,128)(2,1)S(1)} %collective-permute-done.8.refs_1_), channel_id=1, source_target_pairs={{0,68},{1,69},{2,70},{3,71},{4,64},{5,65},{6,66},{7,67},{8,72},{9,... | collective-permute-start | bytes 2949128 | tf_op jit(solution)/shard_map/ppermute | solution.py:66
  86.9 8.1 %copy-start.10 = (bf16[2,8,8,3840]{3,2,1,0:T(8,128)(2,1)}, bf16[2,8,8,3840]{3,2,1,0:T(8,128)(2,1)S(1)}, u32[]{:S(2)}) copy-start(bf16[2,8,8,3840]{3,2,1,0:T(8,128)(2,1)S(1)} %collective-permute-done.9.refs_4_.refs_5_) | copy-start | bytes 2949124
  86.9 15.5 %collective-permute-start.17 = (bf16[2,8,8,3840]{3,2,1,0:T(8,128)(2,1)S(1)}, bf16[2,8,8,3840]{3,2,1,0:T(8,128)(2,1)S(1)}, u32[]{:S(2)}, u32[]{:S(2)}) collective-permute-start(bf16[2,8,8,3840]{3,2,1,0:T(8,128)(2,1)S(1)} %collective-permute-done.9.refs_4_.refs_5_), channel_id=1, source_target_pairs={{0,3},{1,2},{2,1},{3,0},{4,7},{5,6},{6,5},{7,4},{8,9},{9,8},{10,11... | collective-permute-start | bytes 2949128 | tf_op jit(solution)/shard_map/ppermute | solution.py:66
  95.0 9.3 %copy-start.18 = (f32[8,8,8,512]{3,2,1,0:T(8,128)}, f32[8,8,8,512]{3,2,1,0:T(8,128)S(1)}, u32[]{:S(2)}) copy-start(f32[8,8,8,512]{3,2,1,0:T(8,128)S(1)} %get-tuple-element.14.refs_3_.refs_1_) | copy-start | bytes 3145732
  95.0 9.3 %copy-start.26 = (f32[8,8,8,512]{3,2,1,0:T(8,128)}, f32[8,8,8,512]{3,2,1,0:T(8,128)S(1)}, u32[]{:S(2)}) copy-start(f32[8,8,8,512]{3,2,1,0:T(8,128)S(1)} %get-tuple-element.15.refs_4_) | copy-start | bytes 3145732
  96.9 7.4 %copy-start.24 = (bf16[2,8,8,3712]{3,2,1,0:T(8,128)(2,1)}, bf16[2,8,8,3712]{3,2,1,0:T(8,128)(2,1)S(1)}, u32[]{:S(2)}) copy-start(bf16[2,8,8,3712]{3,2,1,0:T(8,128)(2,1)S(1)} %collective-permute-done.18.refs_11_) | copy-start | bytes 2850820
  96.9 11.0 %collective-permute-start.11 = (bf16[2,8,8,11392]{3,2,1,0:T(8,128)(2,1)}, bf16[2,8,8,11392]{3,2,1,0:T(8,128)(2,1)}, u32[]{:S(2)}, u32[]{:S(2)}) collective-permute-start(bf16[2,8,8,11392]{3,2,1,0:T(8,128)(2,1)} %pad_maximum_fusion.1), channel_id=1, source_target_pairs={{0,8},{1,9},{2,10},{3,11},{4,12},{5,13},{6,14},{7,15},{8,0},{9,1},... | collective-permute-start | bytes 8749064 | tf_op jit(solution)/shard_map/ppermute | solution.py:62
  102.4 1.9 %copy-start.22 = (bf16[2,8,8,3840]{3,2,1,0:T(8,128)(2,1)}, bf16[2,8,8,3840]{3,2,1,0:T(8,128)(2,1)S(1)}, u32[]{:S(2)}) copy-start(bf16[2,8,8,3840]{3,2,1,0:T(8,128)(2,1)S(1)} %collective-permute-done.17.refs_7_) | copy-start | bytes 2949124
  105.3 13.9 %collective-permute-start.19 = (bf16[2,8,8,11392]{3,2,1,0:T(8,128)(2,1)}, bf16[2,8,8,11392]{3,2,1,0:T(8,128)(2,1)S(1)}, u32[]{:S(2)}, u32[]{:S(2)}) collective-permute-start(bf16[2,8,8,11392]{3,2,1,0:T(8,128)(2,1)} %shard_map.74), channel_id=1, source_target_pairs={{0,8},{1,9},{2,10},{3,11},{4,12},{5,13},{6,14},{7,15},{8,0},{9,1},... | collective-permute-start | bytes 8749064 | tf_op jit(solution)/shard_map/ppermute | solution.py:62
  107.9 1.2 copy-start.19
  109.1 1.2 copy-start.27
  110.3 8.9 %copy-start.5 = (bf16[2,8,8,3840]{3,2,1,0:T(8,128)(2,1)S(1)}, bf16[2,8,8,3840]{3,2,1,0:T(8,128)(2,1)}, u32[]{:S(2)}) copy-start(bf16[2,8,8,3840]{3,2,1,0:T(8,128)(2,1)} %copy-done.4) | copy-start | bytes 2949124
  110.3 8.9 %copy-start.7 = (bf16[2,8,8,3840]{3,2,1,0:T(8,128)(2,1)S(1)}, bf16[2,8,8,3840]{3,2,1,0:T(8,128)(2,1)}, u32[]{:S(2)}) copy-start(bf16[2,8,8,3840]{3,2,1,0:T(8,128)(2,1)} %copy-done.6) | copy-start | bytes 2949124
  110.3 8.9 %copy-start.9 = (bf16[2,8,8,3840]{3,2,1,0:T(8,128)(2,1)S(1)}, bf16[2,8,8,3840]{3,2,1,0:T(8,128)(2,1)}, u32[]{:S(2)}) copy-start(bf16[2,8,8,3840]{3,2,1,0:T(8,128)(2,1)} %copy-done.8) | copy-start | bytes 2949124
  110.3 8.9 %copy-start.11 = (bf16[2,8,8,3840]{3,2,1,0:T(8,128)(2,1)S(1)}, bf16[2,8,8,3840]{3,2,1,0:T(8,128)(2,1)}, u32[]{:S(2)}) copy-start(bf16[2,8,8,3840]{3,2,1,0:T(8,128)(2,1)} %copy-done.10) | copy-start | bytes 2949124
  110.3 8.9 %copy-start.13 = (bf16[2,8,8,3712]{3,2,1,0:T(8,128)(2,1)S(1)}, bf16[2,8,8,3712]{3,2,1,0:T(8,128)(2,1)}, u32[]{:S(2)}) copy-start(bf16[2,8,8,3712]{3,2,1,0:T(8,128)(2,1)} %copy-done.12) | copy-start | bytes 2850820
  110.3 8.9 %copy-start.15 = (bf16[2,8,8,3712]{3,2,1,0:T(8,128)(2,1)S(1)}, bf16[2,8,8,3712]{3,2,1,0:T(8,128)(2,1)}, u32[]{:S(2)}) copy-start(bf16[2,8,8,3712]{3,2,1,0:T(8,128)(2,1)} %copy-done.14) | copy-start | bytes 2850820
  110.4 8.9 %copy-start.21 = (bf16[2,8,8,3840]{3,2,1,0:T(8,128)(2,1)S(1)}, bf16[2,8,8,3840]{3,2,1,0:T(8,128)(2,1)}, u32[]{:S(2)}) copy-start(bf16[2,8,8,3840]{3,2,1,0:T(8,128)(2,1)} %copy-done.20) | copy-start | bytes 2949124
  110.4 9.0 %copy-start.23 = (bf16[2,8,8,3840]{3,2,1,0:T(8,128)(2,1)S(1)}, bf16[2,8,8,3840]{3,2,1,0:T(8,128)(2,1)}, u32[]{:S(2)}) copy-start(bf16[2,8,8,3840]{3,2,1,0:T(8,128)(2,1)} %copy-done.22) | copy-start | bytes 2949124
  110.4 9.3 %copy-start.25 = (bf16[2,8,8,3712]{3,2,1,0:T(8,128)(2,1)S(1)}, bf16[2,8,8,3712]{3,2,1,0:T(8,128)(2,1)}, u32[]{:S(2)}) copy-start(bf16[2,8,8,3712]{3,2,1,0:T(8,128)(2,1)} %copy-done.24) | copy-start | bytes 2850820
  110.4 9.3 %copy-start.28 = (f32[4,4]{1,0:T(4,128)S(1)}, f32[4,4]{1,0:T(4,128)}, u32[]{:S(2)}) copy-start(f32[4,4]{1,0:T(4,128)} %shard_map.70.refs_3_.gram_ref) | copy-start | bytes 196
  141.2 1.2 collective-permute-start.20
  (2 other events, 1.8 us)

commit v3 on v2

v3 whole, which is shorter than its diff:
```python
import functools
import math

import jax
import jax.numpy as jnp
from jax import lax
from jax.experimental import pallas as pl
from jax.experimental.pallas import tpu as pltpu
from jax.sharding import PartitionSpec as P

D = 8192
FF = 14336
BLK = 128
NVAL = 4
TOK = 512
VAL = 512
AXES = ("dp", "seq")
HA = FF // 2
HG = D // 2
C1 = 3840
C2A = HA - C1
C2G = 512
C2 = C2A + C2G
C3G = HG - C2G
IDW = 128
C3 = C3G + IDW
MASKS = ((1, 3), (3, 1))


def coords(i):
    dp, seq = divmod(i, 8)
    c = dp % 2
    z = (dp // 2) % 4
    x = (seq // 4) * 2 + dp // 8
    return {"x": x, "y": seq % 4, "z": z, "c": c}


def index(p):
    dp = ((p["x"] % 2) * 4 + p["z"]) * 2 + p["c"]
    return dp * 8 + (p["x"] // 2) * 4 + p["y"]


def ring_pairs(axis, step):
    pairs = []
    for i in range(128):
        p = coords(i)
        p[axis] ^= MASKS[p["c"]][step]
        pairs.append((i, index(p)))
    return pairs


def core_pairs():
    pairs = []
    for i in range(128):
        p = coords(i)
        p["c"] ^= 1
        pairs.append((i, index(p)))
    return pairs


def swap(x):
    return lax.ppermute(x, AXES, core_pairs())


def hop(x, axis, step):
    return lax.ppermute(x, AXES, ring_pairs(axis, step))


def double(x, axis, step):
    return jnp.stack([x, hop(x, axis, step)])


def pin(x):
    return pltpu.with_memory_space_constraint(x, pltpu.VMEM)


def gate(xs, dep):
    n = len(xs)
    anyspec = pl.BlockSpec(memory_space=pl.ANY)
    return pl.pallas_call(
        lambda *refs: None,
        in_specs=[anyspec] * (n + 1),
        out_specs=[anyspec] * n,
        out_shape=[jax.ShapeDtypeStruct(x.shape, x.dtype) for x in xs],
        input_output_aliases={i: i for i in range(n)},
        cost_estimate=pl.CostEstimate(flops=0, bytes_accessed=0, transcendentals=0),
    )(*[pin(x) for x in xs], dep)


def nt(a, b):
    return lax.dot_general(a, b, (((1,), (1,)), ((), ())), preferred_element_type=jnp.float32)


def self_add(acc, ref):
    acc[0:256, :] += nt(ref[256:512, :], ref[0:256, :])
    acc[256:384, 0:128] += nt(ref[128:256, :], ref[0:128, :])
    acc[384:512, 0:128] += nt(ref[384:512, :], ref[256:384, :])


def self_acts_body(acts_ref, dep_ref, out_ref):
    @pl.when(pl.program_id(0) == 0)
    def _():
        out_ref[...] = jnp.zeros_like(out_ref)

    self_add(out_ref, acts_ref)


def self_grads_body(grads_ref, sa_ref, dep_ref, out_ref, sg, *, steps):
    i = pl.program_id(0)

    @pl.when(i == 0)
    def _():
        sg[...] = jnp.zeros_like(sg)

    self_add(sg, grads_ref)

    @pl.when(i == steps - 1)
    def _():
        k = sa_ref[...] * sg[...]
        rows = lax.broadcasted_iota(jnp.int32, (4, 4), 0)
        cols = lax.broadcasted_iota(jnp.int32, (4, 4), 1)
        out = jnp.zeros((4, 4), jnp.float32)
        spots = (
            (2, 0, 0, 0), (2, 1, 0, 128), (3, 0, 128, 0), (3, 1, 128, 128),
            (1, 0, 256, 0), (3, 2, 384, 0),
        )
        for b, c, r0, c0 in spots:
            s = jnp.sum(k[r0:r0 + 128, c0:c0 + 128])
            out = jnp.where((rows == b) & (cols == c), s, out)
        out_ref[...] = out / (float(BLK) * math.sqrt(float(FF) * float(D)))


KC = 2048


def self_acts(acts, dep):
    return pl.pallas_call(
        self_acts_body,
        grid=(FF // KC,),
        in_specs=[
            pl.BlockSpec((TOK, KC), lambda i: (0, i)),
            pl.BlockSpec(memory_space=pl.ANY),
        ],
        out_specs=pl.BlockSpec((512, 256), lambda i: (0, 0)),
        out_shape=jax.ShapeDtypeStruct((512, 256), jnp.float32),
        compiler_params=pltpu.CompilerParams(vmem_limit_bytes=16 << 20),
        cost_estimate=pl.CostEstimate(
            flops=2 * 512 * 256 * FF, bytes_accessed=2 * TOK * FF, transcendentals=0
        ),
    )(acts, dep)


def self_grads(grads, sa, dep):
    return pl.pallas_call(
        functools.partial(self_grads_body, steps=D // KC),
        grid=(D // KC,),
        in_specs=[
            pl.BlockSpec((TOK, KC), lambda i: (0, i)),
            pl.BlockSpec((512, 256), lambda i: (0, 0)),
            pl.BlockSpec(memory_space=pl.ANY),
        ],
        out_specs=pl.BlockSpec((4, 4), lambda i: (0, 0)),
        out_shape=jax.ShapeDtypeStruct((4, 4), jnp.float32),
        scratch_shapes=[pltpu.VMEM((512, 256), jnp.float32)],
        compiler_params=pltpu.CompilerParams(vmem_limit_bytes=16 << 20),
        cost_estimate=pl.CostEstimate(
            flops=2 * 512 * 256 * D, bytes_accessed=2 * TOK * D, transcendentals=0
        ),
    )(grads, sa, dep)


RUNS = ("y", "z", "x")
STEP5 = ("z", "x", "y")
STEP6 = ("x", "y", "z")
WEIGHT = {"x": 4, "y": 2, "z": 1}


def place(part, k, s4):
    n = s4 * WEIGHT[RUNS[part]]
    if k in (1, 3):
        n += WEIGHT[STEP5[part]]
    if k in (2, 3):
        n += WEIGHT[STEP6[part]]
    return n


WIDTHS = (C1, C2, C3)
STARTS = (0, C1, C1 + C2)
ALLW = C1 + C2 + C3
SEGMENTS = ((("a", 0, C1),), (("a", 0, C2A), ("g", C2A, C2G)), (("g", 0, C3G),))


def train_copies(acts, grads, o, part, dst):
    a0 = pl.multiple_of(o * HA, 128)
    g0 = pl.multiple_of(o * HG, 128)
    if part == 0:
        return [(acts.at[:, pl.ds(a0, C1)], dst.at[:, pl.ds(0, C1)])]
    if part == 1:
        return [
            (acts.at[:, pl.ds(a0 + C1, C2A)], dst.at[:, pl.ds(0, C2A)]),
            (grads.at[:, pl.ds(g0, C2G)], dst.at[:, pl.ds(C2A, C2G)]),
        ]
    return [(grads.at[:, pl.ds(g0 + C2G, C3G)], dst.at[:, pl.ds(0, C3G)])]


def add_rows(acc, half, at, x):
    if half == 0:
        acc[at] += x.reshape(8, 8, TOK)
    else:
        acc[:, at] += x.reshape(8, 8, TOK)


def start_train(core_ref, acts, grads, half, hbuf, sems):
    c = core_ref[0]
    o = c if half == 0 else 1 - c
    todo = []
    for part in range(3):
        moves = train_copies(acts, grads, o, part, hbuf.at[part])
        cps = [pltpu.make_async_copy(a, b, sems.at[part, i]) for i, (a, b) in enumerate(moves)]
        for cp in cps:
            cp.start()
        todo.append(cps)
    return todo


def cols_of(half, part, at, w):
    base = at if half == 0 else STARTS[part] + at
    return slice(base, base + w)


def cross_rows(half, ks, pieces, todo, hbuf, ca, cg):
    for part in range(3):
        for cp in todo[part]:
            cp.wait()
        for name, at, w in SEGMENTS[part]:
            acc = ca if name == "a" else cg
            cols = cols_of(half, part, at, w)
            rows = [pieces[part][i][:, :, :, cols].reshape(128, w) for i in range(len(ks))]
            rows = rows[0] if len(rows) == 1 else jnp.concatenate(rows, axis=0)
            x = nt(rows, hbuf[part, :, at:at + w])
            for i, k in enumerate(ks):
                for s4 in range(2):
                    r = i * 128 + s4 * 64
                    add_rows(acc, half, place(part, k, s4), x[r:r + 64])


def val_rows(core_ref, blocks, name, seen, ka, kg):
    even = jnp.concatenate([x[:32] for x in blocks], axis=0)
    late = jnp.concatenate(blocks[4:], axis=0)
    y = nt(jnp.where(core_ref[0] == 0, even, late), jnp.concatenate(blocks, axis=0))
    acc = ka if name == "a" else kg
    if name in seen:
        acc[...] += y
    else:
        acc[...] = y
        seen.add(name)


def early_own_body(core_ref, acts, grads, dep_ref, *refs):
    pieces = [refs[p * 3:p * 3 + 3] for p in range(3)]
    ca, cg, tok, hbuf, sems = refs[9:]
    tok[...] = jnp.zeros_like(tok)
    todo = start_train(core_ref, acts, grads, 0, hbuf, sems)
    ca[...] = jnp.zeros_like(ca)
    cg[...] = jnp.zeros_like(cg)
    cross_rows(0, (0, 1, 2), pieces, todo, hbuf, ca, cg)


def early_other_body(core_ref, acts, grads, o0, o1, o2, ain, gin, ca, cg, hbuf, sems):
    todo = start_train(core_ref, acts, grads, 1, hbuf, sems)
    cross_rows(1, (0, 1, 2), [(o0, o1, o2)] * 3, todo, hbuf, ca, cg)


def late_own_body(core_ref, acts, grads, *refs):
    pieces = [refs[p * 4:p * 4 + 4] for p in range(3)]
    ca, cg, ka, kg, ids, hbuf, sems = refs[14:]
    todo = start_train(core_ref, acts, grads, 0, hbuf, sems)

    def blocks(part, cols, w):
        out = [None] * 8
        for k in range(4):
            for s4 in range(2):
                out[place(part, k, s4)] = pieces[part][k][s4, :, :, cols].reshape(64, w)
        return out

    for at, x in enumerate(blocks(2, slice(C3G, C3), IDW)):
        ids[at * 64:at * 64 + 64, :] = x.astype(jnp.float32)
    seen = set()
    for part in range(3):
        for name, at, w in SEGMENTS[part]:
            val_rows(core_ref, blocks(part, slice(at, at + w), w), name, seen, ka, kg)
    cross_rows(0, (3,), [p[3:] for p in pieces], todo, hbuf, ca, cg)


def late_other_body(core_ref, acts, grads, o0, o1, o2, o3, ain, gin, kain, kgin, ids,
                    raw_ref, norm_ref, ca, cg, ka, kg, hbuf, sems, vbuf, vsems):
    c = core_ref[0]
    todo = start_train(core_ref, acts, grads, 1, hbuf, sems)

    def moves(part):
        b = part % 2
        cols = pl.ds(STARTS[part], WIDTHS[part])
        return [
            pltpu.make_async_copy(
                o.at[s4, :, :, cols],
                vbuf.at[b, :, place(part, k, s4), :, pl.ds(0, WIDTHS[part])],
                vsems.at[b, k, s4],
            )
            for k, o in enumerate((o0, o1, o2, o3)) for s4 in range(2)
        ]

    for part in range(2):
        for cp in moves(part):
            cp.start()
    cross_rows(1, (3,), [(o3,)] * 3, todo, hbuf, ca, cg)
    seen = {"a", "g"}
    for part in range(3):
        for cp in moves(part):
            cp.wait()
        for name, at, w in SEGMENTS[part]:
            blocks = [vbuf[part % 2, b, :, :, at:at + w].reshape(64, w) for b in range(8)]
            val_rows(core_ref, blocks, name, seen, ka, kg)
        if part == 0:
            for cp in moves(2):
                cp.start()

    cross = ca[...].reshape(VAL, TOK) * cg[...].reshape(VAL, TOK)
    kern = ka[...] * kg[...]
    all_ids = ids[...]
    row_ids = jnp.transpose(all_ids)[0:1, :]
    even = jnp.concatenate([all_ids[b * 64:b * 64 + 32] for b in range(8)], axis=0)
    half_ids = jnp.where(c == 0, even, all_ids[256:512])
    for v in range(NVAL):
        keep = jnp.where(all_ids == float(v), 1.0, 0.0)
        keep = jnp.concatenate([keep] * 4, axis=1)
        raw_ref[v:v + 1, :] = jnp.sum(cross * keep, axis=0, keepdims=True)
        keep = jnp.where(half_ids == float(v), 1.0, 0.0)
        keep = jnp.concatenate([keep] * 4, axis=1)
        part = jnp.sum(kern * keep, axis=0, keepdims=True)
        part = jnp.sum(jnp.where(row_ids == float(v), part, 0.0))
        norm_ref[v:v + 1, :] = jnp.full((1, 128), part, jnp.float32)


ACC = jax.ShapeDtypeStruct((8, 8, 8, TOK), jnp.float32)
KERN = jax.ShapeDtypeStruct((VAL // 2, VAL), jnp.float32)


def local_call(body, core, acts, grads, args, outs, flops, scratch=(), anys=(), aliases=None, mib=21):
    vmem = pl.BlockSpec(memory_space=pltpu.VMEM)
    anyspec = pl.BlockSpec(memory_space=pl.ANY)
    return pl.pallas_call(
        body,
        in_specs=[pl.BlockSpec(memory_space=pltpu.SMEM)] + [anyspec] * 2
        + [anyspec if i in anys else vmem for i in range(len(args))],
        out_specs=[vmem] * len(outs),
        out_shape=outs,
        scratch_shapes=[
            pltpu.VMEM((3, TOK, C1), jnp.bfloat16),
            pltpu.SemaphoreType.DMA((3, 2)),
        ] + list(scratch),
        input_output_aliases={3 + k: v for k, v in (aliases or {}).items()},
        compiler_params=pltpu.CompilerParams(vmem_limit_bytes=mib << 20),
        cost_estimate=pl.CostEstimate(
            flops=flops, bytes_accessed=TOK * (FF + D), transcendentals=0
        ),
    )(core, acts, grads, *[x if i in anys else pin(x) for i, x in enumerate(args)])


def shards(hidden_acts, out_grads, val_acts, val_grads, val_ids):
    hidden_acts = pltpu.with_memory_space_constraint(hidden_acts, pltpu.HBM)
    out_grads = pltpu.with_memory_space_constraint(out_grads, pltpu.HBM)
    core = lax.axis_index("dp") % 2
    first = core == 0
    idcol = jnp.broadcast_to(val_ids[:, None].astype(jnp.bfloat16), (4, IDW))
    halves = [
        jnp.concatenate(
            [val_acts[:, h * HA:(h + 1) * HA], val_grads[:, h * HG:(h + 1) * HG], idcol], axis=1
        )
        for h in range(2)
    ]
    keep = jnp.where(first, halves[0], halves[1])
    got = swap(jnp.where(first, halves[1], halves[0]))
    rows = jnp.concatenate([jnp.where(first, keep, got), jnp.where(first, got, keep)], axis=0)

    rows = double(rows, "z", 0)
    rows = double(rows, "y", 0)
    sa = self_acts(hidden_acts, rows)
    (rows,) = gate([double(rows, "x", 0)], sa)
    rows = rows.reshape(8, 8, ALLW)
    block_gram = self_grads(out_grads, sa, rows)
    piece = [[rows[..., s:s + w]] for s, w in zip(STARTS, WIDTHS)]
    piece = [[double(piece[j][0], RUNS[j], 1)] for j in range(3)]
    for j in range(3):
        piece[j].append(hop(piece[j][0], STEP5[j], 1))
    for j in range(3):
        piece[j].append(hop(piece[j][0], STEP6[j], 1))
    for j in range(3):
        piece[j].append(hop(piece[j][1], STEP6[j], 1))
    joined = [jnp.concatenate([piece[j][k] for j in range(3)], axis=-1) for k in range(4)]
    o0, o1, o2 = [swap(x) for x in joined[:3]]
    call = functools.partial(
        local_call, core=core.reshape(1).astype(jnp.int32), acts=hidden_acts, grads=out_grads
    )
    unit = 2 * 512 * (HA + HG)
    ca, cg, tok = call(
        early_own_body, args=[block_gram] + [piece[j][k] for j in range(3) for k in range(3)],
        outs=[ACC, ACC, jax.ShapeDtypeStruct((8, 128), jnp.float32)],
        flops=384 * unit, anys=(0,),
    )
    (joined3,) = gate(joined[3:], tok)
    o3 = swap(joined3)
    ca, cg = call(
        early_other_body, args=[o0, o1, o2, ca, cg], outs=[ACC, ACC],
        flops=384 * unit, aliases={3: 0, 4: 1},
    )
    ids = jax.ShapeDtypeStruct((VAL, IDW), jnp.float32)
    ca, cg, ka, kg, ids = call(
        late_own_body, args=[piece[j][k] for j in range(3) for k in range(4)] + [ca, cg],
        outs=[ACC, ACC, KERN, KERN, ids], flops=384 * unit, aliases={12: 0, 13: 1},
    )
    raw, norm, *_ = call(
        late_other_body, args=[o0, o1, o2, o3, ca, cg, ka, kg, ids],
        outs=[
            jax.ShapeDtypeStruct((NVAL, TOK), jnp.float32),
            jax.ShapeDtypeStruct((NVAL, 128), jnp.float32),
            ACC, ACC, KERN, KERN,
        ],
        scratch=[
            pltpu.VMEM((2, 8, 8, 8, C1), jnp.bfloat16),
            pltpu.SemaphoreType.DMA((2, 4, 2)),
        ],
        flops=384 * unit, aliases={4: 2, 5: 3, 6: 4, 7: 5}, mib=32,
    )
    norm = norm + swap(norm)
    token_scores = raw * lax.rsqrt(norm[:, :1] + 1e-06)
    return (token_scores, block_gram)


def solution(mesh):
    return jax.shard_map(
        shards,
        mesh=mesh,
        in_specs=(
            P(AXES, None),
            P(AXES, None),
            P(AXES, None),
            P(AXES, None),
            P(AXES),
        ),
        out_specs=(P(None, AXES), P(AXES, None)),
        check_vma=False,
    )
```

time: 144 us -> 145 us (level)
  local copies, waits for them, and re-layouts: 8.95 us -> 18.2 us
  other arithmetic: 15.6 us -> 7.87 us
  Pallas kernels: 53.9 us -> 58.8 us
  starting transfers between devices: 41.1 us -> 38.2 us
  waiting for transfers between devices: 22.7 us -> 20.1 us
    unnamed x58 -> x80, local copies, waits for them, and re-layouts: 4.65 us -> 16.3 us
    pallas_call x3 -> x4, Pallas kernels: 38.1 us -> 43 us  [local_call(): pl.pallas_call(body, in_specs=[pl.BlockSpec(memory_space=pltpu.SMEM)] + [...]
    another operation x7, other arithmetic: 4.68 us -> 0.68 us  [double(): return jnp.stack([x, hop(x, axis, step)])]
    concatenate x4, other arithmetic: 9.25 us -> 5.53 us  [shards(): jnp.concatenate([piece[j][k] for j in range(3)], axis=-1)]
    ppermute x15, waiting for transfers between devices: 20.8 us -> 17.3 us  [hop(): return lax.ppermute(x, AXES, ring_pairs(axis, step))]
    ppermute x15, starting transfers between devices: 16 us -> 13.6 us  [hop(): return lax.ppermute(x, AXES, ring_pairs(axis, step))]
    another operation x2, local copies, waits for them, and re-layouts: 2.54 us -> 0.2 us  [double(): return jnp.stack([x, hop(x, axis, step)])]
  transfers between devices with their start and end apart: 21 -> 21, of which waited for: 8 -> 8; matrix products, arithmetic and copies ran while one was open for 9% -> 4% of each run, Pallas kernels for 23% -> 31%
where the time goes in v3:
time: 145 us; the launch traced here: 144 us
  Pallas kernels  58.8 us (41%)
  starting transfers between devices  38.2 us (26%)
  waiting for transfers between devices  20.1 us (14%)
  local copies, waits for them, and re-layouts  18.2 us (13%)
  other arithmetic  7.87 us (5%)
    pallas_call x4, Pallas kernels, local_call(): pl.pallas_call(body, in_specs=[pl.BlockSpec(memory_space=pltpu.SMEM)] + [...  43 us
    ppermute x6, starting transfers between devices, swap(): return lax.ppermute(x, AXES, core_pairs())  24.6 us
    ppermute x15, waiting for transfers between devices, hop(): return lax.ppermute(x, AXES, ring_pairs(axis, step))  17.3 us
    unnamed x80, local copies, waits for them, and re-layouts  16.3 us
    ppermute x15, starting transfers between devices, hop(): return lax.ppermute(x, AXES, ring_pairs(axis, step))  13.6 us
    pallas_call x1, Pallas kernels, self_acts(): pl.pallas_call(self_acts_body, grid=(FF // KC,), in_specs=[pl.BlockSpec((...  9.49 us
    pallas_call x1, Pallas kernels, self_grads(): pl.pallas_call(functools.partial(self_grads_body, steps=D // KC), grid=(D...  6.34 us
    concatenate x4, other arithmetic, shards(): jnp.concatenate([piece[j][k] for j in range(3)], axis=-1)  5.53 us
  transfers between devices with their start and end apart: 21, of which 8 were waited for; matrix products, arithmetic and copies ran while one was open for 4% of the time, Pallas kernels for 31%

profile of v3, /device:TPU:1, one launch (start us, length us, event | category | flops | bytes accessed | tf_op | source)
XLA Modules:
  0.0 144.4 jit_solution(4801276117082967087)
XLA Ops:
  0.6 0.9 fusion.3
  1.5 0.8 fusion.4
  2.3 0.7 convert_element_type.4
  3.2 1.5 %collective-permute-start = (bf16[4,11392]{1,0:T(4,128)(2,1)S(1)}, bf16[4,11392]{1,0:T(4,128)(2,1)S(1)}, u32[]{:S(2)}, u32[]{:S(2)}) collective-permute-start(bf16[4,11392]{1,0:T(4,128)(2,1)S(1)} %broadcast_select_fusion.2), channel_id=1, source_target_pairs={{0,8},{1,9},{2,10},{3,11},{4,12},{5,13},{6,14},{7,15},{8,0},{9,1},... | collective-permute-start | bytes 273416 | tf_op jit(solution)/shard_map/ppermute | solution.py:62
  4.7 0.9 collective-permute-done
  5.8 3.9 %collective-permute-start.1 = (bf16[8,11392]{1,0:T(8,128)(2,1)S(1)}, bf16[8,11392]{1,0:T(8,128)(2,1)S(1)}, u32[]{:S(2)}, u32[]{:S(2)}) collective-permute-start(bf16[8,11392]{1,0:T(8,128)(2,1)S(1)} %get-tuple-element.39), channel_id=1, source_target_pairs={{0,16},{1,17},{2,18},{3,19},{4,20},{5,21},{6,22},{7,23},{8,56},{9,... | collective-permute-start | bytes 546824 | tf_op jit(solution)/shard_map/ppermute | solution.py:66
  9.7 2.9 %collective-permute-done.1 = bf16[8,11392]{1,0:T(8,128)(2,1)S(1)} collective-permute-done((bf16[8,11392]{1,0:T(8,128)(2,1)S(1)}, bf16[8,11392]{1,0:T(8,128)(2,1)S(1)}, u32[]{:S(2)}, u32[]{:S(2)}) %collective-permute-start.1) | collective-permute-done | bytes 182304 | tf_op jit(solution)/shard_map/ppermute | solution.py:66
  12.7 2.8 %collective-permute-start.2 = (bf16[2,8,11392]{2,1,0:T(8,128)(2,1)S(1)}, bf16[2,8,11392]{2,1,0:T(8,128)(2,1)S(1)}, u32[]{:S(2)}, u32[]{:S(2)}) collective-permute-start(bf16[2,8,11392]{2,1,0:T(8,128)(2,1)S(1)} %get-tuple-element.35), channel_id=1, source_target_pairs={{0,1},{1,0},{2,3},{3,2},{4,5},{5,4},{6,7},{7,6},{8,11},{9,10},{10,... | collective-permute-start | bytes 1093640 | tf_op jit(solution)/shard_map/ppermute | solution.py:66
  15.5 4.9 %collective-permute-done.2 = bf16[2,8,11392]{2,1,0:T(8,128)(2,1)S(1)} collective-permute-done((bf16[2,8,11392]{2,1,0:T(8,128)(2,1)S(1)}, bf16[2,8,11392]{2,1,0:T(8,128)(2,1)S(1)}, u32[]{:S(2)}, u32[]{:S(2)}) %collective-permute-start.2) | collective-permute-done | bytes 364576 | tf_op jit(solution)/shard_map/ppermute | solution.py:66
  20.5 2.6 %collective-permute-start.3 = (bf16[2,2,8,11392]{3,2,1,0:T(8,128)(2,1)S(1)}, bf16[2,2,8,11392]{3,2,1,0:T(8,128)(2,1)S(1)}, u32[]{:S(2)}, u32[]{:S(2)}) collective-permute-start(bf16[2,2,8,11392]{3,2,1,0:T(8,128)(2,1)S(1)} %get-tuple-element.33.dep_ref), channel_id=1, source_target_pairs={{0,64},{1,65},{2,66},{3,67},{4,68},{5,69},{6,70},{7,71},{8,76},{9,... | collective-permute-start | bytes 2187272 | tf_op jit(solution)/shard_map/ppermute | solution.py:66
  23.0 9.5 %shard_map.68.refs_1_.sa_ref = f32[512,256]{1,0:T(8,128)S(1)} custom-call(bf16[512,14336]{1,0:T(8,128)(2,1)} %acts.7, bf16[2,2,8,11392]{3,2,1,0:T(8,128)(2,1)S(1)} %get-tuple-element.33.dep_ref), custom_call_target="tpu_custom_call" | custom-call | flops 3758096384 | bytes 14680064 | tf_op jit(solution)/shard_map/pallas_call | solution.py:137
  32.5 0.8 copy-done.30
  34.0 0.5 copy-done.31
  34.6 6.3 %shard_map.70.dep_ref = f32[4,4]{1,0:T(4,128)} custom-call(bf16[512,8192]{1,0:T(8,128)(2,1)} %grads.7, f32[512,256]{1,0:T(8,128)S(1)} %copy-done.31, bf16[8,8,11392]{2,1,0:T(8,128)(2,1)S(1)} %bitcast.22), custom_call_target="tpu_custom_call" | custom-call | flops 2147483648 | bytes 8388608 | tf_op jit(solution)/shard_map/pallas_call | solution.py:154
  40.9 0.6 collective-permute-done.6
  41.9 1.5 %collective-permute-start.14 = (bf16[2,8,8,3712]{3,2,1,0:T(8,128)(2,1)S(1)}, bf16[2,8,8,3712]{3,2,1,0:T(8,128)(2,1)S(1)}, u32[]{:S(2)}, u32[]{:S(2)}) collective-permute-start(bf16[2,8,8,3712]{3,2,1,0:T(8,128)(2,1)S(1)} %pad_maximum_fusion.6.refs_6_.refs_8_), channel_id=1, source_target_pairs={{0,48},{1,49},{2,50},{3,51},{4,52},{5,53},{6,54},{7,55},{8,24},{9,... | collective-permute-start | bytes 2850824 | tf_op jit(solution)/shard_map/ppermute | solution.py:66
  43.5 1.5 %collective-permute-start.12 = (bf16[2,8,8,3840]{3,2,1,0:T(8,128)(2,1)S(1)}, bf16[2,8,8,3840]{3,2,1,0:T(8,128)(2,1)S(1)}, u32[]{:S(2)}, u32[]{:S(2)}) collective-permute-start(bf16[2,8,8,3840]{3,2,1,0:T(8,128)(2,1)S(1)} %pad_maximum_fusion.4.refs_0_), channel_id=1, source_target_pairs={{0,68},{1,69},{2,70},{3,71},{4,64},{5,65},{6,66},{7,67},{8,72},{9,... | collective-permute-start | bytes 2949128 | tf_op jit(solution)/shard_map/ppermute | solution.py:66
  45.3 1.6 %maximum_maximum_fusion = bf16[2,8,8,11392]{3,2,1,0:T(8,128)(2,1)} fusion(bf16[1,8,8,3712]{3,2,1,0:T(8,128)(2,1)S(1)} %bitcast.28, bf16[1,8,8,3712]{3,2,1,0:T(8,128)(2,1)S(1)} %get-tuple-element.30, bf16[1,8,8,3840]{3,2,1,0:T(8,128)(2,1)S(1)} %bitcast.26, bf16[1,8,8,3840]{3,2,1,0:T(8,128)(2,1)S(1)} %get-tuple-element.27, ...), kind=kLoop, calls=%fused_computation | loop fusion | flops 17498112 | bytes 5832704 | tf_op jit(solution)/shard_map/concatenate | solution.py:399
  47.0 7.6 %collective-permute-done.10.refs_7_.refs_9_ = bf16[2,8,8,3712]{3,2,1,0:T(8,128)(2,1)S(1)} collective-permute-done((bf16[2,8,8,3712]{3,2,1,0:T(8,128)(2,1)S(1)}, bf16[2,8,8,3712]{3,2,1,0:T(8,128)(2,1)S(1)}, u32[]{:S(2)}, u32[]{:S(2)}) %collective-permute-start.10) | collective-permute-done | bytes 950304 | tf_op jit(solution)/shard_map/ppermute | solution.py:66
  54.9 8.8 %collective-permute-start.7 = (bf16[2,8,8,11392]{3,2,1,0:T(8,128)(2,1)}, bf16[2,8,8,11392]{3,2,1,0:T(8,128)(2,1)}, u32[]{:S(2)}, u32[]{:S(2)}) collective-permute-start(bf16[2,8,8,11392]{3,2,1,0:T(8,128)(2,1)} %maximum_maximum_fusion), channel_id=1, source_target_pairs={{0,8},{1,9},{2,10},{3,11},{4,12},{5,13},{6,14},{7,15},{8,0},{9,1},... | collective-permute-start | bytes 8749064 | tf_op jit(solution)/shard_map/ppermute | solution.py:62
  63.8 1.3 collective-permute-done.13.refs_5_.refs_6_
  65.1 1.9 %pad_maximum_fusion.1 = bf16[2,8,8,11392]{3,2,1,0:T(8,128)(2,1)} fusion(bf16[2,8,8,3712]{3,2,1,0:T(8,128)(2,1)S(1)} %collective-permute-done.14.refs_8_.refs_10_, bf16[2,8,8,3840]{3,2,1,0:T(8,128)(2,1)S(1)} %collective-permute-done.13.refs_5_.refs_6_, bf16[2,8,8,3840]{3,2,1,0:T(8,128)(2,1)S(1)} %collective-permute-done.12.refs_2_), kind=kLoop, calls=%fused_computation.2 | loop fusion | flops 8749056 | bytes 5832704 | tf_op jit(solution)/shard_map/concatenate | solution.py:399
  67.0 8.3 %collective-permute-start.15 = (bf16[2,8,8,11392]{3,2,1,0:T(8,128)(2,1)}, bf16[2,8,8,11392]{3,2,1,0:T(8,128)(2,1)}, u32[]{:S(2)}, u32[]{:S(2)}) collective-permute-start(bf16[2,8,8,11392]{3,2,1,0:T(8,128)(2,1)} %pad_maximum_fusion.1), channel_id=1, source_target_pairs={{0,8},{1,9},{2,10},{3,11},{4,12},{5,13},{6,14},{7,15},{8,0},{9,1},... | collective-permute-start | bytes 8749064 | tf_op jit(solution)/shard_map/ppermute | solution.py:62
  75.5 7.7 %shard_map.71 = (f32[8,8,8,512]{3,2,1,0:T(8,128)S(1)}, f32[8,8,8,512]{3,2,1,0:T(8,128)S(1)}, f32[8,128]{1,0:T(8,128)S(1)}) custom-call(s32[1]{0:T(128)} %bitcast.core_ref, bf16[512,14336]{1,0:T(8,128)(2,1)} %acts.7, bf16[512,8192]{1,0:T(8,128)(2,1)} %grads.7, f32[4,4]{1,0:T(4,128)S(1)} %copy-done.38, bf16[2,8,8,3840]{3,2,1,0:T(8,128)(2,1)S(1)} %pad_maximum_fusion.4.refs_0_, ...), custom_call_target="tpu_custom_call" | custom-call | flops 4429185024 | bytes 11534336 | tf_op jit(solution)/shard_map/pallas_call | solution.py:351
  83.3 1.0 copy-done
  84.3 1.0 copy-done.6
  85.2 0.6 copy-done.39
  85.8 1.8 %pad_maximum_fusion = bf16[2,8,8,11392]{3,2,1,0:T(8,128)(2,1)} fusion(bf16[2,8,8,3712]{3,2,1,0:T(8,128)(2,1)S(1)} %collective-permute-done.10.refs_7_.refs_9_, bf16[2,8,8,3840]{3,2,1,0:T(8,128)(2,1)S(1)} %collective-permute-done.9.refs_4_.refs_5_, bf16[2,8,8,3840]{3,2,1,0:T(8,128)(2,1)S(1)} %collective-permute-done.8.refs_1_), kind=kLoop, calls=%fused_computation.1 | loop fusion | flops 8749056 | bytes 5832704 | tf_op jit(solution)/shard_map/concatenate | solution.py:399
  87.6 2.6 %collective-permute-start.11 = (bf16[2,8,8,11392]{3,2,1,0:T(8,128)(2,1)}, bf16[2,8,8,11392]{3,2,1,0:T(8,128)(2,1)}, u32[]{:S(2)}, u32[]{:S(2)}) collective-permute-start(bf16[2,8,8,11392]{3,2,1,0:T(8,128)(2,1)} %pad_maximum_fusion), channel_id=1, source_target_pairs={{0,8},{1,9},{2,10},{3,11},{4,12},{5,13},{6,14},{7,15},{8,0},{9,1},... | collective-permute-start | bytes 8749064 | tf_op jit(solution)/shard_map/ppermute | solution.py:62
  90.4 0.7 copy-done.32
  91.5 3.0 %collective-permute-start.19 = (bf16[2,8,8,11392]{3,2,1,0:T(8,128)(2,1)S(1)}, bf16[2,8,8,11392]{3,2,1,0:T(8,128)(2,1)S(1)}, u32[]{:S(2)}, u32[]{:S(2)}) collective-permute-start(bf16[2,8,8,11392]{3,2,1,0:T(8,128)(2,1)S(1)} %shard_map.72), channel_id=1, source_target_pairs={{0,8},{1,9},{2,10},{3,11},{4,12},{5,13},{6,14},{7,15},{8,0},{9,1},... | collective-permute-start | bytes 8749064 | tf_op jit(solution)/shard_map/ppermute | solution.py:62
  94.5 1.0 collective-permute-done.11.o1
  95.5 1.2 copy-done.1
  96.7 1.2 copy-done.7
  98.0 11.7 %shard_map.73 = (f32[8,8,8,512]{3,2,1,0:T(8,128)S(1)}, f32[8,8,8,512]{3,2,1,0:T(8,128)S(1)}) custom-call(s32[1]{0:T(128)} %bitcast.core_ref, bf16[512,14336]{1,0:T(8,128)(2,1)} %acts.7, bf16[512,8192]{1,0:T(8,128)(2,1)} %grads.7, bf16[2,8,8,11392]{3,2,1,0:T(8,128)(2,1)} %collective-permute-done.7.o0, ...), custom_call_target="tpu_custom_call", output_to_operand_aliasing={{0}: (6, {}), {1}: (7, {})} | custom-call | flops 4429185024 | bytes 11534336 | tf_op jit(solution)/shard_map/pallas_call | solution.py:351
  109.8 1.0 copy-done.2
  110.8 1.0 copy-done.8
  111.9 1.2 copy-done.3
  113.1 1.2 copy-done.9
  114.3 9.2 %shard_map.74 = (f32[8,8,8,512]{3,2,1,0:T(8,128)S(1)}, f32[8,8,8,512]{3,2,1,0:T(8,128)S(1)}, f32[256,512]{1,0:T(8,128)S(1)}, f32[256,512]{1,0:T(8,128)S(1)}, f32[512,128]{1,0:T(8,128)S(1)}) custom-call(s32[1]{0:T(128)} %bitcast.core_ref, bf16[512,14336]{1,0:T(8,128)(2,1)} %acts.7, ...), custom_call_target="tpu_custom_call", output_to_operand_aliasing={{0}: (15, {}), {1}: (16, {})} | custom-call | flops 4429185024 | bytes 11534336 | tf_op jit(solution)/shard_map/pallas_call | solution.py:351
  123.5 1.0 copy-done.4
  124.5 1.0 copy-done.10
  125.5 1.2 copy-done.5
  126.7 1.2 copy-done.11
  128.0 14.3 %shard_map.75 = (f32[4,512]{1,0:T(4,128)S(1)}, f32[4,128]{1,0:T(4,128)S(1)}, f32[8,8,8,512]{3,2,1,0:T(8,128)S(1)}, f32[8,8,8,512]{3,2,1,0:T(8,128)S(1)}, f32[256,512]{1,0:T(8,128)S(1)}, /*index=5*/f32[256,512]{1,0:T(8,128)S(1)}) custom-call(s32[1]{0:T(128)} %bitcast.core_ref, ...), custom_call_target="tpu_custom_call", output_to_operand_aliasing={{2}: (7, {}), {3}: (8, {}), {4}: (9, {}), {5}: (10, {})} | custom-call | flops 4429185024 | bytes 11534336 | tf_op jit(solution)/shard_map/pallas_call | solution.py:351
  142.3 0.5 collective-permute-start.20
  142.7 0.8 collective-permute-done.20
  143.7 0.7 broadcast_multiply_fusion
  (104 shorter events, 3.2 us)
Async XLA Ops:
  3.2 2.4 %collective-permute-start = (bf16[4,11392]{1,0:T(4,128)(2,1)S(1)}, bf16[4,11392]{1,0:T(4,128)(2,1)S(1)}, u32[]{:S(2)}, u32[]{:S(2)}) collective-permute-start(bf16[4,11392]{1,0:T(4,128)(2,1)S(1)} %broadcast_select_fusion.2), channel_id=1, source_target_pairs={{0,8},{1,9},{2,10},{3,11},{4,12},{5,13},{6,14},{7,15},{8,0},{9,1},... | collective-permute-start | bytes 273416 | tf_op jit(solution)/shard_map/ppermute | solution.py:62
  5.8 6.8 %collective-permute-start.1 = (bf16[8,11392]{1,0:T(8,128)(2,1)S(1)}, bf16[8,11392]{1,0:T(8,128)(2,1)S(1)}, u32[]{:S(2)}, u32[]{:S(2)}) collective-permute-start(bf16[8,11392]{1,0:T(8,128)(2,1)S(1)} %get-tuple-element.39), channel_id=1, source_target_pairs={{0,16},{1,17},{2,18},{3,19},{4,20},{5,21},{6,22},{7,23},{8,56},{9,... | collective-permute-start | bytes 546824 | tf_op jit(solution)/shard_map/ppermute | solution.py:66
  12.7 7.7 %collective-permute-start.2 = (bf16[2,8,11392]{2,1,0:T(8,128)(2,1)S(1)}, bf16[2,8,11392]{2,1,0:T(8,128)(2,1)S(1)}, u32[]{:S(2)}, u32[]{:S(2)}) collective-permute-start(bf16[2,8,11392]{2,1,0:T(8,128)(2,1)S(1)} %get-tuple-element.35), channel_id=1, source_target_pairs={{0,1},{1,0},{2,3},{3,2},{4,5},{5,4},{6,7},{7,6},{8,11},{9,10},{10,... | collective-permute-start | bytes 1093640 | tf_op jit(solution)/shard_map/ppermute | solution.py:66
  20.5 12.9 %collective-permute-start.3 = (bf16[2,2,8,11392]{3,2,1,0:T(8,128)(2,1)S(1)}, bf16[2,2,8,11392]{3,2,1,0:T(8,128)(2,1)S(1)}, u32[]{:S(2)}, u32[]{:S(2)}) collective-permute-start(bf16[2,2,8,11392]{3,2,1,0:T(8,128)(2,1)S(1)} %get-tuple-element.33.dep_ref), channel_id=1, source_target_pairs={{0,64},{1,65},{2,66},{3,67},{4,68},{5,69},{6,70},{7,71},{8,76},{9,... | collective-permute-start | bytes 2187272 | tf_op jit(solution)/shard_map/ppermute | solution.py:66
  33.6 7.9 %collective-permute-start.6 = (bf16[8,8,3712]{2,1,0:T(8,128)(2,1)S(1)}, bf16[8,8,3712]{2,1,0:T(8,128)(2,1)S(1)}, u32[]{:S(2)}, u32[]{:S(2)}) collective-permute-start(bf16[8,8,3712]{2,1,0:T(8,128)(2,1)S(1)} %get-tuple-element.31), channel_id=1, source_target_pairs={{0,68},{1,69},{2,70},{3,71},{4,64},{5,65},{6,66},{7,67},{8,72},{9,... | collective-permute-start | bytes 1425416 | tf_op jit(solution)/shard_map/ppermute | solution.py:66
  33.8 9.6 %collective-permute-start.4 = (bf16[8,8,3840]{2,1,0:T(8,128)(2,1)S(1)}, bf16[8,8,3840]{2,1,0:T(8,128)(2,1)S(1)}, u32[]{:S(2)}, u32[]{:S(2)}) collective-permute-start(bf16[8,8,3840]{2,1,0:T(8,128)(2,1)S(1)} %get-tuple-element.29), channel_id=1, source_target_pairs={{0,3},{1,2},{2,1},{3,0},{4,7},{5,6},{6,5},{7,4},{8,9},{9,8},{10,11... | collective-permute-start | bytes 1474568 | tf_op jit(solution)/shard_map/ppermute | solution.py:66
  33.9 11.1 %collective-permute-start.5 = (bf16[8,8,3840]{2,1,0:T(8,128)(2,1)S(1)}, bf16[8,8,3840]{2,1,0:T(8,128)(2,1)S(1)}, u32[]{:S(2)}, u32[]{:S(2)}) collective-permute-start(bf16[8,8,3840]{2,1,0:T(8,128)(2,1)S(1)} %get-tuple-element.28), channel_id=1, source_target_pairs={{0,48},{1,49},{2,50},{3,51},{4,52},{5,53},{6,54},{7,55},{8,24},{9,... | collective-permute-start | bytes 1474568 | tf_op jit(solution)/shard_map/ppermute | solution.py:66
  41.6 33.9 %copy-start.24 = (bf16[2,8,8,3712]{3,2,1,0:T(8,128)(2,1)}, bf16[2,8,8,3712]{3,2,1,0:T(8,128)(2,1)S(1)}, u32[]{:S(2)}) copy-start(bf16[2,8,8,3712]{3,2,1,0:T(8,128)(2,1)S(1)} %pad_maximum_fusion.6.refs_6_.refs_8_) | copy-start | bytes 2850820
  41.6 13.0 %collective-permute-start.10 = (bf16[2,8,8,3712]{3,2,1,0:T(8,128)(2,1)S(1)}, bf16[2,8,8,3712]{3,2,1,0:T(8,128)(2,1)S(1)}, u32[]{:S(2)}, u32[]{:S(2)}) collective-permute-start(bf16[2,8,8,3712]{3,2,1,0:T(8,128)(2,1)S(1)} %pad_maximum_fusion.6.refs_6_.refs_8_), channel_id=1, source_target_pairs={{0,3},{1,2},{2,1},{3,0},{4,7},{5,6},{6,5},{7,4},{8,9},{9,8},{10,11... | collective-permute-start | bytes 2850824 | tf_op jit(solution)/shard_map/ppermute | solution.py:66
  41.9 13.0 %collective-permute-start.14 = (bf16[2,8,8,3712]{3,2,1,0:T(8,128)(2,1)S(1)}, bf16[2,8,8,3712]{3,2,1,0:T(8,128)(2,1)S(1)}, u32[]{:S(2)}, u32[]{:S(2)}) collective-permute-start(bf16[2,8,8,3712]{3,2,1,0:T(8,128)(2,1)S(1)} %pad_maximum_fusion.6.refs_6_.refs_8_), channel_id=1, source_target_pairs={{0,48},{1,49},{2,50},{3,51},{4,52},{5,53},{6,54},{7,55},{8,24},{9,... | collective-permute-start | bytes 2850824 | tf_op jit(solution)/shard_map/ppermute | solution.py:66
  43.5 32.0 %copy-start.12 = (bf16[2,8,8,3840]{3,2,1,0:T(8,128)(2,1)}, bf16[2,8,8,3840]{3,2,1,0:T(8,128)(2,1)S(1)}, u32[]{:S(2)}) copy-start(bf16[2,8,8,3840]{3,2,1,0:T(8,128)(2,1)S(1)} %pad_maximum_fusion.4.refs_0_) | copy-start | bytes 2949124
  43.5 20.3 %collective-permute-start.12 = (bf16[2,8,8,3840]{3,2,1,0:T(8,128)(2,1)S(1)}, bf16[2,8,8,3840]{3,2,1,0:T(8,128)(2,1)S(1)}, u32[]{:S(2)}, u32[]{:S(2)}) collective-permute-start(bf16[2,8,8,3840]{3,2,1,0:T(8,128)(2,1)S(1)} %pad_maximum_fusion.4.refs_0_), channel_id=1, source_target_pairs={{0,68},{1,69},{2,70},{3,71},{4,64},{5,65},{6,66},{7,67},{8,72},{9,... | collective-permute-start | bytes 2949128 | tf_op jit(solution)/shard_map/ppermute | solution.py:66
  45.0 30.3 %collective-permute-start.8 = (bf16[2,8,8,3840]{3,2,1,0:T(8,128)(2,1)S(1)}, bf16[2,8,8,3840]{3,2,1,0:T(8,128)(2,1)S(1)}, u32[]{:S(2)}, u32[]{:S(2)}) collective-permute-start(bf16[2,8,8,3840]{3,2,1,0:T(8,128)(2,1)S(1)} %pad_maximum_fusion.4.refs_0_), channel_id=1, source_target_pairs={{0,48},{1,49},{2,50},{3,51},{4,52},{5,53},{6,54},{7,55},{8,24},{9,... | collective-permute-start | bytes 2949128 | tf_op jit(solution)/shard_map/ppermute | solution.py:66
  45.1 30.3 %copy-start.18 = (bf16[2,8,8,3840]{3,2,1,0:T(8,128)(2,1)}, bf16[2,8,8,3840]{3,2,1,0:T(8,128)(2,1)S(1)}, u32[]{:S(2)}) copy-start(bf16[2,8,8,3840]{3,2,1,0:T(8,128)(2,1)S(1)} %pad_maximum_fusion.5.refs_3_.refs_4_) | copy-start | bytes 2949124
  45.1 20.0 %collective-permute-start.13 = (bf16[2,8,8,3840]{3,2,1,0:T(8,128)(2,1)S(1)}, bf16[2,8,8,3840]{3,2,1,0:T(8,128)(2,1)S(1)}, u32[]{:S(2)}, u32[]{:S(2)}) collective-permute-start(bf16[2,8,8,3840]{3,2,1,0:T(8,128)(2,1)S(1)} %pad_maximum_fusion.5.refs_3_.refs_4_), channel_id=1, source_target_pairs={{0,3},{1,2},{2,1},{3,0},{4,7},{5,6},{6,5},{7,4},{8,9},{9,8},{10,11... | collective-permute-start | bytes 2949128 | tf_op jit(solution)/shard_map/ppermute | solution.py:66
  47.0 28.5 %copy-start.38 = (f32[4,4]{1,0:T(4,128)S(1)}, f32[4,4]{1,0:T(4,128)}, u32[]{:S(2)}) copy-start(f32[4,4]{1,0:T(4,128)} %shard_map.70.dep_ref) | copy-start | bytes 196
  54.6 28.7 %copy-start.26 = (bf16[2,8,8,3712]{3,2,1,0:T(8,128)(2,1)}, bf16[2,8,8,3712]{3,2,1,0:T(8,128)(2,1)S(1)}, u32[]{:S(2)}) copy-start(bf16[2,8,8,3712]{3,2,1,0:T(8,128)(2,1)S(1)} %collective-permute-done.10.refs_7_.refs_9_) | copy-start | bytes 2850820
  54.6 20.8 %collective-permute-start.9 = (bf16[2,8,8,3840]{3,2,1,0:T(8,128)(2,1)S(1)}, bf16[2,8,8,3840]{3,2,1,0:T(8,128)(2,1)S(1)}, u32[]{:S(2)}, u32[]{:S(2)}) collective-permute-start(bf16[2,8,8,3840]{3,2,1,0:T(8,128)(2,1)S(1)} %pad_maximum_fusion.5.refs_3_.refs_4_), channel_id=1, source_target_pairs={{0,68},{1,69},{2,70},{3,71},{4,64},{5,65},{6,66},{7,67},{8,72},{9,... | collective-permute-start | bytes 2949128 | tf_op jit(solution)/shard_map/ppermute | solution.py:66
  54.9 20.6 %copy-start.28 = (bf16[2,8,8,3712]{3,2,1,0:T(8,128)(2,1)}, bf16[2,8,8,3712]{3,2,1,0:T(8,128)(2,1)S(1)}, u32[]{:S(2)}) copy-start(bf16[2,8,8,3712]{3,2,1,0:T(8,128)(2,1)S(1)} %collective-permute-done.14.refs_8_.refs_10_) | copy-start | bytes 2850820
  54.9 39.5 %collective-permute-start.7 = (bf16[2,8,8,11392]{3,2,1,0:T(8,128)(2,1)}, bf16[2,8,8,11392]{3,2,1,0:T(8,128)(2,1)}, u32[]{:S(2)}, u32[]{:S(2)}) collective-permute-start(bf16[2,8,8,11392]{3,2,1,0:T(8,128)(2,1)} %maximum_maximum_fusion), channel_id=1, source_target_pairs={{0,8},{1,9},{2,10},{3,11},{4,12},{5,13},{6,14},{7,15},{8,0},{9,1},... | collective-permute-start | bytes 8749064 | tf_op jit(solution)/shard_map/ppermute | solution.py:62
  63.8 11.7 %copy-start.14 = (bf16[2,8,8,3840]{3,2,1,0:T(8,128)(2,1)}, bf16[2,8,8,3840]{3,2,1,0:T(8,128)(2,1)S(1)}, u32[]{:S(2)}) copy-start(bf16[2,8,8,3840]{3,2,1,0:T(8,128)(2,1)S(1)} %collective-permute-done.12.refs_2_) | copy-start | bytes 2949124
  63.8 23.8 %collective-permute-start.18 = (bf16[2,8,8,3712]{3,2,1,0:T(8,128)(2,1)S(1)}, bf16[2,8,8,3712]{3,2,1,0:T(8,128)(2,1)S(1)}, u32[]{:S(2)}, u32[]{:S(2)}) collective-permute-start(bf16[2,8,8,3712]{3,2,1,0:T(8,128)(2,1)S(1)} %collective-permute-done.10.refs_7_.refs_9_), channel_id=1, source_target_pairs={{0,48},{1,49},{2,50},{3,51},{4,52},{5,53},{6,54},{7,55},{8,24},{9,... | collective-permute-start | bytes 2850824 | tf_op jit(solution)/shard_map/ppermute | solution.py:66
  65.1 10.4 %copy-start.20 = (bf16[2,8,8,3840]{3,2,1,0:T(8,128)(2,1)}, bf16[2,8,8,3840]{3,2,1,0:T(8,128)(2,1)S(1)}, u32[]{:S(2)}) copy-start(bf16[2,8,8,3840]{3,2,1,0:T(8,128)(2,1)S(1)} %collective-permute-done.13.refs_5_.refs_6_) | copy-start | bytes 2949124
  67.0 27.4 %collective-permute-start.15 = (bf16[2,8,8,11392]{3,2,1,0:T(8,128)(2,1)}, bf16[2,8,8,11392]{3,2,1,0:T(8,128)(2,1)}, u32[]{:S(2)}, u32[]{:S(2)}) collective-permute-start(bf16[2,8,8,11392]{3,2,1,0:T(8,128)(2,1)} %pad_maximum_fusion.1), channel_id=1, source_target_pairs={{0,8},{1,9},{2,10},{3,11},{4,12},{5,13},{6,14},{7,15},{8,0},{9,1},... | collective-permute-start | bytes 8749064 | tf_op jit(solution)/shard_map/ppermute | solution.py:62
  75.3 7.9 %copy-start.16 = (bf16[2,8,8,3840]{3,2,1,0:T(8,128)(2,1)}, bf16[2,8,8,3840]{3,2,1,0:T(8,128)(2,1)S(1)}, u32[]{:S(2)}) copy-start(bf16[2,8,8,3840]{3,2,1,0:T(8,128)(2,1)S(1)} %collective-permute-done.8.refs_1_) | copy-start | bytes 2949124
  75.3 14.9 %collective-permute-start.16 = (bf16[2,8,8,3840]{3,2,1,0:T(8,128)(2,1)S(1)}, bf16[2,8,8,3840]{3,2,1,0:T(8,128)(2,1)S(1)}, u32[]{:S(2)}, u32[]{:S(2)}) collective-permute-start(bf16[2,8,8,3840]{3,2,1,0:T(8,128)(2,1)S(1)} %collective-permute-done.8.refs_1_), channel_id=1, source_target_pairs={{0,68},{1,69},{2,70},{3,71},{4,64},{5,65},{6,66},{7,67},{8,72},{9,... | collective-permute-start | bytes 2949128 | tf_op jit(solution)/shard_map/ppermute | solution.py:66
  75.4 7.9 %copy-start.22 = (bf16[2,8,8,3840]{3,2,1,0:T(8,128)(2,1)}, bf16[2,8,8,3840]{3,2,1,0:T(8,128)(2,1)S(1)}, u32[]{:S(2)}) copy-start(bf16[2,8,8,3840]{3,2,1,0:T(8,128)(2,1)S(1)} %collective-permute-done.9.refs_4_.refs_5_) | copy-start | bytes 2949124
  75.4 14.8 %collective-permute-start.17 = (bf16[2,8,8,3840]{3,2,1,0:T(8,128)(2,1)S(1)}, bf16[2,8,8,3840]{3,2,1,0:T(8,128)(2,1)S(1)}, u32[]{:S(2)}, u32[]{:S(2)}) collective-permute-start(bf16[2,8,8,3840]{3,2,1,0:T(8,128)(2,1)S(1)} %collective-permute-done.9.refs_4_.refs_5_), channel_id=1, source_target_pairs={{0,3},{1,2},{2,1},{3,0},{4,7},{5,6},{6,5},{7,4},{8,9},{9,8},{10,11... | collective-permute-start | bytes 2949128 | tf_op jit(solution)/shard_map/ppermute | solution.py:66
  87.6 2.8 %copy-start.36 = (bf16[2,8,8,3712]{3,2,1,0:T(8,128)(2,1)}, bf16[2,8,8,3712]{3,2,1,0:T(8,128)(2,1)S(1)}, u32[]{:S(2)}) copy-start(bf16[2,8,8,3712]{3,2,1,0:T(8,128)(2,1)S(1)} %collective-permute-done.18.refs_11_) | copy-start | bytes 2850820
  87.6 7.9 %collective-permute-start.11 = (bf16[2,8,8,11392]{3,2,1,0:T(8,128)(2,1)}, bf16[2,8,8,11392]{3,2,1,0:T(8,128)(2,1)}, u32[]{:S(2)}, u32[]{:S(2)}) collective-permute-start(bf16[2,8,8,11392]{3,2,1,0:T(8,128)(2,1)} %pad_maximum_fusion), channel_id=1, source_target_pairs={{0,8},{1,9},{2,10},{3,11},{4,12},{5,13},{6,14},{7,15},{8,0},{9,1},... | collective-permute-start | bytes 8749064 | tf_op jit(solution)/shard_map/ppermute | solution.py:62
  90.2 1.3 copy-start.34
  91.5 34.0 %collective-permute-start.19 = (bf16[2,8,8,11392]{3,2,1,0:T(8,128)(2,1)S(1)}, bf16[2,8,8,11392]{3,2,1,0:T(8,128)(2,1)S(1)}, u32[]{:S(2)}, u32[]{:S(2)}) collective-permute-start(bf16[2,8,8,11392]{3,2,1,0:T(8,128)(2,1)S(1)} %shard_map.72), channel_id=1, source_target_pairs={{0,8},{1,9},{2,10},{3,11},{4,12},{5,13},{6,14},{7,15},{8,0},{9,1},... | collective-permute-start | bytes 8749064 | tf_op jit(solution)/shard_map/ppermute | solution.py:62
  95.5 1.2 copy-start.1
  97.9 13.8 %copy-start.13 = (bf16[2,8,8,3840]{3,2,1,0:T(8,128)(2,1)S(1)}, bf16[2,8,8,3840]{3,2,1,0:T(8,128)(2,1)}, u32[]{:S(2)}) copy-start(bf16[2,8,8,3840]{3,2,1,0:T(8,128)(2,1)} %copy-done.12) | copy-start | bytes 2949124
  97.9 13.8 %copy-start.15 = (bf16[2,8,8,3840]{3,2,1,0:T(8,128)(2,1)S(1)}, bf16[2,8,8,3840]{3,2,1,0:T(8,128)(2,1)}, u32[]{:S(2)}) copy-start(bf16[2,8,8,3840]{3,2,1,0:T(8,128)(2,1)} %copy-done.14) | copy-start | bytes 2949124
  98.0 13.8 %copy-start.17 = (bf16[2,8,8,3840]{3,2,1,0:T(8,128)(2,1)S(1)}, bf16[2,8,8,3840]{3,2,1,0:T(8,128)(2,1)}, u32[]{:S(2)}) copy-start(bf16[2,8,8,3840]{3,2,1,0:T(8,128)(2,1)} %copy-done.16) | copy-start | bytes 2949124
  98.0 13.8 %copy-start.19 = (bf16[2,8,8,3840]{3,2,1,0:T(8,128)(2,1)S(1)}, bf16[2,8,8,3840]{3,2,1,0:T(8,128)(2,1)}, u32[]{:S(2)}) copy-start(bf16[2,8,8,3840]{3,2,1,0:T(8,128)(2,1)} %copy-done.18) | copy-start | bytes 2949124
  98.0 13.8 %copy-start.21 = (bf16[2,8,8,3840]{3,2,1,0:T(8,128)(2,1)S(1)}, bf16[2,8,8,3840]{3,2,1,0:T(8,128)(2,1)}, u32[]{:S(2)}) copy-start(bf16[2,8,8,3840]{3,2,1,0:T(8,128)(2,1)} %copy-done.20) | copy-start | bytes 2949124
  98.0 13.8 %copy-start.23 = (bf16[2,8,8,3840]{3,2,1,0:T(8,128)(2,1)S(1)}, bf16[2,8,8,3840]{3,2,1,0:T(8,128)(2,1)}, u32[]{:S(2)}) copy-start(bf16[2,8,8,3840]{3,2,1,0:T(8,128)(2,1)} %copy-done.22) | copy-start | bytes 2949124
  98.0 13.8 %copy-start.25 = (bf16[2,8,8,3712]{3,2,1,0:T(8,128)(2,1)S(1)}, bf16[2,8,8,3712]{3,2,1,0:T(8,128)(2,1)}, u32[]{:S(2)}) copy-start(bf16[2,8,8,3712]{3,2,1,0:T(8,128)(2,1)} %copy-done.24) | copy-start | bytes 2850820
  98.0 13.8 %copy-start.27 = (bf16[2,8,8,3712]{3,2,1,0:T(8,128)(2,1)S(1)}, bf16[2,8,8,3712]{3,2,1,0:T(8,128)(2,1)}, u32[]{:S(2)}) copy-start(bf16[2,8,8,3712]{3,2,1,0:T(8,128)(2,1)} %copy-done.26) | copy-start | bytes 2850820
  98.0 13.8 %copy-start.29 = (bf16[2,8,8,3712]{3,2,1,0:T(8,128)(2,1)S(1)}, bf16[2,8,8,3712]{3,2,1,0:T(8,128)(2,1)}, u32[]{:S(2)}) copy-start(bf16[2,8,8,3712]{3,2,1,0:T(8,128)(2,1)} %copy-done.28) | copy-start | bytes 2850820
  98.0 13.8 %copy-start.33 = (bf16[2,8,8,3840]{3,2,1,0:T(8,128)(2,1)S(1)}, bf16[2,8,8,3840]{3,2,1,0:T(8,128)(2,1)}, u32[]{:S(2)}) copy-start(bf16[2,8,8,3840]{3,2,1,0:T(8,128)(2,1)} %copy-done.32) | copy-start | bytes 2949124
  98.0 13.8 %copy-start.35 = (bf16[2,8,8,3840]{3,2,1,0:T(8,128)(2,1)S(1)}, bf16[2,8,8,3840]{3,2,1,0:T(8,128)(2,1)}, u32[]{:S(2)}) copy-start(bf16[2,8,8,3840]{3,2,1,0:T(8,128)(2,1)} %copy-done.34) | copy-start | bytes 2949124
  98.0 13.8 %copy-start.37 = (bf16[2,8,8,3712]{3,2,1,0:T(8,128)(2,1)S(1)}, bf16[2,8,8,3712]{3,2,1,0:T(8,128)(2,1)}, u32[]{:S(2)}) copy-start(bf16[2,8,8,3712]{3,2,1,0:T(8,128)(2,1)} %copy-done.36) | copy-start | bytes 2850820
  111.9 1.2 copy-start.3
  125.5 1.2 copy-start.5
  142.3 1.3 collective-permute-start.20
  (13 other events, 13.0 us)

commit v4 on v3

v4 whole, which is shorter than its diff:
```python
import functools
import math

import jax
import jax.numpy as jnp
from jax import lax
from jax.experimental import pallas as pl
from jax.experimental.pallas import tpu as pltpu
from jax.sharding import PartitionSpec as P

D = 8192
FF = 14336
BLK = 128
NVAL = 4
TOK = 512
VAL = 512
AXES = ("dp", "seq")
HA = FF // 2
HG = D // 2
C1 = 3840
C2A = HA - C1
C2G = 512
C2 = C2A + C2G
C3G = HG - C2G
IDW = 128
C3 = C3G + IDW
MASKS = ((1, 3), (3, 1))


def coords(i):
    dp, seq = divmod(i, 8)
    c = dp % 2
    z = (dp // 2) % 4
    x = (seq // 4) * 2 + dp // 8
    return {"x": x, "y": seq % 4, "z": z, "c": c}


def index(p):
    dp = ((p["x"] % 2) * 4 + p["z"]) * 2 + p["c"]
    return dp * 8 + (p["x"] // 2) * 4 + p["y"]


def ring_pairs(axis, step):
    pairs = []
    for i in range(128):
        p = coords(i)
        p[axis] ^= MASKS[p["c"]][step]
        pairs.append((i, index(p)))
    return pairs


def core_pairs():
    pairs = []
    for i in range(128):
        p = coords(i)
        p["c"] ^= 1
        pairs.append((i, index(p)))
    return pairs


def swap(x):
    return lax.ppermute(x, AXES, core_pairs())


def hop(x, axis, step):
    return lax.ppermute(x, AXES, ring_pairs(axis, step))


def double(x, axis, step):
    return jnp.stack([x, hop(x, axis, step)])


def pin(x):
    return pltpu.with_memory_space_constraint(x, pltpu.VMEM)


def gate(xs, dep):
    n = len(xs)
    anyspec = pl.BlockSpec(memory_space=pl.ANY)
    return pl.pallas_call(
        lambda *refs: None,
        in_specs=[anyspec] * (n + 1),
        out_specs=[anyspec] * n,
        out_shape=[jax.ShapeDtypeStruct(x.shape, x.dtype) for x in xs],
        input_output_aliases={i: i for i in range(n)},
        cost_estimate=pl.CostEstimate(flops=0, bytes_accessed=0, transcendentals=0),
    )(*[pin(x) for x in xs], dep)


def nt(a, b):
    return lax.dot_general(a, b, (((1,), (1,)), ((), ())), preferred_element_type=jnp.float32)


def self_add(acc, ref):
    acc[0:256, :] += nt(ref[256:512, :], ref[0:256, :])
    acc[256:384, 0:128] += nt(ref[128:256, :], ref[0:128, :])
    acc[384:512, 0:128] += nt(ref[384:512, :], ref[256:384, :])


def self_first_body(x_ref, dep_ref, out_ref):
    @pl.when(pl.program_id(0) == 0)
    def _():
        out_ref[...] = jnp.zeros_like(out_ref)

    self_add(out_ref, x_ref)


def self_last_body(x_ref, first_ref, dep_ref, out_ref, acc, *, steps):
    i = pl.program_id(0)

    @pl.when(i == 0)
    def _():
        acc[...] = jnp.zeros_like(acc)

    self_add(acc, x_ref)

    @pl.when(i == steps - 1)
    def _():
        k = first_ref[...] * acc[...]
        rows = lax.broadcasted_iota(jnp.int32, (4, 4), 0)
        cols = lax.broadcasted_iota(jnp.int32, (4, 4), 1)
        out = jnp.zeros((4, 4), jnp.float32)
        spots = (
            (2, 0, 0, 0), (2, 1, 0, 128), (3, 0, 128, 0), (3, 1, 128, 128),
            (1, 0, 256, 0), (3, 2, 384, 0),
        )
        for b, c, r0, c0 in spots:
            s = jnp.sum(k[r0:r0 + 128, c0:c0 + 128])
            out = jnp.where((rows == b) & (cols == c), s, out)
        out_ref[...] = out / (float(BLK) * math.sqrt(float(FF) * float(D)))


KC = 2048


def self_call(x, dep, first=None):
    width = x.shape[1]
    half = pl.BlockSpec((512, 256), lambda i: (0, 0))
    anyspec = pl.BlockSpec(memory_space=pl.ANY)
    args = [x] + ([] if first is None else [first]) + [dep]
    body = self_first_body
    if first is not None:
        body = functools.partial(self_last_body, steps=width // KC)
    return pl.pallas_call(
        body,
        grid=(width // KC,),
        in_specs=[pl.BlockSpec((TOK, KC), lambda i: (0, i))]
        + ([] if first is None else [half]) + [anyspec],
        out_specs=half if first is None else pl.BlockSpec((4, 4), lambda i: (0, 0)),
        out_shape=jax.ShapeDtypeStruct((512, 256) if first is None else (4, 4), jnp.float32),
        scratch_shapes=[] if first is None else [pltpu.VMEM((512, 256), jnp.float32)],
        compiler_params=pltpu.CompilerParams(vmem_limit_bytes=16 << 20),
        cost_estimate=pl.CostEstimate(
            flops=2 * 512 * 256 * width, bytes_accessed=2 * TOK * width, transcendentals=0
        ),
    )(*args)


RUNS = ("y", "z", "x")
STEP5 = ("z", "x", "y")
STEP6 = ("x", "y", "z")
WEIGHT = {"x": 4, "y": 2, "z": 1}


def place(part, k, s4):
    n = s4 * WEIGHT[RUNS[part]]
    if k in (1, 3):
        n += WEIGHT[STEP5[part]]
    if k in (2, 3):
        n += WEIGHT[STEP6[part]]
    return n


WIDTHS = (C1, C2, C3)
STARTS = (0, C1, C1 + C2)
ALLW = C1 + C2 + C3
ORDER = tuple((half, part) for half in range(2) for part in range(3))
SEGMENTS = ((("a", 0, C1),), (("a", 0, C2A), ("g", C2A, C2G)), (("g", 0, C3G),))


def train_copies(acts, grads, o, part, dst):
    a0 = pl.multiple_of(o * HA, 128)
    g0 = pl.multiple_of(o * HG, 128)
    if part == 0:
        return [(acts.at[:, pl.ds(a0, C1)], dst.at[:, pl.ds(0, C1)])]
    if part == 1:
        return [
            (acts.at[:, pl.ds(a0 + C1, C2A)], dst.at[:, pl.ds(0, C2A)]),
            (grads.at[:, pl.ds(g0, C2G)], dst.at[:, pl.ds(C2A, C2G)]),
        ]
    return [(grads.at[:, pl.ds(g0 + C2G, C3G)], dst.at[:, pl.ds(0, C3G)])]


SLOTS = 3


class Train:
    def __init__(self, core_ref, acts, grads, order, hbuf, sems):
        c = core_ref[0]
        self.hbuf, self.todo = hbuf, []
        for n, (half, part) in enumerate(order):
            slot = n % SLOTS
            moves = train_copies(acts, grads, c if half == 0 else 1 - c, part, hbuf.at[slot])
            self.todo.append(
                [pltpu.make_async_copy(a, b, sems.at[slot, i]) for i, (a, b) in enumerate(moves)]
            )
        for n in range(min(SLOTS, len(order))):
            self.start(n)

    def start(self, n):
        if n < len(self.todo):
            for cp in self.todo[n]:
                cp.start()

    def wait(self, n):
        for cp in self.todo[n]:
            cp.wait()

    def get(self, n, at, w):
        return self.hbuf[n % SLOTS, :, at:at + w]


def cross_rows(part, ks, pieces, train, n, ca, cg):
    train.wait(n)
    for name, at, w in SEGMENTS[part]:
        acc = ca if name == "a" else cg
        rows = [p[:, :, :, at:at + w].reshape(128, w) for p in pieces]
        rows = rows[0] if len(rows) == 1 else jnp.concatenate(rows, axis=0)
        x = nt(rows, train.get(n, at, w))
        for i, k in enumerate(ks):
            for s4 in range(2):
                r = i * 128 + s4 * 64
                acc[place(part, k, s4)] += x[r:r + 64].reshape(8, 8, TOK)
    train.start(n + SLOTS)


def val_rows(core_ref, blocks, name, seen, ka, kg):
    even = jnp.concatenate([x[:32] for x in blocks], axis=0)
    late = jnp.concatenate(blocks[4:], axis=0)
    y = nt(jnp.where(core_ref[0] == 0, even, late), jnp.concatenate(blocks, axis=0))
    acc = ka if name == "a" else kg
    if name in seen:
        acc[...] += y
    else:
        acc[...] = y
        seen.add(name)


def early_body(core_ref, acts, grads, dep_ref, *refs):
    own = [refs[p * 3:p * 3 + 3] for p in range(3)]
    ca, cg, tok, hbuf, sems = refs[9:]
    train = Train(core_ref, acts, grads, ORDER[:3], hbuf, sems)
    tok[...] = jnp.zeros_like(tok)
    ca[...] = jnp.zeros_like(ca)
    cg[...] = jnp.zeros_like(cg)
    for part in range(3):
        cross_rows(part, (0, 1, 2), own[part], train, part, ca, cg)


def late_own_body(core_ref, acts, grads, *refs):
    pieces = [refs[p * 4:p * 4 + 4] for p in range(3)]
    ca, cg, ka, kg, ids, hbuf, sems, pbuf, psems = refs[12:]

    def moves(part):
        b = part % 2
        return [
            pltpu.make_async_copy(
                pieces[part][k], pbuf.at[b, k, :, :, :, pl.ds(0, WIDTHS[part])], psems.at[b, k]
            )
            for k in range(4)
        ]

    for part in range(2):
        for cp in moves(part):
            cp.start()
    train = Train(core_ref, acts, grads, ORDER[:3], hbuf, sems)
    ca[...] = jnp.zeros_like(ca)
    cg[...] = jnp.zeros_like(cg)
    seen = set()
    for part in range(3):
        b = part % 2
        for cp in moves(part):
            cp.wait()

        def blocks(at, w):
            out = [None] * 8
            for k in range(4):
                for s4 in range(2):
                    out[place(part, k, s4)] = pbuf[b, k, s4, :, :, at:at + w].reshape(64, w)
            return out

        for name, at, w in SEGMENTS[part]:
            val_rows(core_ref, blocks(at, w), name, seen, ka, kg)
        if part == 2:
            for at, x in enumerate(blocks(C3G, IDW)):
                ids[at * 64:at * 64 + 64, :] = x.astype(jnp.float32)
        cross_rows(part, (3,), [pbuf.at[b, 3]], train, part, ca, cg)
        if part == 0:
            for cp in moves(2):
                cp.start()


def late_other_body(core_ref, acts, grads, o0, o1, o2, o3, a1, g1, a3, g3, k1, k2, ids,
                    raw_ref, norm_ref, hbuf, sems, vbuf, ca, cg, ka, kg, vsems):
    c = core_ref[0]

    def moves(part):
        b = part % 2
        cols = pl.ds(STARTS[part], WIDTHS[part])
        return [
            pltpu.make_async_copy(
                o.at[s4, :, :, cols],
                vbuf.at[b, :, place(part, k, s4), :, pl.ds(0, WIDTHS[part])],
                vsems.at[b, k, s4],
            )
            for k, o in enumerate((o0, o1, o2, o3)) for s4 in range(2)
        ]

    for part in range(2):
        for cp in moves(part):
            cp.start()
    train = Train(core_ref, acts, grads, ORDER[3:], hbuf, sems)
    ca[...] = (a1[...] + a3[...]).reshape(VAL, TOK)
    cg[...] = (g1[...] + g3[...]).reshape(VAL, TOK)
    ka[...] = k1[...]
    kg[...] = k2[...]
    seen = {"a", "g"}
    for part in range(3):
        for cp in moves(part):
            cp.wait()
        for name, at, w in SEGMENTS[part]:
            blocks = [vbuf[part % 2, b, :, :, at:at + w].reshape(64, w) for b in range(8)]
            val_rows(core_ref, blocks, name, seen, ka, kg)
        train.wait(part)
        for name, at, w in SEGMENTS[part]:
            acc = ca if name == "a" else cg
            rows = vbuf[part % 2, :, :, :, at:at + w].reshape(VAL, w)
            acc[...] += nt(rows, train.get(part, at, w))
        if part == 0:
            for cp in moves(2):
                cp.start()

    cross = ca[...] * cg[...]
    kern = ka[...] * kg[...]
    all_ids = ids[...]
    row_ids = jnp.transpose(all_ids)[0:1, :]
    even = jnp.concatenate([all_ids[b * 64:b * 64 + 32] for b in range(8)], axis=0)
    half_ids = jnp.where(c == 0, even, all_ids[256:512])
    for v in range(NVAL):
        keep = jnp.where(all_ids == float(v), 1.0, 0.0)
        keep = jnp.concatenate([keep] * 4, axis=1)
        raw_ref[v:v + 1, :] = jnp.sum(cross * keep, axis=0, keepdims=True)
        keep = jnp.where(half_ids == float(v), 1.0, 0.0)
        keep = jnp.concatenate([keep] * 4, axis=1)
        part = jnp.sum(kern * keep, axis=0, keepdims=True)
        part = jnp.sum(jnp.where(row_ids == float(v), part, 0.0))
        norm_ref[v:v + 1, :] = jnp.full((1, 128), part, jnp.float32)


ACC = jax.ShapeDtypeStruct((8, 8, 8, TOK), jnp.float32)
KERN = jax.ShapeDtypeStruct((VAL // 2, VAL), jnp.float32)


def local_call(body, core, acts, grads, args, outs, flops, scratch=(), anys=(), mib=28):
    vmem = pl.BlockSpec(memory_space=pltpu.VMEM)
    anyspec = pl.BlockSpec(memory_space=pl.ANY)
    return pl.pallas_call(
        body,
        in_specs=[pl.BlockSpec(memory_space=pltpu.SMEM)] + [anyspec] * 2
        + [anyspec if i in anys else vmem for i in range(len(args))],
        out_specs=[vmem] * len(outs),
        out_shape=outs,
        scratch_shapes=[
            pltpu.VMEM((SLOTS, TOK, C1), jnp.bfloat16),
            pltpu.SemaphoreType.DMA((SLOTS, 2)),
        ] + list(scratch),
        compiler_params=pltpu.CompilerParams(vmem_limit_bytes=mib << 20),
        cost_estimate=pl.CostEstimate(
            flops=flops, bytes_accessed=TOK * (FF + D), transcendentals=0
        ),
    )(core, acts, grads, *[x if i in anys else pin(x) for i, x in enumerate(args)])


def shards(hidden_acts, out_grads, val_acts, val_grads, val_ids):
    hidden_acts = pltpu.with_memory_space_constraint(hidden_acts, pltpu.HBM)
    out_grads = pltpu.with_memory_space_constraint(out_grads, pltpu.HBM)
    core = lax.axis_index("dp") % 2
    first = core == 0
    idcol = jnp.broadcast_to(val_ids[:, None].astype(jnp.bfloat16), (4, IDW))
    halves = [
        jnp.concatenate(
            [val_acts[:, h * HA:(h + 1) * HA], val_grads[:, h * HG:(h + 1) * HG], idcol], axis=1
        )
        for h in range(2)
    ]
    keep = jnp.where(first, halves[0], halves[1])
    got = swap(jnp.where(first, halves[1], halves[0]))
    rows = jnp.concatenate([jnp.where(first, keep, got), jnp.where(first, got, keep)], axis=0)

    rows = double(rows, "z", 0)
    sg = self_call(out_grads, rows)
    (rows,) = gate([double(rows, "y", 0)], sg)
    block_gram = self_call(hidden_acts, rows, sg)
    (rows,) = gate([double(rows, "x", 0)], block_gram)
    rows = rows.reshape(8, 8, ALLW)
    piece = [[rows[..., s:s + w]] for s, w in zip(STARTS, WIDTHS)]
    piece = [[double(piece[j][0], RUNS[j], 1)] for j in range(3)]
    for j in range(3):
        piece[j].append(hop(piece[j][0], STEP5[j], 1))
    for j in range(3):
        piece[j].append(hop(piece[j][0], STEP6[j], 1))
    for j in range(3):
        piece[j].append(hop(piece[j][1], STEP6[j], 1))
    joined = [jnp.concatenate([piece[j][k] for j in range(3)], axis=-1) for k in range(4)]
    o0, o1 = [swap(gate([x], block_gram)[0]) for x in joined[:2]]
    call = functools.partial(
        local_call, core=core.reshape(1).astype(jnp.int32), acts=hidden_acts, grads=out_grads
    )
    unit = 2 * 512 * (HA + HG)
    a1, g1, tok = call(
        early_body,
        args=[block_gram] + [piece[j][k] for j in range(3) for k in range(3)],
        outs=[ACC, ACC, jax.ShapeDtypeStruct((8, 128), jnp.float32)],
        flops=384 * unit, anys=(0,),
    )
    o2, o3 = [swap(gate([x], tok)[0]) for x in joined[2:]]
    ids = jax.ShapeDtypeStruct((VAL, IDW), jnp.float32)
    a3, g3, k1, k2, ids = call(
        late_own_body, args=[piece[j][k] for j in range(3) for k in range(4)],
        outs=[ACC, ACC, KERN, KERN, ids], flops=384 * unit, anys=range(12),
        scratch=[
            pltpu.VMEM((2, 4, 2, 8, 8, C1), jnp.bfloat16),
            pltpu.SemaphoreType.DMA((2, 4)),
        ],
        mib=30,
    )
    raw, norm = call(
        late_other_body, args=[o0, o1, o2, o3, a1, g1, a3, g3, k1, k2, ids],
        outs=[
            jax.ShapeDtypeStruct((NVAL, TOK), jnp.float32),
            jax.ShapeDtypeStruct((NVAL, 128), jnp.float32),
        ],
        scratch=[
            pltpu.VMEM((2, 8, 8, 8, C1), jnp.bfloat16),
            pltpu.VMEM((VAL, TOK), jnp.float32),
            pltpu.VMEM((VAL, TOK), jnp.float32),
            pltpu.VMEM((VAL // 2, VAL), jnp.float32),
            pltpu.VMEM((VAL // 2, VAL), jnp.float32),
            pltpu.SemaphoreType.DMA((2, 4, 2)),
        ],
        flops=768 * unit, mib=34,
    )
    norm = norm + swap(norm)
    token_scores = raw * lax.rsqrt(norm[:, :1] + 1e-06)
    return (token_scores, block_gram)


def solution(mesh):
    return jax.shard_map(
        shards,
        mesh=mesh,
        in_specs=(
            P(AXES, None),
            P(AXES, None),
            P(AXES, None),
            P(AXES, None),
            P(AXES),
        ),
        out_specs=(P(None, AXES), P(AXES, None)),
        check_vma=False,
    )
```

time: 145 us -> 130 us (0.90)
  local copies, waits for them, and re-layouts: 18.2 us -> 5.31 us
  other arithmetic: 7.87 us -> 16 us
  starting transfers between devices: 38.2 us -> 31.8 us
  Pallas kernels: 58.8 us -> 53.8 us
  waiting for transfers between devices: 20.1 us -> 22.1 us
    unnamed x80 -> x16, local copies, waits for them, and re-layouts: 16.3 us -> 3.35 us
    ppermute x6, starting transfers between devices: 24.6 us -> 18.6 us  [swap(): return lax.ppermute(x, AXES, core_pairs())]
    concatenate x4, other arithmetic: 5.53 us -> 10.8 us  [shards(): jnp.concatenate([piece[j][k] for j in range(3)], axis=-1)]
    pallas_call x4 -> x3, Pallas kernels: 43 us -> 38 us  [local_call(): pl.pallas_call(body, in_specs=[pl.BlockSpec(memory_space=pltpu.SMEM)] + [...]
    ppermute x15, waiting for transfers between devices: 17.3 us -> 20.4 us  [hop(): return lax.ppermute(x, AXES, ring_pairs(axis, step))]
    another operation x7, other arithmetic: 0.68 us -> 3.56 us  [double(): return jnp.stack([x, hop(x, axis, step)])]
  transfers between devices with their start and end apart: 21 -> 21, of which waited for: 8 -> 7; matrix products, arithmetic and copies ran while one was open for 4% -> 11% of each run, Pallas kernels for 31% -> 29%
where the time goes in v4:
time: 130 us
  Pallas kernels  53.8 us (41%)
  starting transfers between devices  31.8 us (24%)
  waiting for transfers between devices  22.1 us (17%)
  other arithmetic  16 us (12%)
  local copies, waits for them, and re-layouts  5.31 us (4%)
    pallas_call x3, Pallas kernels, local_call(): pl.pallas_call(body, in_specs=[pl.BlockSpec(memory_space=pltpu.SMEM)] + [...  38 us
    ppermute x15, waiting for transfers between devices, hop(): return lax.ppermute(x, AXES, ring_pairs(axis, step))  20.4 us
    ppermute x6, starting transfers between devices, swap(): return lax.ppermute(x, AXES, core_pairs())  18.6 us
    pallas_call x2, Pallas kernels, self_call(): pl.pallas_call(body, grid=(width // KC,), in_specs=[pl.BlockSpec((TOK, KC...  15.8 us
    ppermute x15, starting transfers between devices, hop(): return lax.ppermute(x, AXES, ring_pairs(axis, step))  13.3 us
    concatenate x4, other arithmetic, shards(): jnp.concatenate([piece[j][k] for j in range(3)], axis=-1)  10.8 us
    another operation x7, other arithmetic, double(): return jnp.stack([x, hop(x, axis, step)])  3.56 us
    unnamed x16, local copies, waits for them, and re-layouts  3.35 us
  transfers between devices with their start and end apart: 21, of which 7 were waited for; matrix products, arithmetic and copies ran while one was open for 11% of the time, Pallas kernels for 29%

profile of v4, /device:TPU:1, one launch (start us, length us, event | category | flops | bytes accessed | tf_op | source)
XLA Modules:
  0.0 130.0 jit_solution(15528061229685241044)
XLA Ops:
  0.6 0.7 convert_element_type.4
  1.3 0.8 fusion.3
  2.1 0.9 fusion.2
  3.2 1.5 %collective-permute-start = (bf16[4,11392]{1,0:T(4,128)(2,1)S(1)}, bf16[4,11392]{1,0:T(4,128)(2,1)S(1)}, u32[]{:S(2)}, u32[]{:S(2)}) collective-permute-start(bf16[4,11392]{1,0:T(4,128)(2,1)S(1)} %broadcast_select_fusion.2), channel_id=1, source_target_pairs={{0,8},{1,9},{2,10},{3,11},{4,12},{5,13},{6,14},{7,15},{8,0},{9,1},... | collective-permute-start | bytes 273416 | tf_op jit(solution)/shard_map/ppermute | solution.py:62
  4.7 0.9 collective-permute-done
  5.6 0.1 broadcast_select_fusion.1
  5.7 0.1 fusion
  5.8 3.9 %collective-permute-start.1 = (bf16[8,11392]{1,0:T(8,128)(2,1)S(1)}, bf16[8,11392]{1,0:T(8,128)(2,1)S(1)}, u32[]{:S(2)}, u32[]{:S(2)}) collective-permute-start(bf16[8,11392]{1,0:T(8,128)(2,1)S(1)} %get-tuple-element.33), channel_id=1, source_target_pairs={{0,16},{1,17},{2,18},{3,19},{4,20},{5,21},{6,22},{7,23},{8,56},{9,... | collective-permute-start | bytes 546824 | tf_op jit(solution)/shard_map/ppermute | solution.py:66
  9.7 2.9 %collective-permute-done.1 = bf16[8,11392]{1,0:T(8,128)(2,1)S(1)} collective-permute-done((bf16[8,11392]{1,0:T(8,128)(2,1)S(1)}, bf16[8,11392]{1,0:T(8,128)(2,1)S(1)}, u32[]{:S(2)}, u32[]{:S(2)}) %collective-permute-start.1) | collective-permute-done | bytes 182304 | tf_op jit(solution)/shard_map/ppermute | solution.py:66
  12.7 2.8 %collective-permute-start.2 = (bf16[2,8,11392]{2,1,0:T(8,128)(2,1)S(1)}, bf16[2,8,11392]{2,1,0:T(8,128)(2,1)S(1)}, u32[]{:S(2)}, u32[]{:S(2)}) collective-permute-start(bf16[2,8,11392]{2,1,0:T(8,128)(2,1)S(1)} %get-tuple-element.29.dep_ref), channel_id=1, source_target_pairs={{0,1},{1,0},{2,3},{3,2},{4,5},{5,4},{6,7},{7,6},{8,11},{9,10},{10,... | collective-permute-start | bytes 1093640 | tf_op jit(solution)/shard_map/ppermute | solution.py:66
  15.5 5.6 %shard_map.68.refs_1_.first_ref = f32[512,256]{1,0:T(8,128)S(1)} custom-call(bf16[512,8192]{1,0:T(8,128)(2,1)} %grads.5, bf16[2,8,11392]{2,1,0:T(8,128)(2,1)S(1)} %get-tuple-element.29.dep_ref), custom_call_target="tpu_custom_call" | custom-call | flops 2147483648 | bytes 8388608 | tf_op jit(solution)/shard_map/pallas_call | solution.py:144
  21.1 0.8 copy-done
  21.9 0.1 pad_maximum_fusion.7.refs_0_
  22.0 2.6 %collective-permute-start.3 = (bf16[2,2,8,11392]{3,2,1,0:T(8,128)(2,1)S(1)}, bf16[2,2,8,11392]{3,2,1,0:T(8,128)(2,1)S(1)}, u32[]{:S(2)}, u32[]{:S(2)}) collective-permute-start(bf16[2,2,8,11392]{3,2,1,0:T(8,128)(2,1)S(1)} %shard_map.69.dep_ref), channel_id=1, source_target_pairs={{0,64},{1,65},{2,66},{3,67},{4,68},{5,69},{6,70},{7,71},{8,76},{9,... | collective-permute-start | bytes 2187272 | tf_op jit(solution)/shard_map/ppermute | solution.py:66
  24.6 10.2 %shard_map.70.refs_1_.dep_ref = f32[4,4]{1,0:T(4,128)} custom-call(bf16[512,14336]{1,0:T(8,128)(2,1)} %acts.5, f32[512,256]{1,0:T(8,128)S(1)} %copy-done.1, bf16[2,2,8,11392]{3,2,1,0:T(8,128)(2,1)S(1)} %shard_map.69.dep_ref), custom_call_target="tpu_custom_call" | custom-call | flops 3758096384 | bytes 14680064 | tf_op jit(solution)/shard_map/pallas_call | solution.py:144
  34.8 0.2 pad_maximum_fusion.3.refs_0_
  35.1 0.1 collective-permute-start.6
  35.1 0.1 slice_bitcast_fusion.2
  35.3 0.1 collective-permute-start.5
  35.4 0.1 collective-permute-start.4
  35.5 7.5 %collective-permute-done.6 = bf16[8,8,3712]{2,1,0:T(8,128)(2,1)S(1)} collective-permute-done((bf16[8,8,3712]{2,1,0:T(8,128)(2,1)S(1)}, bf16[8,8,3712]{2,1,0:T(8,128)(2,1)S(1)}, u32[]{:S(2)}, u32[]{:S(2)}) %collective-permute-start.6) | collective-permute-done | bytes 475168 | tf_op jit(solution)/shard_map/ppermute | solution.py:66
  42.9 1.0 pad_maximum_fusion.6.refs_6_.refs_8_
  44.0 1.1 pad_maximum_fusion.5.refs_3_.refs_4_
  45.0 1.5 %collective-permute-start.13 = (bf16[2,8,8,3840]{3,2,1,0:T(8,128)(2,1)}, bf16[2,8,8,3840]{3,2,1,0:T(8,128)(2,1)}, u32[]{:S(2)}, u32[]{:S(2)}) collective-permute-start(bf16[2,8,8,3840]{3,2,1,0:T(8,128)(2,1)} %pad_maximum_fusion.5.refs_3_.refs_4_), channel_id=1, source_target_pairs={{0,3},{1,2},{2,1},{3,0},{4,7},{5,6},{6,5},{7,4},{8,9},{9,8},{10,11... | collective-permute-start | bytes 2949128 | tf_op jit(solution)/shard_map/ppermute | solution.py:66
  46.5 1.1 pad_maximum_fusion.4.refs_0_
  47.6 1.5 %collective-permute-start.8 = (bf16[2,8,8,3840]{3,2,1,0:T(8,128)(2,1)}, bf16[2,8,8,3840]{3,2,1,0:T(8,128)(2,1)}, u32[]{:S(2)}, u32[]{:S(2)}) collective-permute-start(bf16[2,8,8,3840]{3,2,1,0:T(8,128)(2,1)} %pad_maximum_fusion.4.refs_0_), channel_id=1, source_target_pairs={{0,48},{1,49},{2,50},{3,51},{4,52},{5,53},{6,54},{7,55},{8,24},{9,... | collective-permute-start | bytes 2949128 | tf_op jit(solution)/shard_map/ppermute | solution.py:66
  49.1 1.7 %maximum_maximum_fusion.refs_0_ = bf16[2,8,8,11392]{3,2,1,0:T(8,128)(2,1)} fusion(bf16[1,8,8,3712]{3,2,1,0:T(8,128)(2,1)S(1)} %bitcast.27, bf16[1,8,8,3712]{3,2,1,0:T(8,128)(2,1)S(1)} %get-tuple-element.26, bf16[1,8,8,3840]{3,2,1,0:T(8,128)(2,1)S(1)} %bitcast.23, bf16[1,8,8,3840]{3,2,1,0:T(8,128)(2,1)S(1)} %get-tuple-element.23, ...), kind=kLoop, calls=%fused_computation | loop fusion | flops 17498112 | bytes 5832704 | tf_op jit(solution)/shard_map/concatenate | solution.py:414
  50.7 6.5 %collective-permute-done.10.refs_7_.refs_9_ = bf16[2,8,8,3712]{3,2,1,0:T(8,128)(2,1)} collective-permute-done((bf16[2,8,8,3712]{3,2,1,0:T(8,128)(2,1)}, bf16[2,8,8,3712]{3,2,1,0:T(8,128)(2,1)}, u32[]{:S(2)}, u32[]{:S(2)}) %collective-permute-start.10) | collective-permute-done | bytes 950304 | tf_op jit(solution)/shard_map/ppermute | solution.py:66
  57.2 2.9 %collective-permute-done.9.refs_4_.refs_5_ = bf16[2,8,8,3840]{3,2,1,0:T(8,128)(2,1)} collective-permute-done((bf16[2,8,8,3840]{3,2,1,0:T(8,128)(2,1)}, bf16[2,8,8,3840]{3,2,1,0:T(8,128)(2,1)}, u32[]{:S(2)}, u32[]{:S(2)}) %collective-permute-start.9) | collective-permute-done | bytes 983072 | tf_op jit(solution)/shard_map/ppermute | solution.py:66
  60.1 7.0 %collective-permute-start.7 = (bf16[2,8,8,11392]{3,2,1,0:T(8,128)(2,1)}, bf16[2,8,8,11392]{3,2,1,0:T(8,128)(2,1)}, u32[]{:S(2)}, u32[]{:S(2)}) collective-permute-start(bf16[2,8,8,11392]{3,2,1,0:T(8,128)(2,1)} %shard_map.72), channel_id=1, source_target_pairs={{0,8},{1,9},{2,10},{3,11},{4,12},{5,13},{6,14},{7,15},{8,0},{9,1},... | collective-permute-start | bytes 8749064 | tf_op jit(solution)/shard_map/ppermute | solution.py:62
  67.1 0.6 collective-permute-done.8.refs_1_
  67.7 3.6 %pad_maximum_fusion.refs_0_ = bf16[2,8,8,11392]{3,2,1,0:T(8,128)(2,1)} fusion(bf16[2,8,8,3712]{3,2,1,0:T(8,128)(2,1)} %collective-permute-done.10.refs_7_.refs_9_, bf16[2,8,8,3840]{3,2,1,0:T(8,128)(2,1)} %collective-permute-done.9.refs_4_.refs_5_, bf16[2,8,8,3840]{3,2,1,0:T(8,128)(2,1)} %collective-permute-done.8.refs_1_), kind=kLoop, calls=%fused_computation.1 | loop fusion | flops 8749056 | bytes 5832704 | tf_op jit(solution)/shard_map/concatenate | solution.py:414
  71.3 5.2 %collective-permute-start.11 = (bf16[2,8,8,11392]{3,2,1,0:T(8,128)(2,1)}, bf16[2,8,8,11392]{3,2,1,0:T(8,128)(2,1)}, u32[]{:S(2)}, u32[]{:S(2)}) collective-permute-start(bf16[2,8,8,11392]{3,2,1,0:T(8,128)(2,1)} %shard_map.73), channel_id=1, source_target_pairs={{0,8},{1,9},{2,10},{3,11},{4,12},{5,13},{6,14},{7,15},{8,0},{9,1},... | collective-permute-start | bytes 8749064 | tf_op jit(solution)/shard_map/ppermute | solution.py:62
  76.5 0.7 collective-permute-start.17
  77.3 10.9 %shard_map.74 = (f32[8,8,8,512]{3,2,1,0:T(8,128)S(1)}, f32[8,8,8,512]{3,2,1,0:T(8,128)S(1)}, f32[8,128]{1,0:T(8,128)S(1)}) custom-call(s32[1]{0:T(128)} %bitcast.core_ref, bf16[512,14336]{1,0:T(8,128)(2,1)} %acts.5, bf16[512,8192]{1,0:T(8,128)(2,1)} %grads.5, f32[4,4]{1,0:T(4,128)S(1)} %copy-done.6, bf16[2,8,8,3840]{3,2,1,0:T(8,128)(2,1)} %pad_maximum_fusion.4.refs_0_, ...), custom_call_target="tpu_custom_call" | custom-call | flops 4429185024 | bytes 11534336 | tf_op jit(solution)/shard_map/pallas_call | solution.py:367
  88.2 1.0 copy-done.2
  89.2 1.0 copy-done.4
  90.1 0.6 copy-done.7
  90.7 3.6 %pad_maximum_fusion.1.refs_0_ = bf16[2,8,8,11392]{3,2,1,0:T(8,128)(2,1)} fusion(bf16[2,8,8,3712]{3,2,1,0:T(8,128)(2,1)} %collective-permute-done.14.refs_8_.refs_10_, bf16[2,8,8,3840]{3,2,1,0:T(8,128)(2,1)} %collective-permute-done.13.refs_5_.refs_6_, bf16[2,8,8,3840]{3,2,1,0:T(8,128)(2,1)} %collective-permute-done.12.refs_2_), kind=kLoop, calls=%fused_computation.2 | loop fusion | flops 8749056 | bytes 5832704 | tf_op jit(solution)/shard_map/concatenate | solution.py:414
  94.3 4.2 %collective-permute-start.15 = (bf16[2,8,8,11392]{3,2,1,0:T(8,128)(2,1)}, bf16[2,8,8,11392]{3,2,1,0:T(8,128)(2,1)}, u32[]{:S(2)}, u32[]{:S(2)}) collective-permute-start(bf16[2,8,8,11392]{3,2,1,0:T(8,128)(2,1)} %shard_map.75), channel_id=1, source_target_pairs={{0,8},{1,9},{2,10},{3,11},{4,12},{5,13},{6,14},{7,15},{8,0},{9,1},... | collective-permute-start | bytes 8749064 | tf_op jit(solution)/shard_map/ppermute | solution.py:62
  98.5 2.0 %pad_maximum_fusion.2.refs_0_ = bf16[2,8,8,11392]{3,2,1,0:T(8,128)(2,1)S(1)} fusion(bf16[2,8,8,3712]{3,2,1,0:T(8,128)(2,1)} %collective-permute-done.18.refs_11_, bf16[2,8,8,3840]{3,2,1,0:T(8,128)(2,1)} %collective-permute-done.17.refs_7_, bf16[2,8,8,3840]{3,2,1,0:T(8,128)(2,1)} %collective-permute-done.16.refs_3_), kind=kLoop, calls=%fused_computation.3 | loop fusion | flops 8749056 | bytes 5832704 | tf_op jit(solution)/shard_map/concatenate | solution.py:414
  100.6 0.1 collective-permute-start.19
  100.7 11.0 %shard_map.77 = (f32[8,8,8,512]{3,2,1,0:T(8,128)S(1)}, f32[8,8,8,512]{3,2,1,0:T(8,128)S(1)}, f32[256,512]{1,0:T(8,128)S(1)}, f32[256,512]{1,0:T(8,128)S(1)}, f32[512,128]{1,0:T(8,128)S(1)}) custom-call(s32[1]{0:T(128)} %bitcast.core_ref, bf16[512,14336]{1,0:T(8,128)(2,1)} %acts.5, bf16[512,8192]{1,0:T(8,128)(2,1)} %grads.5, ...), custom_call_target="tpu_custom_call" | custom-call | flops 4429185024 | bytes 11534336 | tf_op jit(solution)/shard_map/pallas_call | solution.py:367
  111.7 16.1 %shard_map.78 = (f32[4,512]{1,0:T(4,128)S(1)}, f32[4,128]{1,0:T(4,128)S(1)}) custom-call(s32[1]{0:T(128)} %bitcast.core_ref, bf16[512,14336]{1,0:T(8,128)(2,1)} %acts.5, bf16[512,8192]{1,0:T(8,128)(2,1)} %grads.5, bf16[2,8,8,11392]{3,2,1,0:T(8,128)(2,1)} %collective-permute-done.7.o0, bf16[2,8,8,11392]{3,2,1,0:T(8,128)(2,1)} %collective-permute-done.11.o1, ...), custom_call_target="tpu_custom_call" | custom-call | flops 8858370048 | bytes 11534336 | tf_op jit(solution)/shard_map/pallas_call | solution.py:367
  127.8 0.5 collective-permute-start.20
  128.3 0.8 collective-permute-done.20
  129.2 0.1 rsqrt_reduce_fusion
  129.3 0.7 broadcast_multiply_fusion
  (43 shorter events, 0.4 us)
Async XLA Ops:
  3.2 2.4 %collective-permute-start = (bf16[4,11392]{1,0:T(4,128)(2,1)S(1)}, bf16[4,11392]{1,0:T(4,128)(2,1)S(1)}, u32[]{:S(2)}, u32[]{:S(2)}) collective-permute-start(bf16[4,11392]{1,0:T(4,128)(2,1)S(1)} %broadcast_select_fusion.2), channel_id=1, source_target_pairs={{0,8},{1,9},{2,10},{3,11},{4,12},{5,13},{6,14},{7,15},{8,0},{9,1},... | collective-permute-start | bytes 273416 | tf_op jit(solution)/shard_map/ppermute | solution.py:62
  5.8 6.8 %collective-permute-start.1 = (bf16[8,11392]{1,0:T(8,128)(2,1)S(1)}, bf16[8,11392]{1,0:T(8,128)(2,1)S(1)}, u32[]{:S(2)}, u32[]{:S(2)}) collective-permute-start(bf16[8,11392]{1,0:T(8,128)(2,1)S(1)} %get-tuple-element.33), channel_id=1, source_target_pairs={{0,16},{1,17},{2,18},{3,19},{4,20},{5,21},{6,22},{7,23},{8,56},{9,... | collective-permute-start | bytes 546824 | tf_op jit(solution)/shard_map/ppermute | solution.py:66
  12.7 9.2 %collective-permute-start.2 = (bf16[2,8,11392]{2,1,0:T(8,128)(2,1)S(1)}, bf16[2,8,11392]{2,1,0:T(8,128)(2,1)S(1)}, u32[]{:S(2)}, u32[]{:S(2)}) collective-permute-start(bf16[2,8,11392]{2,1,0:T(8,128)(2,1)S(1)} %get-tuple-element.29.dep_ref), channel_id=1, source_target_pairs={{0,1},{1,0},{2,3},{3,2},{4,5},{5,4},{6,7},{7,6},{8,11},{9,10},{10,... | collective-permute-start | bytes 1093640 | tf_op jit(solution)/shard_map/ppermute | solution.py:66
  21.1 0.8 copy-start
  21.9 2.7 %copy-start.1 = (f32[512,256]{1,0:T(8,128)S(1)}, f32[512,256]{1,0:T(8,128)}, u32[]{:S(2)}) copy-start(f32[512,256]{1,0:T(8,128)} %copy-done) | copy-start | bytes 1572868
  22.0 12.8 %collective-permute-start.3 = (bf16[2,2,8,11392]{3,2,1,0:T(8,128)(2,1)S(1)}, bf16[2,2,8,11392]{3,2,1,0:T(8,128)(2,1)S(1)}, u32[]{:S(2)}, u32[]{:S(2)}) collective-permute-start(bf16[2,2,8,11392]{3,2,1,0:T(8,128)(2,1)S(1)} %shard_map.69.dep_ref), channel_id=1, source_target_pairs={{0,64},{1,65},{2,66},{3,67},{4,68},{5,69},{6,70},{7,71},{8,76},{9,... | collective-permute-start | bytes 2187272 | tf_op jit(solution)/shard_map/ppermute | solution.py:66
  35.1 7.9 %collective-permute-start.6 = (bf16[8,8,3712]{2,1,0:T(8,128)(2,1)S(1)}, bf16[8,8,3712]{2,1,0:T(8,128)(2,1)S(1)}, u32[]{:S(2)}, u32[]{:S(2)}) collective-permute-start(bf16[8,8,3712]{2,1,0:T(8,128)(2,1)S(1)} %get-tuple-element.27), channel_id=1, source_target_pairs={{0,68},{1,69},{2,70},{3,71},{4,64},{5,65},{6,66},{7,67},{8,72},{9,... | collective-permute-start | bytes 1425416 | tf_op jit(solution)/shard_map/ppermute | solution.py:66
  35.3 8.7 %collective-permute-start.5 = (bf16[8,8,3840]{2,1,0:T(8,128)(2,1)S(1)}, bf16[8,8,3840]{2,1,0:T(8,128)(2,1)S(1)}, u32[]{:S(2)}, u32[]{:S(2)}) collective-permute-start(bf16[8,8,3840]{2,1,0:T(8,128)(2,1)S(1)} %get-tuple-element.24), channel_id=1, source_target_pairs={{0,48},{1,49},{2,50},{3,51},{4,52},{5,53},{6,54},{7,55},{8,24},{9,... | collective-permute-start | bytes 1474568 | tf_op jit(solution)/shard_map/ppermute | solution.py:66
  35.4 11.1 %collective-permute-start.4 = (bf16[8,8,3840]{2,1,0:T(8,128)(2,1)S(1)}, bf16[8,8,3840]{2,1,0:T(8,128)(2,1)S(1)}, u32[]{:S(2)}, u32[]{:S(2)}) collective-permute-start(bf16[8,8,3840]{2,1,0:T(8,128)(2,1)S(1)} %get-tuple-element.25), channel_id=1, source_target_pairs={{0,3},{1,2},{2,1},{3,0},{4,7},{5,6},{6,5},{7,4},{8,9},{9,8},{10,11... | collective-permute-start | bytes 1474568 | tf_op jit(solution)/shard_map/ppermute | solution.py:66
  44.0 27.3 %collective-permute-start.14 = (bf16[2,8,8,3712]{3,2,1,0:T(8,128)(2,1)}, bf16[2,8,8,3712]{3,2,1,0:T(8,128)(2,1)}, u32[]{:S(2)}, u32[]{:S(2)}) collective-permute-start(bf16[2,8,8,3712]{3,2,1,0:T(8,128)(2,1)} %pad_maximum_fusion.6.refs_6_.refs_8_), channel_id=1, source_target_pairs={{0,48},{1,49},{2,50},{3,51},{4,52},{5,53},{6,54},{7,55},{8,24},{9,... | collective-permute-start | bytes 2850824 | tf_op jit(solution)/shard_map/ppermute | solution.py:66
  44.0 13.2 %collective-permute-start.10 = (bf16[2,8,8,3712]{3,2,1,0:T(8,128)(2,1)}, bf16[2,8,8,3712]{3,2,1,0:T(8,128)(2,1)}, u32[]{:S(2)}, u32[]{:S(2)}) collective-permute-start(bf16[2,8,8,3712]{3,2,1,0:T(8,128)(2,1)} %pad_maximum_fusion.6.refs_6_.refs_8_), channel_id=1, source_target_pairs={{0,3},{1,2},{2,1},{3,0},{4,7},{5,6},{6,5},{7,4},{8,9},{9,8},{10,11... | collective-permute-start | bytes 2850824 | tf_op jit(solution)/shard_map/ppermute | solution.py:66
  45.0 31.5 %collective-permute-start.13 = (bf16[2,8,8,3840]{3,2,1,0:T(8,128)(2,1)}, bf16[2,8,8,3840]{3,2,1,0:T(8,128)(2,1)}, u32[]{:S(2)}, u32[]{:S(2)}) collective-permute-start(bf16[2,8,8,3840]{3,2,1,0:T(8,128)(2,1)} %pad_maximum_fusion.5.refs_3_.refs_4_), channel_id=1, source_target_pairs={{0,3},{1,2},{2,1},{3,0},{4,7},{5,6},{6,5},{7,4},{8,9},{9,8},{10,11... | collective-permute-start | bytes 2949128 | tf_op jit(solution)/shard_map/ppermute | solution.py:66
  46.5 13.6 %collective-permute-start.9 = (bf16[2,8,8,3840]{3,2,1,0:T(8,128)(2,1)}, bf16[2,8,8,3840]{3,2,1,0:T(8,128)(2,1)}, u32[]{:S(2)}, u32[]{:S(2)}) collective-permute-start(bf16[2,8,8,3840]{3,2,1,0:T(8,128)(2,1)} %pad_maximum_fusion.5.refs_3_.refs_4_), channel_id=1, source_target_pairs={{0,68},{1,69},{2,70},{3,71},{4,64},{5,65},{6,66},{7,67},{8,72},{9,... | collective-permute-start | bytes 2949128 | tf_op jit(solution)/shard_map/ppermute | solution.py:66
  47.6 20.1 %collective-permute-start.8 = (bf16[2,8,8,3840]{3,2,1,0:T(8,128)(2,1)}, bf16[2,8,8,3840]{3,2,1,0:T(8,128)(2,1)}, u32[]{:S(2)}, u32[]{:S(2)}) collective-permute-start(bf16[2,8,8,3840]{3,2,1,0:T(8,128)(2,1)} %pad_maximum_fusion.4.refs_0_), channel_id=1, source_target_pairs={{0,48},{1,49},{2,50},{3,51},{4,52},{5,53},{6,54},{7,55},{8,24},{9,... | collective-permute-start | bytes 2949128 | tf_op jit(solution)/shard_map/ppermute | solution.py:66
  57.2 20.1 %collective-permute-start.12 = (bf16[2,8,8,3840]{3,2,1,0:T(8,128)(2,1)}, bf16[2,8,8,3840]{3,2,1,0:T(8,128)(2,1)}, u32[]{:S(2)}, u32[]{:S(2)}) collective-permute-start(bf16[2,8,8,3840]{3,2,1,0:T(8,128)(2,1)} %pad_maximum_fusion.4.refs_0_), channel_id=1, source_target_pairs={{0,68},{1,69},{2,70},{3,71},{4,64},{5,65},{6,66},{7,67},{8,72},{9,... | collective-permute-start | bytes 2949128 | tf_op jit(solution)/shard_map/ppermute | solution.py:66
  60.1 51.6 %collective-permute-start.7 = (bf16[2,8,8,11392]{3,2,1,0:T(8,128)(2,1)}, bf16[2,8,8,11392]{3,2,1,0:T(8,128)(2,1)}, u32[]{:S(2)}, u32[]{:S(2)}) collective-permute-start(bf16[2,8,8,11392]{3,2,1,0:T(8,128)(2,1)} %shard_map.72), channel_id=1, source_target_pairs={{0,8},{1,9},{2,10},{3,11},{4,12},{5,13},{6,14},{7,15},{8,0},{9,1},... | collective-permute-start | bytes 8749064 | tf_op jit(solution)/shard_map/ppermute | solution.py:62
  67.7 26.6 %collective-permute-start.18 = (bf16[2,8,8,3712]{3,2,1,0:T(8,128)(2,1)}, bf16[2,8,8,3712]{3,2,1,0:T(8,128)(2,1)}, u32[]{:S(2)}, u32[]{:S(2)}) collective-permute-start(bf16[2,8,8,3712]{3,2,1,0:T(8,128)(2,1)} %collective-permute-done.10.refs_7_.refs_9_), channel_id=1, source_target_pairs={{0,48},{1,49},{2,50},{3,51},{4,52},{5,53},{6,54},{7,55},{8,24},{9,... | collective-permute-start | bytes 2850824 | tf_op jit(solution)/shard_map/ppermute | solution.py:66
  71.3 6.0 %copy-start.6 = (f32[4,4]{1,0:T(4,128)S(1)}, f32[4,4]{1,0:T(4,128)}, u32[]{:S(2)}) copy-start(f32[4,4]{1,0:T(4,128)} %shard_map.70.refs_1_.dep_ref) | copy-start | bytes 196
  71.3 40.4 %collective-permute-start.11 = (bf16[2,8,8,11392]{3,2,1,0:T(8,128)(2,1)}, bf16[2,8,8,11392]{3,2,1,0:T(8,128)(2,1)}, u32[]{:S(2)}, u32[]{:S(2)}) collective-permute-start(bf16[2,8,8,11392]{3,2,1,0:T(8,128)(2,1)} %shard_map.73), channel_id=1, source_target_pairs={{0,8},{1,9},{2,10},{3,11},{4,12},{5,13},{6,14},{7,15},{8,0},{9,1},... | collective-permute-start | bytes 8749064 | tf_op jit(solution)/shard_map/ppermute | solution.py:62
  76.5 22.0 %collective-permute-start.17 = (bf16[2,8,8,3840]{3,2,1,0:T(8,128)(2,1)}, bf16[2,8,8,3840]{3,2,1,0:T(8,128)(2,1)}, u32[]{:S(2)}, u32[]{:S(2)}) collective-permute-start(bf16[2,8,8,3840]{3,2,1,0:T(8,128)(2,1)} %collective-permute-done.9.refs_4_.refs_5_), channel_id=1, source_target_pairs={{0,3},{1,2},{2,1},{3,0},{4,7},{5,6},{6,5},{7,4},{8,9},{9,8},{10,11... | collective-permute-start | bytes 2949128 | tf_op jit(solution)/shard_map/ppermute | solution.py:66
  77.3 21.2 %collective-permute-start.16 = (bf16[2,8,8,3840]{3,2,1,0:T(8,128)(2,1)}, bf16[2,8,8,3840]{3,2,1,0:T(8,128)(2,1)}, u32[]{:S(2)}, u32[]{:S(2)}) collective-permute-start(bf16[2,8,8,3840]{3,2,1,0:T(8,128)(2,1)} %collective-permute-done.8.refs_1_), channel_id=1, source_target_pairs={{0,68},{1,69},{2,70},{3,71},{4,64},{5,65},{6,66},{7,67},{8,72},{9,... | collective-permute-start | bytes 2949128 | tf_op jit(solution)/shard_map/ppermute | solution.py:66
  88.2 1.0 copy-start.2
  89.2 1.0 copy-start.4
  90.1 0.6 copy-start.7
  94.3 17.4 %collective-permute-start.15 = (bf16[2,8,8,11392]{3,2,1,0:T(8,128)(2,1)}, bf16[2,8,8,11392]{3,2,1,0:T(8,128)(2,1)}, u32[]{:S(2)}, u32[]{:S(2)}) collective-permute-start(bf16[2,8,8,11392]{3,2,1,0:T(8,128)(2,1)} %shard_map.75), channel_id=1, source_target_pairs={{0,8},{1,9},{2,10},{3,11},{4,12},{5,13},{6,14},{7,15},{8,0},{9,1},... | collective-permute-start | bytes 8749064 | tf_op jit(solution)/shard_map/ppermute | solution.py:62
  100.5 11.1 %copy-start.3 = (f32[8,8,8,512]{3,2,1,0:T(8,128)S(1)}, f32[8,8,8,512]{3,2,1,0:T(8,128)}, u32[]{:S(2)}) copy-start(f32[8,8,8,512]{3,2,1,0:T(8,128)} %copy-done.2) | copy-start | bytes 3145732
  100.6 11.1 %copy-start.5 = (f32[8,8,8,512]{3,2,1,0:T(8,128)S(1)}, f32[8,8,8,512]{3,2,1,0:T(8,128)}, u32[]{:S(2)}) copy-start(f32[8,8,8,512]{3,2,1,0:T(8,128)} %copy-done.4) | copy-start | bytes 3145732
  100.6 11.1 %collective-permute-start.19 = (bf16[2,8,8,11392]{3,2,1,0:T(8,128)(2,1)S(1)}, bf16[2,8,8,11392]{3,2,1,0:T(8,128)(2,1)S(1)}, u32[]{:S(2)}, u32[]{:S(2)}) collective-permute-start(bf16[2,8,8,11392]{3,2,1,0:T(8,128)(2,1)S(1)} %shard_map.76), channel_id=1, source_target_pairs={{0,8},{1,9},{2,10},{3,11},{4,12},{5,13},{6,14},{7,15},{8,0},{9,1},... | collective-permute-start | bytes 8749064 | tf_op jit(solution)/shard_map/ppermute | solution.py:62
  127.8 1.3 %collective-permute-start.20 = (f32[4,128]{1,0:T(4,128)S(1)}, f32[4,128]{1,0:T(4,128)S(1)}, u32[]{:S(2)}, u32[]{:S(2)}) collective-permute-start(f32[4,128]{1,0:T(4,128)S(1)} %get-tuple-element.21), channel_id=1, source_target_pairs={{0,8},{1,9},{2,10},{3,11},{4,12},{5,13},{6,14},{7,15},{8,0},{9,1},... | collective-permute-start | bytes 6152 | tf_op jit(solution)/shard_map/ppermute | solution.py:62

commit v5 on v4

--- a/solution.py
+++ b/solution.py
@@ -40,11 +40,12 @@
     return dp * 8 + (p["x"] // 2) * 4 + p["y"]
 
 
-def ring_pairs(axis, step):
+def ring_pairs(axes, step):
     pairs = []
     for i in range(128):
         p = coords(i)
-        p[axis] ^= MASKS[p["c"]][step]
+        for axis in axes:
+            p[axis] ^= MASKS[p["c"]][step]
         pairs.append((i, index(p)))
     return pairs
 
@@ -62,8 +63,8 @@
     return lax.ppermute(x, AXES, core_pairs())
 
 
-def hop(x, axis, step):
-    return lax.ppermute(x, AXES, ring_pairs(axis, step))
+def hop(x, axes, step):
+    return lax.ppermute(x, AXES, ring_pairs(axes, step))
 
 
 def double(x, axis, step):
@@ -74,17 +75,18 @@
     return pltpu.with_memory_space_constraint(x, pltpu.VMEM)
 
 
-def gate(xs, dep):
+def gate(xs, *deps):
     n = len(xs)
     anyspec = pl.BlockSpec(memory_space=pl.ANY)
     return pl.pallas_call(
         lambda *refs: None,
-        in_specs=[anyspec] * (n + 1),
+        in_specs=[anyspec] * (n + len(deps)),
         out_specs=[anyspec] * n,
         out_shape=[jax.ShapeDtypeStruct(x.shape, x.dtype) for x in xs],
         input_output_aliases={i: i for i in range(n)},
+        compiler_params=pltpu.CompilerParams(vmem_limit_bytes=1 << 20),
         cost_estimate=pl.CostEstimate(flops=0, bytes_accessed=0, transcendentals=0),
-    )(*[pin(x) for x in xs], dep)
+    )(*[pin(x) for x in xs], *deps)
 
 
 def nt(a, b):
@@ -247,35 +249,40 @@
 
 
 def early_body(core_ref, acts, grads, dep_ref, *refs):
-    own = [refs[p * 3:p * 3 + 3] for p in range(3)]
-    ca, cg, tok, hbuf, sems = refs[9:]
+    own = [refs[p * 2:p * 2 + 2] for p in range(3)]
+    ca, cg, tok, hbuf, sems = refs[6:]
     train = Train(core_ref, acts, grads, ORDER[:3], hbuf, sems)
     tok[...] = jnp.zeros_like(tok)
     ca[...] = jnp.zeros_like(ca)
     cg[...] = jnp.zeros_like(cg)
     for part in range(3):
-        cross_rows(part, (0, 1, 2), own[part], train, part, ca, cg)
+        cross_rows(part, (0, 1), own[part], train, part, ca, cg)
 
 
 def late_own_body(core_ref, acts, grads, *refs):
-    pieces = [refs[p * 4:p * 4 + 4] for p in range(3)]
-    ca, cg, ka, kg, ids, hbuf, sems, pbuf, psems = refs[12:]
+    pieces = [refs[p * 3:p * 3 + 3] for p in range(3)]
+    ain, gin, ca, cg, ka, kg, ids, hbuf, sems, pbuf, psems, asems = refs[9:]
+    sums = [
+        pltpu.make_async_copy(ain, ca, asems.at[0]),
+        pltpu.make_async_copy(gin, cg, asems.at[1]),
+    ]
 
     def moves(part):
         b = part % 2
+        x, a1, last = pieces[part]
         return [
             pltpu.make_async_copy(
-                pieces[part][k], pbuf.at[b, k, :, :, :, pl.ds(0, WIDTHS[part])], psems.at[b, k]
+                src, pbuf.at[b, k, :, :, :, pl.ds(0, WIDTHS[part])], psems.at[b, k]
             )
-            for k in range(4)
+            for k, src in enumerate((x, a1, last.at[0], last.at[1]))
         ]
 
     for part in range(2):
         for cp in moves(part):
             cp.start()
     train = Train(core_ref, acts, grads, ORDER[:3], hbuf, sems)
-    ca[...] = jnp.zeros_like(ca)
-    cg[...] = jnp.zeros_like(cg)
+    for cp in sums:
+        cp.start()
     seen = set()
     for part in range(3):
         b = part % 2
@@ -294,15 +301,24 @@
         if part == 2:
             for at, x in enumerate(blocks(C3G, IDW)):
                 ids[at * 64:at * 64 + 64, :] = x.astype(jnp.float32)
-        cross_rows(part, (3,), [pbuf.at[b, 3]], train, part, ca, cg)
+        if part == 0:
+            for cp in sums:
+                cp.wait()
+        cross_rows(part, (2, 3), [pbuf.at[b, 2], pbuf.at[b, 3]], train, part, ca, cg)
         if part == 0:
             for cp in moves(2):
                 cp.start()
 
 
-def late_other_body(core_ref, acts, grads, o0, o1, o2, o3, a1, g1, a3, g3, k1, k2, ids,
-                    raw_ref, norm_ref, hbuf, sems, vbuf, ca, cg, ka, kg, vsems):
+def late_other_body(core_ref, acts, grads, o0, o1, o2, ain, gin, k1, k2, idin,
+                    raw_ref, norm_ref, hbuf, sems, vbuf, acc_a, acc_g, ka, kg, ids, vsems, asems):
     c = core_ref[0]
+    sums = [
+        pltpu.make_async_copy(x, y, asems.at[i])
+        for i, (x, y) in enumerate(
+            ((ain, acc_a), (gin, acc_g), (k1, ka), (k2, kg), (idin, ids))
+        )
+    ]
 
     def moves(part):
         b = part % 2
@@ -313,34 +329,35 @@
                 vbuf.at[b, :, place(part, k, s4), :, pl.ds(0, WIDTHS[part])],
                 vsems.at[b, k, s4],
             )
-            for k, o in enumerate((o0, o1, o2, o3)) for s4 in range(2)
+            for k, o in enumerate((o0, o1, o2.at[0], o2.at[1])) for s4 in range(2)
         ]
 
     for part in range(2):
         for cp in moves(part):
             cp.start()
     train = Train(core_ref, acts, grads, ORDER[3:], hbuf, sems)
-    ca[...] = (a1[...] + a3[...]).reshape(VAL, TOK)
-    cg[...] = (g1[...] + g3[...]).reshape(VAL, TOK)
-    ka[...] = k1[...]
-    kg[...] = k2[...]
+    for cp in sums:
+        cp.start()
     seen = {"a", "g"}
     for part in range(3):
         for cp in moves(part):
             cp.wait()
+        if part == 0:
+            for cp in sums:
+                cp.wait()
         for name, at, w in SEGMENTS[part]:
             blocks = [vbuf[part % 2, b, :, :, at:at + w].reshape(64, w) for b in range(8)]
             val_rows(core_ref, blocks, name, seen, ka, kg)
         train.wait(part)
         for name, at, w in SEGMENTS[part]:
-            acc = ca if name == "a" else cg
+            acc = acc_a if name == "a" else acc_g
             rows = vbuf[part % 2, :, :, :, at:at + w].reshape(VAL, w)
-            acc[...] += nt(rows, train.get(part, at, w))
+            acc[...] += nt(rows, train.get(part, at, w)).reshape(8, 8, 8, TOK)
         if part == 0:
             for cp in moves(2):
                 cp.start()
 
-    cross = ca[...] * cg[...]
+    cross = acc_a[...].reshape(VAL, TOK) * acc_g[...].reshape(VAL, TOK)
     kern = ka[...] * kg[...]
     all_ids = ids[...]
     row_ids = jnp.transpose(all_ids)[0:1, :]
@@ -397,56 +414,56 @@
     got = swap(jnp.where(first, halves[1], halves[0]))
     rows = jnp.concatenate([jnp.where(first, keep, got), jnp.where(first, got, keep)], axis=0)
 
-    rows = double(rows, "z", 0)
+    near = [
+        hop(rows, [a for a in "xyz" if n & WEIGHT[a]], 0) for n in (1, 2, 4, 3, 5, 6, 7)
+    ]
+    rows = jnp.stack([rows, near[0], near[1], near[3], near[2], near[4], near[5], near[6]])
     sg = self_call(out_grads, rows)
-    (rows,) = gate([double(rows, "y", 0)], sg)
-    block_gram = self_call(hidden_acts, rows, sg)
-    (rows,) = gate([double(rows, "x", 0)], block_gram)
-    rows = rows.reshape(8, 8, ALLW)
-    piece = [[rows[..., s:s + w]] for s, w in zip(STARTS, WIDTHS)]
-    piece = [[double(piece[j][0], RUNS[j], 1)] for j in range(3)]
-    for j in range(3):
-        piece[j].append(hop(piece[j][0], STEP5[j], 1))
-    for j in range(3):
-        piece[j].append(hop(piece[j][0], STEP6[j], 1))
-    for j in range(3):
-        piece[j].append(hop(piece[j][1], STEP6[j], 1))
-    joined = [jnp.concatenate([piece[j][k] for j in range(3)], axis=-1) for k in range(4)]
-    o0, o1 = [swap(gate([x], block_gram)[0]) for x in joined[:2]]
+    x = [double(rows[..., s:s + w], RUNS[j], 1) for j, (s, w) in enumerate(zip(STARTS, WIDTHS))]
+    x = gate(x, sg)
+    block_gram = self_call(hidden_acts, x[1], sg)
+    a1 = [hop(x[j], STEP5[j], 1) for j in range(3)]
+    o0 = swap(gate([jnp.concatenate(x, axis=-1)], sg)[0])
+    pair = gate([jnp.stack([x[j], a1[j]]) for j in range(3)], block_gram, o0)
+    last = [hop(pair[j], STEP6[j], 1) for j in range(3)]
+    o1 = swap(gate([jnp.concatenate(a1, axis=-1)], sg)[0])
     call = functools.partial(
         local_call, core=core.reshape(1).astype(jnp.int32), acts=hidden_acts, grads=out_grads
     )
     unit = 2 * 512 * (HA + HG)
-    a1, g1, tok = call(
-        early_body,
-        args=[block_gram] + [piece[j][k] for j in range(3) for k in range(3)],
+    ca1, cg1, tok = call(
+        early_body, args=[block_gram] + [y for j in range(3) for y in (x[j], a1[j])],
         outs=[ACC, ACC, jax.ShapeDtypeStruct((8, 128), jnp.float32)],
-        flops=384 * unit, anys=(0,),
+        flops=256 * unit, anys=(0,),
     )
-    o2, o3 = [swap(gate([x], tok)[0]) for x in joined[2:]]
+    o2 = swap(gate([jnp.concatenate(last, axis=-1)], tok, o1)[0])
     ids = jax.ShapeDtypeStruct((VAL, IDW), jnp.float32)
-    a3, g3, k1, k2, ids = call(
-        late_own_body, args=[piece[j][k] for j in range(3) for k in range(4)],
-        outs=[ACC, ACC, KERN, KERN, ids], flops=384 * unit, anys=range(12),
+    ca2, cg2, k1, k2, ids = call(
+        late_own_body,
+        args=[y for j in range(3) for y in (x[j], a1[j], last[j])] + [ca1, cg1],
+        outs=[ACC, ACC, KERN, KERN, ids], flops=512 * unit, anys=range(11),
         scratch=[
             pltpu.VMEM((2, 4, 2, 8, 8, C1), jnp.bfloat16),
             pltpu.SemaphoreType.DMA((2, 4)),
+            pltpu.SemaphoreType.DMA((2,)),
         ],
         mib=30,
     )
     raw, norm = call(
-        late_other_body, args=[o0, o1, o2, o3, a1, g1, a3, g3, k1, k2, ids],
+        late_other_body, args=[o0, o1, o2, ca2, cg2, k1, k2, ids], anys=range(8),
         outs=[
             jax.ShapeDtypeStruct((NVAL, TOK), jnp.float32),
             jax.ShapeDtypeStruct((NVAL, 128), jnp.float32),
         ],
         scratch=[
             pltpu.VMEM((2, 8, 8, 8, C1), jnp.bfloat16),
-            pltpu.VMEM((VAL, TOK), jnp.float32),
-            pltpu.VMEM((VAL, TOK), jnp.float32),
+            pltpu.VMEM((8, 8, 8, TOK), jnp.float32),
+            pltpu.VMEM((8, 8, 8, TOK), jnp.float32),
             pltpu.VMEM((VAL // 2, VAL), jnp.float32),
             pltpu.VMEM((VAL // 2, VAL), jnp.float32),
+            pltpu.VMEM((VAL, IDW), jnp.float32),
             pltpu.SemaphoreType.DMA((2, 4, 2)),
+            pltpu.SemaphoreType.DMA((5,)),
         ],
         flops=768 * unit, mib=34,
     )

time: 130 us -> 127 us (0.977)
  Pallas kernels: 53.8 us -> 44.8 us
  starting transfers between devices: 31.8 us -> 40 us
  other arithmetic: 16 us -> 7.87 us
  local copies, waits for them, and re-layouts: 5.31 us -> 10.9 us
    ppermute x15 -> x16, starting transfers between devices: 13.3 us -> 22.4 us  [hop(): return lax.ppermute(x, AXES, ring_pairs(axes, step))]
    pallas_call x3, Pallas kernels: 38 us -> 28.9 us  [local_call(): pl.pallas_call(body, in_specs=[pl.BlockSpec(memory_space=pltpu.SMEM)] + [...]
    unnamed x16 -> x40, local copies, waits for them, and re-layouts: 3.35 us -> 8.96 us
    concatenate x4, other arithmetic: 10.8 us -> 5.28 us  [the longest x1 3.15 us: shards(): o2 = swap(gate([jnp.concatenate(last, axis=-1)], tok, o1)[0])]
    another operation x7 -> x3, other arithmetic: 3.56 us -> 0.28 us  [double(): return jnp.stack([x, hop(x, axis, step)])]
    ppermute x6 -> x5, starting transfers between devices: 18.6 us -> 17.7 us  [swap(): return lax.ppermute(x, AXES, core_pairs())]
    ppermute x15 -> x16, waiting for transfers between devices: 20.4 us -> 20.3 us  [hop(): return lax.ppermute(x, AXES, ring_pairs(axes, step))]
  transfers between devices with their start and end apart: 21 -> 21, of which waited for: 7 -> 9; matrix products, arithmetic and copies ran while one was open for 11% -> 5% of each run, Pallas kernels for 29% -> 25%
where the time goes in v5:
time: 127 us
  Pallas kernels  44.8 us (35%)
  starting transfers between devices  40 us (31%)
  waiting for transfers between devices  22 us (17%)
  local copies, waits for them, and re-layouts  10.9 us (9%)
  other arithmetic  7.87 us (6%)
    pallas_call x3, Pallas kernels, local_call(): pl.pallas_call(body, in_specs=[pl.BlockSpec(memory_space=pltpu.SMEM)] + [...  28.9 us
    ppermute x16, starting transfers between devices, hop(): return lax.ppermute(x, AXES, ring_pairs(axes, step))  22.4 us
    ppermute x16, waiting for transfers between devices, hop(): return lax.ppermute(x, AXES, ring_pairs(axes, step))  20.3 us
    ppermute x5, starting transfers between devices, swap(): return lax.ppermute(x, AXES, core_pairs())  17.7 us
    pallas_call x2, Pallas kernels, self_call(): pl.pallas_call(body, grid=(width // KC,), in_specs=[pl.BlockSpec((TOK, KC...  15.8 us
    unnamed x40, local copies, waits for them, and re-layouts  8.96 us
    concatenate x1, other arithmetic, shards(): o2 = swap(gate([jnp.concatenate(last, axis=-1)], tok, o1)[0])  3.15 us
  transfers between devices with their start and end apart: 21, of which 9 were waited for; matrix products, arithmetic and copies ran while one was open for 5% of the time, Pallas kernels for 25%

profile of v5, /device:TPU:1, one launch (start us, length us, event | category | flops | bytes accessed | tf_op | source)
XLA Modules:
  0.0 126.7 jit_solution(5020631306790141211)
XLA Ops:
  0.6 0.9 fusion
  1.5 0.8 fusion.1
  2.3 0.7 convert_element_type.4
  3.2 1.5 %collective-permute-start = (bf16[4,11392]{1,0:T(4,128)(2,1)S(1)}, bf16[4,11392]{1,0:T(4,128)(2,1)S(1)}, u32[]{:S(2)}, u32[]{:S(2)}) collective-permute-start(bf16[4,11392]{1,0:T(4,128)(2,1)S(1)} %broadcast_select_fusion.2), channel_id=1, source_target_pairs={{0,8},{1,9},{2,10},{3,11},{4,12},{5,13},{6,14},{7,15},{8,0},{9,1},... | collective-permute-start | bytes 273416 | tf_op jit(solution)/shard_map/ppermute | solution.py:63
  4.7 0.9 collective-permute-done
  5.6 0.1 broadcast_select_fusion.1
  5.8 3.9 %collective-permute-start.1 = (bf16[8,11392]{1,0:T(8,128)(2,1)S(1)}, bf16[8,11392]{1,0:T(8,128)(2,1)S(1)}, u32[]{:S(2)}, u32[]{:S(2)}) collective-permute-start(bf16[8,11392]{1,0:T(8,128)(2,1)S(1)} %pad_maximum_fusion.9), channel_id=1, source_target_pairs={{0,16},{1,17},{2,18},{3,19},{4,20},{5,21},{6,22},{7,23},{8,56},{9,... | collective-permute-start | bytes 546824 | tf_op jit(solution)/shard_map/ppermute | solution.py:67
  9.8 2.8 %collective-permute-start.2 = (bf16[8,11392]{1,0:T(8,128)(2,1)S(1)}, bf16[8,11392]{1,0:T(8,128)(2,1)S(1)}, u32[]{:S(2)}, u32[]{:S(2)}) collective-permute-start(bf16[8,11392]{1,0:T(8,128)(2,1)S(1)} %pad_maximum_fusion.9), channel_id=1, source_target_pairs={{0,1},{1,0},{2,3},{3,2},{4,5},{5,4},{6,7},{7,6},{8,11},{9,10},{10,... | collective-permute-start | bytes 546824 | tf_op jit(solution)/shard_map/ppermute | solution.py:67
  12.7 2.5 %collective-permute-start.4 = (bf16[8,11392]{1,0:T(8,128)(2,1)S(1)}, bf16[8,11392]{1,0:T(8,128)(2,1)S(1)}, u32[]{:S(2)}, u32[]{:S(2)}) collective-permute-start(bf16[8,11392]{1,0:T(8,128)(2,1)S(1)} %pad_maximum_fusion.9), channel_id=1, source_target_pairs={{0,64},{1,65},{2,66},{3,67},{4,68},{5,69},{6,70},{7,71},{8,76},{9,... | collective-permute-start | bytes 546824 | tf_op jit(solution)/shard_map/ppermute | solution.py:67
  15.1 2.4 %collective-permute-start.5 = (bf16[8,11392]{1,0:T(8,128)(2,1)S(1)}, bf16[8,11392]{1,0:T(8,128)(2,1)S(1)}, u32[]{:S(2)}, u32[]{:S(2)}) collective-permute-start(bf16[8,11392]{1,0:T(8,128)(2,1)S(1)} %pad_maximum_fusion.9), channel_id=1, source_target_pairs={{0,80},{1,81},{2,82},{3,83},{4,84},{5,85},{6,86},{7,87},{8,124},{9... | collective-permute-start | bytes 546824 | tf_op jit(solution)/shard_map/ppermute | solution.py:67
  17.5 4.8 %collective-permute-start.6 = (bf16[8,11392]{1,0:T(8,128)(2,1)S(1)}, bf16[8,11392]{1,0:T(8,128)(2,1)S(1)}, u32[]{:S(2)}, u32[]{:S(2)}) collective-permute-start(bf16[8,11392]{1,0:T(8,128)(2,1)S(1)} %pad_maximum_fusion.9), channel_id=1, source_target_pairs={{0,65},{1,64},{2,67},{3,66},{4,69},{5,68},{6,71},{7,70},{8,79},{9,... | collective-permute-start | bytes 546824 | tf_op jit(solution)/shard_map/ppermute | solution.py:67
  22.5 0.3 collective-permute-done.5
  22.8 4.3 %collective-permute-done.6 = bf16[8,11392]{1,0:T(8,128)(2,1)S(1)} collective-permute-done((bf16[8,11392]{1,0:T(8,128)(2,1)S(1)}, bf16[8,11392]{1,0:T(8,128)(2,1)S(1)}, u32[]{:S(2)}, u32[]{:S(2)}) %collective-permute-start.6) | collective-permute-done | bytes 182304 | tf_op jit(solution)/shard_map/ppermute | solution.py:67
  27.2 5.1 %collective-permute-done.7 = bf16[8,11392]{1,0:T(8,128)(2,1)S(1)} collective-permute-done((bf16[8,11392]{1,0:T(8,128)(2,1)S(1)}, bf16[8,11392]{1,0:T(8,128)(2,1)S(1)}, u32[]{:S(2)}, u32[]{:S(2)}) %collective-permute-start.7) | collective-permute-done | bytes 182304 | tf_op jit(solution)/shard_map/ppermute | solution.py:67
  32.5 0.1 slice_bitcast_fusion.1
  32.8 5.6 %shard_map.68.refs_3_.refs_1_.first_ref = f32[512,256]{1,0:T(8,128)S(1)} custom-call(bf16[512,8192]{1,0:T(8,128)(2,1)} %grads.5, bf16[8,8,11392]{2,1,0:T(8,128)(2,1)S(1)} %bitcast_dynamic-update-slice_fusion.dep_ref), custom_call_target="tpu_custom_call" | custom-call | flops 2147483648 | bytes 8388608 | tf_op jit(solution)/shard_map/pallas_call | solution.py:146
  38.5 1.5 %collective-permute-done.10 = bf16[8,8,3712]{2,1,0:T(8,128)(2,1)S(1)} collective-permute-done((bf16[8,8,3712]{2,1,0:T(8,128)(2,1)S(1)}, bf16[8,8,3712]{2,1,0:T(8,128)(2,1)S(1)}, u32[]{:S(2)}, u32[]{:S(2)}) %collective-permute-start.10) | collective-permute-done | bytes 475168 | tf_op jit(solution)/shard_map/ppermute | solution.py:67
  40.1 0.3 collective-permute-done.9
  40.6 0.2 pad_maximum_fusion.1.refs_0_
  41.0 1.5 %collective-permute-start.13 = (bf16[2,8,8,3840]{3,2,1,0:T(8,128)(2,1)S(1)}, bf16[2,8,8,3840]{3,2,1,0:T(8,128)(2,1)S(1)}, u32[]{:S(2)}, u32[]{:S(2)}) collective-permute-start(bf16[2,8,8,3840]{3,2,1,0:T(8,128)(2,1)S(1)} %get-tuple-element.19.dep_ref.refs_2_.refs_3_), channel_id=1, source_target_pairs={{0,68},{1,69},{2,70},{3,71},{4,64},{5,65},{6,66},{7,67},{8,72},{9,... | collective-permute-start | bytes 2949128 | tf_op jit(solution)/shard_map/ppermute | solution.py:67
  42.6 1.4 %collective-permute-start.12 = (bf16[2,8,8,3840]{3,2,1,0:T(8,128)(2,1)S(1)}, bf16[2,8,8,3840]{3,2,1,0:T(8,128)(2,1)S(1)}, u32[]{:S(2)}, u32[]{:S(2)}) collective-permute-start(bf16[2,8,8,3840]{3,2,1,0:T(8,128)(2,1)S(1)} %get-tuple-element.18.refs_0_), channel_id=1, source_target_pairs={{0,48},{1,49},{2,50},{3,51},{4,52},{5,53},{6,54},{7,55},{8,24},{9,... | collective-permute-start | bytes 2949128 | tf_op jit(solution)/shard_map/ppermute | solution.py:67
  43.9 10.2 %shard_map.72.refs_3_.dep_ref = f32[4,4]{1,0:T(4,128)} custom-call(bf16[512,14336]{1,0:T(8,128)(2,1)} %acts.5, f32[512,256]{1,0:T(8,128)S(1)} %shard_map.68.refs_3_.refs_1_.first_ref, bf16[2,8,8,3840]{3,2,1,0:T(8,128)(2,1)S(1)} %get-tuple-element.19.dep_ref.refs_2_.refs_3_), custom_call_target="tpu_custom_call" | custom-call | flops 3758096384 | bytes 14680064 | tf_op jit(solution)/shard_map/pallas_call | solution.py:146
  54.1 0.2 pad_maximum_fusion.5.refs_2_
  54.4 0.2 pad_maximum_fusion.4.refs_1_
  54.5 1.3 collective-permute-done.12.refs_1_
  55.8 0.2 pad_maximum_fusion.3.refs_0_
  56.0 0.5 copy-done.16
  56.5 1.6 %copy-done.4 = bf16[2,8,8,11392]{3,2,1,0:T(8,128)(2,1)} copy-done((bf16[2,8,8,11392]{3,2,1,0:T(8,128)(2,1)}, bf16[2,8,8,11392]{3,2,1,0:T(8,128)(2,1)S(1)}, u32[]{:S(2)}) %copy-start.4) | copy-done | bytes 2916376
  58.1 0.2 collective-permute-start.16
  58.3 1.4 %collective-permute-start.17 = (bf16[2,2,8,8,3840]{4,3,2,1,0:T(8,128)(2,1)S(1)}, bf16[2,2,8,8,3840]{4,3,2,1,0:T(8,128)(2,1)}, u32[]{:S(2)}, u32[]{:S(2)}) collective-permute-start(bf16[2,2,8,8,3840]{4,3,2,1,0:T(8,128)(2,1)S(1)} %get-tuple-element.22), channel_id=1, source_target_pairs={{0,3},{1,2},{2,1},{3,0},{4,7},{5,6},{6,5},{7,4},{8,9},{9,8},{10,11... | collective-permute-start | bytes 5898248 | tf_op jit(solution)/shard_map/ppermute | solution.py:67
  59.7 1.1 collective-permute-start.18
  60.7 1.8 %pad_maximum_fusion.2.refs_0_ = bf16[2,8,8,11392]{3,2,1,0:T(8,128)(2,1)} fusion(bf16[2,8,8,3712]{3,2,1,0:T(8,128)(2,1)S(1)} %collective-permute-done.14.refs_5_.refs_7_, bf16[2,8,8,3840]{3,2,1,0:T(8,128)(2,1)S(1)} %collective-permute-done.13.refs_3_.refs_4_, bf16[2,8,8,3840]{3,2,1,0:T(8,128)(2,1)S(1)} %collective-permute-done.12.refs_1_), kind=kLoop, calls=%fused_computation.2 | loop fusion | flops 8749056 | bytes 5832704 | tf_op jit(solution)/shard_map/concatenate | solution.py:429
  62.6 5.1 %collective-permute-start.15 = (bf16[2,8,8,11392]{3,2,1,0:T(8,128)(2,1)}, bf16[2,8,8,11392]{3,2,1,0:T(8,128)(2,1)}, u32[]{:S(2)}, u32[]{:S(2)}) collective-permute-start(bf16[2,8,8,11392]{3,2,1,0:T(8,128)(2,1)} %shard_map.71), channel_id=1, source_target_pairs={{0,8},{1,9},{2,10},{3,11},{4,12},{5,13},{6,14},{7,15},{8,0},{9,1},... | collective-permute-start | bytes 8749064 | tf_op jit(solution)/shard_map/ppermute | solution.py:63
  67.7 5.9 %shard_map.74 = (f32[8,8,8,512]{3,2,1,0:T(8,128)S(1)}, f32[8,8,8,512]{3,2,1,0:T(8,128)S(1)}, f32[8,128]{1,0:T(8,128)S(1)}) custom-call(s32[1]{0:T(128)} %bitcast.core_ref, bf16[512,14336]{1,0:T(8,128)(2,1)} %acts.5, bf16[512,8192]{1,0:T(8,128)(2,1)} %grads.5, f32[4,4]{1,0:T(4,128)S(1)} %copy-done.16, bf16[2,8,8,3840]{3,2,1,0:T(8,128)(2,1)S(1)} %get-tuple-element.18.refs_0_, ...), custom_call_target="tpu_custom_call" | custom-call | flops 2952790016 | bytes 11534336 | tf_op jit(solution)/shard_map/pallas_call | solution.py:384
  73.6 1.0 copy-done.10
  74.5 1.0 copy-done.12
  75.5 7.3 %collective-permute-done.18.refs_8_ = bf16[2,2,8,8,3712]{4,3,2,1,0:T(8,128)(2,1)S(1)} collective-permute-done((bf16[2,2,8,8,3712]{4,3,2,1,0:T(8,128)(2,1)S(1)}, bf16[2,2,8,8,3712]{4,3,2,1,0:T(8,128)(2,1)S(1)}, u32[]{:S(2)}, u32[]{:S(2)}) %collective-permute-start.18) | collective-permute-done | bytes 1900576 | tf_op jit(solution)/shard_map/ppermute | solution.py:67
  82.8 1.2 copy-done.8
  84.1 1.4 %copy-done.6 = bf16[2,2,8,8,3840]{4,3,2,1,0:T(8,128)(2,1)} copy-done((bf16[2,2,8,8,3840]{4,3,2,1,0:T(8,128)(2,1)}, bf16[2,2,8,8,3840]{4,3,2,1,0:T(8,128)(2,1)S(1)}, u32[]{:S(2)}) %copy-start.6) | copy-done | bytes 1966104
  85.5 3.1 %pad_maximum_fusion.refs_0_ = bf16[2,2,8,8,11392]{4,3,2,1,0:T(8,128)(2,1)S(1)} fusion(bf16[2,2,8,8,3712]{4,3,2,1,0:T(8,128)(2,1)} %copy-done.8, bf16[2,2,8,8,3840]{4,3,2,1,0:T(8,128)(2,1)} %collective-permute-done.17.refs_5_, bf16[2,2,8,8,3840]{4,3,2,1,0:T(8,128)(2,1)} %copy-done.6), kind=kLoop, calls=%fused_computation | loop fusion | flops 17498112 | bytes 11665408 | tf_op jit(solution)/shard_map/concatenate | solution.py:439
  88.7 7.8 %collective-permute-start.19 = (bf16[2,2,8,8,11392]{4,3,2,1,0:T(8,128)(2,1)S(1)}, bf16[2,2,8,8,11392]{4,3,2,1,0:T(8,128)(2,1)S(1)}, u32[]{:S(2)}, u32[]{:S(2)}) collective-permute-start(bf16[2,2,8,8,11392]{4,3,2,1,0:T(8,128)(2,1)S(1)} %shard_map.75), channel_id=1, source_target_pairs={{0,8},{1,9},{2,10},{3,11},{4,12},{5,13},{6,14},{7,15},{8,0},{9,1},... | collective-permute-start | bytes 17498120 | tf_op jit(solution)/shard_map/ppermute | solution.py:63
  96.6 10.5 %shard_map.76 = (f32[8,8,8,512]{3,2,1,0:T(8,128)S(1)}, f32[8,8,8,512]{3,2,1,0:T(8,128)S(1)}, f32[256,512]{1,0:T(8,128)S(1)}, f32[256,512]{1,0:T(8,128)S(1)}, f32[512,128]{1,0:T(8,128)S(1)}) custom-call(s32[1]{0:T(128)} %bitcast.core_ref, bf16[512,14336]{1,0:T(8,128)(2,1)} %acts.5, bf16[512,8192]{1,0:T(8,128)(2,1)} %grads.5, ...), custom_call_target="tpu_custom_call" | custom-call | flops 5905580032 | bytes 11534336 | tf_op jit(solution)/shard_map/pallas_call | solution.py:384
  107.1 1.0 copy-done.14
  108.1 1.2 copy-done.15
  109.3 12.6 %shard_map.77 = (f32[4,512]{1,0:T(4,128)S(1)}, f32[4,128]{1,0:T(4,128)S(1)}) custom-call(s32[1]{0:T(128)} %bitcast.core_ref, bf16[512,14336]{1,0:T(8,128)(2,1)} %acts.5, bf16[512,8192]{1,0:T(8,128)(2,1)} %grads.5, bf16[2,8,8,11392]{3,2,1,0:T(8,128)(2,1)S(1)} %copy-done.5, bf16[2,8,8,11392]{3,2,1,0:T(8,128)(2,1)} %collective-permute-done.15.refs_2_.o1, ...), custom_call_target="tpu_custom_call" | custom-call | flops 8858370048 | bytes 11534336 | tf_op jit(solution)/shard_map/pallas_call | solution.py:384
  121.9 3.1 %collective-permute-start.20 = (f32[4,128]{1,0:T(4,128)S(1)}, f32[4,128]{1,0:T(4,128)S(1)}, u32[]{:S(2)}, u32[]{:S(2)}) collective-permute-start(f32[4,128]{1,0:T(4,128)S(1)} %get-tuple-element.33), channel_id=1, source_target_pairs={{0,8},{1,9},{2,10},{3,11},{4,12},{5,13},{6,14},{7,15},{8,0},{9,1},... | collective-permute-start | bytes 6152 | tf_op jit(solution)/shard_map/ppermute | solution.py:63
  125.0 0.8 collective-permute-done.20
  126.0 0.7 broadcast_multiply_fusion
  (67 shorter events, 1.6 us)
Async XLA Ops:
  3.2 2.4 %collective-permute-start = (bf16[4,11392]{1,0:T(4,128)(2,1)S(1)}, bf16[4,11392]{1,0:T(4,128)(2,1)S(1)}, u32[]{:S(2)}, u32[]{:S(2)}) collective-permute-start(bf16[4,11392]{1,0:T(4,128)(2,1)S(1)} %broadcast_select_fusion.2), channel_id=1, source_target_pairs={{0,8},{1,9},{2,10},{3,11},{4,12},{5,13},{6,14},{7,15},{8,0},{9,1},... | collective-permute-start | bytes 273416 | tf_op jit(solution)/shard_map/ppermute | solution.py:63
  5.8 11.7 %collective-permute-start.1 = (bf16[8,11392]{1,0:T(8,128)(2,1)S(1)}, bf16[8,11392]{1,0:T(8,128)(2,1)S(1)}, u32[]{:S(2)}, u32[]{:S(2)}) collective-permute-start(bf16[8,11392]{1,0:T(8,128)(2,1)S(1)} %pad_maximum_fusion.9), channel_id=1, source_target_pairs={{0,16},{1,17},{2,18},{3,19},{4,20},{5,21},{6,22},{7,23},{8,56},{9,... | collective-permute-start | bytes 546824 | tf_op jit(solution)/shard_map/ppermute | solution.py:67
  9.8 12.5 %collective-permute-start.2 = (bf16[8,11392]{1,0:T(8,128)(2,1)S(1)}, bf16[8,11392]{1,0:T(8,128)(2,1)S(1)}, u32[]{:S(2)}, u32[]{:S(2)}) collective-permute-start(bf16[8,11392]{1,0:T(8,128)(2,1)S(1)} %pad_maximum_fusion.9), channel_id=1, source_target_pairs={{0,1},{1,0},{2,3},{3,2},{4,5},{5,4},{6,7},{7,6},{8,11},{9,10},{10,... | collective-permute-start | bytes 546824 | tf_op jit(solution)/shard_map/ppermute | solution.py:67
  12.7 9.8 %collective-permute-start.3 = (bf16[8,11392]{1,0:T(8,128)(2,1)S(1)}, bf16[8,11392]{1,0:T(8,128)(2,1)S(1)}, u32[]{:S(2)}, u32[]{:S(2)}) collective-permute-start(bf16[8,11392]{1,0:T(8,128)(2,1)S(1)} %pad_maximum_fusion.9), channel_id=1, source_target_pairs={{0,17},{1,16},{2,19},{3,18},{4,21},{5,20},{6,23},{7,22},{8,59},{9,... | collective-permute-start | bytes 546824 | tf_op jit(solution)/shard_map/ppermute | solution.py:67
  12.7 9.8 %collective-permute-start.4 = (bf16[8,11392]{1,0:T(8,128)(2,1)S(1)}, bf16[8,11392]{1,0:T(8,128)(2,1)S(1)}, u32[]{:S(2)}, u32[]{:S(2)}) collective-permute-start(bf16[8,11392]{1,0:T(8,128)(2,1)S(1)} %pad_maximum_fusion.9), channel_id=1, source_target_pairs={{0,64},{1,65},{2,66},{3,67},{4,68},{5,69},{6,70},{7,71},{8,76},{9,... | collective-permute-start | bytes 546824 | tf_op jit(solution)/shard_map/ppermute | solution.py:67
  15.1 7.7 %collective-permute-start.5 = (bf16[8,11392]{1,0:T(8,128)(2,1)S(1)}, bf16[8,11392]{1,0:T(8,128)(2,1)S(1)}, u32[]{:S(2)}, u32[]{:S(2)}) collective-permute-start(bf16[8,11392]{1,0:T(8,128)(2,1)S(1)} %pad_maximum_fusion.9), channel_id=1, source_target_pairs={{0,80},{1,81},{2,82},{3,83},{4,84},{5,85},{6,86},{7,87},{8,124},{9... | collective-permute-start | bytes 546824 | tf_op jit(solution)/shard_map/ppermute | solution.py:67
  17.5 9.6 %collective-permute-start.6 = (bf16[8,11392]{1,0:T(8,128)(2,1)S(1)}, bf16[8,11392]{1,0:T(8,128)(2,1)S(1)}, u32[]{:S(2)}, u32[]{:S(2)}) collective-permute-start(bf16[8,11392]{1,0:T(8,128)(2,1)S(1)} %pad_maximum_fusion.9), channel_id=1, source_target_pairs={{0,65},{1,64},{2,67},{3,66},{4,69},{5,68},{6,71},{7,70},{8,79},{9,... | collective-permute-start | bytes 546824 | tf_op jit(solution)/shard_map/ppermute | solution.py:67
  22.3 10.0 %collective-permute-start.7 = (bf16[8,11392]{1,0:T(8,128)(2,1)S(1)}, bf16[8,11392]{1,0:T(8,128)(2,1)S(1)}, u32[]{:S(2)}, u32[]{:S(2)}) collective-permute-start(bf16[8,11392]{1,0:T(8,128)(2,1)S(1)} %pad_maximum_fusion.9), channel_id=1, source_target_pairs={{0,81},{1,80},{2,83},{3,82},{4,85},{5,84},{6,87},{7,86},{8,127},{9... | collective-permute-start | bytes 546824 | tf_op jit(solution)/shard_map/ppermute | solution.py:67
  32.4 7.6 %collective-permute-start.10 = (bf16[8,8,3712]{2,1,0:T(8,128)(2,1)S(1)}, bf16[8,8,3712]{2,1,0:T(8,128)(2,1)S(1)}, u32[]{:S(2)}, u32[]{:S(2)}) collective-permute-start(bf16[8,8,3712]{2,1,0:T(8,128)(2,1)S(1)} %get-tuple-element.35), channel_id=1, source_target_pairs={{0,68},{1,69},{2,70},{3,71},{4,64},{5,65},{6,66},{7,67},{8,72},{9,... | collective-permute-start | bytes 1425416 | tf_op jit(solution)/shard_map/ppermute | solution.py:67
  32.6 7.8 %collective-permute-start.9 = (bf16[8,8,3840]{2,1,0:T(8,128)(2,1)S(1)}, bf16[8,8,3840]{2,1,0:T(8,128)(2,1)S(1)}, u32[]{:S(2)}, u32[]{:S(2)}) collective-permute-start(bf16[8,8,3840]{2,1,0:T(8,128)(2,1)S(1)} %get-tuple-element.38), channel_id=1, source_target_pairs={{0,48},{1,49},{2,50},{3,51},{4,52},{5,53},{6,54},{7,55},{8,24},{9,... | collective-permute-start | bytes 1474568 | tf_op jit(solution)/shard_map/ppermute | solution.py:67
  32.7 7.8 %collective-permute-start.8 = (bf16[8,8,3840]{2,1,0:T(8,128)(2,1)S(1)}, bf16[8,8,3840]{2,1,0:T(8,128)(2,1)S(1)}, u32[]{:S(2)}, u32[]{:S(2)}) collective-permute-start(bf16[8,8,3840]{2,1,0:T(8,128)(2,1)S(1)} %get-tuple-element.39), channel_id=1, source_target_pairs={{0,3},{1,2},{2,1},{3,0},{4,7},{5,6},{6,5},{7,4},{8,9},{9,8},{10,11... | collective-permute-start | bytes 1474568 | tf_op jit(solution)/shard_map/ppermute | solution.py:67
  40.9 15.2 %collective-permute-start.11 = (bf16[2,8,8,11392]{3,2,1,0:T(8,128)(2,1)S(1)}, bf16[2,8,8,11392]{3,2,1,0:T(8,128)(2,1)S(1)}, u32[]{:S(2)}, u32[]{:S(2)}) collective-permute-start(bf16[2,8,8,11392]{3,2,1,0:T(8,128)(2,1)S(1)} %shard_map.70), channel_id=1, source_target_pairs={{0,8},{1,9},{2,10},{3,11},{4,12},{5,13},{6,14},{7,15},{8,0},{9,1},... | collective-permute-start | bytes 8749064 | tf_op jit(solution)/shard_map/ppermute | solution.py:63
  40.9 13.2 %collective-permute-start.14 = (bf16[2,8,8,3712]{3,2,1,0:T(8,128)(2,1)S(1)}, bf16[2,8,8,3712]{3,2,1,0:T(8,128)(2,1)S(1)}, u32[]{:S(2)}, u32[]{:S(2)}) collective-permute-start(bf16[2,8,8,3712]{3,2,1,0:T(8,128)(2,1)S(1)} %get-tuple-element.20.refs_4_.refs_6_), channel_id=1, source_target_pairs={{0,3},{1,2},{2,1},{3,0},{4,7},{5,6},{6,5},{7,4},{8,9},{9,8},{10,11... | collective-permute-start | bytes 2850824 | tf_op jit(solution)/shard_map/ppermute | solution.py:67
  41.0 13.3 %collective-permute-start.13 = (bf16[2,8,8,3840]{3,2,1,0:T(8,128)(2,1)S(1)}, bf16[2,8,8,3840]{3,2,1,0:T(8,128)(2,1)S(1)}, u32[]{:S(2)}, u32[]{:S(2)}) collective-permute-start(bf16[2,8,8,3840]{3,2,1,0:T(8,128)(2,1)S(1)} %get-tuple-element.19.dep_ref.refs_2_.refs_3_), channel_id=1, source_target_pairs={{0,68},{1,69},{2,70},{3,71},{4,64},{5,65},{6,66},{7,67},{8,72},{9,... | collective-permute-start | bytes 2949128 | tf_op jit(solution)/shard_map/ppermute | solution.py:67
  42.6 13.2 %collective-permute-start.12 = (bf16[2,8,8,3840]{3,2,1,0:T(8,128)(2,1)S(1)}, bf16[2,8,8,3840]{3,2,1,0:T(8,128)(2,1)S(1)}, u32[]{:S(2)}, u32[]{:S(2)}) collective-permute-start(bf16[2,8,8,3840]{3,2,1,0:T(8,128)(2,1)S(1)} %get-tuple-element.18.refs_0_), channel_id=1, source_target_pairs={{0,48},{1,49},{2,50},{3,51},{4,52},{5,53},{6,54},{7,55},{8,24},{9,... | collective-permute-start | bytes 2949128 | tf_op jit(solution)/shard_map/ppermute | solution.py:67
  54.1 13.5 %copy-start.2 = (bf16[2,8,8,3712]{3,2,1,0:T(8,128)(2,1)}, bf16[2,8,8,3712]{3,2,1,0:T(8,128)(2,1)S(1)}, u32[]{:S(2)}) copy-start(bf16[2,8,8,3712]{3,2,1,0:T(8,128)(2,1)S(1)} %collective-permute-done.14.refs_5_.refs_7_) | copy-start | bytes 2850820
  55.8 11.9 %copy-start = (bf16[2,8,8,3840]{3,2,1,0:T(8,128)(2,1)}, bf16[2,8,8,3840]{3,2,1,0:T(8,128)(2,1)S(1)}, u32[]{:S(2)}) copy-start(bf16[2,8,8,3840]{3,2,1,0:T(8,128)(2,1)S(1)} %collective-permute-done.12.refs_1_) | copy-start | bytes 2949124
  55.8 0.7 copy-start.16
  56.5 1.6 %copy-start.4 = (bf16[2,8,8,11392]{3,2,1,0:T(8,128)(2,1)}, bf16[2,8,8,11392]{3,2,1,0:T(8,128)(2,1)S(1)}, u32[]{:S(2)}) copy-start(bf16[2,8,8,11392]{3,2,1,0:T(8,128)(2,1)S(1)} %collective-permute-done.11.refs_4_.o0) | copy-start | bytes 8749060
  58.1 24.8 %collective-permute-start.16 = (bf16[2,2,8,8,3840]{4,3,2,1,0:T(8,128)(2,1)S(1)}, bf16[2,2,8,8,3840]{4,3,2,1,0:T(8,128)(2,1)S(1)}, u32[]{:S(2)}, u32[]{:S(2)}) collective-permute-start(bf16[2,2,8,8,3840]{4,3,2,1,0:T(8,128)(2,1)S(1)} %get-tuple-element.21), channel_id=1, source_target_pairs={{0,68},{1,69},{2,70},{3,71},{4,64},{5,65},{6,66},{7,67},{8,72},{9,... | collective-permute-start | bytes 5898248 | tf_op jit(solution)/shard_map/ppermute | solution.py:67
  58.3 27.2 %collective-permute-start.17 = (bf16[2,2,8,8,3840]{4,3,2,1,0:T(8,128)(2,1)S(1)}, bf16[2,2,8,8,3840]{4,3,2,1,0:T(8,128)(2,1)}, u32[]{:S(2)}, u32[]{:S(2)}) collective-permute-start(bf16[2,2,8,8,3840]{4,3,2,1,0:T(8,128)(2,1)S(1)} %get-tuple-element.22), channel_id=1, source_target_pairs={{0,3},{1,2},{2,1},{3,0},{4,7},{5,6},{6,5},{7,4},{8,9},{9,8},{10,11... | collective-permute-start | bytes 5898248 | tf_op jit(solution)/shard_map/ppermute | solution.py:67
  59.7 23.2 %collective-permute-start.18 = (bf16[2,2,8,8,3712]{4,3,2,1,0:T(8,128)(2,1)S(1)}, bf16[2,2,8,8,3712]{4,3,2,1,0:T(8,128)(2,1)S(1)}, u32[]{:S(2)}, u32[]{:S(2)}) collective-permute-start(bf16[2,2,8,8,3712]{4,3,2,1,0:T(8,128)(2,1)S(1)} %get-tuple-element.23), channel_id=1, source_target_pairs={{0,48},{1,49},{2,50},{3,51},{4,52},{5,53},{6,54},{7,55},{8,24},{9,... | collective-permute-start | bytes 5701640 | tf_op jit(solution)/shard_map/ppermute | solution.py:67
  62.6 26.1 %collective-permute-start.15 = (bf16[2,8,8,11392]{3,2,1,0:T(8,128)(2,1)}, bf16[2,8,8,11392]{3,2,1,0:T(8,128)(2,1)}, u32[]{:S(2)}, u32[]{:S(2)}) collective-permute-start(bf16[2,8,8,11392]{3,2,1,0:T(8,128)(2,1)} %shard_map.71), channel_id=1, source_target_pairs={{0,8},{1,9},{2,10},{3,11},{4,12},{5,13},{6,14},{7,15},{8,0},{9,1},... | collective-permute-start | bytes 8749064 | tf_op jit(solution)/shard_map/ppermute | solution.py:63
  73.5 1.0 copy-start.10
  74.5 1.0 copy-start.12
  82.8 1.2 copy-start.8
  84.1 1.4 %copy-start.6 = (bf16[2,2,8,8,3840]{4,3,2,1,0:T(8,128)(2,1)}, bf16[2,2,8,8,3840]{4,3,2,1,0:T(8,128)(2,1)S(1)}, u32[]{:S(2)}) copy-start(bf16[2,2,8,8,3840]{4,3,2,1,0:T(8,128)(2,1)S(1)} %collective-permute-done.16.refs_2_) | copy-start | bytes 5898244
  88.6 7.9 %copy-start.1 = (bf16[2,8,8,3840]{3,2,1,0:T(8,128)(2,1)S(1)}, bf16[2,8,8,3840]{3,2,1,0:T(8,128)(2,1)}, u32[]{:S(2)}) copy-start(bf16[2,8,8,3840]{3,2,1,0:T(8,128)(2,1)} %copy-done) | copy-start | bytes 2949124
  88.6 7.9 %copy-start.3 = (bf16[2,8,8,3712]{3,2,1,0:T(8,128)(2,1)S(1)}, bf16[2,8,8,3712]{3,2,1,0:T(8,128)(2,1)}, u32[]{:S(2)}) copy-start(bf16[2,8,8,3712]{3,2,1,0:T(8,128)(2,1)} %copy-done.2) | copy-start | bytes 2850820
  88.6 7.9 %copy-start.7 = (bf16[2,2,8,8,3840]{4,3,2,1,0:T(8,128)(2,1)S(1)}, bf16[2,2,8,8,3840]{4,3,2,1,0:T(8,128)(2,1)}, u32[]{:S(2)}) copy-start(bf16[2,2,8,8,3840]{4,3,2,1,0:T(8,128)(2,1)} %copy-done.6) | copy-start | bytes 5898244
  88.7 7.9 %copy-start.9 = (bf16[2,2,8,8,3712]{4,3,2,1,0:T(8,128)(2,1)S(1)}, bf16[2,2,8,8,3712]{4,3,2,1,0:T(8,128)(2,1)}, u32[]{:S(2)}) copy-start(bf16[2,2,8,8,3712]{4,3,2,1,0:T(8,128)(2,1)} %copy-done.8) | copy-start | bytes 5701636
  88.7 7.9 %copy-start.11 = (f32[8,8,8,512]{3,2,1,0:T(8,128)S(1)}, f32[8,8,8,512]{3,2,1,0:T(8,128)}, u32[]{:S(2)}) copy-start(f32[8,8,8,512]{3,2,1,0:T(8,128)} %copy-done.10) | copy-start | bytes 3145732
  88.7 7.9 %copy-start.13 = (f32[8,8,8,512]{3,2,1,0:T(8,128)S(1)}, f32[8,8,8,512]{3,2,1,0:T(8,128)}, u32[]{:S(2)}) copy-start(f32[8,8,8,512]{3,2,1,0:T(8,128)} %copy-done.12) | copy-start | bytes 3145732
  88.7 19.4 %collective-permute-start.19 = (bf16[2,2,8,8,11392]{4,3,2,1,0:T(8,128)(2,1)S(1)}, bf16[2,2,8,8,11392]{4,3,2,1,0:T(8,128)(2,1)S(1)}, u32[]{:S(2)}, u32[]{:S(2)}) collective-permute-start(bf16[2,2,8,8,11392]{4,3,2,1,0:T(8,128)(2,1)S(1)} %shard_map.75), channel_id=1, source_target_pairs={{0,8},{1,9},{2,10},{3,11},{4,12},{5,13},{6,14},{7,15},{8,0},{9,1},... | collective-permute-start | bytes 17498120 | tf_op jit(solution)/shard_map/ppermute | solution.py:63
  96.6 11.5 %copy-start.5 = (bf16[2,8,8,11392]{3,2,1,0:T(8,128)(2,1)S(1)}, bf16[2,8,8,11392]{3,2,1,0:T(8,128)(2,1)}, u32[]{:S(2)}) copy-start(bf16[2,8,8,11392]{3,2,1,0:T(8,128)(2,1)} %copy-done.4) | copy-start | bytes 8749060
  107.1 1.0 copy-start.14
  108.1 1.2 copy-start.15
  121.9 4.0 %collective-permute-start.20 = (f32[4,128]{1,0:T(4,128)S(1)}, f32[4,128]{1,0:T(4,128)S(1)}, u32[]{:S(2)}, u32[]{:S(2)}) collective-permute-start(f32[4,128]{1,0:T(4,128)S(1)} %get-tuple-element.33), channel_id=1, source_target_pairs={{0,8},{1,9},{2,10},{3,11},{4,12},{5,13},{6,14},{7,15},{8,0},{9,1},... | collective-permute-start | bytes 6152 | tf_op jit(solution)/shard_map/ppermute | solution.py:63

commit v6 on v5

v6 whole, which is shorter than its diff:
```python
import functools
import math

import jax
import jax.numpy as jnp
from jax import lax
from jax.experimental import pallas as pl
from jax.experimental.pallas import tpu as pltpu
from jax.sharding import PartitionSpec as P

D = 8192
FF = 14336
BLK = 128
NVAL = 4
TOK = 512
VAL = 512
AXES = ("dp", "seq")
HA = FF // 2
HG = D // 2
C1 = 3840
C2A = HA - C1
C2G = 512
C2 = C2A + C2G
C3G = HG - C2G
IDW = 128
C3 = C3G + IDW
MASKS = ((1, 3), (3, 1))


def coords(i):
    dp, seq = divmod(i, 8)
    c = dp % 2
    z = (dp // 2) % 4
    x = (seq // 4) * 2 + dp // 8
    return {"x": x, "y": seq % 4, "z": z, "c": c}


def index(p):
    dp = ((p["x"] % 2) * 4 + p["z"]) * 2 + p["c"]
    return dp * 8 + (p["x"] // 2) * 4 + p["y"]


def ring_pairs(axes, step):
    pairs = []
    for i in range(128):
        p = coords(i)
        for axis in axes:
            p[axis] ^= MASKS[p["c"]][step]
        pairs.append((i, index(p)))
    return pairs


def core_pairs():
    pairs = []
    for i in range(128):
        p = coords(i)
        p["c"] ^= 1
        pairs.append((i, index(p)))
    return pairs


def swap(x):
    return lax.ppermute(x, AXES, core_pairs())


def hop(x, axes, step):
    return lax.ppermute(x, AXES, ring_pairs(axes, step))


def double(x, axis, step):
    return jnp.stack([x, hop(x, axis, step)])


def pin(x):
    return pltpu.with_memory_space_constraint(x, pltpu.VMEM)


def gate(xs, *deps, space=pltpu.VMEM):
    n = len(xs)
    anyspec = pl.BlockSpec(memory_space=pl.ANY)
    return pl.pallas_call(
        lambda *refs: None,
        in_specs=[anyspec] * (n + len(deps)),
        out_specs=[anyspec] * n,
        out_shape=[jax.ShapeDtypeStruct(x.shape, x.dtype) for x in xs],
        input_output_aliases={i: i for i in range(n)},
        compiler_params=pltpu.CompilerParams(vmem_limit_bytes=1 << 20),
        cost_estimate=pl.CostEstimate(flops=0, bytes_accessed=0, transcendentals=0),
    )(*[pltpu.with_memory_space_constraint(x, space) for x in xs], *deps)


def nt(a, b):
    return lax.dot_general(a, b, (((1,), (1,)), ((), ())), preferred_element_type=jnp.float32)


def self_add(acc, ref):
    acc[0:256, :] += nt(ref[256:512, :], ref[0:256, :])
    acc[256:384, 0:128] += nt(ref[128:256, :], ref[0:128, :])
    acc[384:512, 0:128] += nt(ref[384:512, :], ref[256:384, :])


def self_first_body(x_ref, dep_ref, out_ref):
    @pl.when(pl.program_id(0) == 0)
    def _():
        out_ref[...] = jnp.zeros_like(out_ref)

    self_add(out_ref, x_ref)


def self_last_body(x_ref, first_ref, dep_ref, out_ref, acc, *, steps):
    i = pl.program_id(0)

    @pl.when(i == 0)
    def _():
        acc[...] = jnp.zeros_like(acc)

    self_add(acc, x_ref)

    @pl.when(i == steps - 1)
    def _():
        k = first_ref[...] * acc[...]
        rows = lax.broadcasted_iota(jnp.int32, (4, 4), 0)
        cols = lax.broadcasted_iota(jnp.int32, (4, 4), 1)
        out = jnp.zeros((4, 4), jnp.float32)
        spots = (
            (2, 0, 0, 0), (2, 1, 0, 128), (3, 0, 128, 0), (3, 1, 128, 128),
            (1, 0, 256, 0), (3, 2, 384, 0),
        )
        for b, c, r0, c0 in spots:
            s = jnp.sum(k[r0:r0 + 128, c0:c0 + 128])
            out = jnp.where((rows == b) & (cols == c), s, out)
        out_ref[...] = out / (float(BLK) * math.sqrt(float(FF) * float(D)))


KC = 2048


def self_call(x, dep, first=None):
    width = x.shape[1]
    half = pl.BlockSpec((512, 256), lambda i: (0, 0))
    anyspec = pl.BlockSpec(memory_space=pl.ANY)
    args = [x] + ([] if first is None else [first]) + [dep]
    body = self_first_body
    if first is not None:
        body = functools.partial(self_last_body, steps=width // KC)
    return pl.pallas_call(
        body,
        grid=(width // KC,),
        in_specs=[pl.BlockSpec((TOK, KC), lambda i: (0, i))]
        + ([] if first is None else [half]) + [anyspec],
        out_specs=half if first is None else pl.BlockSpec((4, 4), lambda i: (0, 0)),
        out_shape=jax.ShapeDtypeStruct((512, 256) if first is None else (4, 4), jnp.float32),
        scratch_shapes=[] if first is None else [pltpu.VMEM((512, 256), jnp.float32)],
        compiler_params=pltpu.CompilerParams(vmem_limit_bytes=16 << 20),
        cost_estimate=pl.CostEstimate(
            flops=2 * 512 * 256 * width, bytes_accessed=2 * TOK * width, transcendentals=0
        ),
    )(*args)


RUNS = ("y", "z", "x")
STEP5 = ("z", "x", "y")
STEP6 = ("x", "y", "z")
WEIGHT = {"x": 4, "y": 2, "z": 1}


def place(part, k, s4):
    n = s4 * WEIGHT[RUNS[part]]
    if k in (1, 3):
        n += WEIGHT[STEP5[part]]
    if k in (2, 3):
        n += WEIGHT[STEP6[part]]
    return n


WIDTHS = (C1, C2, C3)
STARTS = (0, C1, C1 + C2)
ALLW = C1 + C2 + C3
FULL = (
    (("a", 0, 0, C1),),
    (("a", C1, 0, C2A), ("g", 0, C2A, C2G)),
    (("g", C2G, 0, C3G),),
)
SETAT = ((0, 0, 0), (2048, 1792, 1792))
SETW = ((2048, 1792, 1792), (C1 - 2048, C2 - 1792, C3 - 1792))
SETS = (
    ((("a", 0, 0, 2048),), (("a", C1, 0, 1792),), (("g", C2G, 0, 1792),)),
    (
        (("a", 2048, 0, C1 - 2048),),
        (("a", C1 + 1792, 0, C2A - 1792), ("g", 0, C2A - 1792, C2G)),
        (("g", C2G + 1792, 0, C3G - 1792),),
    ),
)
SETMAX = 2048


class Train:
    def __init__(self, core_ref, acts, grads, half, parts, hbuf, sems):
        c = core_ref[0]
        o = c if half == 0 else 1 - c
        self.hbuf, self.todo = hbuf, []
        for part, segments in enumerate(parts):
            cps = []
            for i, (name, col, at, w) in enumerate(segments):
                src, step = (acts, HA) if name == "a" else (grads, HG)
                first = pl.multiple_of(o * step + col, 128)
                cps.append(pltpu.make_async_copy(
                    src.at[:, pl.ds(first, w)], hbuf.at[part, :, pl.ds(at, w)], sems.at[part, i]
                ))
            for cp in cps:
                cp.start()
            self.todo.append(cps)

    def wait(self, part):
        for cp in self.todo[part]:
            cp.wait()

    def get(self, part, at, w):
        return self.hbuf[part, :, at:at + w]


def cross_rows(part, segments, ks, pieces, train, ca, cg):
    train.wait(part)
    for name, _, at, w in segments:
        acc = ca if name == "a" else cg
        rows = [p[:, :, :, at:at + w].reshape(128, w) for p in pieces]
        x = nt(jnp.concatenate(rows, axis=0), train.get(part, at, w))
        for i, k in enumerate(ks):
            for s4 in range(2):
                r = i * 128 + s4 * 64
                acc[place(part, k, s4)] += x[r:r + 64].reshape(8, 8, TOK)


def val_rows(core_ref, blocks, ka, kg, name, seen):
    even = jnp.concatenate([x[:32] for x in blocks], axis=0)
    late = jnp.concatenate(blocks[4:], axis=0)
    y = nt(jnp.where(core_ref[0] == 0, even, late), jnp.concatenate(blocks, axis=0))
    acc = ka if name == "a" else kg
    if name in seen:
        acc[...] += y
    else:
        acc[...] = y
        seen.add(name)


def early_body(core_ref, acts, grads, dep_ref, *refs):
    own = [refs[p * 2:p * 2 + 2] for p in range(3)]
    ca, cg, tok, hbuf, sems = refs[6:]
    train = Train(core_ref, acts, grads, 0, FULL, hbuf, sems)
    tok[...] = jnp.zeros_like(tok)
    ca[...] = jnp.zeros_like(ca)
    cg[...] = jnp.zeros_like(cg)
    for part in range(3):
        cross_rows(part, FULL[part], (0, 1), own[part], train, ca, cg)


def bring(moves, sems):
    cps = [pltpu.make_async_copy(x, y, sems.at[i]) for i, (x, y) in enumerate(moves)]
    for cp in cps:
        cp.start()
    return cps


def late_own_body(core_ref, acts, grads, *refs, which):
    pieces = [refs[p * 3:p * 3 + 3] for p in range(3)]
    n = 2 + 2 * which
    ins, refs = refs[9:9 + n], refs[9 + n:]
    ca, cg, ka, kg = refs[:4]
    if which:
        ids = refs[4]
    hbuf, sems, pbuf, psems, asems = refs[4 + which:]
    sums = bring(list(zip(ins, (ca, cg, ka, kg))), asems)
    todo = []
    for part in range(3):
        x, a1, last = pieces[part]
        w = SETW[which][part]
        cols = pl.ds(SETAT[which][part], w)
        srcs = (x.at[:, :, :, cols], a1.at[:, :, :, cols], last.at[0], last.at[1])
        todo.append(bring(
            [(src, pbuf.at[part, k, :, :, :, pl.ds(0, w)]) for k, src in enumerate(srcs)],
            psems.at[part],
        ))
    train = Train(core_ref, acts, grads, 0, SETS[which], hbuf, sems)
    seen = {"a", "g"} if which else set()
    for part in range(3):
        for cp in todo[part]:
            cp.wait()
        if part == 0:
            for cp in sums:
                cp.wait()

        def blocks(at, w):
            out = [None] * 8
            for k in range(4):
                for s4 in range(2):
                    out[place(part, k, s4)] = pbuf[part, k, s4, :, :, at:at + w].reshape(64, w)
            return out

        for name, _, at, w in SETS[which][part]:
            val_rows(core_ref, blocks(at, w), ka, kg, name, seen)
        if which and part == 2:
            for b, x in enumerate(blocks(SETW[1][2] - IDW, IDW)):
                ids[b * 64:b * 64 + 64, :] = x.astype(jnp.float32)
        cross_rows(
            part, SETS[which][part], (2, 3), [pbuf.at[part, 2], pbuf.at[part, 3]], train, ca, cg
        )


def late_other_body(core_ref, acts, grads, o0, o1, o2, o3, o4, ain, gin, k1, k2, *refs, which):
    c = core_ref[0]
    lasts = (o2, o3, o4)
    if which:
        idin, raw_ref, norm_ref, hbuf, sems, vbuf, acc_a, acc_g, ka, kg, ids, vsems, asems = refs
        extra = [(idin, ids)]
    else:
        acc_a, acc_g, ka, kg, tok, hbuf, sems, vbuf, vsems, asems = refs
        tok[...] = jnp.zeros_like(tok)
        extra = []
    sums = bring([(ain, acc_a), (gin, acc_g), (k1, ka), (k2, kg)] + extra, asems)
    todo = []
    for part in range(3):
        w = SETW[which][part]
        cols = pl.ds(STARTS[part] + SETAT[which][part], w)
        todo.append(bring(
            [
                (
                    o.at[s4, :, :, cols] if k < 2 else o.at[s4],
                    vbuf.at[part, :, place(part, k, s4), :, pl.ds(0, w)],
                )
                for k, o in enumerate((o0, o1, lasts[part].at[0], lasts[part].at[1]))
                for s4 in range(2)
            ],
            vsems.at[part],
        ))
    train = Train(core_ref, acts, grads, 1, SETS[which], hbuf, sems)
    seen = {"a", "g"}
    for part in range(3):
        for cp in todo[part]:
            cp.wait()
        if part == 0:
            for cp in sums:
                cp.wait()
        for name, _, at, w in SETS[which][part]:
            blocks = [vbuf[part, b, :, :, at:at + w].reshape(64, w) for b in range(8)]
            val_rows(core_ref, blocks, ka, kg, name, seen)
        train.wait(part)
        for name, _, at, w in SETS[which][part]:
            acc = acc_a if name == "a" else acc_g
            rows = vbuf[part, :, :, :, at:at + w].reshape(VAL, w)
            acc[...] += nt(rows, train.get(part, at, w)).reshape(8, 8, 8, TOK)
    if not which:
        return

    cross = acc_a[...].reshape(VAL, TOK) * acc_g[...].reshape(VAL, TOK)
    kern = ka[...] * kg[...]
    all_ids = ids[...]
    row_ids = jnp.transpose(all_ids)[0:1, :]
    even = jnp.concatenate([all_ids[b * 64:b * 64 + 32] for b in range(8)], axis=0)
    half_ids = jnp.where(c == 0, even, all_ids[256:512])
    for v in range(NVAL):
        keep = jnp.where(all_ids == float(v), 1.0, 0.0)
        keep = jnp.concatenate([keep] * 4, axis=1)
        raw_ref[v:v + 1, :] = jnp.sum(cross * keep, axis=0, keepdims=True)
        keep = jnp.where(half_ids == float(v), 1.0, 0.0)
        keep = jnp.concatenate([keep] * 4, axis=1)
        part = jnp.sum(kern * keep, axis=0, keepdims=True)
        part = jnp.sum(jnp.where(row_ids == float(v), part, 0.0))
        norm_ref[v:v + 1, :] = jnp.full((1, 128), part, jnp.float32)


ACC = jax.ShapeDtypeStruct((8, 8, 8, TOK), jnp.float32)
KERN = jax.ShapeDtypeStruct((VAL // 2, VAL), jnp.float32)


TOKEN = jax.ShapeDtypeStruct((8, 128), jnp.float32)
IDS = jax.ShapeDtypeStruct((VAL, IDW), jnp.float32)


def local_call(body, core, acts, grads, args, outs, flops, width, scratch=(), pinned=(), mib=26):
    vmem = pl.BlockSpec(memory_space=pltpu.VMEM)
    anyspec = pl.BlockSpec(memory_space=pl.ANY)
    return pl.pallas_call(
        body,
        in_specs=[pl.BlockSpec(memory_space=pltpu.SMEM)] + [anyspec] * 2
        + [vmem if i in pinned else anyspec for i in range(len(args))],
        out_specs=[vmem] * len(outs),
        out_shape=outs,
        scratch_shapes=[
            pltpu.VMEM((3, TOK, width), jnp.bfloat16),
            pltpu.SemaphoreType.DMA((3, 2)),
        ] + list(scratch),
        compiler_params=pltpu.CompilerParams(vmem_limit_bytes=mib << 20),
        cost_estimate=pl.CostEstimate(
            flops=flops, bytes_accessed=TOK * (FF + D), transcendentals=0
        ),
    )(core, acts, grads, *[pin(x) if i in pinned else x for i, x in enumerate(args)])


def shards(hidden_acts, out_grads, val_acts, val_grads, val_ids):
    hidden_acts = pltpu.with_memory_space_constraint(hidden_acts, pltpu.HBM)
    out_grads = pltpu.with_memory_space_constraint(out_grads, pltpu.HBM)
    core = lax.axis_index("dp") % 2
    first = core == 0
    idcol = jnp.broadcast_to(val_ids[:, None].astype(jnp.bfloat16), (4, IDW))
    halves = [
        jnp.concatenate(
            [val_acts[:, h * HA:(h + 1) * HA], val_grads[:, h * HG:(h + 1) * HG], idcol], axis=1
        )
        for h in range(2)
    ]
    keep = jnp.where(first, halves[0], halves[1])
    got = swap(jnp.where(first, halves[1], halves[0]))
    rows = jnp.concatenate([jnp.where(first, keep, got), jnp.where(first, got, keep)], axis=0)

    near = [
        hop(rows, [a for a in "xyz" if n & WEIGHT[a]], 0) for n in (1, 2, 4, 3, 5, 6, 7)
    ]
    rows = jnp.stack([rows, near[0], near[1], near[3], near[2], near[4], near[5], near[6]])
    sg = self_call(out_grads, rows)
    x = [double(rows[..., s:s + w], RUNS[j], 1) for j, (s, w) in enumerate(zip(STARTS, WIDTHS))]
    x = gate(x, sg)
    block_gram = self_call(hidden_acts, x[1], sg)
    a1 = [hop(x[j], STEP5[j], 1) for j in range(3)]
    o0 = swap(gate([jnp.concatenate(x, axis=-1)], sg)[0])
    pair = gate([jnp.stack([x[j], a1[j]]) for j in range(3)], block_gram, o0)
    last = [
        [hop(pair[j][..., a:a + w], STEP6[j], 1) for j, (a, w) in enumerate(zip(at, width))]
        for at, width in zip(SETAT, SETW)
    ]
    o1 = swap(gate([jnp.concatenate(a1, axis=-1)], sg)[0])
    call = functools.partial(
        local_call, core=core.reshape(1).astype(jnp.int32), acts=hidden_acts, grads=out_grads
    )
    unit = 512 * (HA + HG)
    ca, cg, tok = call(
        early_body, args=[block_gram] + [y for j in range(3) for y in (x[j], a1[j])],
        outs=[ACC, ACC, TOKEN], flops=512 * unit, width=C1, pinned=range(1, 7), mib=28,
    )
    sums = [ca, cg]
    for which in range(2):
        got = [gate([y], tok, *([] if which else [o1]))[0] for y in last[which]]
        swapped = [swap(y) for y in got]
        sums = call(
            functools.partial(late_own_body, which=which),
            args=[y for j in range(3) for y in (x[j], a1[j], got[j])] + list(sums),
            outs=[ACC, ACC, KERN, KERN] + [IDS] * which, flops=512 * unit, width=SETMAX,
            scratch=[
                pltpu.VMEM((3, 4, 2, 8, 8, SETMAX), jnp.bfloat16),
                pltpu.SemaphoreType.DMA((3, 4)),
                pltpu.SemaphoreType.DMA((4,)),
            ],
        )
        outs = [ACC, ACC, KERN, KERN, TOKEN]
        scratch = [pltpu.VMEM((3, 8, 8, 8, SETMAX), jnp.bfloat16)]
        if which:
            outs = [
                jax.ShapeDtypeStruct((NVAL, TOK), jnp.float32),
                jax.ShapeDtypeStruct((NVAL, 128), jnp.float32),
            ]
            scratch += [pltpu.VMEM(a.shape, a.dtype) for a in (ACC, ACC, KERN, KERN, IDS)]
        outs = call(
            functools.partial(late_other_body, which=which),
            args=[o0, o1] + swapped + list(sums), outs=outs, flops=768 * unit, width=SETMAX,
            scratch=scratch + [
                pltpu.SemaphoreType.DMA((3, 8)),
                pltpu.SemaphoreType.DMA((5,)),
            ],
        )
        sums, tok = outs[:4], outs[-1]
    raw, norm = outs
    norm = norm + swap(norm)
    token_scores = raw * lax.rsqrt(norm[:, :1] + 1e-06)
    return (token_scores, block_gram)


def solution(mesh):
    return jax.shard_map(
        shards,
        mesh=mesh,
        in_specs=(
            P(AXES, None),
            P(AXES, None),
            P(AXES, None),
            P(AXES, None),
            P(AXES),
        ),
        out_specs=(P(None, AXES), P(AXES, None)),
        check_vma=False,
    )
```

time: 127 us -> 139 us (1.094)
  waiting for transfers between devices: 22 us -> 38.2 us
  local copies, waits for them, and re-layouts: 10.9 us -> 3.06 us
  other arithmetic: 7.87 us -> 3.08 us
  starting transfers between devices: 40 us -> 44.5 us
  Pallas kernels: 44.8 us -> 48.9 us
    ppermute x16 -> x19, waiting for transfers between devices: 20.3 us -> 36.4 us  [hop(): return lax.ppermute(x, AXES, ring_pairs(axes, step))]
    unnamed x40 -> x8, local copies, waits for them, and re-layouts: 8.96 us -> 0.6 us
    pallas_call x3 -> x5, Pallas kernels: 28.9 us -> 33.1 us  [local_call(): pl.pallas_call(body, in_specs=[pl.BlockSpec(memory_space=pltpu.SMEM)] + [...]
    concatenate x1 -> x0, other arithmetic: 3.15 us -> none  [shards(): o2 = swap(gate([jnp.concatenate(last, axis=-1)], tok, o1)[0])]
    ppermute x5 -> x10, starting transfers between devices: 17.7 us -> 20.5 us  [swap(): return lax.ppermute(x, AXES, core_pairs())]
    ppermute x16 -> x19, starting transfers between devices: 22.4 us -> 24.1 us  [hop(): return lax.ppermute(x, AXES, ring_pairs(axes, step))]
    concatenate x1, other arithmetic: 1.83 us -> 0.19 us  [shards(): o1 = swap(gate([jnp.concatenate(a1, axis=-1)], sg)[0])]
  transfers between devices with their start and end apart: 21 -> 29, of which waited for: 9 -> 12; matrix products, arithmetic and copies ran while one was open for 5% -> 1% of each run, Pallas kernels for 25% -> 30%
where the time goes in v6:
time: 139 us
  Pallas kernels  48.9 us (35%)
  starting transfers between devices  44.5 us (32%)
  waiting for transfers between devices  38.2 us (27%)
  other arithmetic  3.08 us (2%)
  local copies, waits for them, and re-layouts  3.06 us (2%)
    ppermute x19, waiting for transfers between devices, hop(): return lax.ppermute(x, AXES, ring_pairs(axes, step))  36.4 us
    pallas_call x5, Pallas kernels, local_call(): pl.pallas_call(body, in_specs=[pl.BlockSpec(memory_space=pltpu.SMEM)] + [...  33.1 us
    ppermute x19, starting transfers between devices, hop(): return lax.ppermute(x, AXES, ring_pairs(axes, step))  24.1 us
    ppermute x10, starting transfers between devices, swap(): return lax.ppermute(x, AXES, core_pairs())  20.5 us
    pallas_call x2, Pallas kernels, self_call(): pl.pallas_call(body, grid=(width // KC,), in_specs=[pl.BlockSpec((TOK, KC...  15.8 us
  transfers between devices with their start and end apart: 29, of which 12 were waited for; matrix products, arithmetic and copies ran while one was open for 1% of the time, Pallas kernels for 30%

profile of v6, /device:TPU:1, one launch (start us, length us, event | category | flops | bytes accessed | tf_op | source)
XLA Modules:
  0.0 138.9 jit_solution(3622831793609301424)
XLA Ops:
  0.6 0.7 convert_element_type.4
  1.3 0.8 fusion.1
  2.1 0.9 fusion
  3.2 1.5 %collective-permute-start = (bf16[4,11392]{1,0:T(4,128)(2,1)S(1)}, bf16[4,11392]{1,0:T(4,128)(2,1)S(1)}, u32[]{:S(2)}, u32[]{:S(2)}) collective-permute-start(bf16[4,11392]{1,0:T(4,128)(2,1)S(1)} %broadcast_select_fusion.2), channel_id=1, source_target_pairs={{0,8},{1,9},{2,10},{3,11},{4,12},{5,13},{6,14},{7,15},{8,0},{9,1},... | collective-permute-start | bytes 273416 | tf_op jit(solution)/shard_map/ppermute | solution.py:63
  4.7 0.9 collective-permute-done
  5.8 5.1 %collective-permute-start.6 = (bf16[8,11392]{1,0:T(8,128)(2,1)S(1)}, bf16[8,11392]{1,0:T(8,128)(2,1)S(1)}, u32[]{:S(2)}, u32[]{:S(2)}) collective-permute-start(bf16[8,11392]{1,0:T(8,128)(2,1)S(1)} %pad_maximum_fusion.8), channel_id=1, source_target_pairs={{0,65},{1,64},{2,67},{3,66},{4,69},{5,68},{6,71},{7,70},{8,79},{9,... | collective-permute-start | bytes 546824 | tf_op jit(solution)/shard_map/ppermute | solution.py:67
  10.9 3.7 %collective-permute-start.5 = (bf16[8,11392]{1,0:T(8,128)(2,1)S(1)}, bf16[8,11392]{1,0:T(8,128)(2,1)S(1)}, u32[]{:S(2)}, u32[]{:S(2)}) collective-permute-start(bf16[8,11392]{1,0:T(8,128)(2,1)S(1)} %pad_maximum_fusion.8), channel_id=1, source_target_pairs={{0,80},{1,81},{2,82},{3,83},{4,84},{5,85},{6,86},{7,87},{8,124},{9... | collective-permute-start | bytes 546824 | tf_op jit(solution)/shard_map/ppermute | solution.py:67
  14.6 2.5 %collective-permute-start.4 = (bf16[8,11392]{1,0:T(8,128)(2,1)S(1)}, bf16[8,11392]{1,0:T(8,128)(2,1)S(1)}, u32[]{:S(2)}, u32[]{:S(2)}) collective-permute-start(bf16[8,11392]{1,0:T(8,128)(2,1)S(1)} %pad_maximum_fusion.8), channel_id=1, source_target_pairs={{0,64},{1,65},{2,66},{3,67},{4,68},{5,69},{6,70},{7,71},{8,76},{9,... | collective-permute-start | bytes 546824 | tf_op jit(solution)/shard_map/ppermute | solution.py:67
  17.1 2.3 %collective-permute-start.1 = (bf16[8,11392]{1,0:T(8,128)(2,1)S(1)}, bf16[8,11392]{1,0:T(8,128)(2,1)S(1)}, u32[]{:S(2)}, u32[]{:S(2)}) collective-permute-start(bf16[8,11392]{1,0:T(8,128)(2,1)S(1)} %pad_maximum_fusion.8), channel_id=1, source_target_pairs={{0,16},{1,17},{2,18},{3,19},{4,20},{5,21},{6,22},{7,23},{8,56},{9,... | collective-permute-start | bytes 546824 | tf_op jit(solution)/shard_map/ppermute | solution.py:67
  19.5 3.7 %collective-permute-done.1 = bf16[8,11392]{1,0:T(8,128)(2,1)S(1)} collective-permute-done((bf16[8,11392]{1,0:T(8,128)(2,1)S(1)}, bf16[8,11392]{1,0:T(8,128)(2,1)S(1)}, u32[]{:S(2)}, u32[]{:S(2)}) %collective-permute-start.1) | collective-permute-done | bytes 182304 | tf_op jit(solution)/shard_map/ppermute | solution.py:67
  23.1 3.5 %collective-permute-start.2 = (bf16[8,11392]{1,0:T(8,128)(2,1)S(1)}, bf16[8,11392]{1,0:T(8,128)(2,1)S(1)}, u32[]{:S(2)}, u32[]{:S(2)}) collective-permute-start(bf16[8,11392]{1,0:T(8,128)(2,1)S(1)} %pad_maximum_fusion.8), channel_id=1, source_target_pairs={{0,1},{1,0},{2,3},{3,2},{4,5},{5,4},{6,7},{7,6},{8,11},{9,10},{10,... | collective-permute-start | bytes 546824 | tf_op jit(solution)/shard_map/ppermute | solution.py:67
  26.7 2.9 %collective-permute-done.2 = bf16[8,11392]{1,0:T(8,128)(2,1)S(1)} collective-permute-done((bf16[8,11392]{1,0:T(8,128)(2,1)S(1)}, bf16[8,11392]{1,0:T(8,128)(2,1)S(1)}, u32[]{:S(2)}, u32[]{:S(2)}) %collective-permute-start.2) | collective-permute-done | bytes 182304 | tf_op jit(solution)/shard_map/ppermute | solution.py:67
  29.5 3.4 %collective-permute-start.7 = (bf16[8,11392]{1,0:T(8,128)(2,1)S(1)}, bf16[8,11392]{1,0:T(8,128)(2,1)S(1)}, u32[]{:S(2)}, u32[]{:S(2)}) collective-permute-start(bf16[8,11392]{1,0:T(8,128)(2,1)S(1)} %pad_maximum_fusion.8), channel_id=1, source_target_pairs={{0,81},{1,80},{2,83},{3,82},{4,85},{5,84},{6,87},{7,86},{8,127},{9... | collective-permute-start | bytes 546824 | tf_op jit(solution)/shard_map/ppermute | solution.py:67
  33.1 6.3 %collective-permute-done.7 = bf16[8,11392]{1,0:T(8,128)(2,1)S(1)} collective-permute-done((bf16[8,11392]{1,0:T(8,128)(2,1)S(1)}, bf16[8,11392]{1,0:T(8,128)(2,1)S(1)}, u32[]{:S(2)}, u32[]{:S(2)}) %collective-permute-start.7) | collective-permute-done | bytes 182304 | tf_op jit(solution)/shard_map/ppermute | solution.py:67
  39.5 0.1 slice_bitcast_fusion.1
  39.8 5.6 %shard_map.68.refs_3_.refs_1_.first_ref = f32[512,256]{1,0:T(8,128)S(1)} custom-call(bf16[512,8192]{1,0:T(8,128)(2,1)} %grads.9, bf16[8,8,11392]{2,1,0:T(8,128)(2,1)S(1)} %bitcast_dynamic-update-slice_fusion.dep_ref), custom_call_target="tpu_custom_call" | custom-call | flops 2147483648 | bytes 8388608 | tf_op jit(solution)/shard_map/pallas_call | solution.py:146
  45.5 1.5 %collective-permute-done.10 = bf16[8,8,3712]{2,1,0:T(8,128)(2,1)S(1)} collective-permute-done((bf16[8,8,3712]{2,1,0:T(8,128)(2,1)S(1)}, bf16[8,8,3712]{2,1,0:T(8,128)(2,1)S(1)}, u32[]{:S(2)}, u32[]{:S(2)}) %collective-permute-start.10) | collective-permute-done | bytes 475168 | tf_op jit(solution)/shard_map/ppermute | solution.py:67
  47.1 0.3 collective-permute-done.9
  47.5 5.9 %collective-permute-done.8 = bf16[8,8,3840]{2,1,0:T(8,128)(2,1)S(1)} collective-permute-done((bf16[8,8,3840]{2,1,0:T(8,128)(2,1)S(1)}, bf16[8,8,3840]{2,1,0:T(8,128)(2,1)S(1)}, u32[]{:S(2)}, u32[]{:S(2)}) %collective-permute-start.8) | collective-permute-done | bytes 491552 | tf_op jit(solution)/shard_map/ppermute | solution.py:67
  53.7 1.3 collective-permute-start.12
  54.9 1.4 collective-permute-start.13
  56.3 0.2 pad_maximum_fusion.refs_0_
  56.5 2.1 %collective-permute-start.11 = (bf16[2,8,8,11392]{3,2,1,0:T(8,128)(2,1)S(1)}, bf16[2,8,8,11392]{3,2,1,0:T(8,128)(2,1)S(1)}, u32[]{:S(2)}, u32[]{:S(2)}) collective-permute-start(bf16[2,8,8,11392]{3,2,1,0:T(8,128)(2,1)S(1)} %shard_map.70), channel_id=1, source_target_pairs={{0,8},{1,9},{2,10},{3,11},{4,12},{5,13},{6,14},{7,15},{8,0},{9,1},... | collective-permute-start | bytes 8749064 | tf_op jit(solution)/shard_map/ppermute | solution.py:63
  58.6 7.9 %collective-permute-done.14.refs_5_.refs_7_ = bf16[2,8,8,3712]{3,2,1,0:T(8,128)(2,1)S(1)} collective-permute-done((bf16[2,8,8,3712]{3,2,1,0:T(8,128)(2,1)S(1)}, bf16[2,8,8,3712]{3,2,1,0:T(8,128)(2,1)S(1)}, u32[]{:S(2)}, u32[]{:S(2)}) %collective-permute-start.14) | collective-permute-done | bytes 950304 | tf_op jit(solution)/shard_map/ppermute | solution.py:67
  66.5 0.4 collective-permute-done.12.refs_1_
  67.0 1.2 collective-permute-done.13.refs_3_.refs_4_
  68.2 0.2 pad_maximum_fusion.1.refs_0_
  68.4 4.6 %collective-permute-start.15 = (bf16[2,8,8,11392]{3,2,1,0:T(8,128)(2,1)S(1)}, bf16[2,8,8,11392]{3,2,1,0:T(8,128)(2,1)S(1)}, u32[]{:S(2)}, u32[]{:S(2)}) collective-permute-start(bf16[2,8,8,11392]{3,2,1,0:T(8,128)(2,1)S(1)} %shard_map.71), channel_id=1, source_target_pairs={{0,8},{1,9},{2,10},{3,11},{4,12},{5,13},{6,14},{7,15},{8,0},{9,1},... | collective-permute-start | bytes 8749064 | tf_op jit(solution)/shard_map/ppermute | solution.py:63
  73.0 10.2 %shard_map.72.refs_3_.dep_ref = f32[4,4]{1,0:T(4,128)} custom-call(bf16[512,14336]{1,0:T(8,128)(2,1)} %acts.9, f32[512,256]{1,0:T(8,128)S(1)} %shard_map.68.refs_3_.refs_1_.first_ref, bf16[2,8,8,3840]{3,2,1,0:T(8,128)(2,1)S(1)} %get-tuple-element.28.dep_ref.refs_2_.refs_3_), custom_call_target="tpu_custom_call" | custom-call | flops 3758096384 | bytes 14680064 | tf_op jit(solution)/shard_map/pallas_call | solution.py:146
  83.2 0.2 pad_maximum_fusion.4.refs_2_
  83.4 0.2 pad_maximum_fusion.3.refs_1_
  83.6 0.2 pad_maximum_fusion.2.refs_0_
  83.8 0.5 copy-done
  84.7 0.1 collective-permute-start.21
  84.8 5.9 %shard_map.74 = (f32[8,8,8,512]{3,2,1,0:T(8,128)S(1)}, f32[8,8,8,512]{3,2,1,0:T(8,128)S(1)}, f32[8,128]{1,0:T(8,128)S(1)}) custom-call(s32[1]{0:T(128)} %bitcast.core_ref, bf16[512,14336]{1,0:T(8,128)(2,1)} %acts.9, bf16[512,8192]{1,0:T(8,128)(2,1)} %grads.9, f32[4,4]{1,0:T(4,128)S(1)} %copy-done, bf16[2,8,8,3840]{3,2,1,0:T(8,128)(2,1)S(1)} %get-tuple-element.27.refs_0_, ...), custom_call_target="tpu_custom_call" | custom-call | flops 2952790016 | bytes 11534336 | tf_op jit(solution)/shard_map/pallas_call | solution.py:382
  90.7 6.2 %collective-permute-done.19.refs_0_ = bf16[2,2,8,8,1792]{4,3,2,1,0:T(8,128)(2,1)S(1)} collective-permute-done((bf16[2,2,8,8,1792]{4,3,2,1,0:T(8,128)(2,1)S(1)}, bf16[2,2,8,8,1792]{4,3,2,1,0:T(8,128)(2,1)S(1)}, u32[]{:S(2)}, u32[]{:S(2)}) %collective-permute-start.19) | collective-permute-done | bytes 917536 | tf_op jit(solution)/shard_map/ppermute | solution.py:67
  97.0 2.1 %collective-permute-start.20 = (bf16[2,2,8,8,1792]{4,3,2,1,0:T(8,128)(2,1)S(1)}, bf16[2,2,8,8,1792]{4,3,2,1,0:T(8,128)(2,1)S(1)}, u32[]{:S(2)}, u32[]{:S(2)}) collective-permute-start(bf16[2,2,8,8,1792]{4,3,2,1,0:T(8,128)(2,1)S(1)} %shard_map.76.refs_5_), channel_id=1, source_target_pairs={{0,8},{1,9},{2,10},{3,11},{4,12},{5,13},{6,14},{7,15},{8,0},{9,1},... | collective-permute-start | bytes 2752520 | tf_op jit(solution)/shard_map/ppermute | solution.py:63
  99.1 2.6 %collective-permute-start.18 = (bf16[2,2,8,8,2048]{4,3,2,1,0:T(8,128)(2,1)S(1)}, bf16[2,2,8,8,2048]{4,3,2,1,0:T(8,128)(2,1)S(1)}, u32[]{:S(2)}, u32[]{:S(2)}) collective-permute-start(bf16[2,2,8,8,2048]{4,3,2,1,0:T(8,128)(2,1)S(1)} %shard_map.75.refs_2_), channel_id=1, source_target_pairs={{0,8},{1,9},{2,10},{3,11},{4,12},{5,13},{6,14},{7,15},{8,0},{9,1},... | collective-permute-start | bytes 3145736 | tf_op jit(solution)/shard_map/ppermute | solution.py:63
  102.1 0.1 collective-permute-start.26
  102.4 5.8 %shard_map.78 = (f32[8,8,8,512]{3,2,1,0:T(8,128)S(1)}, f32[8,8,8,512]{3,2,1,0:T(8,128)S(1)}, f32[256,512]{1,0:T(8,128)S(1)}, f32[256,512]{1,0:T(8,128)S(1)}) custom-call(s32[1]{0:T(128)} %bitcast.core_ref, bf16[512,14336]{1,0:T(8,128)(2,1)} %acts.9, bf16[512,8192]{1,0:T(8,128)(2,1)} %grads.9, bf16[2,8,8,3840]{3,2,1,0:T(8,128)(2,1)S(1)} %get-tuple-element.27.refs_0_, ...), custom_call_target="tpu_custom_call" | custom-call | flops 2952790016 | bytes 11534336 | tf_op jit(solution)/shard_map/pallas_call | solution.py:382
  108.3 7.7 %shard_map.79 = (f32[8,8,8,512]{3,2,1,0:T(8,128)S(1)}, f32[8,8,8,512]{3,2,1,0:T(8,128)S(1)}, f32[256,512]{1,0:T(8,128)S(1)}, f32[256,512]{1,0:T(8,128)S(1)}, f32[8,128]{1,0:T(8,128)S(1)}) custom-call(s32[1]{0:T(128)} %bitcast.core_ref, bf16[512,14336]{1,0:T(8,128)(2,1)} %acts.9, bf16[512,8192]{1,0:T(8,128)(2,1)} %grads.9, ...), custom_call_target="tpu_custom_call" | custom-call | flops 4429185024 | bytes 11534336 | tf_op jit(solution)/shard_map/pallas_call | solution.py:382
  116.0 6.6 %collective-permute-start.25 = (bf16[2,2,8,8,2048]{4,3,2,1,0:T(8,128)(2,1)S(1)}, bf16[2,2,8,8,2048]{4,3,2,1,0:T(8,128)(2,1)S(1)}, u32[]{:S(2)}, u32[]{:S(2)}) collective-permute-start(bf16[2,2,8,8,2048]{4,3,2,1,0:T(8,128)(2,1)S(1)} %shard_map.81.refs_5_), channel_id=1, source_target_pairs={{0,8},{1,9},{2,10},{3,11},{4,12},{5,13},{6,14},{7,15},{8,0},{9,1},... | collective-permute-start | bytes 3145736 | tf_op jit(solution)/shard_map/ppermute | solution.py:63
  122.7 0.4 collective-permute-start.23
  123.1 5.8 %shard_map.83 = (f32[8,8,8,512]{3,2,1,0:T(8,128)S(1)}, f32[8,8,8,512]{3,2,1,0:T(8,128)S(1)}, f32[256,512]{1,0:T(8,128)S(1)}, f32[256,512]{1,0:T(8,128)S(1)}, f32[512,128]{1,0:T(8,128)S(1)}) custom-call(s32[1]{0:T(128)} %bitcast.core_ref, bf16[512,14336]{1,0:T(8,128)(2,1)} %acts.9, bf16[512,8192]{1,0:T(8,128)(2,1)} %grads.9, ...), custom_call_target="tpu_custom_call" | custom-call | flops 2952790016 | bytes 11534336 | tf_op jit(solution)/shard_map/pallas_call | solution.py:382
  128.9 7.9 %shard_map.84 = (f32[4,512]{1,0:T(4,128)S(1)}, f32[4,128]{1,0:T(4,128)S(1)}) custom-call(s32[1]{0:T(128)} %bitcast.core_ref, bf16[512,14336]{1,0:T(8,128)(2,1)} %acts.9, bf16[512,8192]{1,0:T(8,128)(2,1)} %grads.9, bf16[2,8,8,11392]{3,2,1,0:T(8,128)(2,1)S(1)} %collective-permute-done.11.refs_4_.o0, ...), custom_call_target="tpu_custom_call" | custom-call | flops 4429185024 | bytes 11534336 | tf_op jit(solution)/shard_map/pallas_call | solution.py:382
  136.8 0.4 collective-permute-start.28
  137.2 0.9 collective-permute-done.28
  138.2 0.7 broadcast_multiply_fusion
  (63 shorter events, 2.5 us)
Async XLA Ops:
  3.2 2.4 %collective-permute-start = (bf16[4,11392]{1,0:T(4,128)(2,1)S(1)}, bf16[4,11392]{1,0:T(4,128)(2,1)S(1)}, u32[]{:S(2)}, u32[]{:S(2)}) collective-permute-start(bf16[4,11392]{1,0:T(4,128)(2,1)S(1)} %broadcast_select_fusion.2), channel_id=1, source_target_pairs={{0,8},{1,9},{2,10},{3,11},{4,12},{5,13},{6,14},{7,15},{8,0},{9,1},... | collective-permute-start | bytes 273416 | tf_op jit(solution)/shard_map/ppermute | solution.py:63
  5.8 27.2 %collective-permute-start.6 = (bf16[8,11392]{1,0:T(8,128)(2,1)S(1)}, bf16[8,11392]{1,0:T(8,128)(2,1)S(1)}, u32[]{:S(2)}, u32[]{:S(2)}) collective-permute-start(bf16[8,11392]{1,0:T(8,128)(2,1)S(1)} %pad_maximum_fusion.8), channel_id=1, source_target_pairs={{0,65},{1,64},{2,67},{3,66},{4,69},{5,68},{6,71},{7,70},{8,79},{9,... | collective-permute-start | bytes 546824 | tf_op jit(solution)/shard_map/ppermute | solution.py:67
  10.9 22.1 %collective-permute-start.5 = (bf16[8,11392]{1,0:T(8,128)(2,1)S(1)}, bf16[8,11392]{1,0:T(8,128)(2,1)S(1)}, u32[]{:S(2)}, u32[]{:S(2)}) collective-permute-start(bf16[8,11392]{1,0:T(8,128)(2,1)S(1)} %pad_maximum_fusion.8), channel_id=1, source_target_pairs={{0,80},{1,81},{2,82},{3,83},{4,84},{5,85},{6,86},{7,87},{8,124},{9... | collective-permute-start | bytes 546824 | tf_op jit(solution)/shard_map/ppermute | solution.py:67
  14.6 18.4 %collective-permute-start.4 = (bf16[8,11392]{1,0:T(8,128)(2,1)S(1)}, bf16[8,11392]{1,0:T(8,128)(2,1)S(1)}, u32[]{:S(2)}, u32[]{:S(2)}) collective-permute-start(bf16[8,11392]{1,0:T(8,128)(2,1)S(1)} %pad_maximum_fusion.8), channel_id=1, source_target_pairs={{0,64},{1,65},{2,66},{3,67},{4,68},{5,69},{6,70},{7,71},{8,76},{9,... | collective-permute-start | bytes 546824 | tf_op jit(solution)/shard_map/ppermute | solution.py:67
  17.1 15.9 %collective-permute-start.3 = (bf16[8,11392]{1,0:T(8,128)(2,1)S(1)}, bf16[8,11392]{1,0:T(8,128)(2,1)S(1)}, u32[]{:S(2)}, u32[]{:S(2)}) collective-permute-start(bf16[8,11392]{1,0:T(8,128)(2,1)S(1)} %pad_maximum_fusion.8), channel_id=1, source_target_pairs={{0,17},{1,16},{2,19},{3,18},{4,21},{5,20},{6,23},{7,22},{8,59},{9,... | collective-permute-start | bytes 546824 | tf_op jit(solution)/shard_map/ppermute | solution.py:67
  17.1 6.1 %collective-permute-start.1 = (bf16[8,11392]{1,0:T(8,128)(2,1)S(1)}, bf16[8,11392]{1,0:T(8,128)(2,1)S(1)}, u32[]{:S(2)}, u32[]{:S(2)}) collective-permute-start(bf16[8,11392]{1,0:T(8,128)(2,1)S(1)} %pad_maximum_fusion.8), channel_id=1, source_target_pairs={{0,16},{1,17},{2,18},{3,19},{4,20},{5,21},{6,22},{7,23},{8,56},{9,... | collective-permute-start | bytes 546824 | tf_op jit(solution)/shard_map/ppermute | solution.py:67
  23.1 6.4 %collective-permute-start.2 = (bf16[8,11392]{1,0:T(8,128)(2,1)S(1)}, bf16[8,11392]{1,0:T(8,128)(2,1)S(1)}, u32[]{:S(2)}, u32[]{:S(2)}) collective-permute-start(bf16[8,11392]{1,0:T(8,128)(2,1)S(1)} %pad_maximum_fusion.8), channel_id=1, source_target_pairs={{0,1},{1,0},{2,3},{3,2},{4,5},{5,4},{6,7},{7,6},{8,11},{9,10},{10,... | collective-permute-start | bytes 546824 | tf_op jit(solution)/shard_map/ppermute | solution.py:67
  29.5 9.8 %collective-permute-start.7 = (bf16[8,11392]{1,0:T(8,128)(2,1)S(1)}, bf16[8,11392]{1,0:T(8,128)(2,1)S(1)}, u32[]{:S(2)}, u32[]{:S(2)}) collective-permute-start(bf16[8,11392]{1,0:T(8,128)(2,1)S(1)} %pad_maximum_fusion.8), channel_id=1, source_target_pairs={{0,81},{1,80},{2,83},{3,82},{4,85},{5,84},{6,87},{7,86},{8,127},{9... | collective-permute-start | bytes 546824 | tf_op jit(solution)/shard_map/ppermute | solution.py:67
  39.4 7.6 %collective-permute-start.10 = (bf16[8,8,3712]{2,1,0:T(8,128)(2,1)S(1)}, bf16[8,8,3712]{2,1,0:T(8,128)(2,1)S(1)}, u32[]{:S(2)}, u32[]{:S(2)}) collective-permute-start(bf16[8,8,3712]{2,1,0:T(8,128)(2,1)S(1)} %get-tuple-element.53), channel_id=1, source_target_pairs={{0,68},{1,69},{2,70},{3,71},{4,64},{5,65},{6,66},{7,67},{8,72},{9,... | collective-permute-start | bytes 1425416 | tf_op jit(solution)/shard_map/ppermute | solution.py:67
  39.7 7.8 %collective-permute-start.9 = (bf16[8,8,3840]{2,1,0:T(8,128)(2,1)S(1)}, bf16[8,8,3840]{2,1,0:T(8,128)(2,1)S(1)}, u32[]{:S(2)}, u32[]{:S(2)}) collective-permute-start(bf16[8,8,3840]{2,1,0:T(8,128)(2,1)S(1)} %get-tuple-element.56), channel_id=1, source_target_pairs={{0,48},{1,49},{2,50},{3,51},{4,52},{5,53},{6,54},{7,55},{8,24},{9,... | collective-permute-start | bytes 1474568 | tf_op jit(solution)/shard_map/ppermute | solution.py:67
  45.4 8.1 %collective-permute-start.8 = (bf16[8,8,3840]{2,1,0:T(8,128)(2,1)S(1)}, bf16[8,8,3840]{2,1,0:T(8,128)(2,1)S(1)}, u32[]{:S(2)}, u32[]{:S(2)}) collective-permute-start(bf16[8,8,3840]{2,1,0:T(8,128)(2,1)S(1)} %get-tuple-element.57), channel_id=1, source_target_pairs={{0,3},{1,2},{2,1},{3,0},{4,7},{5,6},{6,5},{7,4},{8,9},{9,8},{10,11... | collective-permute-start | bytes 1474568 | tf_op jit(solution)/shard_map/ppermute | solution.py:67
  53.6 13.0 %collective-permute-start.14 = (bf16[2,8,8,3712]{3,2,1,0:T(8,128)(2,1)S(1)}, bf16[2,8,8,3712]{3,2,1,0:T(8,128)(2,1)S(1)}, u32[]{:S(2)}, u32[]{:S(2)}) collective-permute-start(bf16[2,8,8,3712]{3,2,1,0:T(8,128)(2,1)S(1)} %get-tuple-element.29.refs_4_.refs_6_), channel_id=1, source_target_pairs={{0,3},{1,2},{2,1},{3,0},{4,7},{5,6},{6,5},{7,4},{8,9},{9,8},{10,11... | collective-permute-start | bytes 2850824 | tf_op jit(solution)/shard_map/ppermute | solution.py:67
  53.7 13.3 %collective-permute-start.12 = (bf16[2,8,8,3840]{3,2,1,0:T(8,128)(2,1)S(1)}, bf16[2,8,8,3840]{3,2,1,0:T(8,128)(2,1)S(1)}, u32[]{:S(2)}, u32[]{:S(2)}) collective-permute-start(bf16[2,8,8,3840]{3,2,1,0:T(8,128)(2,1)S(1)} %get-tuple-element.27.refs_0_), channel_id=1, source_target_pairs={{0,48},{1,49},{2,50},{3,51},{4,52},{5,53},{6,54},{7,55},{8,24},{9,... | collective-permute-start | bytes 2949128 | tf_op jit(solution)/shard_map/ppermute | solution.py:67
  54.9 13.2 %collective-permute-start.13 = (bf16[2,8,8,3840]{3,2,1,0:T(8,128)(2,1)S(1)}, bf16[2,8,8,3840]{3,2,1,0:T(8,128)(2,1)S(1)}, u32[]{:S(2)}, u32[]{:S(2)}) collective-permute-start(bf16[2,8,8,3840]{3,2,1,0:T(8,128)(2,1)S(1)} %get-tuple-element.28.dep_ref.refs_2_.refs_3_), channel_id=1, source_target_pairs={{0,68},{1,69},{2,70},{3,71},{4,64},{5,65},{6,66},{7,67},{8,72},{9,... | collective-permute-start | bytes 2949128 | tf_op jit(solution)/shard_map/ppermute | solution.py:67
  56.5 27.3 %collective-permute-start.11 = (bf16[2,8,8,11392]{3,2,1,0:T(8,128)(2,1)S(1)}, bf16[2,8,8,11392]{3,2,1,0:T(8,128)(2,1)S(1)}, u32[]{:S(2)}, u32[]{:S(2)}) collective-permute-start(bf16[2,8,8,11392]{3,2,1,0:T(8,128)(2,1)S(1)} %shard_map.70), channel_id=1, source_target_pairs={{0,8},{1,9},{2,10},{3,11},{4,12},{5,13},{6,14},{7,15},{8,0},{9,1},... | collective-permute-start | bytes 8749064 | tf_op jit(solution)/shard_map/ppermute | solution.py:63
  68.4 28.6 %collective-permute-start.15 = (bf16[2,8,8,11392]{3,2,1,0:T(8,128)(2,1)S(1)}, bf16[2,8,8,11392]{3,2,1,0:T(8,128)(2,1)S(1)}, u32[]{:S(2)}, u32[]{:S(2)}) collective-permute-start(bf16[2,8,8,11392]{3,2,1,0:T(8,128)(2,1)S(1)} %shard_map.71), channel_id=1, source_target_pairs={{0,8},{1,9},{2,10},{3,11},{4,12},{5,13},{6,14},{7,15},{8,0},{9,1},... | collective-permute-start | bytes 8749064 | tf_op jit(solution)/shard_map/ppermute | solution.py:63
  83.6 0.7 copy-start
  84.3 12.6 %collective-permute-start.19 = (bf16[2,2,8,8,1792]{4,3,2,1,0:T(8,128)(2,1)S(1)}, bf16[2,2,8,8,1792]{4,3,2,1,0:T(8,128)(2,1)S(1)}, u32[]{:S(2)}, u32[]{:S(2)}) collective-permute-start(bf16[2,2,8,8,1792]{4,3,2,1,0:T(8,128)(2,1)S(1)} %slice.51), channel_id=1, source_target_pairs={{0,3},{1,2},{2,1},{3,0},{4,7},{5,6},{6,5},{7,4},{8,9},{9,8},{10,11... | collective-permute-start | bytes 2752520 | tf_op jit(solution)/shard_map/ppermute | solution.py:67
  84.5 14.5 %collective-permute-start.17 = (bf16[2,2,8,8,2048]{4,3,2,1,0:T(8,128)(2,1)S(1)}, bf16[2,2,8,8,2048]{4,3,2,1,0:T(8,128)(2,1)S(1)}, u32[]{:S(2)}, u32[]{:S(2)}) collective-permute-start(bf16[2,2,8,8,2048]{4,3,2,1,0:T(8,128)(2,1)S(1)} %slice.50), channel_id=1, source_target_pairs={{0,68},{1,69},{2,70},{3,71},{4,64},{5,65},{6,66},{7,67},{8,72},{9,... | collective-permute-start | bytes 3145736 | tf_op jit(solution)/shard_map/ppermute | solution.py:67
  84.7 17.0 %collective-permute-start.21 = (bf16[2,2,8,8,1792]{4,3,2,1,0:T(8,128)(2,1)S(1)}, bf16[2,2,8,8,1792]{4,3,2,1,0:T(8,128)(2,1)S(1)}, u32[]{:S(2)}, u32[]{:S(2)}) collective-permute-start(bf16[2,2,8,8,1792]{4,3,2,1,0:T(8,128)(2,1)S(1)} %slice.52), channel_id=1, source_target_pairs={{0,48},{1,49},{2,50},{3,51},{4,52},{5,53},{6,54},{7,55},{8,24},{9,... | collective-permute-start | bytes 2752520 | tf_op jit(solution)/shard_map/ppermute | solution.py:67
  97.0 5.4 %collective-permute-start.20 = (bf16[2,2,8,8,1792]{4,3,2,1,0:T(8,128)(2,1)S(1)}, bf16[2,2,8,8,1792]{4,3,2,1,0:T(8,128)(2,1)S(1)}, u32[]{:S(2)}, u32[]{:S(2)}) collective-permute-start(bf16[2,2,8,8,1792]{4,3,2,1,0:T(8,128)(2,1)S(1)} %shard_map.76.refs_5_), channel_id=1, source_target_pairs={{0,8},{1,9},{2,10},{3,11},{4,12},{5,13},{6,14},{7,15},{8,0},{9,1},... | collective-permute-start | bytes 2752520 | tf_op jit(solution)/shard_map/ppermute | solution.py:63
  99.1 9.2 %collective-permute-start.18 = (bf16[2,2,8,8,2048]{4,3,2,1,0:T(8,128)(2,1)S(1)}, bf16[2,2,8,8,2048]{4,3,2,1,0:T(8,128)(2,1)S(1)}, u32[]{:S(2)}, u32[]{:S(2)}) collective-permute-start(bf16[2,2,8,8,2048]{4,3,2,1,0:T(8,128)(2,1)S(1)} %shard_map.75.refs_2_), channel_id=1, source_target_pairs={{0,8},{1,9},{2,10},{3,11},{4,12},{5,13},{6,14},{7,15},{8,0},{9,1},... | collective-permute-start | bytes 3145736 | tf_op jit(solution)/shard_map/ppermute | solution.py:63
  101.7 6.5 %collective-permute-start.22 = (bf16[2,2,8,8,1792]{4,3,2,1,0:T(8,128)(2,1)S(1)}, bf16[2,2,8,8,1792]{4,3,2,1,0:T(8,128)(2,1)S(1)}, u32[]{:S(2)}, u32[]{:S(2)}) collective-permute-start(bf16[2,2,8,8,1792]{4,3,2,1,0:T(8,128)(2,1)S(1)} %shard_map.77.refs_8_), channel_id=1, source_target_pairs={{0,8},{1,9},{2,10},{3,11},{4,12},{5,13},{6,14},{7,15},{8,0},{9,1},... | collective-permute-start | bytes 2752520 | tf_op jit(solution)/shard_map/ppermute | solution.py:63
  101.9 14.1 %collective-permute-start.24 = (bf16[2,2,8,8,2048]{4,3,2,1,0:T(8,128)(2,1)S(1)}, bf16[2,2,8,8,2048]{4,3,2,1,0:T(8,128)(2,1)S(1)}, u32[]{:S(2)}, u32[]{:S(2)}) collective-permute-start(bf16[2,2,8,8,2048]{4,3,2,1,0:T(8,128)(2,1)S(1)} %slice.53), channel_id=1, source_target_pairs={{0,3},{1,2},{2,1},{3,0},{4,7},{5,6},{6,5},{7,4},{8,9},{9,8},{10,11... | collective-permute-start | bytes 3145736 | tf_op jit(solution)/shard_map/ppermute | solution.py:67
  102.1 20.5 %collective-permute-start.26 = (bf16[2,2,8,8,1920]{4,3,2,1,0:T(8,128)(2,1)S(1)}, bf16[2,2,8,8,1920]{4,3,2,1,0:T(8,128)(2,1)S(1)}, u32[]{:S(2)}, u32[]{:S(2)}) collective-permute-start(bf16[2,2,8,8,1920]{4,3,2,1,0:T(8,128)(2,1)S(1)} %slice.54), channel_id=1, source_target_pairs={{0,48},{1,49},{2,50},{3,51},{4,52},{5,53},{6,54},{7,55},{8,24},{9,... | collective-permute-start | bytes 2949128 | tf_op jit(solution)/shard_map/ppermute | solution.py:67
  102.3 20.4 %collective-permute-start.16 = (bf16[2,2,8,8,1792]{4,3,2,1,0:T(8,128)(2,1)S(1)}, bf16[2,2,8,8,1792]{4,3,2,1,0:T(8,128)(2,1)S(1)}, u32[]{:S(2)}, u32[]{:S(2)}) collective-permute-start(bf16[2,2,8,8,1792]{4,3,2,1,0:T(8,128)(2,1)S(1)} %slice.49), channel_id=1, source_target_pairs={{0,68},{1,69},{2,70},{3,71},{4,64},{5,65},{6,66},{7,67},{8,72},{9,... | collective-permute-start | bytes 2752520 | tf_op jit(solution)/shard_map/ppermute | solution.py:67
  116.0 12.9 %collective-permute-start.25 = (bf16[2,2,8,8,2048]{4,3,2,1,0:T(8,128)(2,1)S(1)}, bf16[2,2,8,8,2048]{4,3,2,1,0:T(8,128)(2,1)S(1)}, u32[]{:S(2)}, u32[]{:S(2)}) collective-permute-start(bf16[2,2,8,8,2048]{4,3,2,1,0:T(8,128)(2,1)S(1)} %shard_map.81.refs_5_), channel_id=1, source_target_pairs={{0,8},{1,9},{2,10},{3,11},{4,12},{5,13},{6,14},{7,15},{8,0},{9,1},... | collective-permute-start | bytes 3145736 | tf_op jit(solution)/shard_map/ppermute | solution.py:63
  122.6 6.3 %collective-permute-start.27 = (bf16[2,2,8,8,1920]{4,3,2,1,0:T(8,128)(2,1)S(1)}, bf16[2,2,8,8,1920]{4,3,2,1,0:T(8,128)(2,1)S(1)}, u32[]{:S(2)}, u32[]{:S(2)}) collective-permute-start(bf16[2,2,8,8,1920]{4,3,2,1,0:T(8,128)(2,1)S(1)} %shard_map.82.refs_8_), channel_id=1, source_target_pairs={{0,8},{1,9},{2,10},{3,11},{4,12},{5,13},{6,14},{7,15},{8,0},{9,1},... | collective-permute-start | bytes 2949128 | tf_op jit(solution)/shard_map/ppermute | solution.py:63
  122.7 6.2 %collective-permute-start.23 = (bf16[2,2,8,8,1792]{4,3,2,1,0:T(8,128)(2,1)S(1)}, bf16[2,2,8,8,1792]{4,3,2,1,0:T(8,128)(2,1)S(1)}, u32[]{:S(2)}, u32[]{:S(2)}) collective-permute-start(bf16[2,2,8,8,1792]{4,3,2,1,0:T(8,128)(2,1)S(1)} %shard_map.80.refs_2_), channel_id=1, source_target_pairs={{0,8},{1,9},{2,10},{3,11},{4,12},{5,13},{6,14},{7,15},{8,0},{9,1},... | collective-permute-start | bytes 2752520 | tf_op jit(solution)/shard_map/ppermute | solution.py:63
  136.8 1.2 collective-permute-start.28

commit v7 on v6

--- a/solution.py
+++ b/solution.py
@@ -412,30 +412,33 @@
     got = swap(jnp.where(first, halves[1], halves[0]))
     rows = jnp.concatenate([jnp.where(first, keep, got), jnp.where(first, got, keep)], axis=0)
 
-    near = [
-        hop(rows, [a for a in "xyz" if n & WEIGHT[a]], 0) for n in (1, 2, 4, 3, 5, 6, 7)
-    ]
-    rows = jnp.stack([rows, near[0], near[1], near[3], near[2], near[4], near[5], near[6]])
-    sg = self_call(out_grads, rows)
+    def send(block, n):
+        return hop(block, [a for a in "xyz" if n & WEIGHT[a]], 0)
+
+    near = {n: send(rows, n) for n in (1, 2, 4, 3)}
+    (again,) = gate([rows], near[1])
+    near.update({n: send(again, n) for n in (5, 6, 7)})
+    rows = jnp.stack([rows] + [near[n] for n in range(1, 8)])
     x = [double(rows[..., s:s + w], RUNS[j], 1) for j, (s, w) in enumerate(zip(STARTS, WIDTHS))]
-    x = gate(x, sg)
-    block_gram = self_call(hidden_acts, x[1], sg)
+    sa = self_call(hidden_acts, x[1])
     a1 = [hop(x[j], STEP5[j], 1) for j in range(3)]
-    o0 = swap(gate([jnp.concatenate(x, axis=-1)], sg)[0])
-    pair = gate([jnp.stack([x[j], a1[j]]) for j in range(3)], block_gram, o0)
+    o0 = swap(jnp.concatenate(x, axis=-1))
+    pair = gate([jnp.stack([x[j], a1[j]]) for j in range(3)], sa, o0)
     last = [
         [hop(pair[j][..., a:a + w], STEP6[j], 1) for j, (a, w) in enumerate(zip(at, width))]
         for at, width in zip(SETAT, SETW)
     ]
-    o1 = swap(gate([jnp.concatenate(a1, axis=-1)], sg)[0])
+    o1 = swap(gate([jnp.concatenate(a1, axis=-1)], pair[0])[0])
     call = functools.partial(
         local_call, core=core.reshape(1).astype(jnp.int32), acts=hidden_acts, grads=out_grads
     )
     unit = 512 * (HA + HG)
     ca, cg, tok = call(
-        early_body, args=[block_gram] + [y for j in range(3) for y in (x[j], a1[j])],
+        early_body, args=[sa] + [y for j in range(3) for y in (x[j], a1[j])],
         outs=[ACC, ACC, TOKEN], flops=512 * unit, width=C1, pinned=range(1, 7), mib=28,
     )
+    block_gram = self_call(out_grads, tok, sa)
+    tok = block_gram
     sums = [ca, cg]
     for which in range(2):
         got = [gate([y], tok, *([] if which else [o1]))[0] for y in last[which]]

time: 139 us -> 115 us (0.83)
  waiting for transfers between devices: 38.2 us -> 23.4 us
  starting transfers between devices: 44.5 us -> 34.9 us
    ppermute x19, waiting for transfers between devices: 36.4 us -> 20.9 us  [hop(): return lax.ppermute(x, AXES, ring_pairs(axes, step))]
    ppermute x10, starting transfers between devices: 20.5 us -> 15.5 us  [swap(): return lax.ppermute(x, AXES, core_pairs())]
    ppermute x19, starting transfers between devices: 24.1 us -> 19.4 us  [hop(): return lax.ppermute(x, AXES, ring_pairs(axes, step))]
  transfers between devices with their start and end apart: 29 -> 29, of which waited for: 12 -> 9; matrix products, arithmetic and copies ran while one was open for 1% -> 2% of each run, Pallas kernels for 30% -> 36%
where the time goes in v7:
time: 115 us
  Pallas kernels  48.9 us (43%)
  starting transfers between devices  34.9 us (30%)
  waiting for transfers between devices  23.4 us (20%)
  local copies, waits for them, and re-layouts  3.27 us (3%)
  other arithmetic  3.22 us (3%)
    pallas_call x5, Pallas kernels, local_call(): pl.pallas_call(body, in_specs=[pl.BlockSpec(memory_space=pltpu.SMEM)] + [...  33.1 us
    ppermute x19, waiting for transfers between devices, hop(): return lax.ppermute(x, AXES, ring_pairs(axes, step))  20.9 us
    ppermute x19, starting transfers between devices, hop(): return lax.ppermute(x, AXES, ring_pairs(axes, step))  19.4 us
    pallas_call x2, Pallas kernels, self_call(): pl.pallas_call(body, grid=(width // KC,), in_specs=[pl.BlockSpec((TOK, KC...  15.8 us
    ppermute x10, starting transfers between devices, swap(): return lax.ppermute(x, AXES, core_pairs())  15.5 us
    ppermute x10, waiting for transfers between devices, swap(): return lax.ppermute(x, AXES, core_pairs())  2.51 us
  transfers between devices with their start and end apart: 29, of which 9 were waited for; matrix products, arithmetic and copies ran while one was open for 2% of the time, Pallas kernels for 36%

profile of v7, /device:TPU:1, one launch (start us, length us, event | category | flops | bytes accessed | tf_op | source)
XLA Modules:
  0.0 114.7 jit_solution(2117917035316500053)
XLA Ops:
  0.6 0.7 convert_element_type.4
  1.3 0.8 fusion.4
  2.1 0.9 fusion.3
  3.2 1.5 %collective-permute-start = (bf16[4,11392]{1,0:T(4,128)(2,1)S(1)}, bf16[4,11392]{1,0:T(4,128)(2,1)S(1)}, u32[]{:S(2)}, u32[]{:S(2)}) collective-permute-start(bf16[4,11392]{1,0:T(4,128)(2,1)S(1)} %broadcast_select_fusion.2), channel_id=1, source_target_pairs={{0,8},{1,9},{2,10},{3,11},{4,12},{5,13},{6,14},{7,15},{8,0},{9,1},... | collective-permute-start | bytes 273416 | tf_op jit(solution)/shard_map/ppermute | solution.py:63
  4.7 0.9 collective-permute-done
  5.8 2.6 %collective-permute-start.4 = (bf16[8,11392]{1,0:T(8,128)(2,1)S(1)}, bf16[8,11392]{1,0:T(8,128)(2,1)S(1)}, u32[]{:S(2)}, u32[]{:S(2)}) collective-permute-start(bf16[8,11392]{1,0:T(8,128)(2,1)S(1)} %pad_maximum_fusion.7.refs_0_), channel_id=1, source_target_pairs={{0,64},{1,65},{2,66},{3,67},{4,68},{5,69},{6,70},{7,71},{8,76},{9,... | collective-permute-start | bytes 546824 | tf_op jit(solution)/shard_map/ppermute | solution.py:67
  8.5 6.2 %collective-permute-start.3 = (bf16[8,11392]{1,0:T(8,128)(2,1)S(1)}, bf16[8,11392]{1,0:T(8,128)(2,1)S(1)}, u32[]{:S(2)}, u32[]{:S(2)}) collective-permute-start(bf16[8,11392]{1,0:T(8,128)(2,1)S(1)} %pad_maximum_fusion.7.refs_0_), channel_id=1, source_target_pairs={{0,17},{1,16},{2,19},{3,18},{4,21},{5,20},{6,23},{7,22},{8,59},{9,... | collective-permute-start | bytes 546824 | tf_op jit(solution)/shard_map/ppermute | solution.py:67
  14.7 0.3 collective-permute-start.1
  15.1 2.5 %collective-permute-done.3 = bf16[8,11392]{1,0:T(8,128)(2,1)S(1)} collective-permute-done((bf16[8,11392]{1,0:T(8,128)(2,1)S(1)}, bf16[8,11392]{1,0:T(8,128)(2,1)S(1)}, u32[]{:S(2)}, u32[]{:S(2)}) %collective-permute-start.3) | collective-permute-done | bytes 182304 | tf_op jit(solution)/shard_map/ppermute | solution.py:67
  17.6 2.7 %collective-permute-done.2 = bf16[8,11392]{1,0:T(8,128)(2,1)S(1)} collective-permute-done((bf16[8,11392]{1,0:T(8,128)(2,1)S(1)}, bf16[8,11392]{1,0:T(8,128)(2,1)S(1)}, u32[]{:S(2)}, u32[]{:S(2)}) %collective-permute-start.2) | collective-permute-done | bytes 182304 | tf_op jit(solution)/shard_map/ppermute | solution.py:67
  20.2 4.0 %collective-permute-start.7 = (bf16[8,11392]{1,0:T(8,128)(2,1)S(1)}, bf16[8,11392]{1,0:T(8,128)(2,1)S(1)}, u32[]{:S(2)}, u32[]{:S(2)}) collective-permute-start(bf16[8,11392]{1,0:T(8,128)(2,1)S(1)} %shard_map.68), channel_id=1, source_target_pairs={{0,81},{1,80},{2,83},{3,82},{4,85},{5,84},{6,87},{7,86},{8,127},{9... | collective-permute-start | bytes 546824 | tf_op jit(solution)/shard_map/ppermute | solution.py:67
  24.2 2.1 %collective-permute-start.6 = (bf16[8,11392]{1,0:T(8,128)(2,1)S(1)}, bf16[8,11392]{1,0:T(8,128)(2,1)S(1)}, u32[]{:S(2)}, u32[]{:S(2)}) collective-permute-start(bf16[8,11392]{1,0:T(8,128)(2,1)S(1)} %shard_map.68), channel_id=1, source_target_pairs={{0,65},{1,64},{2,67},{3,66},{4,69},{5,68},{6,71},{7,70},{8,79},{9,... | collective-permute-start | bytes 546824 | tf_op jit(solution)/shard_map/ppermute | solution.py:67
  26.4 1.1 collective-permute-start.5
  27.5 6.7 %collective-permute-done.5 = bf16[8,11392]{1,0:T(8,128)(2,1)S(1)} collective-permute-done((bf16[8,11392]{1,0:T(8,128)(2,1)S(1)}, bf16[8,11392]{1,0:T(8,128)(2,1)S(1)}, u32[]{:S(2)}, u32[]{:S(2)}) %collective-permute-start.5) | collective-permute-done | bytes 182304 | tf_op jit(solution)/shard_map/ppermute | solution.py:67
  34.5 0.1 slice_bitcast_fusion.2
  34.8 7.5 %collective-permute-done.10 = bf16[8,8,3712]{2,1,0:T(8,128)(2,1)S(1)} collective-permute-done((bf16[8,8,3712]{2,1,0:T(8,128)(2,1)S(1)}, bf16[8,8,3712]{2,1,0:T(8,128)(2,1)S(1)}, u32[]{:S(2)}, u32[]{:S(2)}) %collective-permute-start.10) | collective-permute-done | bytes 475168 | tf_op jit(solution)/shard_map/ppermute | solution.py:67
  42.3 0.1 fusion
  42.5 0.2 collective-permute-done.9
  42.7 0.1 fusion.1
  42.8 1.5 %collective-permute-start.13 = (bf16[2,8,8,3840]{3,2,1,0:T(8,128)(2,1)S(1)}, bf16[2,8,8,3840]{3,2,1,0:T(8,128)(2,1)S(1)}, u32[]{:S(2)}, u32[]{:S(2)}) collective-permute-start(bf16[2,8,8,3840]{3,2,1,0:T(8,128)(2,1)S(1)} %get-tuple-element.53.dep_ref.refs_2_.refs_3_), channel_id=1, source_target_pairs={{0,68},{1,69},{2,70},{3,71},{4,64},{5,65},{6,66},{7,67},{8,72},{9,... | collective-permute-start | bytes 2949128 | tf_op jit(solution)/shard_map/ppermute | solution.py:67
  44.3 0.2 maximum_maximum_fusion
  44.6 0.1 fusion.2
  44.8 2.0 %collective-permute-start.11 = (bf16[2,8,8,11392]{3,2,1,0:T(8,128)(2,1)S(1)}, bf16[2,8,8,11392]{3,2,1,0:T(8,128)(2,1)S(1)}, u32[]{:S(2)}, u32[]{:S(2)}) collective-permute-start(bf16[2,8,8,11392]{3,2,1,0:T(8,128)(2,1)S(1)} %maximum_maximum_fusion), channel_id=1, source_target_pairs={{0,8},{1,9},{2,10},{3,11},{4,12},{5,13},{6,14},{7,15},{8,0},{9,1},... | collective-permute-start | bytes 8749064 | tf_op jit(solution)/shard_map/ppermute | solution.py:63
  46.8 9.5 %shard_map.69.refs_3_.dep_ref.first_ref = f32[512,256]{1,0:T(8,128)S(1)} custom-call(bf16[512,14336]{1,0:T(8,128)(2,1)} %acts.9, bf16[2,8,8,3840]{3,2,1,0:T(8,128)(2,1)S(1)} %get-tuple-element.53.dep_ref.refs_2_.refs_3_), custom_call_target="tpu_custom_call" | custom-call | flops 3758096384 | bytes 14680064 | tf_op jit(solution)/shard_map/pallas_call | solution.py:146
  56.3 0.2 pad_maximum_fusion.3.refs_2_
  56.5 0.2 pad_maximum_fusion.2.refs_1_
  56.7 1.3 %collective-permute-done.12.refs_1_ = bf16[2,8,8,3840]{3,2,1,0:T(8,128)(2,1)S(1)} collective-permute-done((bf16[2,8,8,3840]{3,2,1,0:T(8,128)(2,1)S(1)}, bf16[2,8,8,3840]{3,2,1,0:T(8,128)(2,1)S(1)}, u32[]{:S(2)}, u32[]{:S(2)}) %collective-permute-start.12) | collective-permute-done | bytes 983072 | tf_op jit(solution)/shard_map/ppermute | solution.py:67
  58.0 0.2 pad_maximum_fusion.1.refs_0_
  58.2 0.2 pad_maximum_fusion.refs_0_
  58.5 2.0 %collective-permute-start.15 = (bf16[2,8,8,11392]{3,2,1,0:T(8,128)(2,1)S(1)}, bf16[2,8,8,11392]{3,2,1,0:T(8,128)(2,1)S(1)}, u32[]{:S(2)}, u32[]{:S(2)}) collective-permute-start(bf16[2,8,8,11392]{3,2,1,0:T(8,128)(2,1)S(1)} %shard_map.71), channel_id=1, source_target_pairs={{0,8},{1,9},{2,10},{3,11},{4,12},{5,13},{6,14},{7,15},{8,0},{9,1},... | collective-permute-start | bytes 8749064 | tf_op jit(solution)/shard_map/ppermute | solution.py:63
  60.7 0.4 collective-permute-start.17
  61.2 5.9 %shard_map.72 = (f32[8,8,8,512]{3,2,1,0:T(8,128)S(1)}, f32[8,8,8,512]{3,2,1,0:T(8,128)S(1)}, f32[8,128]{1,0:T(8,128)S(1)}) custom-call(s32[1]{0:T(128)} %bitcast.core_ref, bf16[512,14336]{1,0:T(8,128)(2,1)} %acts.9, bf16[512,8192]{1,0:T(8,128)(2,1)} %grads.9, f32[512,256]{1,0:T(8,128)S(1)} %shard_map.69.refs_3_.dep_ref.first_ref, ...), custom_call_target="tpu_custom_call" | custom-call | flops 2952790016 | bytes 11534336 | tf_op jit(solution)/shard_map/pallas_call | solution.py:382
  67.1 6.3 %shard_map.73.refs_1_ = f32[4,4]{1,0:T(4,128)} custom-call(bf16[512,8192]{1,0:T(8,128)(2,1)} %grads.9, f32[512,256]{1,0:T(8,128)S(1)} %shard_map.69.refs_3_.dep_ref.first_ref, f32[8,128]{1,0:T(8,128)S(1)} %get-tuple-element.25.dep_ref), custom_call_target="tpu_custom_call" | custom-call | flops 2147483648 | bytes 8388608 | tf_op jit(solution)/shard_map/pallas_call | solution.py:146
  73.5 0.7 copy-done
  74.2 5.3 %collective-permute-start.20 = (bf16[2,2,8,8,1792]{4,3,2,1,0:T(8,128)(2,1)S(1)}, bf16[2,2,8,8,1792]{4,3,2,1,0:T(8,128)(2,1)S(1)}, u32[]{:S(2)}, u32[]{:S(2)}) collective-permute-start(bf16[2,2,8,8,1792]{4,3,2,1,0:T(8,128)(2,1)S(1)} %shard_map.75.refs_5_), channel_id=1, source_target_pairs={{0,8},{1,9},{2,10},{3,11},{4,12},{5,13},{6,14},{7,15},{8,0},{9,1},... | collective-permute-start | bytes 2752520 | tf_op jit(solution)/shard_map/ppermute | solution.py:63
  79.6 0.4 collective-permute-start.22
  80.0 0.1 slice.53
  80.1 0.5 collective-permute-start.24
  80.9 0.7 collective-permute-done.20.o3
  81.6 5.8 %shard_map.77 = (f32[8,8,8,512]{3,2,1,0:T(8,128)S(1)}, f32[8,8,8,512]{3,2,1,0:T(8,128)S(1)}, f32[256,512]{1,0:T(8,128)S(1)}, f32[256,512]{1,0:T(8,128)S(1)}) custom-call(s32[1]{0:T(128)} %bitcast.core_ref, bf16[512,14336]{1,0:T(8,128)(2,1)} %acts.9, bf16[512,8192]{1,0:T(8,128)(2,1)} %grads.9, bf16[2,8,8,3840]{3,2,1,0:T(8,128)(2,1)S(1)} %get-tuple-element.55.refs_0_, ...), custom_call_target="tpu_custom_call" | custom-call | flops 2952790016 | bytes 11534336 | tf_op jit(solution)/shard_map/pallas_call | solution.py:382
  87.4 7.7 %shard_map.78 = (f32[8,8,8,512]{3,2,1,0:T(8,128)S(1)}, f32[8,8,8,512]{3,2,1,0:T(8,128)S(1)}, f32[256,512]{1,0:T(8,128)S(1)}, f32[256,512]{1,0:T(8,128)S(1)}, f32[8,128]{1,0:T(8,128)S(1)}) custom-call(s32[1]{0:T(128)} %bitcast.core_ref, bf16[512,14336]{1,0:T(8,128)(2,1)} %acts.9, bf16[512,8192]{1,0:T(8,128)(2,1)} %grads.9, ...), custom_call_target="tpu_custom_call" | custom-call | flops 4429185024 | bytes 11534336 | tf_op jit(solution)/shard_map/pallas_call | solution.py:382
  95.1 3.3 %collective-permute-start.25 = (bf16[2,2,8,8,2048]{4,3,2,1,0:T(8,128)(2,1)S(1)}, bf16[2,2,8,8,2048]{4,3,2,1,0:T(8,128)(2,1)S(1)}, u32[]{:S(2)}, u32[]{:S(2)}) collective-permute-start(bf16[2,2,8,8,2048]{4,3,2,1,0:T(8,128)(2,1)S(1)} %shard_map.80.refs_5_), channel_id=1, source_target_pairs={{0,8},{1,9},{2,10},{3,11},{4,12},{5,13},{6,14},{7,15},{8,0},{9,1},... | collective-permute-start | bytes 3145736 | tf_op jit(solution)/shard_map/ppermute | solution.py:63
  98.5 0.4 collective-permute-start.23
  98.9 5.8 %shard_map.82 = (f32[8,8,8,512]{3,2,1,0:T(8,128)S(1)}, f32[8,8,8,512]{3,2,1,0:T(8,128)S(1)}, f32[256,512]{1,0:T(8,128)S(1)}, f32[256,512]{1,0:T(8,128)S(1)}, f32[512,128]{1,0:T(8,128)S(1)}) custom-call(s32[1]{0:T(128)} %bitcast.core_ref, bf16[512,14336]{1,0:T(8,128)(2,1)} %acts.9, bf16[512,8192]{1,0:T(8,128)(2,1)} %grads.9, ...), custom_call_target="tpu_custom_call" | custom-call | flops 2952790016 | bytes 11534336 | tf_op jit(solution)/shard_map/pallas_call | solution.py:382
  104.8 7.9 %shard_map.83 = (f32[4,512]{1,0:T(4,128)S(1)}, f32[4,128]{1,0:T(4,128)S(1)}) custom-call(s32[1]{0:T(128)} %bitcast.core_ref, bf16[512,14336]{1,0:T(8,128)(2,1)} %acts.9, bf16[512,8192]{1,0:T(8,128)(2,1)} %grads.9, bf16[2,8,8,11392]{3,2,1,0:T(8,128)(2,1)S(1)} %collective-permute-done.11.refs_4_.o0, ...), custom_call_target="tpu_custom_call" | custom-call | flops 4429185024 | bytes 11534336 | tf_op jit(solution)/shard_map/pallas_call | solution.py:382
  112.7 0.4 collective-permute-start.28
  113.1 0.8 collective-permute-done.28
  114.0 0.7 broadcast_multiply_fusion
  (62 shorter events, 2.1 us)
Async XLA Ops:
  3.2 2.4 %collective-permute-start = (bf16[4,11392]{1,0:T(4,128)(2,1)S(1)}, bf16[4,11392]{1,0:T(4,128)(2,1)S(1)}, u32[]{:S(2)}, u32[]{:S(2)}) collective-permute-start(bf16[4,11392]{1,0:T(4,128)(2,1)S(1)} %broadcast_select_fusion.2), channel_id=1, source_target_pairs={{0,8},{1,9},{2,10},{3,11},{4,12},{5,13},{6,14},{7,15},{8,0},{9,1},... | collective-permute-start | bytes 273416 | tf_op jit(solution)/shard_map/ppermute | solution.py:63
  5.8 9.2 %collective-permute-start.4 = (bf16[8,11392]{1,0:T(8,128)(2,1)S(1)}, bf16[8,11392]{1,0:T(8,128)(2,1)S(1)}, u32[]{:S(2)}, u32[]{:S(2)}) collective-permute-start(bf16[8,11392]{1,0:T(8,128)(2,1)S(1)} %pad_maximum_fusion.7.refs_0_), channel_id=1, source_target_pairs={{0,64},{1,65},{2,66},{3,67},{4,68},{5,69},{6,70},{7,71},{8,76},{9,... | collective-permute-start | bytes 546824 | tf_op jit(solution)/shard_map/ppermute | solution.py:67
  8.5 9.1 %collective-permute-start.3 = (bf16[8,11392]{1,0:T(8,128)(2,1)S(1)}, bf16[8,11392]{1,0:T(8,128)(2,1)S(1)}, u32[]{:S(2)}, u32[]{:S(2)}) collective-permute-start(bf16[8,11392]{1,0:T(8,128)(2,1)S(1)} %pad_maximum_fusion.7.refs_0_), channel_id=1, source_target_pairs={{0,17},{1,16},{2,19},{3,18},{4,21},{5,20},{6,23},{7,22},{8,59},{9,... | collective-permute-start | bytes 546824 | tf_op jit(solution)/shard_map/ppermute | solution.py:67
  14.7 5.6 %collective-permute-start.2 = (bf16[8,11392]{1,0:T(8,128)(2,1)S(1)}, bf16[8,11392]{1,0:T(8,128)(2,1)S(1)}, u32[]{:S(2)}, u32[]{:S(2)}) collective-permute-start(bf16[8,11392]{1,0:T(8,128)(2,1)S(1)} %pad_maximum_fusion.7.refs_0_), channel_id=1, source_target_pairs={{0,1},{1,0},{2,3},{3,2},{4,5},{5,4},{6,7},{7,6},{8,11},{9,10},{10,... | collective-permute-start | bytes 546824 | tf_op jit(solution)/shard_map/ppermute | solution.py:67
  14.7 5.6 %collective-permute-start.1 = (bf16[8,11392]{1,0:T(8,128)(2,1)S(1)}, bf16[8,11392]{1,0:T(8,128)(2,1)S(1)}, u32[]{:S(2)}, u32[]{:S(2)}) collective-permute-start(bf16[8,11392]{1,0:T(8,128)(2,1)S(1)} %pad_maximum_fusion.7.refs_0_), channel_id=1, source_target_pairs={{0,16},{1,17},{2,18},{3,19},{4,20},{5,21},{6,22},{7,23},{8,56},{9,... | collective-permute-start | bytes 546824 | tf_op jit(solution)/shard_map/ppermute | solution.py:67
  20.2 14.0 %collective-permute-start.7 = (bf16[8,11392]{1,0:T(8,128)(2,1)S(1)}, bf16[8,11392]{1,0:T(8,128)(2,1)S(1)}, u32[]{:S(2)}, u32[]{:S(2)}) collective-permute-start(bf16[8,11392]{1,0:T(8,128)(2,1)S(1)} %shard_map.68), channel_id=1, source_target_pairs={{0,81},{1,80},{2,83},{3,82},{4,85},{5,84},{6,87},{7,86},{8,127},{9... | collective-permute-start | bytes 546824 | tf_op jit(solution)/shard_map/ppermute | solution.py:67
  24.2 10.0 %collective-permute-start.6 = (bf16[8,11392]{1,0:T(8,128)(2,1)S(1)}, bf16[8,11392]{1,0:T(8,128)(2,1)S(1)}, u32[]{:S(2)}, u32[]{:S(2)}) collective-permute-start(bf16[8,11392]{1,0:T(8,128)(2,1)S(1)} %shard_map.68), channel_id=1, source_target_pairs={{0,65},{1,64},{2,67},{3,66},{4,69},{5,68},{6,71},{7,70},{8,79},{9,... | collective-permute-start | bytes 546824 | tf_op jit(solution)/shard_map/ppermute | solution.py:67
  26.4 7.9 %collective-permute-start.5 = (bf16[8,11392]{1,0:T(8,128)(2,1)S(1)}, bf16[8,11392]{1,0:T(8,128)(2,1)S(1)}, u32[]{:S(2)}, u32[]{:S(2)}) collective-permute-start(bf16[8,11392]{1,0:T(8,128)(2,1)S(1)} %shard_map.68), channel_id=1, source_target_pairs={{0,80},{1,81},{2,82},{3,83},{4,84},{5,85},{6,86},{7,87},{8,124},{9... | collective-permute-start | bytes 546824 | tf_op jit(solution)/shard_map/ppermute | solution.py:67
  34.4 7.9 %collective-permute-start.10 = (bf16[8,8,3712]{2,1,0:T(8,128)(2,1)S(1)}, bf16[8,8,3712]{2,1,0:T(8,128)(2,1)S(1)}, u32[]{:S(2)}, u32[]{:S(2)}) collective-permute-start(bf16[8,8,3712]{2,1,0:T(8,128)(2,1)S(1)} %get-tuple-element.51), channel_id=1, source_target_pairs={{0,68},{1,69},{2,70},{3,71},{4,64},{5,65},{6,66},{7,67},{8,72},{9,... | collective-permute-start | bytes 1425416 | tf_op jit(solution)/shard_map/ppermute | solution.py:67
  34.6 8.1 %collective-permute-start.9 = (bf16[8,8,3840]{2,1,0:T(8,128)(2,1)S(1)}, bf16[8,8,3840]{2,1,0:T(8,128)(2,1)S(1)}, u32[]{:S(2)}, u32[]{:S(2)}) collective-permute-start(bf16[8,8,3840]{2,1,0:T(8,128)(2,1)S(1)} %get-tuple-element.48), channel_id=1, source_target_pairs={{0,48},{1,49},{2,50},{3,51},{4,52},{5,53},{6,54},{7,55},{8,24},{9,... | collective-permute-start | bytes 1474568 | tf_op jit(solution)/shard_map/ppermute | solution.py:67
  34.7 9.6 %collective-permute-start.8 = (bf16[8,8,3840]{2,1,0:T(8,128)(2,1)S(1)}, bf16[8,8,3840]{2,1,0:T(8,128)(2,1)S(1)}, u32[]{:S(2)}, u32[]{:S(2)}) collective-permute-start(bf16[8,8,3840]{2,1,0:T(8,128)(2,1)S(1)} %get-tuple-element.49), channel_id=1, source_target_pairs={{0,3},{1,2},{2,1},{3,0},{4,7},{5,6},{6,5},{7,4},{8,9},{9,8},{10,11... | collective-permute-start | bytes 1474568 | tf_op jit(solution)/shard_map/ppermute | solution.py:67
  42.4 13.9 %collective-permute-start.14 = (bf16[2,8,8,3712]{3,2,1,0:T(8,128)(2,1)S(1)}, bf16[2,8,8,3712]{3,2,1,0:T(8,128)(2,1)S(1)}, u32[]{:S(2)}, u32[]{:S(2)}) collective-permute-start(bf16[2,8,8,3712]{3,2,1,0:T(8,128)(2,1)S(1)} %get-tuple-element.57.refs_4_.refs_6_), channel_id=1, source_target_pairs={{0,3},{1,2},{2,1},{3,0},{4,7},{5,6},{6,5},{7,4},{8,9},{9,8},{10,11... | collective-permute-start | bytes 2850824 | tf_op jit(solution)/shard_map/ppermute | solution.py:67
  42.8 13.7 %collective-permute-start.13 = (bf16[2,8,8,3840]{3,2,1,0:T(8,128)(2,1)S(1)}, bf16[2,8,8,3840]{3,2,1,0:T(8,128)(2,1)S(1)}, u32[]{:S(2)}, u32[]{:S(2)}) collective-permute-start(bf16[2,8,8,3840]{3,2,1,0:T(8,128)(2,1)S(1)} %get-tuple-element.53.dep_ref.refs_2_.refs_3_), channel_id=1, source_target_pairs={{0,68},{1,69},{2,70},{3,71},{4,64},{5,65},{6,66},{7,67},{8,72},{9,... | collective-permute-start | bytes 2949128 | tf_op jit(solution)/shard_map/ppermute | solution.py:67
  44.7 13.3 %collective-permute-start.12 = (bf16[2,8,8,3840]{3,2,1,0:T(8,128)(2,1)S(1)}, bf16[2,8,8,3840]{3,2,1,0:T(8,128)(2,1)S(1)}, u32[]{:S(2)}, u32[]{:S(2)}) collective-permute-start(bf16[2,8,8,3840]{3,2,1,0:T(8,128)(2,1)S(1)} %get-tuple-element.55.refs_0_), channel_id=1, source_target_pairs={{0,48},{1,49},{2,50},{3,51},{4,52},{5,53},{6,54},{7,55},{8,24},{9,... | collective-permute-start | bytes 2949128 | tf_op jit(solution)/shard_map/ppermute | solution.py:67
  44.8 13.6 %collective-permute-start.11 = (bf16[2,8,8,11392]{3,2,1,0:T(8,128)(2,1)S(1)}, bf16[2,8,8,11392]{3,2,1,0:T(8,128)(2,1)S(1)}, u32[]{:S(2)}, u32[]{:S(2)}) collective-permute-start(bf16[2,8,8,11392]{3,2,1,0:T(8,128)(2,1)S(1)} %maximum_maximum_fusion), channel_id=1, source_target_pairs={{0,8},{1,9},{2,10},{3,11},{4,12},{5,13},{6,14},{7,15},{8,0},{9,1},... | collective-permute-start | bytes 8749064 | tf_op jit(solution)/shard_map/ppermute | solution.py:63
  58.5 15.0 %collective-permute-start.15 = (bf16[2,8,8,11392]{3,2,1,0:T(8,128)(2,1)S(1)}, bf16[2,8,8,11392]{3,2,1,0:T(8,128)(2,1)S(1)}, u32[]{:S(2)}, u32[]{:S(2)}) collective-permute-start(bf16[2,8,8,11392]{3,2,1,0:T(8,128)(2,1)S(1)} %shard_map.71), channel_id=1, source_target_pairs={{0,8},{1,9},{2,10},{3,11},{4,12},{5,13},{6,14},{7,15},{8,0},{9,1},... | collective-permute-start | bytes 8749064 | tf_op jit(solution)/shard_map/ppermute | solution.py:63
  60.5 13.0 %collective-permute-start.19 = (bf16[2,2,8,8,1792]{4,3,2,1,0:T(8,128)(2,1)S(1)}, bf16[2,2,8,8,1792]{4,3,2,1,0:T(8,128)(2,1)S(1)}, u32[]{:S(2)}, u32[]{:S(2)}) collective-permute-start(bf16[2,2,8,8,1792]{4,3,2,1,0:T(8,128)(2,1)S(1)} %slice.51), channel_id=1, source_target_pairs={{0,3},{1,2},{2,1},{3,0},{4,7},{5,6},{6,5},{7,4},{8,9},{9,8},{10,11... | collective-permute-start | bytes 2752520 | tf_op jit(solution)/shard_map/ppermute | solution.py:67
  60.7 18.8 %collective-permute-start.17 = (bf16[2,2,8,8,2048]{4,3,2,1,0:T(8,128)(2,1)S(1)}, bf16[2,2,8,8,2048]{4,3,2,1,0:T(8,128)(2,1)S(1)}, u32[]{:S(2)}, u32[]{:S(2)}) collective-permute-start(bf16[2,2,8,8,2048]{4,3,2,1,0:T(8,128)(2,1)S(1)} %slice.50), channel_id=1, source_target_pairs={{0,68},{1,69},{2,70},{3,71},{4,64},{5,65},{6,66},{7,67},{8,72},{9,... | collective-permute-start | bytes 3145736 | tf_op jit(solution)/shard_map/ppermute | solution.py:67
  61.2 18.4 %collective-permute-start.21 = (bf16[2,2,8,8,1792]{4,3,2,1,0:T(8,128)(2,1)S(1)}, bf16[2,2,8,8,1792]{4,3,2,1,0:T(8,128)(2,1)S(1)}, u32[]{:S(2)}, u32[]{:S(2)}) collective-permute-start(bf16[2,2,8,8,1792]{4,3,2,1,0:T(8,128)(2,1)S(1)} %slice.52), channel_id=1, source_target_pairs={{0,48},{1,49},{2,50},{3,51},{4,52},{5,53},{6,54},{7,55},{8,24},{9,... | collective-permute-start | bytes 2752520 | tf_op jit(solution)/shard_map/ppermute | solution.py:67
  73.5 0.7 copy-start
  74.2 7.4 %collective-permute-start.20 = (bf16[2,2,8,8,1792]{4,3,2,1,0:T(8,128)(2,1)S(1)}, bf16[2,2,8,8,1792]{4,3,2,1,0:T(8,128)(2,1)S(1)}, u32[]{:S(2)}, u32[]{:S(2)}) collective-permute-start(bf16[2,2,8,8,1792]{4,3,2,1,0:T(8,128)(2,1)S(1)} %shard_map.75.refs_5_), channel_id=1, source_target_pairs={{0,8},{1,9},{2,10},{3,11},{4,12},{5,13},{6,14},{7,15},{8,0},{9,1},... | collective-permute-start | bytes 2752520 | tf_op jit(solution)/shard_map/ppermute | solution.py:63
  79.5 7.9 %collective-permute-start.18 = (bf16[2,2,8,8,2048]{4,3,2,1,0:T(8,128)(2,1)S(1)}, bf16[2,2,8,8,2048]{4,3,2,1,0:T(8,128)(2,1)S(1)}, u32[]{:S(2)}, u32[]{:S(2)}) collective-permute-start(bf16[2,2,8,8,2048]{4,3,2,1,0:T(8,128)(2,1)S(1)} %shard_map.74.refs_2_), channel_id=1, source_target_pairs={{0,8},{1,9},{2,10},{3,11},{4,12},{5,13},{6,14},{7,15},{8,0},{9,1},... | collective-permute-start | bytes 3145736 | tf_op jit(solution)/shard_map/ppermute | solution.py:63
  79.6 7.8 %collective-permute-start.22 = (bf16[2,2,8,8,1792]{4,3,2,1,0:T(8,128)(2,1)S(1)}, bf16[2,2,8,8,1792]{4,3,2,1,0:T(8,128)(2,1)S(1)}, u32[]{:S(2)}, u32[]{:S(2)}) collective-permute-start(bf16[2,2,8,8,1792]{4,3,2,1,0:T(8,128)(2,1)S(1)} %shard_map.76.refs_8_), channel_id=1, source_target_pairs={{0,8},{1,9},{2,10},{3,11},{4,12},{5,13},{6,14},{7,15},{8,0},{9,1},... | collective-permute-start | bytes 2752520 | tf_op jit(solution)/shard_map/ppermute | solution.py:63
  80.1 15.0 %collective-permute-start.24 = (bf16[2,2,8,8,2048]{4,3,2,1,0:T(8,128)(2,1)S(1)}, bf16[2,2,8,8,2048]{4,3,2,1,0:T(8,128)(2,1)S(1)}, u32[]{:S(2)}, u32[]{:S(2)}) collective-permute-start(bf16[2,2,8,8,2048]{4,3,2,1,0:T(8,128)(2,1)S(1)} %slice.53), channel_id=1, source_target_pairs={{0,3},{1,2},{2,1},{3,0},{4,7},{5,6},{6,5},{7,4},{8,9},{9,8},{10,11... | collective-permute-start | bytes 3145736 | tf_op jit(solution)/shard_map/ppermute | solution.py:67
  80.7 17.7 %collective-permute-start.26 = (bf16[2,2,8,8,1920]{4,3,2,1,0:T(8,128)(2,1)S(1)}, bf16[2,2,8,8,1920]{4,3,2,1,0:T(8,128)(2,1)S(1)}, u32[]{:S(2)}, u32[]{:S(2)}) collective-permute-start(bf16[2,2,8,8,1920]{4,3,2,1,0:T(8,128)(2,1)S(1)} %slice.54), channel_id=1, source_target_pairs={{0,48},{1,49},{2,50},{3,51},{4,52},{5,53},{6,54},{7,55},{8,24},{9,... | collective-permute-start | bytes 2949128 | tf_op jit(solution)/shard_map/ppermute | solution.py:67
  81.6 17.0 %collective-permute-start.16 = (bf16[2,2,8,8,1792]{4,3,2,1,0:T(8,128)(2,1)S(1)}, bf16[2,2,8,8,1792]{4,3,2,1,0:T(8,128)(2,1)S(1)}, u32[]{:S(2)}, u32[]{:S(2)}) collective-permute-start(bf16[2,2,8,8,1792]{4,3,2,1,0:T(8,128)(2,1)S(1)} %slice.49), channel_id=1, source_target_pairs={{0,68},{1,69},{2,70},{3,71},{4,64},{5,65},{6,66},{7,67},{8,72},{9,... | collective-permute-start | bytes 2752520 | tf_op jit(solution)/shard_map/ppermute | solution.py:67
  95.1 9.6 %collective-permute-start.25 = (bf16[2,2,8,8,2048]{4,3,2,1,0:T(8,128)(2,1)S(1)}, bf16[2,2,8,8,2048]{4,3,2,1,0:T(8,128)(2,1)S(1)}, u32[]{:S(2)}, u32[]{:S(2)}) collective-permute-start(bf16[2,2,8,8,2048]{4,3,2,1,0:T(8,128)(2,1)S(1)} %shard_map.80.refs_5_), channel_id=1, source_target_pairs={{0,8},{1,9},{2,10},{3,11},{4,12},{5,13},{6,14},{7,15},{8,0},{9,1},... | collective-permute-start | bytes 3145736 | tf_op jit(solution)/shard_map/ppermute | solution.py:63
  98.4 6.3 %collective-permute-start.27 = (bf16[2,2,8,8,1920]{4,3,2,1,0:T(8,128)(2,1)S(1)}, bf16[2,2,8,8,1920]{4,3,2,1,0:T(8,128)(2,1)S(1)}, u32[]{:S(2)}, u32[]{:S(2)}) collective-permute-start(bf16[2,2,8,8,1920]{4,3,2,1,0:T(8,128)(2,1)S(1)} %shard_map.81.refs_8_), channel_id=1, source_target_pairs={{0,8},{1,9},{2,10},{3,11},{4,12},{5,13},{6,14},{7,15},{8,0},{9,1},... | collective-permute-start | bytes 2949128 | tf_op jit(solution)/shard_map/ppermute | solution.py:63
  98.5 6.2 %collective-permute-start.23 = (bf16[2,2,8,8,1792]{4,3,2,1,0:T(8,128)(2,1)S(1)}, bf16[2,2,8,8,1792]{4,3,2,1,0:T(8,128)(2,1)S(1)}, u32[]{:S(2)}, u32[]{:S(2)}) collective-permute-start(bf16[2,2,8,8,1792]{4,3,2,1,0:T(8,128)(2,1)S(1)} %shard_map.79.refs_2_), channel_id=1, source_target_pairs={{0,8},{1,9},{2,10},{3,11},{4,12},{5,13},{6,14},{7,15},{8,0},{9,1},... | collective-permute-start | bytes 2752520 | tf_op jit(solution)/shard_map/ppermute | solution.py:63
  112.7 1.2 %collective-permute-start.28 = (f32[4,128]{1,0:T(4,128)S(1)}, f32[4,128]{1,0:T(4,128)S(1)}, u32[]{:S(2)}, u32[]{:S(2)}) collective-permute-start(f32[4,128]{1,0:T(4,128)S(1)} %get-tuple-element.45), channel_id=1, source_target_pairs={{0,8},{1,9},{2,10},{3,11},{4,12},{5,13},{6,14},{7,15},{8,0},{9,1},... | collective-permute-start | bytes 6152 | tf_op jit(solution)/shard_map/ppermute | solution.py:63

commit v8 on v7

--- a/solution.py
+++ b/solution.py
@@ -354,18 +354,21 @@
     cross = acc_a[...].reshape(VAL, TOK) * acc_g[...].reshape(VAL, TOK)
     kern = ka[...] * kg[...]
     all_ids = ids[...]
-    row_ids = jnp.transpose(all_ids)[0:1, :]
     even = jnp.concatenate([all_ids[b * 64:b * 64 + 32] for b in range(8)], axis=0)
     half_ids = jnp.where(c == 0, even, all_ids[256:512])
-    for v in range(NVAL):
-        keep = jnp.where(all_ids == float(v), 1.0, 0.0)
-        keep = jnp.concatenate([keep] * 4, axis=1)
-        raw_ref[v:v + 1, :] = jnp.sum(cross * keep, axis=0, keepdims=True)
-        keep = jnp.where(half_ids == float(v), 1.0, 0.0)
-        keep = jnp.concatenate([keep] * 4, axis=1)
-        part = jnp.sum(kern * keep, axis=0, keepdims=True)
-        part = jnp.sum(jnp.where(row_ids == float(v), part, 0.0))
-        norm_ref[v:v + 1, :] = jnp.full((1, 128), part, jnp.float32)
+
+    def onehot(x):
+        n = x.shape[0]
+        want = lax.broadcasted_iota(jnp.int32, (8, n), 0).astype(jnp.float32)
+        return jnp.where(jnp.transpose(x)[0:8, :] == want, 1.0, 0.0)
+
+    def total(a, b):
+        return jnp.dot(a, b, precision=lax.Precision.HIGHEST, preferred_element_type=jnp.float32)
+
+    each = onehot(all_ids)
+    raw_ref[...] = total(each, cross)[0:NVAL]
+    norm = jnp.sum(total(onehot(half_ids), kern) * each, axis=1, keepdims=True)
+    norm_ref[...] = jnp.broadcast_to(norm, (8, 128))[0:NVAL]
 
 
 ACC = jax.ShapeDtypeStruct((8, 8, 8, TOK), jnp.float32)
@@ -416,14 +419,15 @@
         return hop(block, [a for a in "xyz" if n & WEIGHT[a]], 0)
 
     near = {n: send(rows, n) for n in (1, 2, 4, 3)}
-    (again,) = gate([rows], near[1])
+    (again,) = gate([rows], near[3])
     near.update({n: send(again, n) for n in (5, 6, 7)})
-    rows = jnp.stack([rows] + [near[n] for n in range(1, 8)])
+    sg = self_call(out_grads, near[3])
+    (rows,) = gate([jnp.stack([rows] + [near[n] for n in range(1, 8)])], sg)
     x = [double(rows[..., s:s + w], RUNS[j], 1) for j, (s, w) in enumerate(zip(STARTS, WIDTHS))]
-    sa = self_call(hidden_acts, x[1])
+    block_gram = self_call(hidden_acts, x[1], sg)
     a1 = [hop(x[j], STEP5[j], 1) for j in range(3)]
     o0 = swap(jnp.concatenate(x, axis=-1))
-    pair = gate([jnp.stack([x[j], a1[j]]) for j in range(3)], sa, o0)
+    pair = gate([jnp.stack([x[j], a1[j]]) for j in range(3)], block_gram, o0)
     last = [
         [hop(pair[j][..., a:a + w], STEP6[j], 1) for j, (a, w) in enumerate(zip(at, width))]
         for at, width in zip(SETAT, SETW)
@@ -434,11 +438,9 @@
     )
     unit = 512 * (HA + HG)
     ca, cg, tok = call(
-        early_body, args=[sa] + [y for j in range(3) for y in (x[j], a1[j])],
+        early_body, args=[block_gram] + [y for j in range(3) for y in (x[j], a1[j])],
         outs=[ACC, ACC, TOKEN], flops=512 * unit, width=C1, pinned=range(1, 7), mib=28,
     )
-    block_gram = self_call(out_grads, tok, sa)
-    tok = block_gram
     sums = [ca, cg]
     for which in range(2):
         got = [gate([y], tok, *([] if which else [o1]))[0] for y in last[which]]

time: 115 us -> 116 us (level)
  starting transfers between devices: 34.9 us -> 37.1 us
  waiting for transfers between devices: 23.4 us -> 22 us
    ppermute x10, starting transfers between devices: 15.5 us -> 18 us  [swap(): return lax.ppermute(x, AXES, core_pairs())]
  transfers between devices with their start and end apart: 29 -> 29, of which waited for: 9 -> 9; matrix products, arithmetic and copies ran while one was open for 2% -> 2% of each run, Pallas kernels for 36% -> 35%
where the time goes in v8:
time: 116 us
  Pallas kernels  49.3 us (42%)
  starting transfers between devices  37.1 us (32%)
  waiting for transfers between devices  22 us (19%)
  other arithmetic  3.22 us (3%)
  local copies, waits for them, and re-layouts  3.04 us (3%)
    pallas_call x5, Pallas kernels, local_call(): pl.pallas_call(body, in_specs=[pl.BlockSpec(memory_space=pltpu.SMEM)] + [...  33.5 us
    ppermute x19, waiting for transfers between devices, hop(): return lax.ppermute(x, AXES, ring_pairs(axes, step))  20.2 us
    ppermute x19, starting transfers between devices, hop(): return lax.ppermute(x, AXES, ring_pairs(axes, step))  19.1 us
    ppermute x10, starting transfers between devices, swap(): return lax.ppermute(x, AXES, core_pairs())  18 us
    pallas_call x2, Pallas kernels, self_call(): pl.pallas_call(body, grid=(width // KC,), in_specs=[pl.BlockSpec((TOK, KC...  15.8 us
  transfers between devices with their start and end apart: 29, of which 9 were waited for; matrix products, arithmetic and copies ran while one was open for 2% of the time, Pallas kernels for 35%

profile of v8, /device:TPU:1, one launch (start us, length us, event | category | flops | bytes accessed | tf_op | source)
XLA Modules:
  0.0 115.7 jit_solution(2580875745533114001)
XLA Ops:
  0.6 0.7 convert_element_type.4
  1.3 0.8 fusion.4
  2.1 0.9 fusion.3
  3.2 1.5 %collective-permute-start = (bf16[4,11392]{1,0:T(4,128)(2,1)S(1)}, bf16[4,11392]{1,0:T(4,128)(2,1)S(1)}, u32[]{:S(2)}, u32[]{:S(2)}) collective-permute-start(bf16[4,11392]{1,0:T(4,128)(2,1)S(1)} %broadcast_select_fusion.2), channel_id=1, source_target_pairs={{0,8},{1,9},{2,10},{3,11},{4,12},{5,13},{6,14},{7,15},{8,0},{9,1},... | collective-permute-start | bytes 273416 | tf_op jit(solution)/shard_map/ppermute | solution.py:63
  4.7 0.9 collective-permute-done
  5.6 0.1 broadcast_select_fusion.1
  5.8 2.6 %collective-permute-start.4 = (bf16[8,11392]{1,0:T(8,128)(2,1)S(1)}, bf16[8,11392]{1,0:T(8,128)(2,1)S(1)}, u32[]{:S(2)}, u32[]{:S(2)}) collective-permute-start(bf16[8,11392]{1,0:T(8,128)(2,1)S(1)} %pad_maximum_fusion.7.refs_0_), channel_id=1, source_target_pairs={{0,64},{1,65},{2,66},{3,67},{4,68},{5,69},{6,70},{7,71},{8,76},{9,... | collective-permute-start | bytes 546824 | tf_op jit(solution)/shard_map/ppermute | solution.py:67
  8.5 6.2 %collective-permute-start.3 = (bf16[8,11392]{1,0:T(8,128)(2,1)S(1)}, bf16[8,11392]{1,0:T(8,128)(2,1)S(1)}, u32[]{:S(2)}, u32[]{:S(2)}) collective-permute-start(bf16[8,11392]{1,0:T(8,128)(2,1)S(1)} %pad_maximum_fusion.7.refs_0_), channel_id=1, source_target_pairs={{0,17},{1,16},{2,19},{3,18},{4,21},{5,20},{6,23},{7,22},{8,59},{9,... | collective-permute-start | bytes 546824 | tf_op jit(solution)/shard_map/ppermute | solution.py:67
  14.7 0.3 collective-permute-start.1
  15.1 2.5 %collective-permute-done.3.refs_1_.dep_ref = bf16[8,11392]{1,0:T(8,128)(2,1)S(1)} collective-permute-done((bf16[8,11392]{1,0:T(8,128)(2,1)S(1)}, bf16[8,11392]{1,0:T(8,128)(2,1)S(1)}, u32[]{:S(2)}, u32[]{:S(2)}) %collective-permute-start.3) | collective-permute-done | bytes 182304 | tf_op jit(solution)/shard_map/ppermute | solution.py:67
  17.6 2.7 %collective-permute-done.2 = bf16[8,11392]{1,0:T(8,128)(2,1)S(1)} collective-permute-done((bf16[8,11392]{1,0:T(8,128)(2,1)S(1)}, bf16[8,11392]{1,0:T(8,128)(2,1)S(1)}, u32[]{:S(2)}, u32[]{:S(2)}) %collective-permute-start.2) | collective-permute-done | bytes 182304 | tf_op jit(solution)/shard_map/ppermute | solution.py:67
  20.2 4.0 %collective-permute-start.7 = (bf16[8,11392]{1,0:T(8,128)(2,1)S(1)}, bf16[8,11392]{1,0:T(8,128)(2,1)S(1)}, u32[]{:S(2)}, u32[]{:S(2)}) collective-permute-start(bf16[8,11392]{1,0:T(8,128)(2,1)S(1)} %shard_map.68), channel_id=1, source_target_pairs={{0,81},{1,80},{2,83},{3,82},{4,85},{5,84},{6,87},{7,86},{8,127},{9... | collective-permute-start | bytes 546824 | tf_op jit(solution)/shard_map/ppermute | solution.py:67
  24.2 2.1 %collective-permute-start.6 = (bf16[8,11392]{1,0:T(8,128)(2,1)S(1)}, bf16[8,11392]{1,0:T(8,128)(2,1)S(1)}, u32[]{:S(2)}, u32[]{:S(2)}) collective-permute-start(bf16[8,11392]{1,0:T(8,128)(2,1)S(1)} %shard_map.68), channel_id=1, source_target_pairs={{0,65},{1,64},{2,67},{3,66},{4,69},{5,68},{6,71},{7,70},{8,79},{9,... | collective-permute-start | bytes 546824 | tf_op jit(solution)/shard_map/ppermute | solution.py:67
  26.4 1.1 collective-permute-start.5
  27.5 5.6 %shard_map.69.refs_1_.first_ref = f32[512,256]{1,0:T(8,128)S(1)} custom-call(bf16[512,8192]{1,0:T(8,128)(2,1)} %grads.9, bf16[8,11392]{1,0:T(8,128)(2,1)S(1)} %collective-permute-done.3.refs_1_.dep_ref), custom_call_target="tpu_custom_call" | custom-call | flops 2147483648 | bytes 8388608 | tf_op jit(solution)/shard_map/pallas_call | solution.py:146
  33.2 1.1 collective-permute-done.5
  34.5 0.1 slice_bitcast_fusion.2
  34.8 7.5 %collective-permute-done.10 = bf16[8,8,3712]{2,1,0:T(8,128)(2,1)S(1)} collective-permute-done((bf16[8,8,3712]{2,1,0:T(8,128)(2,1)S(1)}, bf16[8,8,3712]{2,1,0:T(8,128)(2,1)S(1)}, u32[]{:S(2)}, u32[]{:S(2)}) %collective-permute-start.10) | collective-permute-done | bytes 475168 | tf_op jit(solution)/shard_map/ppermute | solution.py:67
  42.3 0.1 fusion
  42.5 0.2 collective-permute-done.9
  42.7 0.1 fusion.1
  42.8 1.5 %collective-permute-start.13 = (bf16[2,8,8,3840]{3,2,1,0:T(8,128)(2,1)S(1)}, bf16[2,8,8,3840]{3,2,1,0:T(8,128)(2,1)S(1)}, u32[]{:S(2)}, u32[]{:S(2)}) collective-permute-start(bf16[2,8,8,3840]{3,2,1,0:T(8,128)(2,1)S(1)} %get-tuple-element.53.dep_ref.refs_2_.refs_3_), channel_id=1, source_target_pairs={{0,68},{1,69},{2,70},{3,71},{4,64},{5,65},{6,66},{7,67},{8,72},{9,... | collective-permute-start | bytes 2949128 | tf_op jit(solution)/shard_map/ppermute | solution.py:67
  44.4 0.2 maximum_maximum_fusion
  44.6 0.1 fusion.2
  44.8 2.3 %collective-permute-start.11 = (bf16[2,8,8,11392]{3,2,1,0:T(8,128)(2,1)S(1)}, bf16[2,8,8,11392]{3,2,1,0:T(8,128)(2,1)S(1)}, u32[]{:S(2)}, u32[]{:S(2)}) collective-permute-start(bf16[2,8,8,11392]{3,2,1,0:T(8,128)(2,1)S(1)} %maximum_maximum_fusion), channel_id=1, source_target_pairs={{0,8},{1,9},{2,10},{3,11},{4,12},{5,13},{6,14},{7,15},{8,0},{9,1},... | collective-permute-start | bytes 8749064 | tf_op jit(solution)/shard_map/ppermute | solution.py:63
  47.1 10.2 %shard_map.71.refs_3_.dep_ref = f32[4,4]{1,0:T(4,128)} custom-call(bf16[512,14336]{1,0:T(8,128)(2,1)} %acts.9, f32[512,256]{1,0:T(8,128)S(1)} %shard_map.69.refs_1_.first_ref, bf16[2,8,8,3840]{3,2,1,0:T(8,128)(2,1)S(1)} %get-tuple-element.53.dep_ref.refs_2_.refs_3_), custom_call_target="tpu_custom_call" | custom-call | flops 3758096384 | bytes 14680064 | tf_op jit(solution)/shard_map/pallas_call | solution.py:146
  57.3 0.2 pad_maximum_fusion.3.refs_2_
  57.5 0.2 pad_maximum_fusion.2.refs_1_
  57.7 0.3 collective-permute-done.12.refs_1_
  58.0 0.2 pad_maximum_fusion.1.refs_0_
  58.2 0.2 pad_maximum_fusion.refs_0_
  58.5 0.5 copy-done
  58.9 1.9 %collective-permute-start.15 = (bf16[2,8,8,11392]{3,2,1,0:T(8,128)(2,1)S(1)}, bf16[2,8,8,11392]{3,2,1,0:T(8,128)(2,1)S(1)}, u32[]{:S(2)}, u32[]{:S(2)}) collective-permute-start(bf16[2,8,8,11392]{3,2,1,0:T(8,128)(2,1)S(1)} %shard_map.73), channel_id=1, source_target_pairs={{0,8},{1,9},{2,10},{3,11},{4,12},{5,13},{6,14},{7,15},{8,0},{9,1},... | collective-permute-start | bytes 8749064 | tf_op jit(solution)/shard_map/ppermute | solution.py:63
  61.1 0.4 collective-permute-start.17
  61.6 5.9 %shard_map.74 = (f32[8,8,8,512]{3,2,1,0:T(8,128)S(1)}, f32[8,8,8,512]{3,2,1,0:T(8,128)S(1)}, f32[8,128]{1,0:T(8,128)S(1)}) custom-call(s32[1]{0:T(128)} %bitcast.core_ref, bf16[512,14336]{1,0:T(8,128)(2,1)} %acts.9, bf16[512,8192]{1,0:T(8,128)(2,1)} %grads.9, f32[4,4]{1,0:T(4,128)S(1)} %copy-done, bf16[2,8,8,3840]{3,2,1,0:T(8,128)(2,1)S(1)} %get-tuple-element.55.refs_0_, ...), custom_call_target="tpu_custom_call" | custom-call | flops 2952790016 | bytes 11534336 | tf_op jit(solution)/shard_map/pallas_call | solution.py:385
  67.5 6.0 %collective-permute-done.19.refs_0_ = bf16[2,2,8,8,1792]{4,3,2,1,0:T(8,128)(2,1)S(1)} collective-permute-done((bf16[2,2,8,8,1792]{4,3,2,1,0:T(8,128)(2,1)S(1)}, bf16[2,2,8,8,1792]{4,3,2,1,0:T(8,128)(2,1)S(1)}, u32[]{:S(2)}, u32[]{:S(2)}) %collective-permute-start.19) | collective-permute-done | bytes 917536 | tf_op jit(solution)/shard_map/ppermute | solution.py:67
  73.5 2.1 %collective-permute-start.20 = (bf16[2,2,8,8,1792]{4,3,2,1,0:T(8,128)(2,1)S(1)}, bf16[2,2,8,8,1792]{4,3,2,1,0:T(8,128)(2,1)S(1)}, u32[]{:S(2)}, u32[]{:S(2)}) collective-permute-start(bf16[2,2,8,8,1792]{4,3,2,1,0:T(8,128)(2,1)S(1)} %shard_map.76.refs_5_), channel_id=1, source_target_pairs={{0,8},{1,9},{2,10},{3,11},{4,12},{5,13},{6,14},{7,15},{8,0},{9,1},... | collective-permute-start | bytes 2752520 | tf_op jit(solution)/shard_map/ppermute | solution.py:63
  75.6 4.0 %collective-permute-start.18 = (bf16[2,2,8,8,2048]{4,3,2,1,0:T(8,128)(2,1)S(1)}, bf16[2,2,8,8,2048]{4,3,2,1,0:T(8,128)(2,1)S(1)}, u32[]{:S(2)}, u32[]{:S(2)}) collective-permute-start(bf16[2,2,8,8,2048]{4,3,2,1,0:T(8,128)(2,1)S(1)} %shard_map.75.refs_2_), channel_id=1, source_target_pairs={{0,8},{1,9},{2,10},{3,11},{4,12},{5,13},{6,14},{7,15},{8,0},{9,1},... | collective-permute-start | bytes 3145736 | tf_op jit(solution)/shard_map/ppermute | solution.py:63
  80.3 5.8 %shard_map.78 = (f32[8,8,8,512]{3,2,1,0:T(8,128)S(1)}, f32[8,8,8,512]{3,2,1,0:T(8,128)S(1)}, f32[256,512]{1,0:T(8,128)S(1)}, f32[256,512]{1,0:T(8,128)S(1)}) custom-call(s32[1]{0:T(128)} %bitcast.core_ref, bf16[512,14336]{1,0:T(8,128)(2,1)} %acts.9, bf16[512,8192]{1,0:T(8,128)(2,1)} %grads.9, bf16[2,8,8,3840]{3,2,1,0:T(8,128)(2,1)S(1)} %get-tuple-element.55.refs_0_, ...), custom_call_target="tpu_custom_call" | custom-call | flops 2952790016 | bytes 11534336 | tf_op jit(solution)/shard_map/pallas_call | solution.py:385
  86.1 7.7 %shard_map.79 = (f32[8,8,8,512]{3,2,1,0:T(8,128)S(1)}, f32[8,8,8,512]{3,2,1,0:T(8,128)S(1)}, f32[256,512]{1,0:T(8,128)S(1)}, f32[256,512]{1,0:T(8,128)S(1)}, f32[8,128]{1,0:T(8,128)S(1)}) custom-call(s32[1]{0:T(128)} %bitcast.core_ref, bf16[512,14336]{1,0:T(8,128)(2,1)} %acts.9, bf16[512,8192]{1,0:T(8,128)(2,1)} %grads.9, ...), custom_call_target="tpu_custom_call" | custom-call | flops 4429185024 | bytes 11534336 | tf_op jit(solution)/shard_map/pallas_call | solution.py:385
  93.9 5.2 %collective-permute-start.25 = (bf16[2,2,8,8,2048]{4,3,2,1,0:T(8,128)(2,1)S(1)}, bf16[2,2,8,8,2048]{4,3,2,1,0:T(8,128)(2,1)S(1)}, u32[]{:S(2)}, u32[]{:S(2)}) collective-permute-start(bf16[2,2,8,8,2048]{4,3,2,1,0:T(8,128)(2,1)S(1)} %shard_map.81.refs_5_), channel_id=1, source_target_pairs={{0,8},{1,9},{2,10},{3,11},{4,12},{5,13},{6,14},{7,15},{8,0},{9,1},... | collective-permute-start | bytes 3145736 | tf_op jit(solution)/shard_map/ppermute | solution.py:63
  99.2 0.4 collective-permute-start.23
  99.6 5.8 %shard_map.83 = (f32[8,8,8,512]{3,2,1,0:T(8,128)S(1)}, f32[8,8,8,512]{3,2,1,0:T(8,128)S(1)}, f32[256,512]{1,0:T(8,128)S(1)}, f32[256,512]{1,0:T(8,128)S(1)}, f32[512,128]{1,0:T(8,128)S(1)}) custom-call(s32[1]{0:T(128)} %bitcast.core_ref, bf16[512,14336]{1,0:T(8,128)(2,1)} %acts.9, bf16[512,8192]{1,0:T(8,128)(2,1)} %grads.9, ...), custom_call_target="tpu_custom_call" | custom-call | flops 2952790016 | bytes 11534336 | tf_op jit(solution)/shard_map/pallas_call | solution.py:385
  105.4 8.3 %shard_map.84 = (f32[4,512]{1,0:T(4,128)S(1)}, f32[4,128]{1,0:T(4,128)S(1)}) custom-call(s32[1]{0:T(128)} %bitcast.core_ref, bf16[512,14336]{1,0:T(8,128)(2,1)} %acts.9, bf16[512,8192]{1,0:T(8,128)(2,1)} %grads.9, bf16[2,8,8,11392]{3,2,1,0:T(8,128)(2,1)S(1)} %collective-permute-done.11.refs_4_.o0, ...), custom_call_target="tpu_custom_call" | custom-call | flops 4429185024 | bytes 11534336 | tf_op jit(solution)/shard_map/pallas_call | solution.py:385
  113.7 0.4 collective-permute-start.28
  114.1 0.8 collective-permute-done.28
  114.9 0.1 rsqrt_reduce_fusion
  115.1 0.7 broadcast_multiply_fusion
  (63 shorter events, 2.2 us)
Async XLA Ops:
  3.2 2.4 %collective-permute-start = (bf16[4,11392]{1,0:T(4,128)(2,1)S(1)}, bf16[4,11392]{1,0:T(4,128)(2,1)S(1)}, u32[]{:S(2)}, u32[]{:S(2)}) collective-permute-start(bf16[4,11392]{1,0:T(4,128)(2,1)S(1)} %broadcast_select_fusion.2), channel_id=1, source_target_pairs={{0,8},{1,9},{2,10},{3,11},{4,12},{5,13},{6,14},{7,15},{8,0},{9,1},... | collective-permute-start | bytes 273416 | tf_op jit(solution)/shard_map/ppermute | solution.py:63
  5.8 9.2 %collective-permute-start.4 = (bf16[8,11392]{1,0:T(8,128)(2,1)S(1)}, bf16[8,11392]{1,0:T(8,128)(2,1)S(1)}, u32[]{:S(2)}, u32[]{:S(2)}) collective-permute-start(bf16[8,11392]{1,0:T(8,128)(2,1)S(1)} %pad_maximum_fusion.7.refs_0_), channel_id=1, source_target_pairs={{0,64},{1,65},{2,66},{3,67},{4,68},{5,69},{6,70},{7,71},{8,76},{9,... | collective-permute-start | bytes 546824 | tf_op jit(solution)/shard_map/ppermute | solution.py:67
  8.5 9.1 %collective-permute-start.3 = (bf16[8,11392]{1,0:T(8,128)(2,1)S(1)}, bf16[8,11392]{1,0:T(8,128)(2,1)S(1)}, u32[]{:S(2)}, u32[]{:S(2)}) collective-permute-start(bf16[8,11392]{1,0:T(8,128)(2,1)S(1)} %pad_maximum_fusion.7.refs_0_), channel_id=1, source_target_pairs={{0,17},{1,16},{2,19},{3,18},{4,21},{5,20},{6,23},{7,22},{8,59},{9,... | collective-permute-start | bytes 546824 | tf_op jit(solution)/shard_map/ppermute | solution.py:67
  14.7 5.6 %collective-permute-start.2 = (bf16[8,11392]{1,0:T(8,128)(2,1)S(1)}, bf16[8,11392]{1,0:T(8,128)(2,1)S(1)}, u32[]{:S(2)}, u32[]{:S(2)}) collective-permute-start(bf16[8,11392]{1,0:T(8,128)(2,1)S(1)} %pad_maximum_fusion.7.refs_0_), channel_id=1, source_target_pairs={{0,1},{1,0},{2,3},{3,2},{4,5},{5,4},{6,7},{7,6},{8,11},{9,10},{10,... | collective-permute-start | bytes 546824 | tf_op jit(solution)/shard_map/ppermute | solution.py:67
  14.7 5.6 %collective-permute-start.1 = (bf16[8,11392]{1,0:T(8,128)(2,1)S(1)}, bf16[8,11392]{1,0:T(8,128)(2,1)S(1)}, u32[]{:S(2)}, u32[]{:S(2)}) collective-permute-start(bf16[8,11392]{1,0:T(8,128)(2,1)S(1)} %pad_maximum_fusion.7.refs_0_), channel_id=1, source_target_pairs={{0,16},{1,17},{2,18},{3,19},{4,20},{5,21},{6,22},{7,23},{8,56},{9,... | collective-permute-start | bytes 546824 | tf_op jit(solution)/shard_map/ppermute | solution.py:67
  20.2 14.0 %collective-permute-start.7 = (bf16[8,11392]{1,0:T(8,128)(2,1)S(1)}, bf16[8,11392]{1,0:T(8,128)(2,1)S(1)}, u32[]{:S(2)}, u32[]{:S(2)}) collective-permute-start(bf16[8,11392]{1,0:T(8,128)(2,1)S(1)} %shard_map.68), channel_id=1, source_target_pairs={{0,81},{1,80},{2,83},{3,82},{4,85},{5,84},{6,87},{7,86},{8,127},{9... | collective-permute-start | bytes 546824 | tf_op jit(solution)/shard_map/ppermute | solution.py:67
  24.2 10.0 %collective-permute-start.6 = (bf16[8,11392]{1,0:T(8,128)(2,1)S(1)}, bf16[8,11392]{1,0:T(8,128)(2,1)S(1)}, u32[]{:S(2)}, u32[]{:S(2)}) collective-permute-start(bf16[8,11392]{1,0:T(8,128)(2,1)S(1)} %shard_map.68), channel_id=1, source_target_pairs={{0,65},{1,64},{2,67},{3,66},{4,69},{5,68},{6,71},{7,70},{8,79},{9,... | collective-permute-start | bytes 546824 | tf_op jit(solution)/shard_map/ppermute | solution.py:67
  26.4 7.9 %collective-permute-start.5 = (bf16[8,11392]{1,0:T(8,128)(2,1)S(1)}, bf16[8,11392]{1,0:T(8,128)(2,1)S(1)}, u32[]{:S(2)}, u32[]{:S(2)}) collective-permute-start(bf16[8,11392]{1,0:T(8,128)(2,1)S(1)} %shard_map.68), channel_id=1, source_target_pairs={{0,80},{1,81},{2,82},{3,83},{4,84},{5,85},{6,86},{7,87},{8,124},{9... | collective-permute-start | bytes 546824 | tf_op jit(solution)/shard_map/ppermute | solution.py:67
  34.4 7.9 %collective-permute-start.10 = (bf16[8,8,3712]{2,1,0:T(8,128)(2,1)S(1)}, bf16[8,8,3712]{2,1,0:T(8,128)(2,1)S(1)}, u32[]{:S(2)}, u32[]{:S(2)}) collective-permute-start(bf16[8,8,3712]{2,1,0:T(8,128)(2,1)S(1)} %get-tuple-element.51), channel_id=1, source_target_pairs={{0,68},{1,69},{2,70},{3,71},{4,64},{5,65},{6,66},{7,67},{8,72},{9,... | collective-permute-start | bytes 1425416 | tf_op jit(solution)/shard_map/ppermute | solution.py:67
  34.6 8.1 %collective-permute-start.9 = (bf16[8,8,3840]{2,1,0:T(8,128)(2,1)S(1)}, bf16[8,8,3840]{2,1,0:T(8,128)(2,1)S(1)}, u32[]{:S(2)}, u32[]{:S(2)}) collective-permute-start(bf16[8,8,3840]{2,1,0:T(8,128)(2,1)S(1)} %get-tuple-element.48), channel_id=1, source_target_pairs={{0,48},{1,49},{2,50},{3,51},{4,52},{5,53},{6,54},{7,55},{8,24},{9,... | collective-permute-start | bytes 1474568 | tf_op jit(solution)/shard_map/ppermute | solution.py:67
  34.7 9.6 %collective-permute-start.8 = (bf16[8,8,3840]{2,1,0:T(8,128)(2,1)S(1)}, bf16[8,8,3840]{2,1,0:T(8,128)(2,1)S(1)}, u32[]{:S(2)}, u32[]{:S(2)}) collective-permute-start(bf16[8,8,3840]{2,1,0:T(8,128)(2,1)S(1)} %get-tuple-element.49), channel_id=1, source_target_pairs={{0,3},{1,2},{2,1},{3,0},{4,7},{5,6},{6,5},{7,4},{8,9},{9,8},{10,11... | collective-permute-start | bytes 1474568 | tf_op jit(solution)/shard_map/ppermute | solution.py:67
  42.4 14.9 %collective-permute-start.14 = (bf16[2,8,8,3712]{3,2,1,0:T(8,128)(2,1)S(1)}, bf16[2,8,8,3712]{3,2,1,0:T(8,128)(2,1)S(1)}, u32[]{:S(2)}, u32[]{:S(2)}) collective-permute-start(bf16[2,8,8,3712]{3,2,1,0:T(8,128)(2,1)S(1)} %get-tuple-element.57.refs_4_.refs_6_), channel_id=1, source_target_pairs={{0,3},{1,2},{2,1},{3,0},{4,7},{5,6},{6,5},{7,4},{8,9},{9,8},{10,11... | collective-permute-start | bytes 2850824 | tf_op jit(solution)/shard_map/ppermute | solution.py:67
  42.8 14.7 %collective-permute-start.13 = (bf16[2,8,8,3840]{3,2,1,0:T(8,128)(2,1)S(1)}, bf16[2,8,8,3840]{3,2,1,0:T(8,128)(2,1)S(1)}, u32[]{:S(2)}, u32[]{:S(2)}) collective-permute-start(bf16[2,8,8,3840]{3,2,1,0:T(8,128)(2,1)S(1)} %get-tuple-element.53.dep_ref.refs_2_.refs_3_), channel_id=1, source_target_pairs={{0,68},{1,69},{2,70},{3,71},{4,64},{5,65},{6,66},{7,67},{8,72},{9,... | collective-permute-start | bytes 2949128 | tf_op jit(solution)/shard_map/ppermute | solution.py:67
  44.7 13.3 %collective-permute-start.12 = (bf16[2,8,8,3840]{3,2,1,0:T(8,128)(2,1)S(1)}, bf16[2,8,8,3840]{3,2,1,0:T(8,128)(2,1)S(1)}, u32[]{:S(2)}, u32[]{:S(2)}) collective-permute-start(bf16[2,8,8,3840]{3,2,1,0:T(8,128)(2,1)S(1)} %get-tuple-element.55.refs_0_), channel_id=1, source_target_pairs={{0,48},{1,49},{2,50},{3,51},{4,52},{5,53},{6,54},{7,55},{8,24},{9,... | collective-permute-start | bytes 2949128 | tf_op jit(solution)/shard_map/ppermute | solution.py:67
  44.8 13.6 %collective-permute-start.11 = (bf16[2,8,8,11392]{3,2,1,0:T(8,128)(2,1)S(1)}, bf16[2,8,8,11392]{3,2,1,0:T(8,128)(2,1)S(1)}, u32[]{:S(2)}, u32[]{:S(2)}) collective-permute-start(bf16[2,8,8,11392]{3,2,1,0:T(8,128)(2,1)S(1)} %maximum_maximum_fusion), channel_id=1, source_target_pairs={{0,8},{1,9},{2,10},{3,11},{4,12},{5,13},{6,14},{7,15},{8,0},{9,1},... | collective-permute-start | bytes 8749064 | tf_op jit(solution)/shard_map/ppermute | solution.py:63
  58.2 0.7 copy-start
  58.9 14.6 %collective-permute-start.15 = (bf16[2,8,8,11392]{3,2,1,0:T(8,128)(2,1)S(1)}, bf16[2,8,8,11392]{3,2,1,0:T(8,128)(2,1)S(1)}, u32[]{:S(2)}, u32[]{:S(2)}) collective-permute-start(bf16[2,8,8,11392]{3,2,1,0:T(8,128)(2,1)S(1)} %shard_map.73), channel_id=1, source_target_pairs={{0,8},{1,9},{2,10},{3,11},{4,12},{5,13},{6,14},{7,15},{8,0},{9,1},... | collective-permute-start | bytes 8749064 | tf_op jit(solution)/shard_map/ppermute | solution.py:63
  60.9 12.6 %collective-permute-start.19 = (bf16[2,2,8,8,1792]{4,3,2,1,0:T(8,128)(2,1)S(1)}, bf16[2,2,8,8,1792]{4,3,2,1,0:T(8,128)(2,1)S(1)}, u32[]{:S(2)}, u32[]{:S(2)}) collective-permute-start(bf16[2,2,8,8,1792]{4,3,2,1,0:T(8,128)(2,1)S(1)} %slice.51), channel_id=1, source_target_pairs={{0,3},{1,2},{2,1},{3,0},{4,7},{5,6},{6,5},{7,4},{8,9},{9,8},{10,11... | collective-permute-start | bytes 2752520 | tf_op jit(solution)/shard_map/ppermute | solution.py:67
  61.1 14.5 %collective-permute-start.17 = (bf16[2,2,8,8,2048]{4,3,2,1,0:T(8,128)(2,1)S(1)}, bf16[2,2,8,8,2048]{4,3,2,1,0:T(8,128)(2,1)S(1)}, u32[]{:S(2)}, u32[]{:S(2)}) collective-permute-start(bf16[2,2,8,8,2048]{4,3,2,1,0:T(8,128)(2,1)S(1)} %slice.50), channel_id=1, source_target_pairs={{0,68},{1,69},{2,70},{3,71},{4,64},{5,65},{6,66},{7,67},{8,72},{9,... | collective-permute-start | bytes 3145736 | tf_op jit(solution)/shard_map/ppermute | solution.py:67
  61.5 18.1 %collective-permute-start.21 = (bf16[2,2,8,8,1792]{4,3,2,1,0:T(8,128)(2,1)S(1)}, bf16[2,2,8,8,1792]{4,3,2,1,0:T(8,128)(2,1)S(1)}, u32[]{:S(2)}, u32[]{:S(2)}) collective-permute-start(bf16[2,2,8,8,1792]{4,3,2,1,0:T(8,128)(2,1)S(1)} %slice.52), channel_id=1, source_target_pairs={{0,48},{1,49},{2,50},{3,51},{4,52},{5,53},{6,54},{7,55},{8,24},{9,... | collective-permute-start | bytes 2752520 | tf_op jit(solution)/shard_map/ppermute | solution.py:67
  73.5 6.7 %collective-permute-start.20 = (bf16[2,2,8,8,1792]{4,3,2,1,0:T(8,128)(2,1)S(1)}, bf16[2,2,8,8,1792]{4,3,2,1,0:T(8,128)(2,1)S(1)}, u32[]{:S(2)}, u32[]{:S(2)}) collective-permute-start(bf16[2,2,8,8,1792]{4,3,2,1,0:T(8,128)(2,1)S(1)} %shard_map.76.refs_5_), channel_id=1, source_target_pairs={{0,8},{1,9},{2,10},{3,11},{4,12},{5,13},{6,14},{7,15},{8,0},{9,1},... | collective-permute-start | bytes 2752520 | tf_op jit(solution)/shard_map/ppermute | solution.py:63
  75.6 10.6 %collective-permute-start.18 = (bf16[2,2,8,8,2048]{4,3,2,1,0:T(8,128)(2,1)S(1)}, bf16[2,2,8,8,2048]{4,3,2,1,0:T(8,128)(2,1)S(1)}, u32[]{:S(2)}, u32[]{:S(2)}) collective-permute-start(bf16[2,2,8,8,2048]{4,3,2,1,0:T(8,128)(2,1)S(1)} %shard_map.75.refs_2_), channel_id=1, source_target_pairs={{0,8},{1,9},{2,10},{3,11},{4,12},{5,13},{6,14},{7,15},{8,0},{9,1},... | collective-permute-start | bytes 3145736 | tf_op jit(solution)/shard_map/ppermute | solution.py:63
  79.6 6.5 %collective-permute-start.22 = (bf16[2,2,8,8,1792]{4,3,2,1,0:T(8,128)(2,1)S(1)}, bf16[2,2,8,8,1792]{4,3,2,1,0:T(8,128)(2,1)S(1)}, u32[]{:S(2)}, u32[]{:S(2)}) collective-permute-start(bf16[2,2,8,8,1792]{4,3,2,1,0:T(8,128)(2,1)S(1)} %shard_map.77.refs_8_), channel_id=1, source_target_pairs={{0,8},{1,9},{2,10},{3,11},{4,12},{5,13},{6,14},{7,15},{8,0},{9,1},... | collective-permute-start | bytes 2752520 | tf_op jit(solution)/shard_map/ppermute | solution.py:63
  79.8 14.0 %collective-permute-start.24 = (bf16[2,2,8,8,2048]{4,3,2,1,0:T(8,128)(2,1)S(1)}, bf16[2,2,8,8,2048]{4,3,2,1,0:T(8,128)(2,1)S(1)}, u32[]{:S(2)}, u32[]{:S(2)}) collective-permute-start(bf16[2,2,8,8,2048]{4,3,2,1,0:T(8,128)(2,1)S(1)} %slice.53), channel_id=1, source_target_pairs={{0,3},{1,2},{2,1},{3,0},{4,7},{5,6},{6,5},{7,4},{8,9},{9,8},{10,11... | collective-permute-start | bytes 3145736 | tf_op jit(solution)/shard_map/ppermute | solution.py:67
  80.0 19.0 %collective-permute-start.26 = (bf16[2,2,8,8,1920]{4,3,2,1,0:T(8,128)(2,1)S(1)}, bf16[2,2,8,8,1920]{4,3,2,1,0:T(8,128)(2,1)S(1)}, u32[]{:S(2)}, u32[]{:S(2)}) collective-permute-start(bf16[2,2,8,8,1920]{4,3,2,1,0:T(8,128)(2,1)S(1)} %slice.54), channel_id=1, source_target_pairs={{0,48},{1,49},{2,50},{3,51},{4,52},{5,53},{6,54},{7,55},{8,24},{9,... | collective-permute-start | bytes 2949128 | tf_op jit(solution)/shard_map/ppermute | solution.py:67
  80.2 19.0 %collective-permute-start.16 = (bf16[2,2,8,8,1792]{4,3,2,1,0:T(8,128)(2,1)S(1)}, bf16[2,2,8,8,1792]{4,3,2,1,0:T(8,128)(2,1)S(1)}, u32[]{:S(2)}, u32[]{:S(2)}) collective-permute-start(bf16[2,2,8,8,1792]{4,3,2,1,0:T(8,128)(2,1)S(1)} %slice.49), channel_id=1, source_target_pairs={{0,68},{1,69},{2,70},{3,71},{4,64},{5,65},{6,66},{7,67},{8,72},{9,... | collective-permute-start | bytes 2752520 | tf_op jit(solution)/shard_map/ppermute | solution.py:67
  93.9 11.5 %collective-permute-start.25 = (bf16[2,2,8,8,2048]{4,3,2,1,0:T(8,128)(2,1)S(1)}, bf16[2,2,8,8,2048]{4,3,2,1,0:T(8,128)(2,1)S(1)}, u32[]{:S(2)}, u32[]{:S(2)}) collective-permute-start(bf16[2,2,8,8,2048]{4,3,2,1,0:T(8,128)(2,1)S(1)} %shard_map.81.refs_5_), channel_id=1, source_target_pairs={{0,8},{1,9},{2,10},{3,11},{4,12},{5,13},{6,14},{7,15},{8,0},{9,1},... | collective-permute-start | bytes 3145736 | tf_op jit(solution)/shard_map/ppermute | solution.py:63
  99.0 6.3 %collective-permute-start.27 = (bf16[2,2,8,8,1920]{4,3,2,1,0:T(8,128)(2,1)S(1)}, bf16[2,2,8,8,1920]{4,3,2,1,0:T(8,128)(2,1)S(1)}, u32[]{:S(2)}, u32[]{:S(2)}) collective-permute-start(bf16[2,2,8,8,1920]{4,3,2,1,0:T(8,128)(2,1)S(1)} %shard_map.82.refs_8_), channel_id=1, source_target_pairs={{0,8},{1,9},{2,10},{3,11},{4,12},{5,13},{6,14},{7,15},{8,0},{9,1},... | collective-permute-start | bytes 2949128 | tf_op jit(solution)/shard_map/ppermute | solution.py:63
  99.2 6.2 %collective-permute-start.23 = (bf16[2,2,8,8,1792]{4,3,2,1,0:T(8,128)(2,1)S(1)}, bf16[2,2,8,8,1792]{4,3,2,1,0:T(8,128)(2,1)S(1)}, u32[]{:S(2)}, u32[]{:S(2)}) collective-permute-start(bf16[2,2,8,8,1792]{4,3,2,1,0:T(8,128)(2,1)S(1)} %shard_map.80.refs_2_), channel_id=1, source_target_pairs={{0,8},{1,9},{2,10},{3,11},{4,12},{5,13},{6,14},{7,15},{8,0},{9,1},... | collective-permute-start | bytes 2752520 | tf_op jit(solution)/shard_map/ppermute | solution.py:63
  113.7 1.2 %collective-permute-start.28 = (f32[4,128]{1,0:T(4,128)S(1)}, f32[4,128]{1,0:T(4,128)S(1)}, u32[]{:S(2)}, u32[]{:S(2)}) collective-permute-start(f32[4,128]{1,0:T(4,128)S(1)} %get-tuple-element.45), channel_id=1, source_target_pairs={{0,8},{1,9},{2,10},{3,11},{4,12},{5,13},{6,14},{7,15},{8,0},{9,1},... | collective-permute-start | bytes 6152 | tf_op jit(solution)/shard_map/ppermute | solution.py:63

commit v9 on v7

--- a/solution.py
+++ b/solution.py
@@ -207,9 +207,11 @@
                 cps.append(pltpu.make_async_copy(
                     src.at[:, pl.ds(first, w)], hbuf.at[part, :, pl.ds(at, w)], sems.at[part, i]
                 ))
-            for cp in cps:
-                cp.start()
             self.todo.append(cps)
+
+    def go(self, part):
+        for cp in self.todo[part]:
+            cp.start()
 
     def wait(self, part):
         for cp in self.todo[part]:
@@ -231,11 +233,22 @@
                 acc[place(part, k, s4)] += x[r:r + 64].reshape(8, 8, TOK)
 
 
-def val_rows(core_ref, blocks, ka, kg, name, seen):
+def once(cps):
+    left = list(cps)
+
+    def wait():
+        while left:
+            left.pop().wait()
+
+    return wait
+
+
+def val_rows(core_ref, blocks, ka, kg, name, seen, ready):
     even = jnp.concatenate([x[:32] for x in blocks], axis=0)
     late = jnp.concatenate(blocks[4:], axis=0)
     y = nt(jnp.where(core_ref[0] == 0, even, late), jnp.concatenate(blocks, axis=0))
     acc = ka if name == "a" else kg
+    ready()
     if name in seen:
         acc[...] += y
     else:
@@ -247,6 +260,8 @@
     own = [refs[p * 2:p * 2 + 2] for p in range(3)]
     ca, cg, tok, hbuf, sems = refs[6:]
     train = Train(core_ref, acts, grads, 0, FULL, hbuf, sems)
+    for part in range(3):
+        train.go(part)
     tok[...] = jnp.zeros_like(tok)
     ca[...] = jnp.zeros_like(ca)
     cg[...] = jnp.zeros_like(cg)
@@ -269,7 +284,7 @@
     if which:
         ids = refs[4]
     hbuf, sems, pbuf, psems, asems = refs[4 + which:]
-    sums = bring(list(zip(ins, (ca, cg, ka, kg))), asems)
+    train = Train(core_ref, acts, grads, 0, SETS[which], hbuf, sems)
     todo = []
     for part in range(3):
         x, a1, last = pieces[part]
@@ -280,14 +295,13 @@
             [(src, pbuf.at[part, k, :, :, :, pl.ds(0, w)]) for k, src in enumerate(srcs)],
             psems.at[part],
         ))
-    train = Train(core_ref, acts, grads, 0, SETS[which], hbuf, sems)
+        train.go(part)
+        if part == 0:
+            ready = once(bring(list(zip(ins, (ca, cg, ka, kg))), asems))
     seen = {"a", "g"} if which else set()
     for part in range(3):
         for cp in todo[part]:
             cp.wait()
-        if part == 0:
-            for cp in sums:
-                cp.wait()
 
         def blocks(at, w):
             out = [None] * 8
@@ -297,7 +311,7 @@
             return out
 
         for name, _, at, w in SETS[which][part]:
-            val_rows(core_ref, blocks(at, w), ka, kg, name, seen)
+            val_rows(core_ref, blocks(at, w), ka, kg, name, seen, ready)
         if which and part == 2:
             for b, x in enumerate(blocks(SETW[1][2] - IDW, IDW)):
                 ids[b * 64:b * 64 + 64, :] = x.astype(jnp.float32)
@@ -316,15 +330,16 @@
         acc_a, acc_g, ka, kg, tok, hbuf, sems, vbuf, vsems, asems = refs
         tok[...] = jnp.zeros_like(tok)
         extra = []
-    sums = bring([(ain, acc_a), (gin, acc_g), (k1, ka), (k2, kg)] + extra, asems)
+    train = Train(core_ref, acts, grads, 1, SETS[which], hbuf, sems)
     todo = []
     for part in range(3):
         w = SETW[which][part]
         cols = pl.ds(STARTS[part] + SETAT[which][part], w)
+        first = 0 if which else sum(SETW[0][:part])
         todo.append(bring(
             [
                 (
-                    o.at[s4, :, :, cols] if k < 2 else o.at[s4],
+                    o.at[s4, :, :, cols] if k < 2 else o.at[s4, :, :, pl.ds(first, w)],
                     vbuf.at[part, :, place(part, k, s4), :, pl.ds(0, w)],
                 )
                 for k, o in enumerate((o0, o1, lasts[part].at[0], lasts[part].at[1]))
@@ -332,17 +347,17 @@
             ],
             vsems.at[part],
         ))
-    train = Train(core_ref, acts, grads, 1, SETS[which], hbuf, sems)
+        train.go(part)
+        if part == 0:
+            sums = [(ain, acc_a), (gin, acc_g), (k1, ka), (k2, kg)] + extra
+            ready = once(bring(sums, asems))
     seen = {"a", "g"}
     for part in range(3):
         for cp in todo[part]:
             cp.wait()
-        if part == 0:
-            for cp in sums:
-                cp.wait()
         for name, _, at, w in SETS[which][part]:
             blocks = [vbuf[part, b, :, :, at:at + w].reshape(64, w) for b in range(8)]
-            val_rows(core_ref, blocks, ka, kg, name, seen)
+            val_rows(core_ref, blocks, ka, kg, name, seen, ready)
         train.wait(part)
         for name, _, at, w in SETS[which][part]:
             acc = acc_a if name == "a" else acc_g
@@ -391,7 +406,7 @@
         ] + list(scratch),
         compiler_params=pltpu.CompilerParams(vmem_limit_bytes=mib << 20),
         cost_estimate=pl.CostEstimate(
-            flops=flops, bytes_accessed=TOK * (FF + D), transcendentals=0
+            flops=flops, bytes_accessed=TOK * (FF + D) if flops else 0, transcendentals=0
         ),
     )(core, acts, grads, *[pin(x) if i in pinned else x for i, x in enumerate(args)])
 
@@ -416,37 +431,42 @@
         return hop(block, [a for a in "xyz" if n & WEIGHT[a]], 0)
 
     near = {n: send(rows, n) for n in (1, 2, 4, 3)}
-    (again,) = gate([rows], near[1])
+    (again,) = gate([rows], near[3])
     near.update({n: send(again, n) for n in (5, 6, 7)})
-    rows = jnp.stack([rows] + [near[n] for n in range(1, 8)])
+    sg = self_call(out_grads, near[3])
+    (rows,) = gate([jnp.stack([rows] + [near[n] for n in range(1, 8)])], sg)
     x = [double(rows[..., s:s + w], RUNS[j], 1) for j, (s, w) in enumerate(zip(STARTS, WIDTHS))]
-    sa = self_call(hidden_acts, x[1])
+    block_gram = self_call(hidden_acts, x[1], sg)
     a1 = [hop(x[j], STEP5[j], 1) for j in range(3)]
     o0 = swap(jnp.concatenate(x, axis=-1))
-    pair = gate([jnp.stack([x[j], a1[j]]) for j in range(3)], sa, o0)
-    last = [
-        [hop(pair[j][..., a:a + w], STEP6[j], 1) for j, (a, w) in enumerate(zip(at, width))]
+    pair = gate([jnp.stack([x[j], a1[j]]) for j in range(3)], block_gram, o0)
+    cut = [
+        [pair[j][..., a:a + w] for j, (a, w) in enumerate(zip(at, width))]
         for at, width in zip(SETAT, SETW)
     ]
+    last = [[hop(y, STEP6[j], 1) for j, y in enumerate(cut[0])]]
     o1 = swap(gate([jnp.concatenate(a1, axis=-1)], pair[0])[0])
     call = functools.partial(
         local_call, core=core.reshape(1).astype(jnp.int32), acts=hidden_acts, grads=out_grads
     )
     unit = 512 * (HA + HG)
     ca, cg, tok = call(
-        early_body, args=[sa] + [y for j in range(3) for y in (x[j], a1[j])],
+        early_body, args=[block_gram] + [y for j in range(3) for y in (x[j], a1[j])],
         outs=[ACC, ACC, TOKEN], flops=512 * unit, width=C1, pinned=range(1, 7), mib=28,
     )
-    block_gram = self_call(out_grads, tok, sa)
-    tok = block_gram
+    last.append([hop(y, STEP6[j], 1) for j, y in enumerate(cut[1])])
     sums = [ca, cg]
     for which in range(2):
-        got = [gate([y], tok, *([] if which else [o1]))[0] for y in last[which]]
-        swapped = [swap(y) for y in got]
+        got = last[which]
+        if which:
+            got = [gate([y], tok)[0] for y in got]
+            swapped = [swap(y) for y in got]
+        else:
+            swapped = [swap(gate([jnp.concatenate(got, axis=-1)], tok, o1)[0])] * 3
         sums = call(
             functools.partial(late_own_body, which=which),
             args=[y for j in range(3) for y in (x[j], a1[j], got[j])] + list(sums),
-            outs=[ACC, ACC, KERN, KERN] + [IDS] * which, flops=512 * unit, width=SETMAX,
+            outs=[ACC, ACC, KERN, KERN] + [IDS] * which, flops=512 * unit * which, width=SETMAX,
             scratch=[
                 pltpu.VMEM((3, 4, 2, 8, 8, SETMAX), jnp.bfloat16),
                 pltpu.SemaphoreType.DMA((3, 4)),
@@ -463,7 +483,7 @@
             scratch += [pltpu.VMEM(a.shape, a.dtype) for a in (ACC, ACC, KERN, KERN, IDS)]
         outs = call(
             functools.partial(late_other_body, which=which),
-            args=[o0, o1] + swapped + list(sums), outs=outs, flops=768 * unit, width=SETMAX,
+            args=[o0, o1] + swapped + list(sums), outs=outs, flops=768 * unit * which, width=SETMAX,
             scratch=scratch + [
                 pltpu.SemaphoreType.DMA((3, 8)),
                 pltpu.SemaphoreType.DMA((5,)),

time: 115 us -> 114 us (level)
  Pallas kernels: 48.9 us -> 46.5 us
  waiting for transfers between devices: 23.4 us -> 24.7 us
    pallas_call x5, Pallas kernels: 33.1 us -> 30.6 us  [local_call(): pl.pallas_call(body, in_specs=[pl.BlockSpec(memory_space=pltpu.SMEM)] + [...]
    ppermute x19, waiting for transfers between devices: 20.9 us -> 22.9 us  [hop(): return lax.ppermute(x, AXES, ring_pairs(axes, step))]
    ppermute x10 -> x8, waiting for transfers between devices: 2.51 us -> 1.79 us  [swap(): return lax.ppermute(x, AXES, core_pairs())]
    ppermute x10 -> x8, starting transfers between devices: 15.5 us -> 15.4 us  [swap(): return lax.ppermute(x, AXES, core_pairs())]
  transfers between devices with their start and end apart: 29 -> 27, of which waited for: 9 -> 12; matrix products, arithmetic and copies ran while one was open for 2% -> 2% of each run, Pallas kernels for 36% -> 35%
where the time goes in v9:
time: 114 us; the launch traced here: 113 us
  Pallas kernels  46.5 us (41%)
  starting transfers between devices  34.5 us (30%)
  waiting for transfers between devices  24.7 us (22%)
  other arithmetic  3.42 us (3%)
  local copies, waits for them, and re-layouts  3.04 us (3%)
    pallas_call x5, Pallas kernels, local_call(): pl.pallas_call(body, in_specs=[pl.BlockSpec(memory_space=pltpu.SMEM)] + [...  30.6 us
    ppermute x19, waiting for transfers between devices, hop(): return lax.ppermute(x, AXES, ring_pairs(axes, step))  22.9 us
    ppermute x19, starting transfers between devices, hop(): return lax.ppermute(x, AXES, ring_pairs(axes, step))  19.1 us
    pallas_call x2, Pallas kernels, self_call(): pl.pallas_call(body, grid=(width // KC,), in_specs=[pl.BlockSpec((TOK, KC...  15.9 us
    ppermute x8, starting transfers between devices, swap(): return lax.ppermute(x, AXES, core_pairs())  15.4 us
  transfers between devices with their start and end apart: 27, of which 12 were waited for; matrix products, arithmetic and copies ran while one was open for 2% of the time, Pallas kernels for 35%

profile of v9, /device:TPU:1, one launch (start us, length us, event | category | flops | bytes accessed | tf_op | source)
XLA Modules:
  0.0 113.2 jit_solution(7122417495887122411)
XLA Ops:
  0.6 0.7 convert_element_type.4
  1.3 0.8 fusion.4
  2.1 0.9 fusion.3
  3.2 1.5 %collective-permute-start = (bf16[4,11392]{1,0:T(4,128)(2,1)S(1)}, bf16[4,11392]{1,0:T(4,128)(2,1)S(1)}, u32[]{:S(2)}, u32[]{:S(2)}) collective-permute-start(bf16[4,11392]{1,0:T(4,128)(2,1)S(1)} %broadcast_select_fusion.2), channel_id=1, source_target_pairs={{0,8},{1,9},{2,10},{3,11},{4,12},{5,13},{6,14},{7,15},{8,0},{9,1},... | collective-permute-start | bytes 273416 | tf_op jit(solution)/shard_map/ppermute | solution.py:63
  4.7 0.9 collective-permute-done
  5.8 2.6 %collective-permute-start.4 = (bf16[8,11392]{1,0:T(8,128)(2,1)S(1)}, bf16[8,11392]{1,0:T(8,128)(2,1)S(1)}, u32[]{:S(2)}, u32[]{:S(2)}) collective-permute-start(bf16[8,11392]{1,0:T(8,128)(2,1)S(1)} %pad_maximum_fusion.8.refs_0_), channel_id=1, source_target_pairs={{0,64},{1,65},{2,66},{3,67},{4,68},{5,69},{6,70},{7,71},{8,76},{9,... | collective-permute-start | bytes 546824 | tf_op jit(solution)/shard_map/ppermute | solution.py:67
  8.5 6.2 %collective-permute-start.3 = (bf16[8,11392]{1,0:T(8,128)(2,1)S(1)}, bf16[8,11392]{1,0:T(8,128)(2,1)S(1)}, u32[]{:S(2)}, u32[]{:S(2)}) collective-permute-start(bf16[8,11392]{1,0:T(8,128)(2,1)S(1)} %pad_maximum_fusion.8.refs_0_), channel_id=1, source_target_pairs={{0,17},{1,16},{2,19},{3,18},{4,21},{5,20},{6,23},{7,22},{8,59},{9,... | collective-permute-start | bytes 546824 | tf_op jit(solution)/shard_map/ppermute | solution.py:67
  14.7 0.3 collective-permute-start.1
  15.1 2.5 %collective-permute-done.3.refs_1_.dep_ref = bf16[8,11392]{1,0:T(8,128)(2,1)S(1)} collective-permute-done((bf16[8,11392]{1,0:T(8,128)(2,1)S(1)}, bf16[8,11392]{1,0:T(8,128)(2,1)S(1)}, u32[]{:S(2)}, u32[]{:S(2)}) %collective-permute-start.3) | collective-permute-done | bytes 182304 | tf_op jit(solution)/shard_map/ppermute | solution.py:67
  17.6 2.7 %collective-permute-done.2 = bf16[8,11392]{1,0:T(8,128)(2,1)S(1)} collective-permute-done((bf16[8,11392]{1,0:T(8,128)(2,1)S(1)}, bf16[8,11392]{1,0:T(8,128)(2,1)S(1)}, u32[]{:S(2)}, u32[]{:S(2)}) %collective-permute-start.2) | collective-permute-done | bytes 182304 | tf_op jit(solution)/shard_map/ppermute | solution.py:67
  20.2 4.0 %collective-permute-start.7 = (bf16[8,11392]{1,0:T(8,128)(2,1)S(1)}, bf16[8,11392]{1,0:T(8,128)(2,1)S(1)}, u32[]{:S(2)}, u32[]{:S(2)}) collective-permute-start(bf16[8,11392]{1,0:T(8,128)(2,1)S(1)} %shard_map.68), channel_id=1, source_target_pairs={{0,81},{1,80},{2,83},{3,82},{4,85},{5,84},{6,87},{7,86},{8,127},{9... | collective-permute-start | bytes 546824 | tf_op jit(solution)/shard_map/ppermute | solution.py:67
  24.2 2.1 %collective-permute-start.6 = (bf16[8,11392]{1,0:T(8,128)(2,1)S(1)}, bf16[8,11392]{1,0:T(8,128)(2,1)S(1)}, u32[]{:S(2)}, u32[]{:S(2)}) collective-permute-start(bf16[8,11392]{1,0:T(8,128)(2,1)S(1)} %shard_map.68), channel_id=1, source_target_pairs={{0,65},{1,64},{2,67},{3,66},{4,69},{5,68},{6,71},{7,70},{8,79},{9,... | collective-permute-start | bytes 546824 | tf_op jit(solution)/shard_map/ppermute | solution.py:67
  26.4 1.1 collective-permute-start.5
  27.5 5.6 %shard_map.69.refs_1_.first_ref = f32[512,256]{1,0:T(8,128)S(1)} custom-call(bf16[512,8192]{1,0:T(8,128)(2,1)} %grads.9, bf16[8,11392]{1,0:T(8,128)(2,1)S(1)} %collective-permute-done.3.refs_1_.dep_ref), custom_call_target="tpu_custom_call" | custom-call | flops 2147483648 | bytes 8388608 | tf_op jit(solution)/shard_map/pallas_call | solution.py:146
  33.2 1.1 collective-permute-done.5
  34.5 0.1 slice_bitcast_fusion.2
  34.8 7.5 %collective-permute-done.10 = bf16[8,8,3712]{2,1,0:T(8,128)(2,1)S(1)} collective-permute-done((bf16[8,8,3712]{2,1,0:T(8,128)(2,1)S(1)}, bf16[8,8,3712]{2,1,0:T(8,128)(2,1)S(1)}, u32[]{:S(2)}, u32[]{:S(2)}) %collective-permute-start.10) | collective-permute-done | bytes 475168 | tf_op jit(solution)/shard_map/ppermute | solution.py:67
  42.3 0.1 fusion
  42.5 0.2 collective-permute-done.9
  42.7 0.1 fusion.1
  42.8 1.5 %collective-permute-start.13 = (bf16[2,8,8,3840]{3,2,1,0:T(8,128)(2,1)S(1)}, bf16[2,8,8,3840]{3,2,1,0:T(8,128)(2,1)S(1)}, u32[]{:S(2)}, u32[]{:S(2)}) collective-permute-start(bf16[2,8,8,3840]{3,2,1,0:T(8,128)(2,1)S(1)} %get-tuple-element.53.dep_ref.refs_2_.refs_3_), channel_id=1, source_target_pairs={{0,68},{1,69},{2,70},{3,71},{4,64},{5,65},{6,66},{7,67},{8,72},{9,... | collective-permute-start | bytes 2949128 | tf_op jit(solution)/shard_map/ppermute | solution.py:67
  44.4 0.2 maximum_maximum_fusion
  44.6 0.1 fusion.2
  44.8 2.3 %collective-permute-start.11 = (bf16[2,8,8,11392]{3,2,1,0:T(8,128)(2,1)S(1)}, bf16[2,8,8,11392]{3,2,1,0:T(8,128)(2,1)S(1)}, u32[]{:S(2)}, u32[]{:S(2)}) collective-permute-start(bf16[2,8,8,11392]{3,2,1,0:T(8,128)(2,1)S(1)} %maximum_maximum_fusion), channel_id=1, source_target_pairs={{0,8},{1,9},{2,10},{3,11},{4,12},{5,13},{6,14},{7,15},{8,0},{9,1},... | collective-permute-start | bytes 8749064 | tf_op jit(solution)/shard_map/ppermute | solution.py:63
  47.1 10.2 %shard_map.71.refs_3_.dep_ref = f32[4,4]{1,0:T(4,128)} custom-call(bf16[512,14336]{1,0:T(8,128)(2,1)} %acts.9, f32[512,256]{1,0:T(8,128)S(1)} %shard_map.69.refs_1_.first_ref, bf16[2,8,8,3840]{3,2,1,0:T(8,128)(2,1)S(1)} %get-tuple-element.53.dep_ref.refs_2_.refs_3_), custom_call_target="tpu_custom_call" | custom-call | flops 3758096384 | bytes 14680064 | tf_op jit(solution)/shard_map/pallas_call | solution.py:146
  57.3 0.2 pad_maximum_fusion.4.refs_2_
  57.5 0.2 pad_maximum_fusion.3.refs_1_
  57.7 0.3 collective-permute-done.12.refs_1_
  58.0 0.2 pad_maximum_fusion.2.refs_0_
  58.2 0.2 pad_maximum_fusion.refs_0_
  58.5 0.5 copy-done
  58.9 1.9 %collective-permute-start.15 = (bf16[2,8,8,11392]{3,2,1,0:T(8,128)(2,1)S(1)}, bf16[2,8,8,11392]{3,2,1,0:T(8,128)(2,1)S(1)}, u32[]{:S(2)}, u32[]{:S(2)}) collective-permute-start(bf16[2,8,8,11392]{3,2,1,0:T(8,128)(2,1)S(1)} %shard_map.73), channel_id=1, source_target_pairs={{0,8},{1,9},{2,10},{3,11},{4,12},{5,13},{6,14},{7,15},{8,0},{9,1},... | collective-permute-start | bytes 8749064 | tf_op jit(solution)/shard_map/ppermute | solution.py:63
  60.9 0.4 collective-permute-start.17
  61.6 5.9 %shard_map.74 = (f32[8,8,8,512]{3,2,1,0:T(8,128)S(1)}, f32[8,8,8,512]{3,2,1,0:T(8,128)S(1)}, f32[8,128]{1,0:T(8,128)S(1)}) custom-call(s32[1]{0:T(128)} %bitcast.core_ref, bf16[512,14336]{1,0:T(8,128)(2,1)} %acts.9, bf16[512,8192]{1,0:T(8,128)(2,1)} %grads.9, f32[4,4]{1,0:T(4,128)S(1)} %copy-done, bf16[2,8,8,3840]{3,2,1,0:T(8,128)(2,1)S(1)} %get-tuple-element.55.refs_0_, ...), custom_call_target="tpu_custom_call" | custom-call | flops 2952790016 | bytes 11534336 | tf_op jit(solution)/shard_map/pallas_call | solution.py:397
  67.5 6.5 %collective-permute-done.19.refs_8_ = bf16[2,2,8,8,1792]{4,3,2,1,0:T(8,128)(2,1)S(1)} collective-permute-done((bf16[2,2,8,8,1792]{4,3,2,1,0:T(8,128)(2,1)S(1)}, bf16[2,2,8,8,1792]{4,3,2,1,0:T(8,128)(2,1)S(1)}, u32[]{:S(2)}, u32[]{:S(2)}) %collective-permute-start.19) | collective-permute-done | bytes 917536 | tf_op jit(solution)/shard_map/ppermute | solution.py:67
  74.2 0.8 collective-permute-done.17.refs_2_
  74.9 0.2 pad_maximum_fusion.1.refs_0_
  75.2 4.6 %collective-permute-start.20 = (bf16[2,2,8,8,5632]{4,3,2,1,0:T(8,128)(2,1)S(1)}, bf16[2,2,8,8,5632]{4,3,2,1,0:T(8,128)(2,1)S(1)}, u32[]{:S(2)}, u32[]{:S(2)}) collective-permute-start(bf16[2,2,8,8,5632]{4,3,2,1,0:T(8,128)(2,1)S(1)} %shard_map.75), channel_id=1, source_target_pairs={{0,8},{1,9},{2,10},{3,11},{4,12},{5,13},{6,14},{7,15},{8,0},{9,1},... | collective-permute-start | bytes 8650760 | tf_op jit(solution)/shard_map/ppermute | solution.py:63
  80.3 5.4 %shard_map.76 = (f32[8,8,8,512]{3,2,1,0:T(8,128)S(1)}, f32[8,8,8,512]{3,2,1,0:T(8,128)S(1)}, f32[256,512]{1,0:T(8,128)S(1)}, f32[256,512]{1,0:T(8,128)S(1)}) custom-call(s32[1]{0:T(128)} %bitcast.core_ref, bf16[512,14336]{1,0:T(8,128)(2,1)} %acts.9, bf16[512,8192]{1,0:T(8,128)(2,1)} %grads.9, bf16[2,8,8,3840]{3,2,1,0:T(8,128)(2,1)S(1)} %get-tuple-element.55.refs_0_, ...), custom_call_target="tpu_custom_call" | custom-call | tf_op jit(solution)/shard_map/pallas_call | solution.py:397
  85.7 6.9 %shard_map.77 = (f32[8,8,8,512]{3,2,1,0:T(8,128)S(1)}, f32[8,8,8,512]{3,2,1,0:T(8,128)S(1)}, f32[256,512]{1,0:T(8,128)S(1)}, f32[256,512]{1,0:T(8,128)S(1)}, f32[8,128]{1,0:T(8,128)S(1)}) custom-call(s32[1]{0:T(128)} %bitcast.core_ref, bf16[512,14336]{1,0:T(8,128)(2,1)} %acts.9, bf16[512,8192]{1,0:T(8,128)(2,1)} %grads.9, ...), custom_call_target="tpu_custom_call" | custom-call | tf_op jit(solution)/shard_map/pallas_call | solution.py:397
  92.6 1.3 %collective-permute-done.22.refs_0_ = bf16[2,2,8,8,2048]{4,3,2,1,0:T(8,128)(2,1)S(1)} collective-permute-done((bf16[2,2,8,8,2048]{4,3,2,1,0:T(8,128)(2,1)S(1)}, bf16[2,2,8,8,2048]{4,3,2,1,0:T(8,128)(2,1)S(1)}, u32[]{:S(2)}, u32[]{:S(2)}) %collective-permute-start.22) | collective-permute-done | bytes 1048608 | tf_op jit(solution)/shard_map/ppermute | solution.py:67
  93.9 4.3 %collective-permute-start.23 = (bf16[2,2,8,8,2048]{4,3,2,1,0:T(8,128)(2,1)S(1)}, bf16[2,2,8,8,2048]{4,3,2,1,0:T(8,128)(2,1)S(1)}, u32[]{:S(2)}, u32[]{:S(2)}) collective-permute-start(bf16[2,2,8,8,2048]{4,3,2,1,0:T(8,128)(2,1)S(1)} %shard_map.79.refs_5_), channel_id=1, source_target_pairs={{0,8},{1,9},{2,10},{3,11},{4,12},{5,13},{6,14},{7,15},{8,0},{9,1},... | collective-permute-start | bytes 3145736 | tf_op jit(solution)/shard_map/ppermute | solution.py:63
  98.3 0.4 collective-permute-start.21
  98.7 5.2 %shard_map.81 = (f32[8,8,8,512]{3,2,1,0:T(8,128)S(1)}, f32[8,8,8,512]{3,2,1,0:T(8,128)S(1)}, f32[256,512]{1,0:T(8,128)S(1)}, f32[256,512]{1,0:T(8,128)S(1)}, f32[512,128]{1,0:T(8,128)S(1)}) custom-call(s32[1]{0:T(128)} %bitcast.core_ref, bf16[512,14336]{1,0:T(8,128)(2,1)} %acts.9, bf16[512,8192]{1,0:T(8,128)(2,1)} %grads.9, ...), custom_call_target="tpu_custom_call" | custom-call | flops 2952790016 | bytes 11534336 | tf_op jit(solution)/shard_map/pallas_call | solution.py:397
  104.0 7.2 %shard_map.82 = (f32[4,512]{1,0:T(4,128)S(1)}, f32[4,128]{1,0:T(4,128)S(1)}) custom-call(s32[1]{0:T(128)} %bitcast.core_ref, bf16[512,14336]{1,0:T(8,128)(2,1)} %acts.9, bf16[512,8192]{1,0:T(8,128)(2,1)} %grads.9, bf16[2,8,8,11392]{3,2,1,0:T(8,128)(2,1)S(1)} %collective-permute-done.11.refs_4_.o0, ...), custom_call_target="tpu_custom_call" | custom-call | flops 4429185024 | bytes 11534336 | tf_op jit(solution)/shard_map/pallas_call | solution.py:397
  111.2 0.4 collective-permute-start.26
  111.6 0.8 collective-permute-done.26
  112.6 0.7 broadcast_multiply_fusion
  (58 shorter events, 2.4 us)
Async XLA Ops:
  3.2 2.4 %collective-permute-start = (bf16[4,11392]{1,0:T(4,128)(2,1)S(1)}, bf16[4,11392]{1,0:T(4,128)(2,1)S(1)}, u32[]{:S(2)}, u32[]{:S(2)}) collective-permute-start(bf16[4,11392]{1,0:T(4,128)(2,1)S(1)} %broadcast_select_fusion.2), channel_id=1, source_target_pairs={{0,8},{1,9},{2,10},{3,11},{4,12},{5,13},{6,14},{7,15},{8,0},{9,1},... | collective-permute-start | bytes 273416 | tf_op jit(solution)/shard_map/ppermute | solution.py:63
  5.8 9.2 %collective-permute-start.4 = (bf16[8,11392]{1,0:T(8,128)(2,1)S(1)}, bf16[8,11392]{1,0:T(8,128)(2,1)S(1)}, u32[]{:S(2)}, u32[]{:S(2)}) collective-permute-start(bf16[8,11392]{1,0:T(8,128)(2,1)S(1)} %pad_maximum_fusion.8.refs_0_), channel_id=1, source_target_pairs={{0,64},{1,65},{2,66},{3,67},{4,68},{5,69},{6,70},{7,71},{8,76},{9,... | collective-permute-start | bytes 546824 | tf_op jit(solution)/shard_map/ppermute | solution.py:67
  8.5 9.1 %collective-permute-start.3 = (bf16[8,11392]{1,0:T(8,128)(2,1)S(1)}, bf16[8,11392]{1,0:T(8,128)(2,1)S(1)}, u32[]{:S(2)}, u32[]{:S(2)}) collective-permute-start(bf16[8,11392]{1,0:T(8,128)(2,1)S(1)} %pad_maximum_fusion.8.refs_0_), channel_id=1, source_target_pairs={{0,17},{1,16},{2,19},{3,18},{4,21},{5,20},{6,23},{7,22},{8,59},{9,... | collective-permute-start | bytes 546824 | tf_op jit(solution)/shard_map/ppermute | solution.py:67
  14.7 5.6 %collective-permute-start.2 = (bf16[8,11392]{1,0:T(8,128)(2,1)S(1)}, bf16[8,11392]{1,0:T(8,128)(2,1)S(1)}, u32[]{:S(2)}, u32[]{:S(2)}) collective-permute-start(bf16[8,11392]{1,0:T(8,128)(2,1)S(1)} %pad_maximum_fusion.8.refs_0_), channel_id=1, source_target_pairs={{0,1},{1,0},{2,3},{3,2},{4,5},{5,4},{6,7},{7,6},{8,11},{9,10},{10,... | collective-permute-start | bytes 546824 | tf_op jit(solution)/shard_map/ppermute | solution.py:67
  14.7 5.6 %collective-permute-start.1 = (bf16[8,11392]{1,0:T(8,128)(2,1)S(1)}, bf16[8,11392]{1,0:T(8,128)(2,1)S(1)}, u32[]{:S(2)}, u32[]{:S(2)}) collective-permute-start(bf16[8,11392]{1,0:T(8,128)(2,1)S(1)} %pad_maximum_fusion.8.refs_0_), channel_id=1, source_target_pairs={{0,16},{1,17},{2,18},{3,19},{4,20},{5,21},{6,22},{7,23},{8,56},{9,... | collective-permute-start | bytes 546824 | tf_op jit(solution)/shard_map/ppermute | solution.py:67
  20.2 14.0 %collective-permute-start.7 = (bf16[8,11392]{1,0:T(8,128)(2,1)S(1)}, bf16[8,11392]{1,0:T(8,128)(2,1)S(1)}, u32[]{:S(2)}, u32[]{:S(2)}) collective-permute-start(bf16[8,11392]{1,0:T(8,128)(2,1)S(1)} %shard_map.68), channel_id=1, source_target_pairs={{0,81},{1,80},{2,83},{3,82},{4,85},{5,84},{6,87},{7,86},{8,127},{9... | collective-permute-start | bytes 546824 | tf_op jit(solution)/shard_map/ppermute | solution.py:67
  24.2 10.0 %collective-permute-start.6 = (bf16[8,11392]{1,0:T(8,128)(2,1)S(1)}, bf16[8,11392]{1,0:T(8,128)(2,1)S(1)}, u32[]{:S(2)}, u32[]{:S(2)}) collective-permute-start(bf16[8,11392]{1,0:T(8,128)(2,1)S(1)} %shard_map.68), channel_id=1, source_target_pairs={{0,65},{1,64},{2,67},{3,66},{4,69},{5,68},{6,71},{7,70},{8,79},{9,... | collective-permute-start | bytes 546824 | tf_op jit(solution)/shard_map/ppermute | solution.py:67
  26.4 7.9 %collective-permute-start.5 = (bf16[8,11392]{1,0:T(8,128)(2,1)S(1)}, bf16[8,11392]{1,0:T(8,128)(2,1)S(1)}, u32[]{:S(2)}, u32[]{:S(2)}) collective-permute-start(bf16[8,11392]{1,0:T(8,128)(2,1)S(1)} %shard_map.68), channel_id=1, source_target_pairs={{0,80},{1,81},{2,82},{3,83},{4,84},{5,85},{6,86},{7,87},{8,124},{9... | collective-permute-start | bytes 546824 | tf_op jit(solution)/shard_map/ppermute | solution.py:67
  34.4 7.9 %collective-permute-start.10 = (bf16[8,8,3712]{2,1,0:T(8,128)(2,1)S(1)}, bf16[8,8,3712]{2,1,0:T(8,128)(2,1)S(1)}, u32[]{:S(2)}, u32[]{:S(2)}) collective-permute-start(bf16[8,8,3712]{2,1,0:T(8,128)(2,1)S(1)} %get-tuple-element.51), channel_id=1, source_target_pairs={{0,68},{1,69},{2,70},{3,71},{4,64},{5,65},{6,66},{7,67},{8,72},{9,... | collective-permute-start | bytes 1425416 | tf_op jit(solution)/shard_map/ppermute | solution.py:67
  34.6 8.1 %collective-permute-start.9 = (bf16[8,8,3840]{2,1,0:T(8,128)(2,1)S(1)}, bf16[8,8,3840]{2,1,0:T(8,128)(2,1)S(1)}, u32[]{:S(2)}, u32[]{:S(2)}) collective-permute-start(bf16[8,8,3840]{2,1,0:T(8,128)(2,1)S(1)} %get-tuple-element.48), channel_id=1, source_target_pairs={{0,48},{1,49},{2,50},{3,51},{4,52},{5,53},{6,54},{7,55},{8,24},{9,... | collective-permute-start | bytes 1474568 | tf_op jit(solution)/shard_map/ppermute | solution.py:67
  34.7 9.6 %collective-permute-start.8 = (bf16[8,8,3840]{2,1,0:T(8,128)(2,1)S(1)}, bf16[8,8,3840]{2,1,0:T(8,128)(2,1)S(1)}, u32[]{:S(2)}, u32[]{:S(2)}) collective-permute-start(bf16[8,8,3840]{2,1,0:T(8,128)(2,1)S(1)} %get-tuple-element.49), channel_id=1, source_target_pairs={{0,3},{1,2},{2,1},{3,0},{4,7},{5,6},{6,5},{7,4},{8,9},{9,8},{10,11... | collective-permute-start | bytes 1474568 | tf_op jit(solution)/shard_map/ppermute | solution.py:67
  42.4 14.9 %collective-permute-start.14 = (bf16[2,8,8,3712]{3,2,1,0:T(8,128)(2,1)S(1)}, bf16[2,8,8,3712]{3,2,1,0:T(8,128)(2,1)S(1)}, u32[]{:S(2)}, u32[]{:S(2)}) collective-permute-start(bf16[2,8,8,3712]{3,2,1,0:T(8,128)(2,1)S(1)} %get-tuple-element.57.refs_4_.refs_6_), channel_id=1, source_target_pairs={{0,3},{1,2},{2,1},{3,0},{4,7},{5,6},{6,5},{7,4},{8,9},{9,8},{10,11... | collective-permute-start | bytes 2850824 | tf_op jit(solution)/shard_map/ppermute | solution.py:67
  42.8 14.7 %collective-permute-start.13 = (bf16[2,8,8,3840]{3,2,1,0:T(8,128)(2,1)S(1)}, bf16[2,8,8,3840]{3,2,1,0:T(8,128)(2,1)S(1)}, u32[]{:S(2)}, u32[]{:S(2)}) collective-permute-start(bf16[2,8,8,3840]{3,2,1,0:T(8,128)(2,1)S(1)} %get-tuple-element.53.dep_ref.refs_2_.refs_3_), channel_id=1, source_target_pairs={{0,68},{1,69},{2,70},{3,71},{4,64},{5,65},{6,66},{7,67},{8,72},{9,... | collective-permute-start | bytes 2949128 | tf_op jit(solution)/shard_map/ppermute | solution.py:67
  44.7 13.3 %collective-permute-start.12 = (bf16[2,8,8,3840]{3,2,1,0:T(8,128)(2,1)S(1)}, bf16[2,8,8,3840]{3,2,1,0:T(8,128)(2,1)S(1)}, u32[]{:S(2)}, u32[]{:S(2)}) collective-permute-start(bf16[2,8,8,3840]{3,2,1,0:T(8,128)(2,1)S(1)} %get-tuple-element.55.refs_0_), channel_id=1, source_target_pairs={{0,48},{1,49},{2,50},{3,51},{4,52},{5,53},{6,54},{7,55},{8,24},{9,... | collective-permute-start | bytes 2949128 | tf_op jit(solution)/shard_map/ppermute | solution.py:67
  44.8 13.6 %collective-permute-start.11 = (bf16[2,8,8,11392]{3,2,1,0:T(8,128)(2,1)S(1)}, bf16[2,8,8,11392]{3,2,1,0:T(8,128)(2,1)S(1)}, u32[]{:S(2)}, u32[]{:S(2)}) collective-permute-start(bf16[2,8,8,11392]{3,2,1,0:T(8,128)(2,1)S(1)} %maximum_maximum_fusion), channel_id=1, source_target_pairs={{0,8},{1,9},{2,10},{3,11},{4,12},{5,13},{6,14},{7,15},{8,0},{9,1},... | collective-permute-start | bytes 8749064 | tf_op jit(solution)/shard_map/ppermute | solution.py:63
  58.2 0.7 copy-start
  58.9 16.2 %collective-permute-start.15 = (bf16[2,8,8,11392]{3,2,1,0:T(8,128)(2,1)S(1)}, bf16[2,8,8,11392]{3,2,1,0:T(8,128)(2,1)S(1)}, u32[]{:S(2)}, u32[]{:S(2)}) collective-permute-start(bf16[2,8,8,11392]{3,2,1,0:T(8,128)(2,1)S(1)} %shard_map.73), channel_id=1, source_target_pairs={{0,8},{1,9},{2,10},{3,11},{4,12},{5,13},{6,14},{7,15},{8,0},{9,1},... | collective-permute-start | bytes 8749064 | tf_op jit(solution)/shard_map/ppermute | solution.py:63
  60.9 14.0 %collective-permute-start.17 = (bf16[2,2,8,8,2048]{4,3,2,1,0:T(8,128)(2,1)S(1)}, bf16[2,2,8,8,2048]{4,3,2,1,0:T(8,128)(2,1)S(1)}, u32[]{:S(2)}, u32[]{:S(2)}) collective-permute-start(bf16[2,2,8,8,2048]{4,3,2,1,0:T(8,128)(2,1)S(1)} %slice.50), channel_id=1, source_target_pairs={{0,68},{1,69},{2,70},{3,71},{4,64},{5,65},{6,66},{7,67},{8,72},{9,... | collective-permute-start | bytes 3145736 | tf_op jit(solution)/shard_map/ppermute | solution.py:67
  61.4 12.6 %collective-permute-start.19 = (bf16[2,2,8,8,1792]{4,3,2,1,0:T(8,128)(2,1)S(1)}, bf16[2,2,8,8,1792]{4,3,2,1,0:T(8,128)(2,1)S(1)}, u32[]{:S(2)}, u32[]{:S(2)}) collective-permute-start(bf16[2,2,8,8,1792]{4,3,2,1,0:T(8,128)(2,1)S(1)} %slice.52), channel_id=1, source_target_pairs={{0,48},{1,49},{2,50},{3,51},{4,52},{5,53},{6,54},{7,55},{8,24},{9,... | collective-permute-start | bytes 2752520 | tf_op jit(solution)/shard_map/ppermute | solution.py:67
  61.5 12.6 %collective-permute-start.18 = (bf16[2,2,8,8,1792]{4,3,2,1,0:T(8,128)(2,1)S(1)}, bf16[2,2,8,8,1792]{4,3,2,1,0:T(8,128)(2,1)S(1)}, u32[]{:S(2)}, u32[]{:S(2)}) collective-permute-start(bf16[2,2,8,8,1792]{4,3,2,1,0:T(8,128)(2,1)S(1)} %slice.51), channel_id=1, source_target_pairs={{0,3},{1,2},{2,1},{3,0},{4,7},{5,6},{6,5},{7,4},{8,9},{9,8},{10,11... | collective-permute-start | bytes 2752520 | tf_op jit(solution)/shard_map/ppermute | solution.py:67
  75.2 10.6 %collective-permute-start.20 = (bf16[2,2,8,8,5632]{4,3,2,1,0:T(8,128)(2,1)S(1)}, bf16[2,2,8,8,5632]{4,3,2,1,0:T(8,128)(2,1)S(1)}, u32[]{:S(2)}, u32[]{:S(2)}) collective-permute-start(bf16[2,2,8,8,5632]{4,3,2,1,0:T(8,128)(2,1)S(1)} %shard_map.75), channel_id=1, source_target_pairs={{0,8},{1,9},{2,10},{3,11},{4,12},{5,13},{6,14},{7,15},{8,0},{9,1},... | collective-permute-start | bytes 8650760 | tf_op jit(solution)/shard_map/ppermute | solution.py:63
  79.9 14.0 %collective-permute-start.22 = (bf16[2,2,8,8,2048]{4,3,2,1,0:T(8,128)(2,1)S(1)}, bf16[2,2,8,8,2048]{4,3,2,1,0:T(8,128)(2,1)S(1)}, u32[]{:S(2)}, u32[]{:S(2)}) collective-permute-start(bf16[2,2,8,8,2048]{4,3,2,1,0:T(8,128)(2,1)S(1)} %slice.53), channel_id=1, source_target_pairs={{0,3},{1,2},{2,1},{3,0},{4,7},{5,6},{6,5},{7,4},{8,9},{9,8},{10,11... | collective-permute-start | bytes 3145736 | tf_op jit(solution)/shard_map/ppermute | solution.py:67
  80.1 18.1 %collective-permute-start.24 = (bf16[2,2,8,8,1920]{4,3,2,1,0:T(8,128)(2,1)S(1)}, bf16[2,2,8,8,1920]{4,3,2,1,0:T(8,128)(2,1)S(1)}, u32[]{:S(2)}, u32[]{:S(2)}) collective-permute-start(bf16[2,2,8,8,1920]{4,3,2,1,0:T(8,128)(2,1)S(1)} %slice.54), channel_id=1, source_target_pairs={{0,48},{1,49},{2,50},{3,51},{4,52},{5,53},{6,54},{7,55},{8,24},{9,... | collective-permute-start | bytes 2949128 | tf_op jit(solution)/shard_map/ppermute | solution.py:67
  80.2 18.0 %collective-permute-start.16 = (bf16[2,2,8,8,1792]{4,3,2,1,0:T(8,128)(2,1)S(1)}, bf16[2,2,8,8,1792]{4,3,2,1,0:T(8,128)(2,1)S(1)}, u32[]{:S(2)}, u32[]{:S(2)}) collective-permute-start(bf16[2,2,8,8,1792]{4,3,2,1,0:T(8,128)(2,1)S(1)} %slice.49), channel_id=1, source_target_pairs={{0,68},{1,69},{2,70},{3,71},{4,64},{5,65},{6,66},{7,67},{8,72},{9,... | collective-permute-start | bytes 2752520 | tf_op jit(solution)/shard_map/ppermute | solution.py:67
  93.9 10.1 %collective-permute-start.23 = (bf16[2,2,8,8,2048]{4,3,2,1,0:T(8,128)(2,1)S(1)}, bf16[2,2,8,8,2048]{4,3,2,1,0:T(8,128)(2,1)S(1)}, u32[]{:S(2)}, u32[]{:S(2)}) collective-permute-start(bf16[2,2,8,8,2048]{4,3,2,1,0:T(8,128)(2,1)S(1)} %shard_map.79.refs_5_), channel_id=1, source_target_pairs={{0,8},{1,9},{2,10},{3,11},{4,12},{5,13},{6,14},{7,15},{8,0},{9,1},... | collective-permute-start | bytes 3145736 | tf_op jit(solution)/shard_map/ppermute | solution.py:63
  98.2 5.8 %collective-permute-start.25 = (bf16[2,2,8,8,1920]{4,3,2,1,0:T(8,128)(2,1)S(1)}, bf16[2,2,8,8,1920]{4,3,2,1,0:T(8,128)(2,1)S(1)}, u32[]{:S(2)}, u32[]{:S(2)}) collective-permute-start(bf16[2,2,8,8,1920]{4,3,2,1,0:T(8,128)(2,1)S(1)} %shard_map.80.refs_8_), channel_id=1, source_target_pairs={{0,8},{1,9},{2,10},{3,11},{4,12},{5,13},{6,14},{7,15},{8,0},{9,1},... | collective-permute-start | bytes 2949128 | tf_op jit(solution)/shard_map/ppermute | solution.py:63
  98.3 5.7 %collective-permute-start.21 = (bf16[2,2,8,8,1792]{4,3,2,1,0:T(8,128)(2,1)S(1)}, bf16[2,2,8,8,1792]{4,3,2,1,0:T(8,128)(2,1)S(1)}, u32[]{:S(2)}, u32[]{:S(2)}) collective-permute-start(bf16[2,2,8,8,1792]{4,3,2,1,0:T(8,128)(2,1)S(1)} %shard_map.78.refs_2_), channel_id=1, source_target_pairs={{0,8},{1,9},{2,10},{3,11},{4,12},{5,13},{6,14},{7,15},{8,0},{9,1},... | collective-permute-start | bytes 2752520 | tf_op jit(solution)/shard_map/ppermute | solution.py:63
  111.2 1.2 %collective-permute-start.26 = (f32[4,128]{1,0:T(4,128)S(1)}, f32[4,128]{1,0:T(4,128)S(1)}, u32[]{:S(2)}, u32[]{:S(2)}) collective-permute-start(f32[4,128]{1,0:T(4,128)S(1)} %get-tuple-element.45), channel_id=1, source_target_pairs={{0,8},{1,9},{2,10},{3,11},{4,12},{5,13},{6,14},{7,15},{8,0},{9,1},... | collective-permute-start | bytes 6152 | tf_op jit(solution)/shard_map/ppermute | solution.py:63

commit v10 on v9

--- a/solution.py
+++ b/solution.py
@@ -411,30 +411,49 @@
     )(core, acts, grads, *[pin(x) if i in pinned else x for i, x in enumerate(args)])
 
 
+def prepare_body(core_ref, ids_ref, acts_ref, grads_ref, keep_ref, away_ref):
+    first = core_ref[0] == 0
+    for at, ref, w in ((0, acts_ref, HA), (HA, grads_ref, HG)):
+        low, high = ref[:, 0:w], ref[:, w:2 * w]
+        keep_ref[:, at:at + w] = jnp.where(first, low, high)
+        away_ref[:, at:at + w] = jnp.where(first, high, low)
+    row = lax.broadcasted_iota(jnp.int32, (4, IDW), 0)
+    ids = jnp.zeros((4, IDW), jnp.float32)
+    for r in range(4):
+        ids = jnp.where(row == r, ids_ref[r].astype(jnp.float32), ids)
+    keep_ref[:, HA + HG:] = ids.astype(jnp.bfloat16)
+    away_ref[:, HA + HG:] = ids.astype(jnp.bfloat16)
+
+
+def prepare(core, val_acts, val_grads, val_ids):
+    vmem = pl.BlockSpec(memory_space=pltpu.VMEM)
+    smem = pl.BlockSpec(memory_space=pltpu.SMEM)
+    return pl.pallas_call(
+        prepare_body,
+        in_specs=[smem, smem, vmem, vmem],
+        out_specs=[vmem, vmem],
+        out_shape=[jax.ShapeDtypeStruct((4, ALLW), jnp.bfloat16)] * 2,
+        compiler_params=pltpu.CompilerParams(vmem_limit_bytes=4 << 20),
+        cost_estimate=pl.CostEstimate(flops=0, bytes_accessed=720896, transcendentals=0),
+    )(core, val_ids, val_acts, val_grads)
+
+
 def shards(hidden_acts, out_grads, val_acts, val_grads, val_ids):
     hidden_acts = pltpu.with_memory_space_constraint(hidden_acts, pltpu.HBM)
     out_grads = pltpu.with_memory_space_constraint(out_grads, pltpu.HBM)
     core = lax.axis_index("dp") % 2
     first = core == 0
-    idcol = jnp.broadcast_to(val_ids[:, None].astype(jnp.bfloat16), (4, IDW))
-    halves = [
-        jnp.concatenate(
-            [val_acts[:, h * HA:(h + 1) * HA], val_grads[:, h * HG:(h + 1) * HG], idcol], axis=1
-        )
-        for h in range(2)
-    ]
-    keep = jnp.where(first, halves[0], halves[1])
-    got = swap(jnp.where(first, halves[1], halves[0]))
+    core = core.reshape(1).astype(jnp.int32)
+    keep, away = prepare(core, val_acts, val_grads, val_ids)
+    got = swap(away)
     rows = jnp.concatenate([jnp.where(first, keep, got), jnp.where(first, got, keep)], axis=0)
 
     def send(block, n):
         return hop(block, [a for a in "xyz" if n & WEIGHT[a]], 0)
 
-    near = {n: send(rows, n) for n in (1, 2, 4, 3)}
-    (again,) = gate([rows], near[3])
-    near.update({n: send(again, n) for n in (5, 6, 7)})
-    sg = self_call(out_grads, near[3])
-    (rows,) = gate([jnp.stack([rows] + [near[n] for n in range(1, 8)])], sg)
+    rows = jnp.stack([rows] + [send(rows, n) for n in (1, 2, 3)])
+    sg = self_call(out_grads, rows)
+    (rows,) = gate([jnp.concatenate([rows, send(rows, 4)], axis=0)], sg)
     x = [double(rows[..., s:s + w], RUNS[j], 1) for j, (s, w) in enumerate(zip(STARTS, WIDTHS))]
     block_gram = self_call(hidden_acts, x[1], sg)
     a1 = [hop(x[j], STEP5[j], 1) for j in range(3)]
@@ -447,7 +466,7 @@
     last = [[hop(y, STEP6[j], 1) for j, y in enumerate(cut[0])]]
     o1 = swap(gate([jnp.concatenate(a1, axis=-1)], pair[0])[0])
     call = functools.partial(
-        local_call, core=core.reshape(1).astype(jnp.int32), acts=hidden_acts, grads=out_grads
+        local_call, core=core, acts=hidden_acts, grads=out_grads
     )
     unit = 512 * (HA + HG)
     ca, cg, tok = call(

time: 114 us -> 114 us (level)
  starting transfers between devices: 34.5 us -> 29.8 us
  waiting for transfers between devices: 24.7 us -> 29.1 us
    ppermute x19 -> x16, starting transfers between devices: 19.1 us -> 11.9 us  [hop(): return lax.ppermute(x, AXES, ring_pairs(axes, step))]
    ppermute x19 -> x16, waiting for transfers between devices: 22.9 us -> 27.3 us  [hop(): return lax.ppermute(x, AXES, ring_pairs(axes, step))]
    ppermute x8, starting transfers between devices: 15.4 us -> 18 us  [swap(): return lax.ppermute(x, AXES, core_pairs())]
    unnamed x8 -> x11, local copies, waits for them, and re-layouts: 0.57 us -> 2.9 us
    slice x2 -> x0, local copies, waits for them, and re-layouts: 1.69 us -> none  [the longest x1 0.89 us: shards(): val_acts[:, h * HA:(h + 1) * HA]]
  transfers between devices with their start and end apart: 27 -> 24, of which waited for: 12 -> 11; matrix products, arithmetic and copies ran while one was open for 2% -> 2% of each run, Pallas kernels for 35% -> 35%
where the time goes in v10:
time: 114 us; the launch traced here: 113 us
  Pallas kernels  47 us (41%)
  starting transfers between devices  29.8 us (26%)
  waiting for transfers between devices  29.1 us (26%)
  local copies, waits for them, and re-layouts  3.66 us (3%)
  other arithmetic  2.76 us (2%)
    pallas_call x5, Pallas kernels, local_call(): pl.pallas_call(body, in_specs=[pl.BlockSpec(memory_space=pltpu.SMEM)] + [...  30.6 us
    ppermute x16, waiting for transfers between devices, hop(): return lax.ppermute(x, AXES, ring_pairs(axes, step))  27.3 us
    ppermute x8, starting transfers between devices, swap(): return lax.ppermute(x, AXES, core_pairs())  18 us
    pallas_call x2, Pallas kernels, self_call(): pl.pallas_call(body, grid=(width // KC,), in_specs=[pl.BlockSpec((TOK, KC...  15.8 us
    ppermute x16, starting transfers between devices, hop(): return lax.ppermute(x, AXES, ring_pairs(axes, step))  11.9 us
    unnamed x11, local copies, waits for them, and re-layouts  2.9 us
  transfers between devices with their start and end apart: 24, of which 11 were waited for; matrix products, arithmetic and copies ran while one was open for 2% of the time, Pallas kernels for 35%

profile of v10, /device:TPU:1, one launch (start us, length us, event | category | flops | bytes accessed | tf_op | source)
XLA Modules:
  0.0 113.4 jit_solution(17130123585389596079)
XLA Ops:
  0.7 0.9 copy-done
  1.5 0.8 copy-done.1
  2.4 0.7 copy-done.3
  3.0 0.6 shard_map.68
  3.6 1.5 %collective-permute-start = (bf16[4,11392]{1,0:T(4,128)(2,1)S(1)}, bf16[4,11392]{1,0:T(4,128)(2,1)S(1)}, u32[]{:S(2)}, u32[]{:S(2)}) collective-permute-start(bf16[4,11392]{1,0:T(4,128)(2,1)S(1)} %get-tuple-element.27), channel_id=1, source_target_pairs={{0,8},{1,9},{2,10},{3,11},{4,12},{5,13},{6,14},{7,15},{8,0},{9,1},... | collective-permute-start | bytes 273416 | tf_op jit(solution)/shard_map/ppermute | solution.py:63
  5.1 0.9 collective-permute-done
  6.2 2.9 %collective-permute-start.2 = (bf16[8,11392]{1,0:T(8,128)(2,1)S(1)}, bf16[8,11392]{1,0:T(8,128)(2,1)S(1)}, u32[]{:S(2)}, u32[]{:S(2)}) collective-permute-start(bf16[8,11392]{1,0:T(8,128)(2,1)S(1)} %get-tuple-element.63), channel_id=1, source_target_pairs={{0,1},{1,0},{2,3},{3,2},{4,5},{5,4},{6,7},{7,6},{8,11},{9,10},{10,... | collective-permute-start | bytes 546824 | tf_op jit(solution)/shard_map/ppermute | solution.py:67
  9.1 3.8 %collective-permute-start.1 = (bf16[8,11392]{1,0:T(8,128)(2,1)S(1)}, bf16[8,11392]{1,0:T(8,128)(2,1)S(1)}, u32[]{:S(2)}, u32[]{:S(2)}) collective-permute-start(bf16[8,11392]{1,0:T(8,128)(2,1)S(1)} %get-tuple-element.63), channel_id=1, source_target_pairs={{0,16},{1,17},{2,18},{3,19},{4,20},{5,21},{6,22},{7,23},{8,56},{9,... | collective-permute-start | bytes 546824 | tf_op jit(solution)/shard_map/ppermute | solution.py:67
  13.0 2.9 %collective-permute-done.1 = bf16[8,11392]{1,0:T(8,128)(2,1)S(1)} collective-permute-done((bf16[8,11392]{1,0:T(8,128)(2,1)S(1)}, bf16[8,11392]{1,0:T(8,128)(2,1)S(1)}, u32[]{:S(2)}, u32[]{:S(2)}) %collective-permute-start.1) | collective-permute-done | bytes 182304 | tf_op jit(solution)/shard_map/ppermute | solution.py:67
  15.9 4.6 %collective-permute-done.3 = bf16[8,11392]{1,0:T(8,128)(2,1)S(1)} collective-permute-done((bf16[8,11392]{1,0:T(8,128)(2,1)S(1)}, bf16[8,11392]{1,0:T(8,128)(2,1)S(1)}, u32[]{:S(2)}, u32[]{:S(2)}) %collective-permute-start.3) | collective-permute-done | bytes 182304 | tf_op jit(solution)/shard_map/ppermute | solution.py:67
  20.6 0.1 pad_maximum_fusion.8.dep_ref
  20.7 2.6 %collective-permute-start.4 = (bf16[4,8,11392]{2,1,0:T(8,128)(2,1)S(1)}, bf16[4,8,11392]{2,1,0:T(8,128)(2,1)S(1)}, u32[]{:S(2)}, u32[]{:S(2)}) collective-permute-start(bf16[4,8,11392]{2,1,0:T(8,128)(2,1)S(1)} %pad_maximum_fusion.8.dep_ref), channel_id=1, source_target_pairs={{0,64},{1,65},{2,66},{3,67},{4,68},{5,69},{6,70},{7,71},{8,76},{9,... | collective-permute-start | bytes 2187272 | tf_op jit(solution)/shard_map/ppermute | solution.py:67
  23.3 5.6 %shard_map.69.refs_1_.first_ref = f32[512,256]{1,0:T(8,128)S(1)} custom-call(bf16[512,8192]{1,0:T(8,128)(2,1)} %grads.9, bf16[4,8,11392]{2,1,0:T(8,128)(2,1)S(1)} %pad_maximum_fusion.8.dep_ref), custom_call_target="tpu_custom_call" | custom-call | flops 2147483648 | bytes 8388608 | tf_op jit(solution)/shard_map/pallas_call | solution.py:146
  29.0 3.2 %collective-permute-done.4 = bf16[4,8,11392]{2,1,0:T(8,128)(2,1)S(1)} collective-permute-done((bf16[4,8,11392]{2,1,0:T(8,128)(2,1)S(1)}, bf16[4,8,11392]{2,1,0:T(8,128)(2,1)S(1)}, u32[]{:S(2)}, u32[]{:S(2)}) %collective-permute-start.4) | collective-permute-done | bytes 729120 | tf_op jit(solution)/shard_map/ppermute | solution.py:67
  32.5 0.1 slice_bitcast_fusion.2
  32.8 7.5 %collective-permute-done.7 = bf16[8,8,3712]{2,1,0:T(8,128)(2,1)S(1)} collective-permute-done((bf16[8,8,3712]{2,1,0:T(8,128)(2,1)S(1)}, bf16[8,8,3712]{2,1,0:T(8,128)(2,1)S(1)}, u32[]{:S(2)}, u32[]{:S(2)}) %collective-permute-start.7) | collective-permute-done | bytes 475168 | tf_op jit(solution)/shard_map/ppermute | solution.py:67
  40.2 0.1 fusion.1
  40.5 0.2 collective-permute-done.6
  40.6 0.1 fusion.2
  40.8 1.5 %collective-permute-start.10 = (bf16[2,8,8,3840]{3,2,1,0:T(8,128)(2,1)S(1)}, bf16[2,8,8,3840]{3,2,1,0:T(8,128)(2,1)S(1)}, u32[]{:S(2)}, u32[]{:S(2)}) collective-permute-start(bf16[2,8,8,3840]{3,2,1,0:T(8,128)(2,1)S(1)} %get-tuple-element.57.dep_ref.refs_2_.refs_3_), channel_id=1, source_target_pairs={{0,68},{1,69},{2,70},{3,71},{4,64},{5,65},{6,66},{7,67},{8,72},{9,... | collective-permute-start | bytes 2949128 | tf_op jit(solution)/shard_map/ppermute | solution.py:67
  42.3 0.2 maximum_maximum_fusion
  42.5 0.1 fusion.3
  42.8 4.6 %collective-permute-start.8 = (bf16[2,8,8,11392]{3,2,1,0:T(8,128)(2,1)S(1)}, bf16[2,8,8,11392]{3,2,1,0:T(8,128)(2,1)S(1)}, u32[]{:S(2)}, u32[]{:S(2)}) collective-permute-start(bf16[2,8,8,11392]{3,2,1,0:T(8,128)(2,1)S(1)} %maximum_maximum_fusion), channel_id=1, source_target_pairs={{0,8},{1,9},{2,10},{3,11},{4,12},{5,13},{6,14},{7,15},{8,0},{9,1},... | collective-permute-start | bytes 8749064 | tf_op jit(solution)/shard_map/ppermute | solution.py:63
  47.3 10.2 %shard_map.71.refs_3_.dep_ref = f32[4,4]{1,0:T(4,128)} custom-call(bf16[512,14336]{1,0:T(8,128)(2,1)} %acts.9, f32[512,256]{1,0:T(8,128)S(1)} %shard_map.69.refs_1_.first_ref, bf16[2,8,8,3840]{3,2,1,0:T(8,128)(2,1)S(1)} %get-tuple-element.57.dep_ref.refs_2_.refs_3_), custom_call_target="tpu_custom_call" | custom-call | flops 3758096384 | bytes 14680064 | tf_op jit(solution)/shard_map/pallas_call | solution.py:146
  57.5 0.2 pad_maximum_fusion.4.refs_2_
  57.7 0.2 pad_maximum_fusion.3.refs_1_
  57.9 0.2 pad_maximum_fusion.2.refs_0_
  58.1 0.2 pad_maximum_fusion.refs_0_
  58.4 0.5 copy-done.2
  58.8 2.5 %collective-permute-start.12 = (bf16[2,8,8,11392]{3,2,1,0:T(8,128)(2,1)S(1)}, bf16[2,8,8,11392]{3,2,1,0:T(8,128)(2,1)S(1)}, u32[]{:S(2)}, u32[]{:S(2)}) collective-permute-start(bf16[2,8,8,11392]{3,2,1,0:T(8,128)(2,1)S(1)} %shard_map.73), channel_id=1, source_target_pairs={{0,8},{1,9},{2,10},{3,11},{4,12},{5,13},{6,14},{7,15},{8,0},{9,1},... | collective-permute-start | bytes 8749064 | tf_op jit(solution)/shard_map/ppermute | solution.py:63
  61.3 0.1 slice.34
  61.8 5.9 %shard_map.74 = (f32[8,8,8,512]{3,2,1,0:T(8,128)S(1)}, f32[8,8,8,512]{3,2,1,0:T(8,128)S(1)}, f32[8,128]{1,0:T(8,128)S(1)}) custom-call(s32[1]{0:T(128)} %bitcast.core_ref, bf16[512,14336]{1,0:T(8,128)(2,1)} %acts.9, bf16[512,8192]{1,0:T(8,128)(2,1)} %grads.9, f32[4,4]{1,0:T(4,128)S(1)} %copy-done.2, bf16[2,8,8,3840]{3,2,1,0:T(8,128)(2,1)S(1)} %get-tuple-element.59.refs_0_, ...), custom_call_target="tpu_custom_call" | custom-call | flops 2952790016 | bytes 11534336 | tf_op jit(solution)/shard_map/pallas_call | solution.py:397
  67.7 6.5 %collective-permute-done.16.refs_8_ = bf16[2,2,8,8,1792]{4,3,2,1,0:T(8,128)(2,1)S(1)} collective-permute-done((bf16[2,2,8,8,1792]{4,3,2,1,0:T(8,128)(2,1)S(1)}, bf16[2,2,8,8,1792]{4,3,2,1,0:T(8,128)(2,1)S(1)}, u32[]{:S(2)}, u32[]{:S(2)}) %collective-permute-start.16) | collective-permute-done | bytes 917536 | tf_op jit(solution)/shard_map/ppermute | solution.py:67
  74.3 1.1 collective-permute-done.14.refs_2_
  75.4 0.2 pad_maximum_fusion.1.refs_0_
  75.7 4.4 %collective-permute-start.17 = (bf16[2,2,8,8,5632]{4,3,2,1,0:T(8,128)(2,1)S(1)}, bf16[2,2,8,8,5632]{4,3,2,1,0:T(8,128)(2,1)S(1)}, u32[]{:S(2)}, u32[]{:S(2)}) collective-permute-start(bf16[2,2,8,8,5632]{4,3,2,1,0:T(8,128)(2,1)S(1)} %shard_map.75), channel_id=1, source_target_pairs={{0,8},{1,9},{2,10},{3,11},{4,12},{5,13},{6,14},{7,15},{8,0},{9,1},... | collective-permute-start | bytes 8650760 | tf_op jit(solution)/shard_map/ppermute | solution.py:63
  80.4 0.3 collective-permute-start.21
  80.8 5.4 %shard_map.76 = (f32[8,8,8,512]{3,2,1,0:T(8,128)S(1)}, f32[8,8,8,512]{3,2,1,0:T(8,128)S(1)}, f32[256,512]{1,0:T(8,128)S(1)}, f32[256,512]{1,0:T(8,128)S(1)}) custom-call(s32[1]{0:T(128)} %bitcast.core_ref, bf16[512,14336]{1,0:T(8,128)(2,1)} %acts.9, bf16[512,8192]{1,0:T(8,128)(2,1)} %grads.9, bf16[2,8,8,3840]{3,2,1,0:T(8,128)(2,1)S(1)} %get-tuple-element.59.refs_0_, ...), custom_call_target="tpu_custom_call" | custom-call | tf_op jit(solution)/shard_map/pallas_call | solution.py:397
  86.2 6.9 %shard_map.77 = (f32[8,8,8,512]{3,2,1,0:T(8,128)S(1)}, f32[8,8,8,512]{3,2,1,0:T(8,128)S(1)}, f32[256,512]{1,0:T(8,128)S(1)}, f32[256,512]{1,0:T(8,128)S(1)}, f32[8,128]{1,0:T(8,128)S(1)}) custom-call(s32[1]{0:T(128)} %bitcast.core_ref, bf16[512,14336]{1,0:T(8,128)(2,1)} %acts.9, bf16[512,8192]{1,0:T(8,128)(2,1)} %grads.9, ...), custom_call_target="tpu_custom_call" | custom-call | tf_op jit(solution)/shard_map/pallas_call | solution.py:397
  93.1 1.1 collective-permute-done.19.refs_0_
  94.2 4.2 %collective-permute-start.20 = (bf16[2,2,8,8,2048]{4,3,2,1,0:T(8,128)(2,1)S(1)}, bf16[2,2,8,8,2048]{4,3,2,1,0:T(8,128)(2,1)S(1)}, u32[]{:S(2)}, u32[]{:S(2)}) collective-permute-start(bf16[2,2,8,8,2048]{4,3,2,1,0:T(8,128)(2,1)S(1)} %shard_map.79.refs_5_), channel_id=1, source_target_pairs={{0,8},{1,9},{2,10},{3,11},{4,12},{5,13},{6,14},{7,15},{8,0},{9,1},... | collective-permute-start | bytes 3145736 | tf_op jit(solution)/shard_map/ppermute | solution.py:63
  98.5 0.4 collective-permute-start.18
  98.9 5.2 %shard_map.81 = (f32[8,8,8,512]{3,2,1,0:T(8,128)S(1)}, f32[8,8,8,512]{3,2,1,0:T(8,128)S(1)}, f32[256,512]{1,0:T(8,128)S(1)}, f32[256,512]{1,0:T(8,128)S(1)}, f32[512,128]{1,0:T(8,128)S(1)}) custom-call(s32[1]{0:T(128)} %bitcast.core_ref, bf16[512,14336]{1,0:T(8,128)(2,1)} %acts.9, bf16[512,8192]{1,0:T(8,128)(2,1)} %grads.9, ...), custom_call_target="tpu_custom_call" | custom-call | flops 2952790016 | bytes 11534336 | tf_op jit(solution)/shard_map/pallas_call | solution.py:397
  104.2 7.2 %shard_map.82 = (f32[4,512]{1,0:T(4,128)S(1)}, f32[4,128]{1,0:T(4,128)S(1)}) custom-call(s32[1]{0:T(128)} %bitcast.core_ref, bf16[512,14336]{1,0:T(8,128)(2,1)} %acts.9, bf16[512,8192]{1,0:T(8,128)(2,1)} %grads.9, bf16[2,8,8,11392]{3,2,1,0:T(8,128)(2,1)S(1)} %collective-permute-done.8.refs_4_.o0, ...), custom_call_target="tpu_custom_call" | custom-call | flops 4429185024 | bytes 11534336 | tf_op jit(solution)/shard_map/pallas_call | solution.py:397
  111.4 0.4 collective-permute-start.23
  111.8 0.8 collective-permute-done.23
  112.6 0.1 rsqrt_reduce_fusion
  112.8 0.7 broadcast_multiply_fusion
  (51 shorter events, 2.0 us)
Async XLA Ops:
  0.6 0.9 copy-start
  1.5 0.8 copy-start.1
  2.4 0.7 copy-start.3
  3.6 2.4 %collective-permute-start = (bf16[4,11392]{1,0:T(4,128)(2,1)S(1)}, bf16[4,11392]{1,0:T(4,128)(2,1)S(1)}, u32[]{:S(2)}, u32[]{:S(2)}) collective-permute-start(bf16[4,11392]{1,0:T(4,128)(2,1)S(1)} %get-tuple-element.27), channel_id=1, source_target_pairs={{0,8},{1,9},{2,10},{3,11},{4,12},{5,13},{6,14},{7,15},{8,0},{9,1},... | collective-permute-start | bytes 273416 | tf_op jit(solution)/shard_map/ppermute | solution.py:63
  6.2 6.8 %collective-permute-start.2 = (bf16[8,11392]{1,0:T(8,128)(2,1)S(1)}, bf16[8,11392]{1,0:T(8,128)(2,1)S(1)}, u32[]{:S(2)}, u32[]{:S(2)}) collective-permute-start(bf16[8,11392]{1,0:T(8,128)(2,1)S(1)} %get-tuple-element.63), channel_id=1, source_target_pairs={{0,1},{1,0},{2,3},{3,2},{4,5},{5,4},{6,7},{7,6},{8,11},{9,10},{10,... | collective-permute-start | bytes 546824 | tf_op jit(solution)/shard_map/ppermute | solution.py:67
  9.1 6.8 %collective-permute-start.1 = (bf16[8,11392]{1,0:T(8,128)(2,1)S(1)}, bf16[8,11392]{1,0:T(8,128)(2,1)S(1)}, u32[]{:S(2)}, u32[]{:S(2)}) collective-permute-start(bf16[8,11392]{1,0:T(8,128)(2,1)S(1)} %get-tuple-element.63), channel_id=1, source_target_pairs={{0,16},{1,17},{2,18},{3,19},{4,20},{5,21},{6,22},{7,23},{8,56},{9,... | collective-permute-start | bytes 546824 | tf_op jit(solution)/shard_map/ppermute | solution.py:67
  12.9 7.7 %collective-permute-start.3 = (bf16[8,11392]{1,0:T(8,128)(2,1)S(1)}, bf16[8,11392]{1,0:T(8,128)(2,1)S(1)}, u32[]{:S(2)}, u32[]{:S(2)}) collective-permute-start(bf16[8,11392]{1,0:T(8,128)(2,1)S(1)} %get-tuple-element.63), channel_id=1, source_target_pairs={{0,17},{1,16},{2,19},{3,18},{4,21},{5,20},{6,23},{7,22},{8,59},{9,... | collective-permute-start | bytes 546824 | tf_op jit(solution)/shard_map/ppermute | solution.py:67
  20.7 11.5 %collective-permute-start.4 = (bf16[4,8,11392]{2,1,0:T(8,128)(2,1)S(1)}, bf16[4,8,11392]{2,1,0:T(8,128)(2,1)S(1)}, u32[]{:S(2)}, u32[]{:S(2)}) collective-permute-start(bf16[4,8,11392]{2,1,0:T(8,128)(2,1)S(1)} %pad_maximum_fusion.8.dep_ref), channel_id=1, source_target_pairs={{0,64},{1,65},{2,66},{3,67},{4,68},{5,69},{6,70},{7,71},{8,76},{9,... | collective-permute-start | bytes 2187272 | tf_op jit(solution)/shard_map/ppermute | solution.py:67
  32.4 7.9 %collective-permute-start.7 = (bf16[8,8,3712]{2,1,0:T(8,128)(2,1)S(1)}, bf16[8,8,3712]{2,1,0:T(8,128)(2,1)S(1)}, u32[]{:S(2)}, u32[]{:S(2)}) collective-permute-start(bf16[8,8,3712]{2,1,0:T(8,128)(2,1)S(1)} %get-tuple-element.55), channel_id=1, source_target_pairs={{0,68},{1,69},{2,70},{3,71},{4,64},{5,65},{6,66},{7,67},{8,72},{9,... | collective-permute-start | bytes 1425416 | tf_op jit(solution)/shard_map/ppermute | solution.py:67
  32.6 8.1 %collective-permute-start.6 = (bf16[8,8,3840]{2,1,0:T(8,128)(2,1)S(1)}, bf16[8,8,3840]{2,1,0:T(8,128)(2,1)S(1)}, u32[]{:S(2)}, u32[]{:S(2)}) collective-permute-start(bf16[8,8,3840]{2,1,0:T(8,128)(2,1)S(1)} %get-tuple-element.52), channel_id=1, source_target_pairs={{0,48},{1,49},{2,50},{3,51},{4,52},{5,53},{6,54},{7,55},{8,24},{9,... | collective-permute-start | bytes 1474568 | tf_op jit(solution)/shard_map/ppermute | solution.py:67
  32.7 9.6 %collective-permute-start.5 = (bf16[8,8,3840]{2,1,0:T(8,128)(2,1)S(1)}, bf16[8,8,3840]{2,1,0:T(8,128)(2,1)S(1)}, u32[]{:S(2)}, u32[]{:S(2)}) collective-permute-start(bf16[8,8,3840]{2,1,0:T(8,128)(2,1)S(1)} %get-tuple-element.53), channel_id=1, source_target_pairs={{0,3},{1,2},{2,1},{3,0},{4,7},{5,6},{6,5},{7,4},{8,9},{9,8},{10,11... | collective-permute-start | bytes 1474568 | tf_op jit(solution)/shard_map/ppermute | solution.py:67
  40.4 17.2 %collective-permute-start.11 = (bf16[2,8,8,3712]{3,2,1,0:T(8,128)(2,1)S(1)}, bf16[2,8,8,3712]{3,2,1,0:T(8,128)(2,1)S(1)}, u32[]{:S(2)}, u32[]{:S(2)}) collective-permute-start(bf16[2,8,8,3712]{3,2,1,0:T(8,128)(2,1)S(1)} %get-tuple-element.61.refs_4_.refs_6_), channel_id=1, source_target_pairs={{0,3},{1,2},{2,1},{3,0},{4,7},{5,6},{6,5},{7,4},{8,9},{9,8},{10,11... | collective-permute-start | bytes 2850824 | tf_op jit(solution)/shard_map/ppermute | solution.py:67
  40.8 17.0 %collective-permute-start.10 = (bf16[2,8,8,3840]{3,2,1,0:T(8,128)(2,1)S(1)}, bf16[2,8,8,3840]{3,2,1,0:T(8,128)(2,1)S(1)}, u32[]{:S(2)}, u32[]{:S(2)}) collective-permute-start(bf16[2,8,8,3840]{3,2,1,0:T(8,128)(2,1)S(1)} %get-tuple-element.57.dep_ref.refs_2_.refs_3_), channel_id=1, source_target_pairs={{0,68},{1,69},{2,70},{3,71},{4,64},{5,65},{6,66},{7,67},{8,72},{9,... | collective-permute-start | bytes 2949128 | tf_op jit(solution)/shard_map/ppermute | solution.py:67
  42.7 15.3 %collective-permute-start.9 = (bf16[2,8,8,3840]{3,2,1,0:T(8,128)(2,1)S(1)}, bf16[2,8,8,3840]{3,2,1,0:T(8,128)(2,1)S(1)}, u32[]{:S(2)}, u32[]{:S(2)}) collective-permute-start(bf16[2,8,8,3840]{3,2,1,0:T(8,128)(2,1)S(1)} %get-tuple-element.59.refs_0_), channel_id=1, source_target_pairs={{0,48},{1,49},{2,50},{3,51},{4,52},{5,53},{6,54},{7,55},{8,24},{9,... | collective-permute-start | bytes 2949128 | tf_op jit(solution)/shard_map/ppermute | solution.py:67
  42.8 15.6 %collective-permute-start.8 = (bf16[2,8,8,11392]{3,2,1,0:T(8,128)(2,1)S(1)}, bf16[2,8,8,11392]{3,2,1,0:T(8,128)(2,1)S(1)}, u32[]{:S(2)}, u32[]{:S(2)}) collective-permute-start(bf16[2,8,8,11392]{3,2,1,0:T(8,128)(2,1)S(1)} %maximum_maximum_fusion), channel_id=1, source_target_pairs={{0,8},{1,9},{2,10},{3,11},{4,12},{5,13},{6,14},{7,15},{8,0},{9,1},... | collective-permute-start | bytes 8749064 | tf_op jit(solution)/shard_map/ppermute | solution.py:63
  58.1 0.7 copy-start.2
  58.8 16.8 %collective-permute-start.12 = (bf16[2,8,8,11392]{3,2,1,0:T(8,128)(2,1)S(1)}, bf16[2,8,8,11392]{3,2,1,0:T(8,128)(2,1)S(1)}, u32[]{:S(2)}, u32[]{:S(2)}) collective-permute-start(bf16[2,8,8,11392]{3,2,1,0:T(8,128)(2,1)S(1)} %shard_map.73), channel_id=1, source_target_pairs={{0,8},{1,9},{2,10},{3,11},{4,12},{5,13},{6,14},{7,15},{8,0},{9,1},... | collective-permute-start | bytes 8749064 | tf_op jit(solution)/shard_map/ppermute | solution.py:63
  61.4 14.0 %collective-permute-start.14 = (bf16[2,2,8,8,2048]{4,3,2,1,0:T(8,128)(2,1)S(1)}, bf16[2,2,8,8,2048]{4,3,2,1,0:T(8,128)(2,1)S(1)}, u32[]{:S(2)}, u32[]{:S(2)}) collective-permute-start(bf16[2,2,8,8,2048]{4,3,2,1,0:T(8,128)(2,1)S(1)} %slice.34), channel_id=1, source_target_pairs={{0,68},{1,69},{2,70},{3,71},{4,64},{5,65},{6,66},{7,67},{8,72},{9,... | collective-permute-start | bytes 3145736 | tf_op jit(solution)/shard_map/ppermute | solution.py:67
  61.6 12.6 %collective-permute-start.16 = (bf16[2,2,8,8,1792]{4,3,2,1,0:T(8,128)(2,1)S(1)}, bf16[2,2,8,8,1792]{4,3,2,1,0:T(8,128)(2,1)S(1)}, u32[]{:S(2)}, u32[]{:S(2)}) collective-permute-start(bf16[2,2,8,8,1792]{4,3,2,1,0:T(8,128)(2,1)S(1)} %slice.36), channel_id=1, source_target_pairs={{0,48},{1,49},{2,50},{3,51},{4,52},{5,53},{6,54},{7,55},{8,24},{9,... | collective-permute-start | bytes 2752520 | tf_op jit(solution)/shard_map/ppermute | solution.py:67
  61.7 12.6 %collective-permute-start.15 = (bf16[2,2,8,8,1792]{4,3,2,1,0:T(8,128)(2,1)S(1)}, bf16[2,2,8,8,1792]{4,3,2,1,0:T(8,128)(2,1)S(1)}, u32[]{:S(2)}, u32[]{:S(2)}) collective-permute-start(bf16[2,2,8,8,1792]{4,3,2,1,0:T(8,128)(2,1)S(1)} %slice.35), channel_id=1, source_target_pairs={{0,3},{1,2},{2,1},{3,0},{4,7},{5,6},{6,5},{7,4},{8,9},{9,8},{10,11... | collective-permute-start | bytes 2752520 | tf_op jit(solution)/shard_map/ppermute | solution.py:67
  75.7 10.5 %collective-permute-start.17 = (bf16[2,2,8,8,5632]{4,3,2,1,0:T(8,128)(2,1)S(1)}, bf16[2,2,8,8,5632]{4,3,2,1,0:T(8,128)(2,1)S(1)}, u32[]{:S(2)}, u32[]{:S(2)}) collective-permute-start(bf16[2,2,8,8,5632]{4,3,2,1,0:T(8,128)(2,1)S(1)} %shard_map.75), channel_id=1, source_target_pairs={{0,8},{1,9},{2,10},{3,11},{4,12},{5,13},{6,14},{7,15},{8,0},{9,1},... | collective-permute-start | bytes 8650760 | tf_op jit(solution)/shard_map/ppermute | solution.py:63
  80.2 14.0 %collective-permute-start.19 = (bf16[2,2,8,8,2048]{4,3,2,1,0:T(8,128)(2,1)S(1)}, bf16[2,2,8,8,2048]{4,3,2,1,0:T(8,128)(2,1)S(1)}, u32[]{:S(2)}, u32[]{:S(2)}) collective-permute-start(bf16[2,2,8,8,2048]{4,3,2,1,0:T(8,128)(2,1)S(1)} %slice.37), channel_id=1, source_target_pairs={{0,3},{1,2},{2,1},{3,0},{4,7},{5,6},{6,5},{7,4},{8,9},{9,8},{10,11... | collective-permute-start | bytes 3145736 | tf_op jit(solution)/shard_map/ppermute | solution.py:67
  80.4 18.0 %collective-permute-start.21 = (bf16[2,2,8,8,1920]{4,3,2,1,0:T(8,128)(2,1)S(1)}, bf16[2,2,8,8,1920]{4,3,2,1,0:T(8,128)(2,1)S(1)}, u32[]{:S(2)}, u32[]{:S(2)}) collective-permute-start(bf16[2,2,8,8,1920]{4,3,2,1,0:T(8,128)(2,1)S(1)} %slice.38), channel_id=1, source_target_pairs={{0,48},{1,49},{2,50},{3,51},{4,52},{5,53},{6,54},{7,55},{8,24},{9,... | collective-permute-start | bytes 2949128 | tf_op jit(solution)/shard_map/ppermute | solution.py:67
  80.7 17.8 %collective-permute-start.13 = (bf16[2,2,8,8,1792]{4,3,2,1,0:T(8,128)(2,1)S(1)}, bf16[2,2,8,8,1792]{4,3,2,1,0:T(8,128)(2,1)S(1)}, u32[]{:S(2)}, u32[]{:S(2)}) collective-permute-start(bf16[2,2,8,8,1792]{4,3,2,1,0:T(8,128)(2,1)S(1)} %slice.33), channel_id=1, source_target_pairs={{0,68},{1,69},{2,70},{3,71},{4,64},{5,65},{6,66},{7,67},{8,72},{9,... | collective-permute-start | bytes 2752520 | tf_op jit(solution)/shard_map/ppermute | solution.py:67
  94.2 10.0 %collective-permute-start.20 = (bf16[2,2,8,8,2048]{4,3,2,1,0:T(8,128)(2,1)S(1)}, bf16[2,2,8,8,2048]{4,3,2,1,0:T(8,128)(2,1)S(1)}, u32[]{:S(2)}, u32[]{:S(2)}) collective-permute-start(bf16[2,2,8,8,2048]{4,3,2,1,0:T(8,128)(2,1)S(1)} %shard_map.79.refs_5_), channel_id=1, source_target_pairs={{0,8},{1,9},{2,10},{3,11},{4,12},{5,13},{6,14},{7,15},{8,0},{9,1},... | collective-permute-start | bytes 3145736 | tf_op jit(solution)/shard_map/ppermute | solution.py:63
  98.4 5.8 %collective-permute-start.22 = (bf16[2,2,8,8,1920]{4,3,2,1,0:T(8,128)(2,1)S(1)}, bf16[2,2,8,8,1920]{4,3,2,1,0:T(8,128)(2,1)S(1)}, u32[]{:S(2)}, u32[]{:S(2)}) collective-permute-start(bf16[2,2,8,8,1920]{4,3,2,1,0:T(8,128)(2,1)S(1)} %shard_map.80.refs_8_), channel_id=1, source_target_pairs={{0,8},{1,9},{2,10},{3,11},{4,12},{5,13},{6,14},{7,15},{8,0},{9,1},... | collective-permute-start | bytes 2949128 | tf_op jit(solution)/shard_map/ppermute | solution.py:63
  98.5 5.7 %collective-permute-start.18 = (bf16[2,2,8,8,1792]{4,3,2,1,0:T(8,128)(2,1)S(1)}, bf16[2,2,8,8,1792]{4,3,2,1,0:T(8,128)(2,1)S(1)}, u32[]{:S(2)}, u32[]{:S(2)}) collective-permute-start(bf16[2,2,8,8,1792]{4,3,2,1,0:T(8,128)(2,1)S(1)} %shard_map.78.refs_2_), channel_id=1, source_target_pairs={{0,8},{1,9},{2,10},{3,11},{4,12},{5,13},{6,14},{7,15},{8,0},{9,1},... | collective-permute-start | bytes 2752520 | tf_op jit(solution)/shard_map/ppermute | solution.py:63
  111.4 1.2 %collective-permute-start.23 = (f32[4,128]{1,0:T(4,128)S(1)}, f32[4,128]{1,0:T(4,128)S(1)}, u32[]{:S(2)}, u32[]{:S(2)}) collective-permute-start(f32[4,128]{1,0:T(4,128)S(1)} %get-tuple-element.49), channel_id=1, source_target_pairs={{0,8},{1,9},{2,10},{3,11},{4,12},{5,13},{6,14},{7,15},{8,0},{9,1},... | collective-permute-start | bytes 6152 | tf_op jit(solution)/shard_map/ppermute | solution.py:63

commit v11 on v10

--- a/solution.py
+++ b/solution.py
@@ -411,7 +411,10 @@
     )(core, acts, grads, *[pin(x) if i in pinned else x for i, x in enumerate(args)])
 
 
-def prepare_body(core_ref, ids_ref, acts_ref, grads_ref, keep_ref, away_ref):
+def prepare_body(core_ref, ids_in, acts_in, grads_in, keep_ref, away_ref, ids_ref, acts_ref, grads_ref, sems):
+    moves = bring([(acts_in, acts_ref), (grads_in, grads_ref), (ids_in, ids_ref)], sems)
+    for cp in moves:
+        cp.wait()
     first = core_ref[0] == 0
     for at, ref, w in ((0, acts_ref, HA), (HA, grads_ref, HG)):
         low, high = ref[:, 0:w], ref[:, w:2 * w]
@@ -430,12 +433,20 @@
     smem = pl.BlockSpec(memory_space=pltpu.SMEM)
     return pl.pallas_call(
         prepare_body,
-        in_specs=[smem, smem, vmem, vmem],
+        in_specs=[smem] + [pl.BlockSpec(memory_space=pl.ANY)] * 3,
         out_specs=[vmem, vmem],
         out_shape=[jax.ShapeDtypeStruct((4, ALLW), jnp.bfloat16)] * 2,
+        scratch_shapes=[
+            pltpu.SMEM((4,), jnp.int32),
+            pltpu.VMEM((4, FF), jnp.bfloat16),
+            pltpu.VMEM((4, D), jnp.bfloat16),
+            pltpu.SemaphoreType.DMA((3,)),
+        ],
         compiler_params=pltpu.CompilerParams(vmem_limit_bytes=4 << 20),
         cost_estimate=pl.CostEstimate(flops=0, bytes_accessed=720896, transcendentals=0),
-    )(core, val_ids, val_acts, val_grads)
+    )(core, *[
+        pltpu.with_memory_space_constraint(x, pltpu.HBM) for x in (val_ids, val_acts, val_grads)
+    ])
 
 
 def shards(hidden_acts, out_grads, val_acts, val_grads, val_ids):

time: 114 us -> 112 us (0.982)
  local copies, waits for them, and re-layouts: 3.66 us -> 1.27 us
    unnamed x11 -> x5, local copies, waits for them, and re-layouts: 2.9 us -> 0.51 us
where the time goes in v11:
time: 112 us; the launch traced here: 111 us
  Pallas kernels  47.4 us (42%)
  starting transfers between devices  29.8 us (27%)
  waiting for transfers between devices  29.1 us (26%)
  other arithmetic  2.76 us (2%)
  local copies, waits for them, and re-layouts  1.27 us (1%)
    pallas_call x5, Pallas kernels, local_call(): pl.pallas_call(body, in_specs=[pl.BlockSpec(memory_space=pltpu.SMEM)] + [...  30.6 us
    ppermute x16, waiting for transfers between devices, hop(): return lax.ppermute(x, AXES, ring_pairs(axes, step))  27.3 us
    ppermute x8, starting transfers between devices, swap(): return lax.ppermute(x, AXES, core_pairs())  18 us
    pallas_call x2, Pallas kernels, self_call(): pl.pallas_call(body, grid=(width // KC,), in_specs=[pl.BlockSpec((TOK, KC...  15.8 us
    ppermute x16, starting transfers between devices, hop(): return lax.ppermute(x, AXES, ring_pairs(axes, step))  11.9 us
  transfers between devices with their start and end apart: 24, of which 11 were waited for; matrix products, arithmetic and copies ran while one was open for 2% of the time, Pallas kernels for 35%

profile of v11, /device:TPU:1, one launch (start us, length us, event | category | flops | bytes accessed | tf_op | source)
XLA Modules:
  0.0 111.4 jit_solution(453544080432233519)
XLA Ops:
  0.6 1.0 shard_map.68
  1.6 1.5 %collective-permute-start = (bf16[4,11392]{1,0:T(4,128)(2,1)S(1)}, bf16[4,11392]{1,0:T(4,128)(2,1)S(1)}, u32[]{:S(2)}, u32[]{:S(2)}) collective-permute-start(bf16[4,11392]{1,0:T(4,128)(2,1)S(1)} %get-tuple-element.27), channel_id=1, source_target_pairs={{0,8},{1,9},{2,10},{3,11},{4,12},{5,13},{6,14},{7,15},{8,0},{9,1},... | collective-permute-start | bytes 273416 | tf_op jit(solution)/shard_map/ppermute | solution.py:63
  3.1 0.9 collective-permute-done
  4.1 0.1 fusion
  4.2 2.9 %collective-permute-start.2 = (bf16[8,11392]{1,0:T(8,128)(2,1)S(1)}, bf16[8,11392]{1,0:T(8,128)(2,1)S(1)}, u32[]{:S(2)}, u32[]{:S(2)}) collective-permute-start(bf16[8,11392]{1,0:T(8,128)(2,1)S(1)} %get-tuple-element.63), channel_id=1, source_target_pairs={{0,1},{1,0},{2,3},{3,2},{4,5},{5,4},{6,7},{7,6},{8,11},{9,10},{10,... | collective-permute-start | bytes 546824 | tf_op jit(solution)/shard_map/ppermute | solution.py:67
  7.1 3.8 %collective-permute-start.1 = (bf16[8,11392]{1,0:T(8,128)(2,1)S(1)}, bf16[8,11392]{1,0:T(8,128)(2,1)S(1)}, u32[]{:S(2)}, u32[]{:S(2)}) collective-permute-start(bf16[8,11392]{1,0:T(8,128)(2,1)S(1)} %get-tuple-element.63), channel_id=1, source_target_pairs={{0,16},{1,17},{2,18},{3,19},{4,20},{5,21},{6,22},{7,23},{8,56},{9,... | collective-permute-start | bytes 546824 | tf_op jit(solution)/shard_map/ppermute | solution.py:67
  11.0 2.9 %collective-permute-done.1 = bf16[8,11392]{1,0:T(8,128)(2,1)S(1)} collective-permute-done((bf16[8,11392]{1,0:T(8,128)(2,1)S(1)}, bf16[8,11392]{1,0:T(8,128)(2,1)S(1)}, u32[]{:S(2)}, u32[]{:S(2)}) %collective-permute-start.1) | collective-permute-done | bytes 182304 | tf_op jit(solution)/shard_map/ppermute | solution.py:67
  13.9 4.6 %collective-permute-done.3 = bf16[8,11392]{1,0:T(8,128)(2,1)S(1)} collective-permute-done((bf16[8,11392]{1,0:T(8,128)(2,1)S(1)}, bf16[8,11392]{1,0:T(8,128)(2,1)S(1)}, u32[]{:S(2)}, u32[]{:S(2)}) %collective-permute-start.3) | collective-permute-done | bytes 182304 | tf_op jit(solution)/shard_map/ppermute | solution.py:67
  18.6 0.1 pad_maximum_fusion.8.dep_ref
  18.7 2.6 %collective-permute-start.4 = (bf16[4,8,11392]{2,1,0:T(8,128)(2,1)S(1)}, bf16[4,8,11392]{2,1,0:T(8,128)(2,1)S(1)}, u32[]{:S(2)}, u32[]{:S(2)}) collective-permute-start(bf16[4,8,11392]{2,1,0:T(8,128)(2,1)S(1)} %pad_maximum_fusion.8.dep_ref), channel_id=1, source_target_pairs={{0,64},{1,65},{2,66},{3,67},{4,68},{5,69},{6,70},{7,71},{8,76},{9,... | collective-permute-start | bytes 2187272 | tf_op jit(solution)/shard_map/ppermute | solution.py:67
  21.3 5.6 %shard_map.69.refs_1_.first_ref = f32[512,256]{1,0:T(8,128)S(1)} custom-call(bf16[512,8192]{1,0:T(8,128)(2,1)} %grads.9, bf16[4,8,11392]{2,1,0:T(8,128)(2,1)S(1)} %pad_maximum_fusion.8.dep_ref), custom_call_target="tpu_custom_call" | custom-call | flops 2147483648 | bytes 8388608 | tf_op jit(solution)/shard_map/pallas_call | solution.py:146
  27.0 3.2 %collective-permute-done.4 = bf16[4,8,11392]{2,1,0:T(8,128)(2,1)S(1)} collective-permute-done((bf16[4,8,11392]{2,1,0:T(8,128)(2,1)S(1)}, bf16[4,8,11392]{2,1,0:T(8,128)(2,1)S(1)}, u32[]{:S(2)}, u32[]{:S(2)}) %collective-permute-start.4) | collective-permute-done | bytes 729120 | tf_op jit(solution)/shard_map/ppermute | solution.py:67
  30.5 0.1 slice_bitcast_fusion.2
  30.8 7.5 %collective-permute-done.7 = bf16[8,8,3712]{2,1,0:T(8,128)(2,1)S(1)} collective-permute-done((bf16[8,8,3712]{2,1,0:T(8,128)(2,1)S(1)}, bf16[8,8,3712]{2,1,0:T(8,128)(2,1)S(1)}, u32[]{:S(2)}, u32[]{:S(2)}) %collective-permute-start.7) | collective-permute-done | bytes 475168 | tf_op jit(solution)/shard_map/ppermute | solution.py:67
  38.2 0.1 fusion.1
  38.5 0.2 collective-permute-done.6
  38.6 0.1 fusion.2
  38.8 1.5 %collective-permute-start.10 = (bf16[2,8,8,3840]{3,2,1,0:T(8,128)(2,1)S(1)}, bf16[2,8,8,3840]{3,2,1,0:T(8,128)(2,1)S(1)}, u32[]{:S(2)}, u32[]{:S(2)}) collective-permute-start(bf16[2,8,8,3840]{3,2,1,0:T(8,128)(2,1)S(1)} %get-tuple-element.57.dep_ref.refs_2_.refs_3_), channel_id=1, source_target_pairs={{0,68},{1,69},{2,70},{3,71},{4,64},{5,65},{6,66},{7,67},{8,72},{9,... | collective-permute-start | bytes 2949128 | tf_op jit(solution)/shard_map/ppermute | solution.py:67
  40.3 0.2 maximum_maximum_fusion
  40.5 0.1 fusion.3
  40.8 4.6 %collective-permute-start.8 = (bf16[2,8,8,11392]{3,2,1,0:T(8,128)(2,1)S(1)}, bf16[2,8,8,11392]{3,2,1,0:T(8,128)(2,1)S(1)}, u32[]{:S(2)}, u32[]{:S(2)}) collective-permute-start(bf16[2,8,8,11392]{3,2,1,0:T(8,128)(2,1)S(1)} %maximum_maximum_fusion), channel_id=1, source_target_pairs={{0,8},{1,9},{2,10},{3,11},{4,12},{5,13},{6,14},{7,15},{8,0},{9,1},... | collective-permute-start | bytes 8749064 | tf_op jit(solution)/shard_map/ppermute | solution.py:63
  45.3 10.2 %shard_map.71.refs_3_.dep_ref = f32[4,4]{1,0:T(4,128)} custom-call(bf16[512,14336]{1,0:T(8,128)(2,1)} %acts.9, f32[512,256]{1,0:T(8,128)S(1)} %shard_map.69.refs_1_.first_ref, bf16[2,8,8,3840]{3,2,1,0:T(8,128)(2,1)S(1)} %get-tuple-element.57.dep_ref.refs_2_.refs_3_), custom_call_target="tpu_custom_call" | custom-call | flops 3758096384 | bytes 14680064 | tf_op jit(solution)/shard_map/pallas_call | solution.py:146
  55.5 0.2 pad_maximum_fusion.4.refs_2_
  55.7 0.2 pad_maximum_fusion.3.refs_1_
  56.0 0.2 pad_maximum_fusion.2.refs_0_
  56.2 0.2 pad_maximum_fusion.refs_0_
  56.4 0.5 copy-done
  56.8 2.5 %collective-permute-start.12 = (bf16[2,8,8,11392]{3,2,1,0:T(8,128)(2,1)S(1)}, bf16[2,8,8,11392]{3,2,1,0:T(8,128)(2,1)S(1)}, u32[]{:S(2)}, u32[]{:S(2)}) collective-permute-start(bf16[2,8,8,11392]{3,2,1,0:T(8,128)(2,1)S(1)} %shard_map.73), channel_id=1, source_target_pairs={{0,8},{1,9},{2,10},{3,11},{4,12},{5,13},{6,14},{7,15},{8,0},{9,1},... | collective-permute-start | bytes 8749064 | tf_op jit(solution)/shard_map/ppermute | solution.py:63
  59.3 0.1 slice.34
  59.8 5.9 %shard_map.74 = (f32[8,8,8,512]{3,2,1,0:T(8,128)S(1)}, f32[8,8,8,512]{3,2,1,0:T(8,128)S(1)}, f32[8,128]{1,0:T(8,128)S(1)}) custom-call(s32[1]{0:T(128)} %bitcast.core_ref, bf16[512,14336]{1,0:T(8,128)(2,1)} %acts.9, bf16[512,8192]{1,0:T(8,128)(2,1)} %grads.9, f32[4,4]{1,0:T(4,128)S(1)} %copy-done, bf16[2,8,8,3840]{3,2,1,0:T(8,128)(2,1)S(1)} %get-tuple-element.59.refs_0_, ...), custom_call_target="tpu_custom_call" | custom-call | flops 2952790016 | bytes 11534336 | tf_op jit(solution)/shard_map/pallas_call | solution.py:397
  65.7 6.5 %collective-permute-done.16.refs_8_ = bf16[2,2,8,8,1792]{4,3,2,1,0:T(8,128)(2,1)S(1)} collective-permute-done((bf16[2,2,8,8,1792]{4,3,2,1,0:T(8,128)(2,1)S(1)}, bf16[2,2,8,8,1792]{4,3,2,1,0:T(8,128)(2,1)S(1)}, u32[]{:S(2)}, u32[]{:S(2)}) %collective-permute-start.16) | collective-permute-done | bytes 917536 | tf_op jit(solution)/shard_map/ppermute | solution.py:67
  72.3 1.1 collective-permute-done.14.refs_2_
  73.4 0.2 pad_maximum_fusion.1.refs_0_
  73.7 4.4 %collective-permute-start.17 = (bf16[2,2,8,8,5632]{4,3,2,1,0:T(8,128)(2,1)S(1)}, bf16[2,2,8,8,5632]{4,3,2,1,0:T(8,128)(2,1)S(1)}, u32[]{:S(2)}, u32[]{:S(2)}) collective-permute-start(bf16[2,2,8,8,5632]{4,3,2,1,0:T(8,128)(2,1)S(1)} %shard_map.75), channel_id=1, source_target_pairs={{0,8},{1,9},{2,10},{3,11},{4,12},{5,13},{6,14},{7,15},{8,0},{9,1},... | collective-permute-start | bytes 8650760 | tf_op jit(solution)/shard_map/ppermute | solution.py:63
  78.1 0.1 slice.37
  78.4 0.3 collective-permute-start.21
  78.8 5.4 %shard_map.76 = (f32[8,8,8,512]{3,2,1,0:T(8,128)S(1)}, f32[8,8,8,512]{3,2,1,0:T(8,128)S(1)}, f32[256,512]{1,0:T(8,128)S(1)}, f32[256,512]{1,0:T(8,128)S(1)}) custom-call(s32[1]{0:T(128)} %bitcast.core_ref, bf16[512,14336]{1,0:T(8,128)(2,1)} %acts.9, bf16[512,8192]{1,0:T(8,128)(2,1)} %grads.9, bf16[2,8,8,3840]{3,2,1,0:T(8,128)(2,1)S(1)} %get-tuple-element.59.refs_0_, ...), custom_call_target="tpu_custom_call" | custom-call | tf_op jit(solution)/shard_map/pallas_call | solution.py:397
  84.2 6.9 %shard_map.77 = (f32[8,8,8,512]{3,2,1,0:T(8,128)S(1)}, f32[8,8,8,512]{3,2,1,0:T(8,128)S(1)}, f32[256,512]{1,0:T(8,128)S(1)}, f32[256,512]{1,0:T(8,128)S(1)}, f32[8,128]{1,0:T(8,128)S(1)}) custom-call(s32[1]{0:T(128)} %bitcast.core_ref, bf16[512,14336]{1,0:T(8,128)(2,1)} %acts.9, bf16[512,8192]{1,0:T(8,128)(2,1)} %grads.9, ...), custom_call_target="tpu_custom_call" | custom-call | tf_op jit(solution)/shard_map/pallas_call | solution.py:397
  91.1 1.1 collective-permute-done.19.refs_0_
  92.2 4.2 %collective-permute-start.20 = (bf16[2,2,8,8,2048]{4,3,2,1,0:T(8,128)(2,1)S(1)}, bf16[2,2,8,8,2048]{4,3,2,1,0:T(8,128)(2,1)S(1)}, u32[]{:S(2)}, u32[]{:S(2)}) collective-permute-start(bf16[2,2,8,8,2048]{4,3,2,1,0:T(8,128)(2,1)S(1)} %shard_map.79.refs_5_), channel_id=1, source_target_pairs={{0,8},{1,9},{2,10},{3,11},{4,12},{5,13},{6,14},{7,15},{8,0},{9,1},... | collective-permute-start | bytes 3145736 | tf_op jit(solution)/shard_map/ppermute | solution.py:63
  96.4 0.1 collective-permute-start.22
  96.5 0.4 collective-permute-start.18
  96.9 5.3 %shard_map.81 = (f32[8,8,8,512]{3,2,1,0:T(8,128)S(1)}, f32[8,8,8,512]{3,2,1,0:T(8,128)S(1)}, f32[256,512]{1,0:T(8,128)S(1)}, f32[256,512]{1,0:T(8,128)S(1)}, f32[512,128]{1,0:T(8,128)S(1)}) custom-call(s32[1]{0:T(128)} %bitcast.core_ref, bf16[512,14336]{1,0:T(8,128)(2,1)} %acts.9, bf16[512,8192]{1,0:T(8,128)(2,1)} %grads.9, ...), custom_call_target="tpu_custom_call" | custom-call | flops 2952790016 | bytes 11534336 | tf_op jit(solution)/shard_map/pallas_call | solution.py:397
  102.2 7.2 %shard_map.82 = (f32[4,512]{1,0:T(4,128)S(1)}, f32[4,128]{1,0:T(4,128)S(1)}) custom-call(s32[1]{0:T(128)} %bitcast.core_ref, bf16[512,14336]{1,0:T(8,128)(2,1)} %acts.9, bf16[512,8192]{1,0:T(8,128)(2,1)} %grads.9, bf16[2,8,8,11392]{3,2,1,0:T(8,128)(2,1)S(1)} %collective-permute-done.8.refs_4_.o0, ...), custom_call_target="tpu_custom_call" | custom-call | flops 4429185024 | bytes 11534336 | tf_op jit(solution)/shard_map/pallas_call | solution.py:397
  109.4 0.4 collective-permute-start.23
  109.8 0.8 collective-permute-done.23
  110.6 0.1 rsqrt_reduce_fusion
  110.8 0.7 broadcast_multiply_fusion
  (45 shorter events, 1.6 us)
Async XLA Ops:
  1.6 2.4 %collective-permute-start = (bf16[4,11392]{1,0:T(4,128)(2,1)S(1)}, bf16[4,11392]{1,0:T(4,128)(2,1)S(1)}, u32[]{:S(2)}, u32[]{:S(2)}) collective-permute-start(bf16[4,11392]{1,0:T(4,128)(2,1)S(1)} %get-tuple-element.27), channel_id=1, source_target_pairs={{0,8},{1,9},{2,10},{3,11},{4,12},{5,13},{6,14},{7,15},{8,0},{9,1},... | collective-permute-start | bytes 273416 | tf_op jit(solution)/shard_map/ppermute | solution.py:63
  4.2 6.8 %collective-permute-start.2 = (bf16[8,11392]{1,0:T(8,128)(2,1)S(1)}, bf16[8,11392]{1,0:T(8,128)(2,1)S(1)}, u32[]{:S(2)}, u32[]{:S(2)}) collective-permute-start(bf16[8,11392]{1,0:T(8,128)(2,1)S(1)} %get-tuple-element.63), channel_id=1, source_target_pairs={{0,1},{1,0},{2,3},{3,2},{4,5},{5,4},{6,7},{7,6},{8,11},{9,10},{10,... | collective-permute-start | bytes 546824 | tf_op jit(solution)/shard_map/ppermute | solution.py:67
  7.1 6.8 %collective-permute-start.1 = (bf16[8,11392]{1,0:T(8,128)(2,1)S(1)}, bf16[8,11392]{1,0:T(8,128)(2,1)S(1)}, u32[]{:S(2)}, u32[]{:S(2)}) collective-permute-start(bf16[8,11392]{1,0:T(8,128)(2,1)S(1)} %get-tuple-element.63), channel_id=1, source_target_pairs={{0,16},{1,17},{2,18},{3,19},{4,20},{5,21},{6,22},{7,23},{8,56},{9,... | collective-permute-start | bytes 546824 | tf_op jit(solution)/shard_map/ppermute | solution.py:67
  10.9 7.7 %collective-permute-start.3 = (bf16[8,11392]{1,0:T(8,128)(2,1)S(1)}, bf16[8,11392]{1,0:T(8,128)(2,1)S(1)}, u32[]{:S(2)}, u32[]{:S(2)}) collective-permute-start(bf16[8,11392]{1,0:T(8,128)(2,1)S(1)} %get-tuple-element.63), channel_id=1, source_target_pairs={{0,17},{1,16},{2,19},{3,18},{4,21},{5,20},{6,23},{7,22},{8,59},{9,... | collective-permute-start | bytes 546824 | tf_op jit(solution)/shard_map/ppermute | solution.py:67
  18.7 11.5 %collective-permute-start.4 = (bf16[4,8,11392]{2,1,0:T(8,128)(2,1)S(1)}, bf16[4,8,11392]{2,1,0:T(8,128)(2,1)S(1)}, u32[]{:S(2)}, u32[]{:S(2)}) collective-permute-start(bf16[4,8,11392]{2,1,0:T(8,128)(2,1)S(1)} %pad_maximum_fusion.8.dep_ref), channel_id=1, source_target_pairs={{0,64},{1,65},{2,66},{3,67},{4,68},{5,69},{6,70},{7,71},{8,76},{9,... | collective-permute-start | bytes 2187272 | tf_op jit(solution)/shard_map/ppermute | solution.py:67
  30.4 7.9 %collective-permute-start.7 = (bf16[8,8,3712]{2,1,0:T(8,128)(2,1)S(1)}, bf16[8,8,3712]{2,1,0:T(8,128)(2,1)S(1)}, u32[]{:S(2)}, u32[]{:S(2)}) collective-permute-start(bf16[8,8,3712]{2,1,0:T(8,128)(2,1)S(1)} %get-tuple-element.55), channel_id=1, source_target_pairs={{0,68},{1,69},{2,70},{3,71},{4,64},{5,65},{6,66},{7,67},{8,72},{9,... | collective-permute-start | bytes 1425416 | tf_op jit(solution)/shard_map/ppermute | solution.py:67
  30.6 8.1 %collective-permute-start.6 = (bf16[8,8,3840]{2,1,0:T(8,128)(2,1)S(1)}, bf16[8,8,3840]{2,1,0:T(8,128)(2,1)S(1)}, u32[]{:S(2)}, u32[]{:S(2)}) collective-permute-start(bf16[8,8,3840]{2,1,0:T(8,128)(2,1)S(1)} %get-tuple-element.52), channel_id=1, source_target_pairs={{0,48},{1,49},{2,50},{3,51},{4,52},{5,53},{6,54},{7,55},{8,24},{9,... | collective-permute-start | bytes 1474568 | tf_op jit(solution)/shard_map/ppermute | solution.py:67
  30.7 9.6 %collective-permute-start.5 = (bf16[8,8,3840]{2,1,0:T(8,128)(2,1)S(1)}, bf16[8,8,3840]{2,1,0:T(8,128)(2,1)S(1)}, u32[]{:S(2)}, u32[]{:S(2)}) collective-permute-start(bf16[8,8,3840]{2,1,0:T(8,128)(2,1)S(1)} %get-tuple-element.53), channel_id=1, source_target_pairs={{0,3},{1,2},{2,1},{3,0},{4,7},{5,6},{6,5},{7,4},{8,9},{9,8},{10,11... | collective-permute-start | bytes 1474568 | tf_op jit(solution)/shard_map/ppermute | solution.py:67
  38.4 17.2 %collective-permute-start.11 = (bf16[2,8,8,3712]{3,2,1,0:T(8,128)(2,1)S(1)}, bf16[2,8,8,3712]{3,2,1,0:T(8,128)(2,1)S(1)}, u32[]{:S(2)}, u32[]{:S(2)}) collective-permute-start(bf16[2,8,8,3712]{3,2,1,0:T(8,128)(2,1)S(1)} %get-tuple-element.61.refs_4_.refs_6_), channel_id=1, source_target_pairs={{0,3},{1,2},{2,1},{3,0},{4,7},{5,6},{6,5},{7,4},{8,9},{9,8},{10,11... | collective-permute-start | bytes 2850824 | tf_op jit(solution)/shard_map/ppermute | solution.py:67
  38.8 17.0 %collective-permute-start.10 = (bf16[2,8,8,3840]{3,2,1,0:T(8,128)(2,1)S(1)}, bf16[2,8,8,3840]{3,2,1,0:T(8,128)(2,1)S(1)}, u32[]{:S(2)}, u32[]{:S(2)}) collective-permute-start(bf16[2,8,8,3840]{3,2,1,0:T(8,128)(2,1)S(1)} %get-tuple-element.57.dep_ref.refs_2_.refs_3_), channel_id=1, source_target_pairs={{0,68},{1,69},{2,70},{3,71},{4,64},{5,65},{6,66},{7,67},{8,72},{9,... | collective-permute-start | bytes 2949128 | tf_op jit(solution)/shard_map/ppermute | solution.py:67
  40.7 15.3 %collective-permute-start.9 = (bf16[2,8,8,3840]{3,2,1,0:T(8,128)(2,1)S(1)}, bf16[2,8,8,3840]{3,2,1,0:T(8,128)(2,1)S(1)}, u32[]{:S(2)}, u32[]{:S(2)}) collective-permute-start(bf16[2,8,8,3840]{3,2,1,0:T(8,128)(2,1)S(1)} %get-tuple-element.59.refs_0_), channel_id=1, source_target_pairs={{0,48},{1,49},{2,50},{3,51},{4,52},{5,53},{6,54},{7,55},{8,24},{9,... | collective-permute-start | bytes 2949128 | tf_op jit(solution)/shard_map/ppermute | solution.py:67
  40.8 15.6 %collective-permute-start.8 = (bf16[2,8,8,11392]{3,2,1,0:T(8,128)(2,1)S(1)}, bf16[2,8,8,11392]{3,2,1,0:T(8,128)(2,1)S(1)}, u32[]{:S(2)}, u32[]{:S(2)}) collective-permute-start(bf16[2,8,8,11392]{3,2,1,0:T(8,128)(2,1)S(1)} %maximum_maximum_fusion), channel_id=1, source_target_pairs={{0,8},{1,9},{2,10},{3,11},{4,12},{5,13},{6,14},{7,15},{8,0},{9,1},... | collective-permute-start | bytes 8749064 | tf_op jit(solution)/shard_map/ppermute | solution.py:63
  56.1 0.7 copy-start
  56.8 16.8 %collective-permute-start.12 = (bf16[2,8,8,11392]{3,2,1,0:T(8,128)(2,1)S(1)}, bf16[2,8,8,11392]{3,2,1,0:T(8,128)(2,1)S(1)}, u32[]{:S(2)}, u32[]{:S(2)}) collective-permute-start(bf16[2,8,8,11392]{3,2,1,0:T(8,128)(2,1)S(1)} %shard_map.73), channel_id=1, source_target_pairs={{0,8},{1,9},{2,10},{3,11},{4,12},{5,13},{6,14},{7,15},{8,0},{9,1},... | collective-permute-start | bytes 8749064 | tf_op jit(solution)/shard_map/ppermute | solution.py:63
  59.4 14.0 %collective-permute-start.14 = (bf16[2,2,8,8,2048]{4,3,2,1,0:T(8,128)(2,1)S(1)}, bf16[2,2,8,8,2048]{4,3,2,1,0:T(8,128)(2,1)S(1)}, u32[]{:S(2)}, u32[]{:S(2)}) collective-permute-start(bf16[2,2,8,8,2048]{4,3,2,1,0:T(8,128)(2,1)S(1)} %slice.34), channel_id=1, source_target_pairs={{0,68},{1,69},{2,70},{3,71},{4,64},{5,65},{6,66},{7,67},{8,72},{9,... | collective-permute-start | bytes 3145736 | tf_op jit(solution)/shard_map/ppermute | solution.py:67
  59.6 12.6 %collective-permute-start.16 = (bf16[2,2,8,8,1792]{4,3,2,1,0:T(8,128)(2,1)S(1)}, bf16[2,2,8,8,1792]{4,3,2,1,0:T(8,128)(2,1)S(1)}, u32[]{:S(2)}, u32[]{:S(2)}) collective-permute-start(bf16[2,2,8,8,1792]{4,3,2,1,0:T(8,128)(2,1)S(1)} %slice.36), channel_id=1, source_target_pairs={{0,48},{1,49},{2,50},{3,51},{4,52},{5,53},{6,54},{7,55},{8,24},{9,... | collective-permute-start | bytes 2752520 | tf_op jit(solution)/shard_map/ppermute | solution.py:67
  59.7 12.6 %collective-permute-start.15 = (bf16[2,2,8,8,1792]{4,3,2,1,0:T(8,128)(2,1)S(1)}, bf16[2,2,8,8,1792]{4,3,2,1,0:T(8,128)(2,1)S(1)}, u32[]{:S(2)}, u32[]{:S(2)}) collective-permute-start(bf16[2,2,8,8,1792]{4,3,2,1,0:T(8,128)(2,1)S(1)} %slice.35), channel_id=1, source_target_pairs={{0,3},{1,2},{2,1},{3,0},{4,7},{5,6},{6,5},{7,4},{8,9},{9,8},{10,11... | collective-permute-start | bytes 2752520 | tf_op jit(solution)/shard_map/ppermute | solution.py:67
  73.7 10.5 %collective-permute-start.17 = (bf16[2,2,8,8,5632]{4,3,2,1,0:T(8,128)(2,1)S(1)}, bf16[2,2,8,8,5632]{4,3,2,1,0:T(8,128)(2,1)S(1)}, u32[]{:S(2)}, u32[]{:S(2)}) collective-permute-start(bf16[2,2,8,8,5632]{4,3,2,1,0:T(8,128)(2,1)S(1)} %shard_map.75), channel_id=1, source_target_pairs={{0,8},{1,9},{2,10},{3,11},{4,12},{5,13},{6,14},{7,15},{8,0},{9,1},... | collective-permute-start | bytes 8650760 | tf_op jit(solution)/shard_map/ppermute | solution.py:63
  78.2 14.0 %collective-permute-start.19 = (bf16[2,2,8,8,2048]{4,3,2,1,0:T(8,128)(2,1)S(1)}, bf16[2,2,8,8,2048]{4,3,2,1,0:T(8,128)(2,1)S(1)}, u32[]{:S(2)}, u32[]{:S(2)}) collective-permute-start(bf16[2,2,8,8,2048]{4,3,2,1,0:T(8,128)(2,1)S(1)} %slice.37), channel_id=1, source_target_pairs={{0,3},{1,2},{2,1},{3,0},{4,7},{5,6},{6,5},{7,4},{8,9},{9,8},{10,11... | collective-permute-start | bytes 3145736 | tf_op jit(solution)/shard_map/ppermute | solution.py:67
  78.4 18.0 %collective-permute-start.21 = (bf16[2,2,8,8,1920]{4,3,2,1,0:T(8,128)(2,1)S(1)}, bf16[2,2,8,8,1920]{4,3,2,1,0:T(8,128)(2,1)S(1)}, u32[]{:S(2)}, u32[]{:S(2)}) collective-permute-start(bf16[2,2,8,8,1920]{4,3,2,1,0:T(8,128)(2,1)S(1)} %slice.38), channel_id=1, source_target_pairs={{0,48},{1,49},{2,50},{3,51},{4,52},{5,53},{6,54},{7,55},{8,24},{9,... | collective-permute-start | bytes 2949128 | tf_op jit(solution)/shard_map/ppermute | solution.py:67
  78.7 17.8 %collective-permute-start.13 = (bf16[2,2,8,8,1792]{4,3,2,1,0:T(8,128)(2,1)S(1)}, bf16[2,2,8,8,1792]{4,3,2,1,0:T(8,128)(2,1)S(1)}, u32[]{:S(2)}, u32[]{:S(2)}) collective-permute-start(bf16[2,2,8,8,1792]{4,3,2,1,0:T(8,128)(2,1)S(1)} %slice.33), channel_id=1, source_target_pairs={{0,68},{1,69},{2,70},{3,71},{4,64},{5,65},{6,66},{7,67},{8,72},{9,... | collective-permute-start | bytes 2752520 | tf_op jit(solution)/shard_map/ppermute | solution.py:67
  92.2 10.0 %collective-permute-start.20 = (bf16[2,2,8,8,2048]{4,3,2,1,0:T(8,128)(2,1)S(1)}, bf16[2,2,8,8,2048]{4,3,2,1,0:T(8,128)(2,1)S(1)}, u32[]{:S(2)}, u32[]{:S(2)}) collective-permute-start(bf16[2,2,8,8,2048]{4,3,2,1,0:T(8,128)(2,1)S(1)} %shard_map.79.refs_5_), channel_id=1, source_target_pairs={{0,8},{1,9},{2,10},{3,11},{4,12},{5,13},{6,14},{7,15},{8,0},{9,1},... | collective-permute-start | bytes 3145736 | tf_op jit(solution)/shard_map/ppermute | solution.py:63
  96.4 5.8 %collective-permute-start.22 = (bf16[2,2,8,8,1920]{4,3,2,1,0:T(8,128)(2,1)S(1)}, bf16[2,2,8,8,1920]{4,3,2,1,0:T(8,128)(2,1)S(1)}, u32[]{:S(2)}, u32[]{:S(2)}) collective-permute-start(bf16[2,2,8,8,1920]{4,3,2,1,0:T(8,128)(2,1)S(1)} %shard_map.80.refs_8_), channel_id=1, source_target_pairs={{0,8},{1,9},{2,10},{3,11},{4,12},{5,13},{6,14},{7,15},{8,0},{9,1},... | collective-permute-start | bytes 2949128 | tf_op jit(solution)/shard_map/ppermute | solution.py:63
  96.5 5.7 %collective-permute-start.18 = (bf16[2,2,8,8,1792]{4,3,2,1,0:T(8,128)(2,1)S(1)}, bf16[2,2,8,8,1792]{4,3,2,1,0:T(8,128)(2,1)S(1)}, u32[]{:S(2)}, u32[]{:S(2)}) collective-permute-start(bf16[2,2,8,8,1792]{4,3,2,1,0:T(8,128)(2,1)S(1)} %shard_map.78.refs_2_), channel_id=1, source_target_pairs={{0,8},{1,9},{2,10},{3,11},{4,12},{5,13},{6,14},{7,15},{8,0},{9,1},... | collective-permute-start | bytes 2752520 | tf_op jit(solution)/shard_map/ppermute | solution.py:63
  109.4 1.2 %collective-permute-start.23 = (f32[4,128]{1,0:T(4,128)S(1)}, f32[4,128]{1,0:T(4,128)S(1)}, u32[]{:S(2)}, u32[]{:S(2)}) collective-permute-start(f32[4,128]{1,0:T(4,128)S(1)} %get-tuple-element.49), channel_id=1, source_target_pairs={{0,8},{1,9},{2,10},{3,11},{4,12},{5,13},{6,14},{7,15},{8,0},{9,1},... | collective-permute-start | bytes 6152 | tf_op jit(solution)/shard_map/ppermute | solution.py:63

commit v12 on v11

--- a/solution.py
+++ b/solution.py
@@ -181,12 +181,12 @@
     (("a", C1, 0, C2A), ("g", 0, C2A, C2G)),
     (("g", C2G, 0, C3G),),
 )
-SETAT = ((0, 0, 0), (2048, 1792, 1792))
-SETW = ((2048, 1792, 1792), (C1 - 2048, C2 - 1792, C3 - 1792))
+SETAT = ((0, 0, 0), (1792, 1792, 1792))
+SETW = ((1792, 1792, 1792), (C1 - 1792, C2 - 1792, C3 - 1792))
 SETS = (
-    ((("a", 0, 0, 2048),), (("a", C1, 0, 1792),), (("g", C2G, 0, 1792),)),
+    ((("a", 0, 0, 1792),), (("a", C1, 0, 1792),), (("g", C2G, 0, 1792),)),
     (
-        (("a", 2048, 0, C1 - 2048),),
+        (("a", 1792, 0, C1 - 1792),),
         (("a", C1 + 1792, 0, C2A - 1792), ("g", 0, C2A - 1792, C2G)),
         (("g", C2G + 1792, 0, C3G - 1792),),
     ),

time: 112 us -> 112 us (level)
  no operation moved by 1% of the time
where the time goes in v12:
time: 112 us
  Pallas kernels  47.4 us (42%)
  starting transfers between devices  30.9 us (28%)
  waiting for transfers between devices  28.5 us (25%)
  other arithmetic  2.74 us (2%)
  local copies, waits for them, and re-layouts  1.27 us (1%)
    pallas_call x5, Pallas kernels, local_call(): pl.pallas_call(body, in_specs=[pl.BlockSpec(memory_space=pltpu.SMEM)] + [...  30.6 us
    ppermute x16, waiting for transfers between devices, hop(): return lax.ppermute(x, AXES, ring_pairs(axes, step))  26.4 us
    ppermute x8, starting transfers between devices, swap(): return lax.ppermute(x, AXES, core_pairs())  19 us
    pallas_call x2, Pallas kernels, self_call(): pl.pallas_call(body, grid=(width // KC,), in_specs=[pl.BlockSpec((TOK, KC...  15.8 us
    ppermute x16, starting transfers between devices, hop(): return lax.ppermute(x, AXES, ring_pairs(axes, step))  11.9 us
  transfers between devices with their start and end apart: 24, of which 11 were waited for; matrix products, arithmetic and copies ran while one was open for 2% of the time, Pallas kernels for 35%

profile of v12, /device:TPU:1, one launch (start us, length us, event | category | flops | bytes accessed | tf_op | source)
XLA Modules:
  0.0 111.8 jit_solution(16360998850171775906)
XLA Ops:
  0.6 1.0 shard_map.68
  1.6 1.5 %collective-permute-start = (bf16[4,11392]{1,0:T(4,128)(2,1)S(1)}, bf16[4,11392]{1,0:T(4,128)(2,1)S(1)}, u32[]{:S(2)}, u32[]{:S(2)}) collective-permute-start(bf16[4,11392]{1,0:T(4,128)(2,1)S(1)} %get-tuple-element.27), channel_id=1, source_target_pairs={{0,8},{1,9},{2,10},{3,11},{4,12},{5,13},{6,14},{7,15},{8,0},{9,1},... | collective-permute-start | bytes 273416 | tf_op jit(solution)/shard_map/ppermute | solution.py:63
  3.1 0.9 collective-permute-done
  4.1 0.1 fusion
  4.2 2.9 %collective-permute-start.2 = (bf16[8,11392]{1,0:T(8,128)(2,1)S(1)}, bf16[8,11392]{1,0:T(8,128)(2,1)S(1)}, u32[]{:S(2)}, u32[]{:S(2)}) collective-permute-start(bf16[8,11392]{1,0:T(8,128)(2,1)S(1)} %get-tuple-element.63), channel_id=1, source_target_pairs={{0,1},{1,0},{2,3},{3,2},{4,5},{5,4},{6,7},{7,6},{8,11},{9,10},{10,... | collective-permute-start | bytes 546824 | tf_op jit(solution)/shard_map/ppermute | solution.py:67
  7.1 3.8 %collective-permute-start.1 = (bf16[8,11392]{1,0:T(8,128)(2,1)S(1)}, bf16[8,11392]{1,0:T(8,128)(2,1)S(1)}, u32[]{:S(2)}, u32[]{:S(2)}) collective-permute-start(bf16[8,11392]{1,0:T(8,128)(2,1)S(1)} %get-tuple-element.63), channel_id=1, source_target_pairs={{0,16},{1,17},{2,18},{3,19},{4,20},{5,21},{6,22},{7,23},{8,56},{9,... | collective-permute-start | bytes 546824 | tf_op jit(solution)/shard_map/ppermute | solution.py:67
  10.9 0.1 constant_dynamic-update-slice_fusion.4
  11.0 2.9 %collective-permute-done.1 = bf16[8,11392]{1,0:T(8,128)(2,1)S(1)} collective-permute-done((bf16[8,11392]{1,0:T(8,128)(2,1)S(1)}, bf16[8,11392]{1,0:T(8,128)(2,1)S(1)}, u32[]{:S(2)}, u32[]{:S(2)}) %collective-permute-start.1) | collective-permute-done | bytes 182304 | tf_op jit(solution)/shard_map/ppermute | solution.py:67
  13.9 4.6 %collective-permute-done.3 = bf16[8,11392]{1,0:T(8,128)(2,1)S(1)} collective-permute-done((bf16[8,11392]{1,0:T(8,128)(2,1)S(1)}, bf16[8,11392]{1,0:T(8,128)(2,1)S(1)}, u32[]{:S(2)}, u32[]{:S(2)}) %collective-permute-start.3) | collective-permute-done | bytes 182304 | tf_op jit(solution)/shard_map/ppermute | solution.py:67
  18.6 0.1 pad_maximum_fusion.8.dep_ref
  18.7 2.6 %collective-permute-start.4 = (bf16[4,8,11392]{2,1,0:T(8,128)(2,1)S(1)}, bf16[4,8,11392]{2,1,0:T(8,128)(2,1)S(1)}, u32[]{:S(2)}, u32[]{:S(2)}) collective-permute-start(bf16[4,8,11392]{2,1,0:T(8,128)(2,1)S(1)} %pad_maximum_fusion.8.dep_ref), channel_id=1, source_target_pairs={{0,64},{1,65},{2,66},{3,67},{4,68},{5,69},{6,70},{7,71},{8,76},{9,... | collective-permute-start | bytes 2187272 | tf_op jit(solution)/shard_map/ppermute | solution.py:67
  21.3 5.6 %shard_map.69.refs_1_.first_ref = f32[512,256]{1,0:T(8,128)S(1)} custom-call(bf16[512,8192]{1,0:T(8,128)(2,1)} %grads.9, bf16[4,8,11392]{2,1,0:T(8,128)(2,1)S(1)} %pad_maximum_fusion.8.dep_ref), custom_call_target="tpu_custom_call" | custom-call | flops 2147483648 | bytes 8388608 | tf_op jit(solution)/shard_map/pallas_call | solution.py:146
  27.0 3.2 %collective-permute-done.4 = bf16[4,8,11392]{2,1,0:T(8,128)(2,1)S(1)} collective-permute-done((bf16[4,8,11392]{2,1,0:T(8,128)(2,1)S(1)}, bf16[4,8,11392]{2,1,0:T(8,128)(2,1)S(1)}, u32[]{:S(2)}, u32[]{:S(2)}) %collective-permute-start.4) | collective-permute-done | bytes 729120 | tf_op jit(solution)/shard_map/ppermute | solution.py:67
  30.5 0.1 slice_bitcast_fusion.2
  30.8 7.5 %collective-permute-done.7 = bf16[8,8,3712]{2,1,0:T(8,128)(2,1)S(1)} collective-permute-done((bf16[8,8,3712]{2,1,0:T(8,128)(2,1)S(1)}, bf16[8,8,3712]{2,1,0:T(8,128)(2,1)S(1)}, u32[]{:S(2)}, u32[]{:S(2)}) %collective-permute-start.7) | collective-permute-done | bytes 475168 | tf_op jit(solution)/shard_map/ppermute | solution.py:67
  38.2 0.1 fusion.1
  38.5 0.2 collective-permute-done.6
  38.6 0.1 fusion.2
  38.8 1.5 %collective-permute-start.10 = (bf16[2,8,8,3840]{3,2,1,0:T(8,128)(2,1)S(1)}, bf16[2,8,8,3840]{3,2,1,0:T(8,128)(2,1)S(1)}, u32[]{:S(2)}, u32[]{:S(2)}) collective-permute-start(bf16[2,8,8,3840]{3,2,1,0:T(8,128)(2,1)S(1)} %get-tuple-element.57.dep_ref.refs_2_.refs_3_), channel_id=1, source_target_pairs={{0,68},{1,69},{2,70},{3,71},{4,64},{5,65},{6,66},{7,67},{8,72},{9,... | collective-permute-start | bytes 2949128 | tf_op jit(solution)/shard_map/ppermute | solution.py:67
  40.3 0.2 maximum_maximum_fusion
  40.5 0.1 fusion.3
  40.8 4.6 %collective-permute-start.8 = (bf16[2,8,8,11392]{3,2,1,0:T(8,128)(2,1)S(1)}, bf16[2,8,8,11392]{3,2,1,0:T(8,128)(2,1)S(1)}, u32[]{:S(2)}, u32[]{:S(2)}) collective-permute-start(bf16[2,8,8,11392]{3,2,1,0:T(8,128)(2,1)S(1)} %maximum_maximum_fusion), channel_id=1, source_target_pairs={{0,8},{1,9},{2,10},{3,11},{4,12},{5,13},{6,14},{7,15},{8,0},{9,1},... | collective-permute-start | bytes 8749064 | tf_op jit(solution)/shard_map/ppermute | solution.py:63
  45.3 10.2 %shard_map.71.refs_3_.dep_ref = f32[4,4]{1,0:T(4,128)} custom-call(bf16[512,14336]{1,0:T(8,128)(2,1)} %acts.9, f32[512,256]{1,0:T(8,128)S(1)} %shard_map.69.refs_1_.first_ref, bf16[2,8,8,3840]{3,2,1,0:T(8,128)(2,1)S(1)} %get-tuple-element.57.dep_ref.refs_2_.refs_3_), custom_call_target="tpu_custom_call" | custom-call | flops 3758096384 | bytes 14680064 | tf_op jit(solution)/shard_map/pallas_call | solution.py:146
  55.5 0.2 pad_maximum_fusion.4.refs_2_
  55.7 0.2 pad_maximum_fusion.3.refs_1_
  56.0 0.2 pad_maximum_fusion.2.refs_0_
  56.2 0.2 pad_maximum_fusion.refs_0_
  56.4 0.5 copy-done
  56.8 2.5 %collective-permute-start.12 = (bf16[2,8,8,11392]{3,2,1,0:T(8,128)(2,1)S(1)}, bf16[2,8,8,11392]{3,2,1,0:T(8,128)(2,1)S(1)}, u32[]{:S(2)}, u32[]{:S(2)}) collective-permute-start(bf16[2,8,8,11392]{3,2,1,0:T(8,128)(2,1)S(1)} %shard_map.73), channel_id=1, source_target_pairs={{0,8},{1,9},{2,10},{3,11},{4,12},{5,13},{6,14},{7,15},{8,0},{9,1},... | collective-permute-start | bytes 8749064 | tf_op jit(solution)/shard_map/ppermute | solution.py:63
  59.8 5.9 %shard_map.74 = (f32[8,8,8,512]{3,2,1,0:T(8,128)S(1)}, f32[8,8,8,512]{3,2,1,0:T(8,128)S(1)}, f32[8,128]{1,0:T(8,128)S(1)}) custom-call(s32[1]{0:T(128)} %bitcast.core_ref, bf16[512,14336]{1,0:T(8,128)(2,1)} %acts.9, bf16[512,8192]{1,0:T(8,128)(2,1)} %grads.9, f32[4,4]{1,0:T(4,128)S(1)} %copy-done, bf16[2,8,8,3840]{3,2,1,0:T(8,128)(2,1)S(1)} %get-tuple-element.59.refs_0_, ...), custom_call_target="tpu_custom_call" | custom-call | flops 2952790016 | bytes 11534336 | tf_op jit(solution)/shard_map/pallas_call | solution.py:397
  65.7 6.4 %collective-permute-done.14.refs_2_ = bf16[2,2,8,8,1792]{4,3,2,1,0:T(8,128)(2,1)S(1)} collective-permute-done((bf16[2,2,8,8,1792]{4,3,2,1,0:T(8,128)(2,1)S(1)}, bf16[2,2,8,8,1792]{4,3,2,1,0:T(8,128)(2,1)S(1)}, u32[]{:S(2)}, u32[]{:S(2)}) %collective-permute-start.14) | collective-permute-done | bytes 917536 | tf_op jit(solution)/shard_map/ppermute | solution.py:67
  72.1 0.1 collective-permute-done.16.refs_8_
  72.3 0.2 pad_maximum_fusion.1.refs_0_
  72.5 5.4 %collective-permute-start.17 = (bf16[2,2,8,8,5376]{4,3,2,1,0:T(8,128)(2,1)S(1)}, bf16[2,2,8,8,5376]{4,3,2,1,0:T(8,128)(2,1)S(1)}, u32[]{:S(2)}, u32[]{:S(2)}) collective-permute-start(bf16[2,2,8,8,5376]{4,3,2,1,0:T(8,128)(2,1)S(1)} %shard_map.75), channel_id=1, source_target_pairs={{0,8},{1,9},{2,10},{3,11},{4,12},{5,13},{6,14},{7,15},{8,0},{9,1},... | collective-permute-start | bytes 8257544 | tf_op jit(solution)/shard_map/ppermute | solution.py:63
  77.9 0.1 slice.33
  78.1 0.1 slice.37
  78.3 0.3 collective-permute-start.19
  78.7 5.2 %shard_map.76 = (f32[8,8,8,512]{3,2,1,0:T(8,128)S(1)}, f32[8,8,8,512]{3,2,1,0:T(8,128)S(1)}, f32[256,512]{1,0:T(8,128)S(1)}, f32[256,512]{1,0:T(8,128)S(1)}) custom-call(s32[1]{0:T(128)} %bitcast.core_ref, bf16[512,14336]{1,0:T(8,128)(2,1)} %acts.9, bf16[512,8192]{1,0:T(8,128)(2,1)} %grads.9, bf16[2,8,8,3840]{3,2,1,0:T(8,128)(2,1)S(1)} %get-tuple-element.59.refs_0_, ...), custom_call_target="tpu_custom_call" | custom-call | tf_op jit(solution)/shard_map/pallas_call | solution.py:397
  84.0 6.8 %shard_map.77 = (f32[8,8,8,512]{3,2,1,0:T(8,128)S(1)}, f32[8,8,8,512]{3,2,1,0:T(8,128)S(1)}, f32[256,512]{1,0:T(8,128)S(1)}, f32[256,512]{1,0:T(8,128)S(1)}, f32[8,128]{1,0:T(8,128)S(1)}) custom-call(s32[1]{0:T(128)} %bitcast.core_ref, bf16[512,14336]{1,0:T(8,128)(2,1)} %acts.9, bf16[512,8192]{1,0:T(8,128)(2,1)} %grads.9, ...), custom_call_target="tpu_custom_call" | custom-call | tf_op jit(solution)/shard_map/pallas_call | solution.py:397
  90.8 1.3 %collective-permute-done.13.refs_0_ = bf16[2,2,8,8,2048]{4,3,2,1,0:T(8,128)(2,1)S(1)} collective-permute-done((bf16[2,2,8,8,2048]{4,3,2,1,0:T(8,128)(2,1)S(1)}, bf16[2,2,8,8,2048]{4,3,2,1,0:T(8,128)(2,1)S(1)}, u32[]{:S(2)}, u32[]{:S(2)}) %collective-permute-start.13) | collective-permute-done | bytes 1048608 | tf_op jit(solution)/shard_map/ppermute | solution.py:67
  92.1 4.0 %collective-permute-start.18 = (bf16[2,2,8,8,2048]{4,3,2,1,0:T(8,128)(2,1)S(1)}, bf16[2,2,8,8,2048]{4,3,2,1,0:T(8,128)(2,1)S(1)}, u32[]{:S(2)}, u32[]{:S(2)}) collective-permute-start(bf16[2,2,8,8,2048]{4,3,2,1,0:T(8,128)(2,1)S(1)} %shard_map.78.refs_2_), channel_id=1, source_target_pairs={{0,8},{1,9},{2,10},{3,11},{4,12},{5,13},{6,14},{7,15},{8,0},{9,1},... | collective-permute-start | bytes 3145736 | tf_op jit(solution)/shard_map/ppermute | solution.py:63
  96.1 0.5 collective-permute-start.20
  96.5 0.5 collective-permute-start.22
  97.1 5.4 %shard_map.81 = (f32[8,8,8,512]{3,2,1,0:T(8,128)S(1)}, f32[8,8,8,512]{3,2,1,0:T(8,128)S(1)}, f32[256,512]{1,0:T(8,128)S(1)}, f32[256,512]{1,0:T(8,128)S(1)}, f32[512,128]{1,0:T(8,128)S(1)}) custom-call(s32[1]{0:T(128)} %bitcast.core_ref, bf16[512,14336]{1,0:T(8,128)(2,1)} %acts.9, bf16[512,8192]{1,0:T(8,128)(2,1)} %grads.9, ...), custom_call_target="tpu_custom_call" | custom-call | flops 2952790016 | bytes 11534336 | tf_op jit(solution)/shard_map/pallas_call | solution.py:397
  102.5 7.3 %shard_map.82 = (f32[4,512]{1,0:T(4,128)S(1)}, f32[4,128]{1,0:T(4,128)S(1)}) custom-call(s32[1]{0:T(128)} %bitcast.core_ref, bf16[512,14336]{1,0:T(8,128)(2,1)} %acts.9, bf16[512,8192]{1,0:T(8,128)(2,1)} %grads.9, bf16[2,8,8,11392]{3,2,1,0:T(8,128)(2,1)S(1)} %collective-permute-done.8.refs_4_.o0, ...), custom_call_target="tpu_custom_call" | custom-call | flops 4429185024 | bytes 11534336 | tf_op jit(solution)/shard_map/pallas_call | solution.py:397
  109.9 1.1 %collective-permute-done.23 = f32[4,128]{1,0:T(4,128)S(1)} collective-permute-done((f32[4,128]{1,0:T(4,128)S(1)}, f32[4,128]{1,0:T(4,128)S(1)}, u32[]{:S(2)}, u32[]{:S(2)}) %collective-permute-start.23) | collective-permute-done | bytes 2080 | tf_op jit(solution)/shard_map/ppermute | solution.py:63
  111.0 0.1 rsqrt_reduce_fusion
  111.2 0.7 broadcast_multiply_fusion
  (45 shorter events, 1.6 us)
Async XLA Ops:
  1.6 2.4 %collective-permute-start = (bf16[4,11392]{1,0:T(4,128)(2,1)S(1)}, bf16[4,11392]{1,0:T(4,128)(2,1)S(1)}, u32[]{:S(2)}, u32[]{:S(2)}) collective-permute-start(bf16[4,11392]{1,0:T(4,128)(2,1)S(1)} %get-tuple-element.27), channel_id=1, source_target_pairs={{0,8},{1,9},{2,10},{3,11},{4,12},{5,13},{6,14},{7,15},{8,0},{9,1},... | collective-permute-start | bytes 273416 | tf_op jit(solution)/shard_map/ppermute | solution.py:63
  4.2 6.8 %collective-permute-start.2 = (bf16[8,11392]{1,0:T(8,128)(2,1)S(1)}, bf16[8,11392]{1,0:T(8,128)(2,1)S(1)}, u32[]{:S(2)}, u32[]{:S(2)}) collective-permute-start(bf16[8,11392]{1,0:T(8,128)(2,1)S(1)} %get-tuple-element.63), channel_id=1, source_target_pairs={{0,1},{1,0},{2,3},{3,2},{4,5},{5,4},{6,7},{7,6},{8,11},{9,10},{10,... | collective-permute-start | bytes 546824 | tf_op jit(solution)/shard_map/ppermute | solution.py:67
  7.1 6.8 %collective-permute-start.1 = (bf16[8,11392]{1,0:T(8,128)(2,1)S(1)}, bf16[8,11392]{1,0:T(8,128)(2,1)S(1)}, u32[]{:S(2)}, u32[]{:S(2)}) collective-permute-start(bf16[8,11392]{1,0:T(8,128)(2,1)S(1)} %get-tuple-element.63), channel_id=1, source_target_pairs={{0,16},{1,17},{2,18},{3,19},{4,20},{5,21},{6,22},{7,23},{8,56},{9,... | collective-permute-start | bytes 546824 | tf_op jit(solution)/shard_map/ppermute | solution.py:67
  10.9 7.7 %collective-permute-start.3 = (bf16[8,11392]{1,0:T(8,128)(2,1)S(1)}, bf16[8,11392]{1,0:T(8,128)(2,1)S(1)}, u32[]{:S(2)}, u32[]{:S(2)}) collective-permute-start(bf16[8,11392]{1,0:T(8,128)(2,1)S(1)} %get-tuple-element.63), channel_id=1, source_target_pairs={{0,17},{1,16},{2,19},{3,18},{4,21},{5,20},{6,23},{7,22},{8,59},{9,... | collective-permute-start | bytes 546824 | tf_op jit(solution)/shard_map/ppermute | solution.py:67
  18.7 11.5 %collective-permute-start.4 = (bf16[4,8,11392]{2,1,0:T(8,128)(2,1)S(1)}, bf16[4,8,11392]{2,1,0:T(8,128)(2,1)S(1)}, u32[]{:S(2)}, u32[]{:S(2)}) collective-permute-start(bf16[4,8,11392]{2,1,0:T(8,128)(2,1)S(1)} %pad_maximum_fusion.8.dep_ref), channel_id=1, source_target_pairs={{0,64},{1,65},{2,66},{3,67},{4,68},{5,69},{6,70},{7,71},{8,76},{9,... | collective-permute-start | bytes 2187272 | tf_op jit(solution)/shard_map/ppermute | solution.py:67
  30.4 7.9 %collective-permute-start.7 = (bf16[8,8,3712]{2,1,0:T(8,128)(2,1)S(1)}, bf16[8,8,3712]{2,1,0:T(8,128)(2,1)S(1)}, u32[]{:S(2)}, u32[]{:S(2)}) collective-permute-start(bf16[8,8,3712]{2,1,0:T(8,128)(2,1)S(1)} %get-tuple-element.55), channel_id=1, source_target_pairs={{0,68},{1,69},{2,70},{3,71},{4,64},{5,65},{6,66},{7,67},{8,72},{9,... | collective-permute-start | bytes 1425416 | tf_op jit(solution)/shard_map/ppermute | solution.py:67
  30.6 8.1 %collective-permute-start.6 = (bf16[8,8,3840]{2,1,0:T(8,128)(2,1)S(1)}, bf16[8,8,3840]{2,1,0:T(8,128)(2,1)S(1)}, u32[]{:S(2)}, u32[]{:S(2)}) collective-permute-start(bf16[8,8,3840]{2,1,0:T(8,128)(2,1)S(1)} %get-tuple-element.52), channel_id=1, source_target_pairs={{0,48},{1,49},{2,50},{3,51},{4,52},{5,53},{6,54},{7,55},{8,24},{9,... | collective-permute-start | bytes 1474568 | tf_op jit(solution)/shard_map/ppermute | solution.py:67
  30.7 9.6 %collective-permute-start.5 = (bf16[8,8,3840]{2,1,0:T(8,128)(2,1)S(1)}, bf16[8,8,3840]{2,1,0:T(8,128)(2,1)S(1)}, u32[]{:S(2)}, u32[]{:S(2)}) collective-permute-start(bf16[8,8,3840]{2,1,0:T(8,128)(2,1)S(1)} %get-tuple-element.53), channel_id=1, source_target_pairs={{0,3},{1,2},{2,1},{3,0},{4,7},{5,6},{6,5},{7,4},{8,9},{9,8},{10,11... | collective-permute-start | bytes 1474568 | tf_op jit(solution)/shard_map/ppermute | solution.py:67
  38.4 17.2 %collective-permute-start.11 = (bf16[2,8,8,3712]{3,2,1,0:T(8,128)(2,1)S(1)}, bf16[2,8,8,3712]{3,2,1,0:T(8,128)(2,1)S(1)}, u32[]{:S(2)}, u32[]{:S(2)}) collective-permute-start(bf16[2,8,8,3712]{3,2,1,0:T(8,128)(2,1)S(1)} %get-tuple-element.61.refs_4_.refs_6_), channel_id=1, source_target_pairs={{0,3},{1,2},{2,1},{3,0},{4,7},{5,6},{6,5},{7,4},{8,9},{9,8},{10,11... | collective-permute-start | bytes 2850824 | tf_op jit(solution)/shard_map/ppermute | solution.py:67
  38.8 17.0 %collective-permute-start.10 = (bf16[2,8,8,3840]{3,2,1,0:T(8,128)(2,1)S(1)}, bf16[2,8,8,3840]{3,2,1,0:T(8,128)(2,1)S(1)}, u32[]{:S(2)}, u32[]{:S(2)}) collective-permute-start(bf16[2,8,8,3840]{3,2,1,0:T(8,128)(2,1)S(1)} %get-tuple-element.57.dep_ref.refs_2_.refs_3_), channel_id=1, source_target_pairs={{0,68},{1,69},{2,70},{3,71},{4,64},{5,65},{6,66},{7,67},{8,72},{9,... | collective-permute-start | bytes 2949128 | tf_op jit(solution)/shard_map/ppermute | solution.py:67
  40.7 15.3 %collective-permute-start.9 = (bf16[2,8,8,3840]{3,2,1,0:T(8,128)(2,1)S(1)}, bf16[2,8,8,3840]{3,2,1,0:T(8,128)(2,1)S(1)}, u32[]{:S(2)}, u32[]{:S(2)}) collective-permute-start(bf16[2,8,8,3840]{3,2,1,0:T(8,128)(2,1)S(1)} %get-tuple-element.59.refs_0_), channel_id=1, source_target_pairs={{0,48},{1,49},{2,50},{3,51},{4,52},{5,53},{6,54},{7,55},{8,24},{9,... | collective-permute-start | bytes 2949128 | tf_op jit(solution)/shard_map/ppermute | solution.py:67
  40.8 15.6 %collective-permute-start.8 = (bf16[2,8,8,11392]{3,2,1,0:T(8,128)(2,1)S(1)}, bf16[2,8,8,11392]{3,2,1,0:T(8,128)(2,1)S(1)}, u32[]{:S(2)}, u32[]{:S(2)}) collective-permute-start(bf16[2,8,8,11392]{3,2,1,0:T(8,128)(2,1)S(1)} %maximum_maximum_fusion), channel_id=1, source_target_pairs={{0,8},{1,9},{2,10},{3,11},{4,12},{5,13},{6,14},{7,15},{8,0},{9,1},... | collective-permute-start | bytes 8749064 | tf_op jit(solution)/shard_map/ppermute | solution.py:63
  56.1 0.7 copy-start
  56.8 15.7 %collective-permute-start.12 = (bf16[2,8,8,11392]{3,2,1,0:T(8,128)(2,1)S(1)}, bf16[2,8,8,11392]{3,2,1,0:T(8,128)(2,1)S(1)}, u32[]{:S(2)}, u32[]{:S(2)}) collective-permute-start(bf16[2,8,8,11392]{3,2,1,0:T(8,128)(2,1)S(1)} %shard_map.73), channel_id=1, source_target_pairs={{0,8},{1,9},{2,10},{3,11},{4,12},{5,13},{6,14},{7,15},{8,0},{9,1},... | collective-permute-start | bytes 8749064 | tf_op jit(solution)/shard_map/ppermute | solution.py:63
  59.5 12.6 %collective-permute-start.14 = (bf16[2,2,8,8,1792]{4,3,2,1,0:T(8,128)(2,1)S(1)}, bf16[2,2,8,8,1792]{4,3,2,1,0:T(8,128)(2,1)S(1)}, u32[]{:S(2)}, u32[]{:S(2)}) collective-permute-start(bf16[2,2,8,8,1792]{4,3,2,1,0:T(8,128)(2,1)S(1)} %slice.34), channel_id=1, source_target_pairs={{0,68},{1,69},{2,70},{3,71},{4,64},{5,65},{6,66},{7,67},{8,72},{9,... | collective-permute-start | bytes 2752520 | tf_op jit(solution)/shard_map/ppermute | solution.py:67
  59.6 12.6 %collective-permute-start.16 = (bf16[2,2,8,8,1792]{4,3,2,1,0:T(8,128)(2,1)S(1)}, bf16[2,2,8,8,1792]{4,3,2,1,0:T(8,128)(2,1)S(1)}, u32[]{:S(2)}, u32[]{:S(2)}) collective-permute-start(bf16[2,2,8,8,1792]{4,3,2,1,0:T(8,128)(2,1)S(1)} %slice.36), channel_id=1, source_target_pairs={{0,48},{1,49},{2,50},{3,51},{4,52},{5,53},{6,54},{7,55},{8,24},{9,... | collective-permute-start | bytes 2752520 | tf_op jit(solution)/shard_map/ppermute | solution.py:67
  59.7 12.6 %collective-permute-start.15 = (bf16[2,2,8,8,1792]{4,3,2,1,0:T(8,128)(2,1)S(1)}, bf16[2,2,8,8,1792]{4,3,2,1,0:T(8,128)(2,1)S(1)}, u32[]{:S(2)}, u32[]{:S(2)}) collective-permute-start(bf16[2,2,8,8,1792]{4,3,2,1,0:T(8,128)(2,1)S(1)} %slice.35), channel_id=1, source_target_pairs={{0,3},{1,2},{2,1},{3,0},{4,7},{5,6},{6,5},{7,4},{8,9},{9,8},{10,11... | collective-permute-start | bytes 2752520 | tf_op jit(solution)/shard_map/ppermute | solution.py:67
  72.5 11.5 %collective-permute-start.17 = (bf16[2,2,8,8,5376]{4,3,2,1,0:T(8,128)(2,1)S(1)}, bf16[2,2,8,8,5376]{4,3,2,1,0:T(8,128)(2,1)S(1)}, u32[]{:S(2)}, u32[]{:S(2)}) collective-permute-start(bf16[2,2,8,8,5376]{4,3,2,1,0:T(8,128)(2,1)S(1)} %shard_map.75), channel_id=1, source_target_pairs={{0,8},{1,9},{2,10},{3,11},{4,12},{5,13},{6,14},{7,15},{8,0},{9,1},... | collective-permute-start | bytes 8257544 | tf_op jit(solution)/shard_map/ppermute | solution.py:63
  78.0 14.0 %collective-permute-start.13 = (bf16[2,2,8,8,2048]{4,3,2,1,0:T(8,128)(2,1)S(1)}, bf16[2,2,8,8,2048]{4,3,2,1,0:T(8,128)(2,1)S(1)}, u32[]{:S(2)}, u32[]{:S(2)}) collective-permute-start(bf16[2,2,8,8,2048]{4,3,2,1,0:T(8,128)(2,1)S(1)} %slice.33), channel_id=1, source_target_pairs={{0,68},{1,69},{2,70},{3,71},{4,64},{5,65},{6,66},{7,67},{8,72},{9,... | collective-permute-start | bytes 3145736 | tf_op jit(solution)/shard_map/ppermute | solution.py:67
  78.3 17.8 %collective-permute-start.19 = (bf16[2,2,8,8,2048]{4,3,2,1,0:T(8,128)(2,1)S(1)}, bf16[2,2,8,8,2048]{4,3,2,1,0:T(8,128)(2,1)S(1)}, u32[]{:S(2)}, u32[]{:S(2)}) collective-permute-start(bf16[2,2,8,8,2048]{4,3,2,1,0:T(8,128)(2,1)S(1)} %slice.37), channel_id=1, source_target_pairs={{0,3},{1,2},{2,1},{3,0},{4,7},{5,6},{6,5},{7,4},{8,9},{9,8},{10,11... | collective-permute-start | bytes 3145736 | tf_op jit(solution)/shard_map/ppermute | solution.py:67
  78.6 17.9 %collective-permute-start.21 = (bf16[2,2,8,8,1920]{4,3,2,1,0:T(8,128)(2,1)S(1)}, bf16[2,2,8,8,1920]{4,3,2,1,0:T(8,128)(2,1)S(1)}, u32[]{:S(2)}, u32[]{:S(2)}) collective-permute-start(bf16[2,2,8,8,1920]{4,3,2,1,0:T(8,128)(2,1)S(1)} %slice.38), channel_id=1, source_target_pairs={{0,48},{1,49},{2,50},{3,51},{4,52},{5,53},{6,54},{7,55},{8,24},{9,... | collective-permute-start | bytes 2949128 | tf_op jit(solution)/shard_map/ppermute | solution.py:67
  92.1 10.4 %collective-permute-start.18 = (bf16[2,2,8,8,2048]{4,3,2,1,0:T(8,128)(2,1)S(1)}, bf16[2,2,8,8,2048]{4,3,2,1,0:T(8,128)(2,1)S(1)}, u32[]{:S(2)}, u32[]{:S(2)}) collective-permute-start(bf16[2,2,8,8,2048]{4,3,2,1,0:T(8,128)(2,1)S(1)} %shard_map.78.refs_2_), channel_id=1, source_target_pairs={{0,8},{1,9},{2,10},{3,11},{4,12},{5,13},{6,14},{7,15},{8,0},{9,1},... | collective-permute-start | bytes 3145736 | tf_op jit(solution)/shard_map/ppermute | solution.py:63
  96.1 6.4 %collective-permute-start.20 = (bf16[2,2,8,8,2048]{4,3,2,1,0:T(8,128)(2,1)S(1)}, bf16[2,2,8,8,2048]{4,3,2,1,0:T(8,128)(2,1)S(1)}, u32[]{:S(2)}, u32[]{:S(2)}) collective-permute-start(bf16[2,2,8,8,2048]{4,3,2,1,0:T(8,128)(2,1)S(1)} %shard_map.79.refs_5_), channel_id=1, source_target_pairs={{0,8},{1,9},{2,10},{3,11},{4,12},{5,13},{6,14},{7,15},{8,0},{9,1},... | collective-permute-start | bytes 3145736 | tf_op jit(solution)/shard_map/ppermute | solution.py:63
  96.5 5.9 %collective-permute-start.22 = (bf16[2,2,8,8,1920]{4,3,2,1,0:T(8,128)(2,1)S(1)}, bf16[2,2,8,8,1920]{4,3,2,1,0:T(8,128)(2,1)S(1)}, u32[]{:S(2)}, u32[]{:S(2)}) collective-permute-start(bf16[2,2,8,8,1920]{4,3,2,1,0:T(8,128)(2,1)S(1)} %shard_map.80.refs_8_), channel_id=1, source_target_pairs={{0,8},{1,9},{2,10},{3,11},{4,12},{5,13},{6,14},{7,15},{8,0},{9,1},... | collective-permute-start | bytes 2949128 | tf_op jit(solution)/shard_map/ppermute | solution.py:63
  109.8 1.2 %collective-permute-start.23 = (f32[4,128]{1,0:T(4,128)S(1)}, f32[4,128]{1,0:T(4,128)S(1)}, u32[]{:S(2)}, u32[]{:S(2)}) collective-permute-start(f32[4,128]{1,0:T(4,128)S(1)} %get-tuple-element.49), channel_id=1, source_target_pairs={{0,8},{1,9},{2,10},{3,11},{4,12},{5,13},{6,14},{7,15},{8,0},{9,1},... | collective-permute-start | bytes 6152 | tf_op jit(solution)/shard_map/ppermute | solution.py:63
